TPU v7x, 32 devices: a whole 2x2x4 slice. The times are simulated.
32 devices in a mesh: front: 4 (over x, core), grp: 8 (over z, y).
Axes of the slice: x: 2, y: 2, z: 4, core: 2. Of those that a mesh axis runs over, the one named last changes fastest.
Arguments:
- front_in: bfloat16 [4, 8192, 8192], P('front', None, 'grp'), may hold values from -6 to 6
- panel_inverse: float32 [4, 2, 256, 256], P('front'), may hold values from -2 to 2, as said below
- tile_mask: int32 [4, 32, 32], P('front', None, 'grp'), may hold values 0 or 1
- tile_map: int32 [4, 8, 4], P('front', 'grp'), may hold values from 0 to 127, as said below
Outputs:
- front_out: bfloat16 [4, 8192, 8192], P('front', None, 'grp')
- parent_tiles: float32 [128, 256, 256], P(('front', 'grp'))
Inputs may be any that keep to these rules, and one draw needn't show every extreme that they name: `panel_inverse`: lower triangular, with a positive diagonal. `tile_map`: entry s names device s // 4 of the mesh (front slowest), parent front s // 32. The 4 tiles of one front and one index of grp go to exactly 2 tiles each of 2 distinct parent fronts. Of all tiles from fronts' devices with the same grp index that go to one parent front, no two go to the same device of that parent's group.
All inputs are finite; a program needn't handle non-finite values. No bound on the sum of `tile_mask` on one device may be relied on, other than what follows from the above.
Results may differ from a plain program's by a relative error of at most 0.006.
Values may be sent and summed in bfloat16 or wider, within the bound.
No kernel may reach another device: no remote copies, remote signals or barrier semaphores. Data moves between devices by JAX's collectives and lax.ppermute only.
A program may use at most 192 MiB of HBM per device.

v0:
```python
import functools

import jax
import jax.numpy as jnp
from jax import lax
from jax.experimental import pallas as pl
from jax.experimental.pallas import tpu as pltpu
from jax.sharding import PartitionSpec as P

TILE = 256
CHAINS = 2
VMEM_LIMIT = 16 * 1024 * 1024
UPDATE_LIMIT = 32 * 1024 * 1024
HBM = pl.BlockSpec(memory_space=pltpu.HBM)
VMEM = pl.BlockSpec(memory_space=pltpu.VMEM)
SMEM = pl.BlockSpec(memory_space=pltpu.SMEM)


def ring_order(n_grp):
    depth = 4 if n_grp % 4 == 0 and n_grp >= 8 else 1
    width = n_grp // depth
    if depth == 1:
        return list(range(n_grp))
    order = [z * width for z in range(depth)]
    for number, z in enumerate(reversed(range(depth))):
        ys = range(1, width) if number % 2 == 0 else range(width - 1, 0, -1)
        order += [z * width + y for y in ys]
    return order


def routes(n_grp):
    if n_grp == 8:
        climb = [(g, (g + 2) % n_grp) for g in range(n_grp)]
        cross = [(g, g ^ 1) for g in range(n_grp)]
        rules = [[0] * n_grp, [0] * n_grp]
        rules[0][1] = rules[0][n_grp - 1] = rules[1][1] = 1
        return [climb, cross], rules
    cycle = ring_order(n_grp)
    ring = [(g, cycle[(d + 1) % n_grp]) for d, g in enumerate(cycle)]
    return [ring, [(b, a) for a, b in ring]], [[0] * n_grp, [1] * n_grp]


def travel(perms, rules, lists, n_grp, tiles):
    got = []
    missing = {(g, tile) for g in range(n_grp) for tile in range(1, tiles)}
    while missing:
        e = len(got)
        now = []
        for s in (0, 1):
            arrival = [0] * n_grp
            for g, target in perms[s]:
                if g == 0 and e < len(lists[s]):
                    arrival[target] = lists[s][e]
                elif e >= CHAINS:
                    arrival[target] = got[e - CHAINS][rules[s][g]][g]
            now.append(arrival)
            missing -= set(enumerate(arrival))
        got.append(now)
    return got


def delays(perms, rules, n_grp):
    result = [[None] * n_grp, [None] * n_grp]
    for s in (0, 1):
        lists = [[], []]
        lists[s] = [1]
        for e, now in enumerate(travel(perms, rules, lists, n_grp, 2)):
            for arrival in now:
                for g in range(n_grp):
                    if arrival[g] and result[s][g] is None:
                        result[s][g] = e
    return result


def stream_plan(perms, rules, n_grp, tiles, cols_dev, rows_out):
    hops = delays(perms, rules, n_grp)
    picks = [[], []]
    bottom = [tiles - 1 - r for r in range(rows_out)]
    heads = [bottom[0::2], bottom[1::2]]

    def shorter():
        return 0 if len(heads[0] + picks[0]) <= len(heads[1] + picks[1]) else 1

    rest = [(n // cols_dev, n) for n in range(1, tiles) if n not in bottom]
    for g, tile in rest:
        if g and hops[0][g] != hops[1][g]:
            picks[0 if hops[0][g] < hops[1][g] else 1].append((g, tile))
    for g, tile in rest:
        if g and hops[0][g] == hops[1][g]:
            picks[shorter()].append((g, tile))
    for s in (0, 1):
        picks[s].sort(key=lambda item: (-hops[s][item[0]], item[1]))
    for g, tile in rest:
        if g == 0:
            picks[shorter()].append((g, tile))
    return [heads[s] + [tile for _, tile in picks[s]] for s in (0, 1)]


def in_hbm(x):
    return pltpu.with_memory_space_constraint(x, pltpu.HBM)


def split2(x):
    hi = x.astype(jnp.bfloat16)
    return hi, (x - hi.astype(jnp.float32)).astype(jnp.bfloat16)


def dot(a, b):
    return jnp.dot(a, b, preferred_element_type=jnp.float32)


def factor_kernel(tiles, head, mask, front, *refs):
    count = len(tiles)
    if head:
        inverse, outs, (parts, one, blocks, sems, top, top_sem) = refs[0], refs[1 : count + 1], refs[count + 1 :]
    else:
        parts, one, outs, (blocks, sems) = refs[0], refs[1], refs[2 : count + 2], refs[count + 2 :]
    copies = [
        pltpu.make_async_copy(
            front.at[pl.ds(tile * TILE, TILE), pl.ds(0, 2 * TILE)], blocks.at[n], sems.at[n]
        )
        for n, tile in enumerate(tiles)
    ]
    if head:
        top_copy = pltpu.make_async_copy(front.at[pl.ds(TILE, TILE), pl.ds(0, TILE)], top, top_sem)
        top_copy.start()
    for copy in copies:
        copy.start()

    def first_of(x):
        return (dot(x, parts[1]) + dot(x, parts[0])).astype(jnp.bfloat16)

    if head:
        for which in range(2):
            hi, low = split2(inverse[which].T)
            parts[2 * which] = hi
            parts[2 * which + 1] = low
        top_copy.wait()
        one[...] = first_of(top[...]).astype(jnp.float32).T.astype(jnp.bfloat16)
    for begin in range(0, len(tiles), 2):
        group = list(range(begin, min(begin + 2, len(tiles))))
        for n in group:
            copies[n].wait()
        firsts = first_of(jnp.concatenate([blocks[n, :, :TILE] for n in group], axis=0))
        updates = dot(firsts, one[...])
        works = []
        for place, n in enumerate(group):
            keep = mask[tiles[n] : tiles[n] + 1, 1:2] > 0
            update = updates[place * TILE : (place + 1) * TILE]
            works.append(blocks[n, :, TILE:].astype(jnp.float32) - jnp.where(keep, update, 0.0))
        high, low = split2(jnp.concatenate(works, axis=0))
        seconds = (dot(low, parts[2]) + dot(high, parts[3]) + dot(high, parts[2])).astype(jnp.bfloat16)
        for place, n in enumerate(group):
            span = slice(place * TILE, (place + 1) * TILE)
            empty = jnp.zeros((TILE, TILE), jnp.bfloat16)
            outs[n][:, :TILE] = firsts[span] if tiles[n] > 0 else empty
            outs[n][:, TILE:] = seconds[span] if tiles[n] > 1 else empty


def factor(front, mask, tiles, inverse=None, parts=None):
    head = parts is None
    count = len(tiles)
    out_shape = [jax.ShapeDtypeStruct((TILE, 2 * TILE), jnp.bfloat16)] * count
    scratch = [pltpu.VMEM((count, TILE, 2 * TILE), jnp.bfloat16), pltpu.SemaphoreType.DMA((count,))]
    if head:
        out_shape += [
            jax.ShapeDtypeStruct((4, TILE, TILE), jnp.bfloat16),
            jax.ShapeDtypeStruct((TILE, TILE), jnp.bfloat16),
        ]
        scratch += [pltpu.VMEM((TILE, TILE), jnp.bfloat16), pltpu.SemaphoreType.DMA(())]
    operands = (inverse,) if head else parts
    return pl.pallas_call(
        functools.partial(factor_kernel, tuple(tiles), head),
        out_shape=out_shape,
        in_specs=[VMEM, HBM] + [VMEM] * len(operands),
        out_specs=[VMEM] * len(out_shape),
        scratch_shapes=scratch,
        compiler_params=pltpu.CompilerParams(vmem_limit_bytes=VMEM_LIMIT),
        cost_estimate=pl.CostEstimate(
            flops=12 * count * TILE**3, bytes_accessed=4 * count * TILE * 2 * TILE, transcendentals=0
        ),
        name="factor",
    )(mask, in_hbm(front), *operands)


def own_kernel(choices, sources, cols_dev, rows_out, mask, targets, me, front, *refs):
    blocks, (own, bottom, panels, old, sems, old_sem) = refs[:sources], refs[sources:]
    tiles = front.shape[0] // TILE
    width = front.shape[1]

    def copy(part, source):
        return pltpu.make_async_copy(blocks[source], panels.at[part], sems.at[part])

    old_copy = pltpu.make_async_copy(front.at[pl.ds((tiles - rows_out) * TILE, rows_out * TILE)], old, old_sem)
    old_copy.start()
    for part, options in enumerate(choices):
        for g, source in enumerate(options):
            pl.when(me[0] == g)(lambda part=part, source=source: copy(part, source).start())
    lane = lax.broadcasted_iota(jnp.int32, (rows_out * TILE, 128), 1)
    digits = jnp.zeros((rows_out * TILE, 128), jnp.int32)
    for number in range(cols_dev * rows_out):
        target = targets[number]
        digits = jnp.where(lane == 2 * number, target >> 5, digits)
        digits = jnp.where(lane == 2 * number + 1, target & 31, digits)
    bottom[:, width:] = digits.astype(jnp.float32).astype(jnp.bfloat16)
    for part, options in enumerate(choices):
        copy(part, options[0]).wait()
    for c in range(cols_dev):
        own[:, c * TILE : (c + 1) * TILE] = panels[c].astype(jnp.float32).T.astype(jnp.bfloat16)
    old_copy.wait()
    for r in range(rows_out):
        row, rows, panel = tiles - rows_out + r, slice(r * TILE, (r + 1) * TILE), panels.at[cols_dev + r]
        for c in range(cols_dev):
            span = slice(c * TILE, (c + 1) * TILE)
            change = jnp.where(mask[row, c] > 0, dot(panel[...], own[:, span]), 0.0)
            bottom[rows, span] = (old[rows, span].astype(jnp.float32) - change).astype(jnp.bfloat16)

        @pl.when(me[0] == 0)
        def _():
            bottom[rows, : 2 * TILE] = panel[...]


def own_panels(mask, targets, me, front, blocks, choices, rows_out):
    width = front.shape[1]
    parts = len(choices)
    return pl.pallas_call(
        functools.partial(own_kernel, choices, len(blocks), width // TILE, rows_out),
        out_shape=[
            jax.ShapeDtypeStruct((2 * TILE, width), jnp.bfloat16),
            jax.ShapeDtypeStruct((rows_out * TILE, width + 128), jnp.bfloat16),
        ],
        in_specs=[SMEM, SMEM, SMEM, HBM] + [HBM] * len(blocks),
        out_specs=[VMEM, VMEM],
        scratch_shapes=[
            pltpu.VMEM((parts, TILE, 2 * TILE), jnp.bfloat16),
            pltpu.VMEM((rows_out * TILE, width), jnp.bfloat16),
            pltpu.SemaphoreType.DMA((parts,)),
            pltpu.SemaphoreType.DMA(()),
        ],
        compiler_params=pltpu.CompilerParams(vmem_limit_bytes=VMEM_LIMIT),
        cost_estimate=pl.CostEstimate(
            flops=2 * rows_out * TILE * width * 2 * TILE,
            bytes_accessed=4 * parts * TILE * 2 * TILE,
            transcendentals=0,
        ),
        name="own_panels",
    )(mask, targets, me, in_hbm(front), *[in_hbm(block) for block in blocks])


def update_kernel(numbers, cols_dev, start, table, mask, me, own, front, *refs):
    count = len(numbers)
    blocks = refs[:count]
    out, panels, old, new, listed, panel_sems, in_sems, out_sems = refs[-8:]

    def place(row):
        return pl.ds(pl.multiple_of(row * TILE, TILE), TILE)

    def fetch(n, spot):
        return pltpu.make_async_copy(blocks[n], panels.at[spot], panel_sems.at[spot])

    def load(row, spot):
        return pltpu.make_async_copy(front.at[place(row)], old.at[spot], in_sems.at[spot])

    def store(row, spot):
        return pltpu.make_async_copy(new.at[spot], out.at[place(row)], out_sems.at[spot])

    spot = jnp.int32(0)
    for n, number in enumerate(numbers):
        row = table[me[0], number]

        def begin(n=n, row=row, spot=spot):
            listed[spot] = row
            fetch(n, spot).start()
            load(row, spot).start()

        pl.when(row > 0)(begin)
        spot = spot + (row > 0).astype(jnp.int32)
    total = spot
    listed[total] = 0
    if start:
        here = pl.ds(0, TILE)
        top_in = pltpu.make_async_copy(front.at[here], new.at[count], in_sems.at[count])
        top_out = pltpu.make_async_copy(new.at[count], out.at[here], out_sems.at[count])
        top_in.start()
        top_in.wait()
        top_out.start()

    @pl.loop(0, (total + 1) // 2)
    def _(pair):
        first = 2 * pair
        both = first + 1 < total

        def ready(spot):
            fetch(0, spot).wait()
            load(0, spot).wait()

        ready(first)
        pl.when(both)(lambda: ready(first + 1))
        panel = panels[pl.ds(first, 2)].reshape(2 * TILE, 2 * TILE)
        for c in range(cols_dev):
            span = slice(c * TILE, (c + 1) * TILE)
            change = dot(panel, own[:, span])
            for h in (0, 1):
                keep = mask[listed[first + h], c] > 0
                part = jnp.where(keep, change[h * TILE : (h + 1) * TILE], 0.0)
                before = old[first + h, :, span].astype(jnp.float32)
                new[first + h, :, span] = (before - part).astype(jnp.bfloat16)

        @pl.when(me[0] == 0)
        def _():
            for h in (0, 1):
                new[first + h, :, :TILE] = panels[first + h, :, :TILE]

                @pl.when(listed[first + h] > 1)
                def _():
                    new[first + h, :, TILE : 2 * TILE] = panels[first + h, :, TILE:]

        store(listed[first], first).start()
        pl.when(both)(lambda: store(listed[first + 1], first + 1).start())

    @pl.loop(0, total)
    def _(spot):
        store(0, spot).wait()

    if start:
        top_out.wait()


def update(table, mask, me, own, front, numbers, blocks, base=None):
    width = front.shape[1]
    count = len(numbers)
    room = count + count % 2
    operands = [table, mask, me, own, in_hbm(front), *[in_hbm(block) for block in blocks]]
    in_specs = [SMEM, SMEM, SMEM, VMEM, HBM] + [HBM] * count
    aliases = {}
    if base is not None:
        aliases = {len(operands): 0}
        operands.append(in_hbm(base))
        in_specs.append(HBM)
    return pl.pallas_call(
        functools.partial(update_kernel, tuple(numbers), width // TILE, base is None),
        out_shape=jax.ShapeDtypeStruct(front.shape, jnp.bfloat16),
        in_specs=in_specs,
        out_specs=HBM,
        scratch_shapes=[
            pltpu.VMEM((room, TILE, 2 * TILE), jnp.bfloat16),
            pltpu.VMEM((room, TILE, width), jnp.bfloat16),
            pltpu.VMEM((room + 1, TILE, width), jnp.bfloat16),
            pltpu.SMEM((room + 1,), jnp.int32),
            pltpu.SemaphoreType.DMA((room,)),
            pltpu.SemaphoreType.DMA((room + 1,)),
            pltpu.SemaphoreType.DMA((room + 1,)),
        ],
        input_output_aliases=aliases,
        compiler_params=pltpu.CompilerParams(vmem_limit_bytes=UPDATE_LIMIT),
        cost_estimate=pl.CostEstimate(
            flops=2 * count * TILE * width * 2 * TILE, bytes_accessed=4 * count * TILE * width, transcendentals=0
        ),
        name="update",
    )(*operands)


def after(values, *others):
    return lax.optimization_barrier((tuple(values), others))[0]


def one_of(g, members):
    result = g == members[0]
    for member in members[1:]:
        result = result | (g == member)
    return result


def shards(front_in, panel_inverse, tile_mask, tile_map):
    front = front_in[0]
    width = front.shape[1]
    tiles = front.shape[0] // TILE
    cols_dev = width // TILE
    inverse = panel_inverse[0]
    mask = tile_mask[0]
    targets = tile_map[0, 0]
    contrib = targets.shape[0]
    rows_out = contrib // cols_dev
    n_grp = lax.axis_size("grp")
    n_dev = n_grp * lax.axis_size("front")
    slots_dev = n_grp // 2
    g = lax.axis_index("grp")
    me = jnp.reshape(g, (1,)).astype(jnp.int32)
    root = g == 0

    perms, rules = routes(n_grp)
    lists = stream_plan(perms, rules, n_grp, tiles, cols_dev, rows_out)
    got = travel(perms, rules, lists, n_grp, tiles)
    events = len(got)
    longest = max(len(lists[0]), len(lists[1]))

    order = [(e, lists[s][e]) for e in range(longest) for s in (0, 1) if e < len(lists[s])] + [(longest, 0)]
    cuts = [0, 2, 6] + list(range(14, len(order) - 2, 8)) + [len(order)]
    made, parts, where_made = [], None, {}

    def make(e, turn):
        nonlocal parts
        while len(made) < len(cuts) - 1:
            begin, end = cuts[len(made)], cuts[len(made) + 1]
            if order[begin][0] > max(e + 1, e + 2 if begin > 2 else 0):
                break
            names = [tile for _, tile in order[begin:end]]
            for n, tile in enumerate(names):
                where_made[tile] = (len(made), n)
            if parts is None:
                *made_now, parts, one = factor(front, mask, names, inverse=inverse)
                parts = (parts, one)
            else:
                made_now = factor(front, mask, names, parts=after(parts, *turn))
            made.append(made_now)

    make(-2, ())
    odd = [[n for n in range(n_grp) if rules[s][n] != rules[s][0]] for s in (0, 1)]
    others = [one_of(g, odd[s]) if odd[s] else None for s in (0, 1)]
    scalars = [value for value in (root, *others) if value is not None]
    held, turns, turn = [], [], ()
    for e in range(events):
        values = []
        for s in (0, 1):
            value = None
            if e >= CHAINS:
                value = held[e - CHAINS][rules[s][0]]
                if others[s] is not None:
                    value = jnp.where(others[s], held[e - CHAINS][1 - rules[s][0]], value)
            if e < len(lists[s]):
                which, n = where_made[lists[s][e]]
                value = made[which][n] if value is None else jnp.where(root, made[which][n], value)
            values.append(value)
        turn = after(values, *turn, *(scalars if e == 0 else ()))
        turns.append(turn)
        held.append([lax.ppermute(turn[s], "grp", perms[s]) for s in (0, 1)])
        make(e, turn)
        if e + 1 < events and e + 1 >= CHAINS:
            held[e + 1 - CHAINS] = list(after(held[e + 1 - CHAINS], *turn))
    table = []
    for n in range(n_grp):
        line = []
        for now in got:
            for arrival in now:
                line.append(arrival[n] if arrival[n] not in line else 0)
        table.append(line)
    rows = jnp.asarray(table, jnp.int32)

    blocks, names, ready = [], {}, 0

    def choice(tile, n):
        nonlocal ready
        if n == 0:
            name = (-1, tile)
            which, place = where_made[tile]
            block = made[which][place]
        else:
            name = divmod(table[n].index(tile), 2)
            ready = max(ready, name[0])
            block = held[name[0]][name[1]]
        if name not in names:
            names[name] = len(blocks)
            blocks.append(block)
        return names[name]

    choices = [[choice(n * cols_dev + c, n) for n in range(n_grp)] for c in range(cols_dev)]
    choices += [[choice(tiles - rows_out + r, n) for n in range(n_grp)] for r in range(rows_out)]
    own, bottom = own_panels(mask, targets, me, front, blocks, choices, rows_out)

    piece = TILE // n_dev
    pieces = jnp.transpose(bottom.reshape(rows_out, n_dev, piece, width + 128), (1, 0, 2, 3))
    arrived = lax.all_to_all(pieces, ("front", "grp"), split_axis=0, concat_axis=0, tiled=True)

    def parents(arrived):
        digits = arrived[:, 0, 0, width : width + 2 * contrib].astype(jnp.int32).reshape(n_dev * contrib, 2)
        labels = digits[:, 0] * 32 + digits[:, 1]
        blocks = arrived[..., :width].reshape(n_dev, rows_out, piece, cols_dev, TILE)
        blocks = jnp.transpose(blocks, (0, 3, 1, 2, 4)).reshape(n_dev * contrib, piece * TILE)
        picker = labels[None, :] == jnp.arange(n_dev * slots_dev, dtype=jnp.int32)[:, None]
        sums = dot(picker.astype(jnp.bfloat16), blocks).astype(jnp.bfloat16)
        sums = lax.all_to_all(
            sums.reshape(n_dev, slots_dev, piece, TILE), ("front", "grp"), split_axis=0, concat_axis=0, tiled=True
        )
        return jnp.transpose(sums, (1, 0, 2, 3)).reshape(slots_dev, TILE, TILE).astype(jnp.float32)

    result, parent_tiles = None, None
    done, e = 0, ready + CHAINS + 1
    while done < 2 * events:
        at_hand = 2 * min(e - CHAINS + 1, events)
        take = min(at_hand - done, 16)
        if e < events - 1 and take < 16:
            e += 1
            continue
        numbers = list(range(done, done + take))
        done += take
        if e >= events - 1 and parent_tiles is None:
            parent_tiles = parents(after((arrived,), result)[0])
        here = after((me,), *(turns[e] if e < events else (parent_tiles,)))[0]
        result = update(rows, mask, here, own, front, numbers, [held[n // 2][n % 2] for n in numbers], base=result)
        e = min(e + 2, events - 1) if e < events - 1 else e + CHAINS
    return (result[None], parent_tiles)


def solution(mesh):
    in_specs = (
        P("front", None, "grp"),
        P("front", None, None, None),
        P("front", None, "grp"),
        P("front", "grp", None),
    )
    out_specs = (P("front", None, "grp"), P(("front", "grp"), None, None))
    return jax.shard_map(shards, mesh=mesh, in_specs=in_specs, out_specs=out_specs, check_vma=False)
```

profile of v0, /device:TPU:0, one launch (start us, length us, event | category | flops | bytes accessed | tf_op | source)
XLA Modules:
  0.0 189.6 jit_solution(7541967330909840102)
XLA Ops:
  0.6 0.8 copy.69.mask
  1.4 1.0 copy-done.3
  2.4 2.3 %factor.5 = (bf16[256,512]{1,0:T(8,128)(2,1)S(1)}, bf16[256,512]{1,0:T(8,128)(2,1)S(1)}, bf16[4,256,256]{2,1,0:T(8,128)(2,1)S(1)}, bf16[256,256]{1,0:T(8,128)(2,1)S(1)}) custom-call(s32[32,4]{1,0:T(8,128)S(1)} %copy.69.mask, bf16[8192,1024]{1,0:T(8,128)(2,1)} %bitcast.27, f32[2,256,256]{2,1,0:T(8,128)S(1)} %bitcast.25), custom_call_target="tpu_custom_call" | custom-call | flops 402653184 | bytes 1048576 | tf_op jit(solution)/shard_map/factor/pallas_call | solution.py:172
  4.7 3.1 %collective-permute-start.2 = (bf16[256,512]{1,0:T(8,128)(2,1)S(1)}, bf16[256,512]{1,0:T(8,128)(2,1)S(1)}, u32[]{:S(2)}, u32[]{:S(2)}) collective-permute-start(bf16[256,512]{1,0:T(8,128)(2,1)S(1)} %get-tuple-element.147.refs_18_), channel_id=1, source_target_pairs={{0,2},{1,3},{2,4},{3,5},{4,6},{5,7},{6,0},{7,1},{8,10},{9,11},{10,... | collective-permute-start | bytes 786440 | tf_op jit(solution)/shard_map/ppermute | solution.py:436
  7.8 1.5 collective-permute-start.3
  9.3 3.0 %factor.6 = (bf16[256,512]{1,0:T(8,128)(2,1)S(1)}, bf16[256,512]{1,0:T(8,128)(2,1)S(1)}, bf16[256,512]{1,0:T(8,128)(2,1)S(1)}, bf16[256,512]{1,0:T(8,128)(2,1)S(1)}) custom-call(s32[32,4]{1,0:T(8,128)S(1)} %copy.69.mask, bf16[8192,1024]{1,0:T(8,128)(2,1)} %bitcast.28, bf16[4,256,256]{2,1,0:T(8,128)(2,1)S(1)} %get-tuple-element.207.refs_0_, ...), custom_call_target="tpu_custom_call" | custom-call | flops 805306368 | bytes 2097152 | tf_op jit(solution)/shard_map/factor/pallas_call | solution.py:172
  12.3 1.6 collective-permute-start
  14.5 5.0 %factor.7 = (bf16[256,512]{1,0:T(8,128)(2,1)S(1)}, bf16[256,512]{1,0:T(8,128)(2,1)S(1)}, bf16[256,512]{1,0:T(8,128)(2,1)S(1)}, bf16[256,512]{1,0:T(8,128)(2,1)S(...) custom-call(s32[32,4]{1,0:T(8,128)S(1)} %copy.69.mask, ...), custom_call_target="tpu_custom_call" | custom-call | flops 1610612736 | bytes 4194304 | tf_op jit(solution)/shard_map/factor/pallas_call | solution.py:172
  19.5 1.6 collective-permute-start.6
  21.2 1.5 collective-permute-start.7
  23.1 1.5 collective-permute-start.5
  24.6 6.1 %collective-permute-done.6.refs_21_.refs_4_ = bf16[256,512]{1,0:T(8,128)(2,1)S(1)} collective-permute-done((bf16[256,512]{1,0:T(8,128)(2,1)S(1)}, bf16[256,512]{1,0:T(8,128)(2,1)S(1)}, u32[]{:S(2)}, u32[]{:S(2)}) %collective-permute-start.6) | collective-permute-done | bytes 262176 | tf_op jit(solution)/shard_map/ppermute | solution.py:436
  30.8 1.6 collective-permute-start.11
  32.4 3.9 %collective-permute-done.4.refs_6_ = bf16[256,512]{1,0:T(8,128)(2,1)S(1)} collective-permute-done((bf16[256,512]{1,0:T(8,128)(2,1)S(1)}, bf16[256,512]{1,0:T(8,128)(2,1)S(1)}, u32[]{:S(2)}, u32[]{:S(2)}) %collective-permute-start.4) | collective-permute-done | bytes 262176 | tf_op jit(solution)/shard_map/ppermute | solution.py:436
  36.4 1.6 collective-permute-start.9
  38.0 5.0 %factor.8 = (bf16[256,512]{1,0:T(8,128)(2,1)S(1)}, bf16[256,512]{1,0:T(8,128)(2,1)S(1)}, bf16[256,512]{1,0:T(8,128)(2,1)S(1)}, bf16[256,512]{1,0:T(8,128)(2,1)S(...) custom-call(s32[32,4]{1,0:T(8,128)S(1)} %copy.69.mask, ...), custom_call_target="tpu_custom_call" | custom-call | flops 1610612736 | bytes 4194304 | tf_op jit(solution)/shard_map/factor/pallas_call | solution.py:172
  43.1 1.5 collective-permute-start.14
  45.1 2.4 %collective-permute-done.8.refs_10_ = bf16[256,512]{1,0:T(8,128)(2,1)S(1)} collective-permute-done((bf16[256,512]{1,0:T(8,128)(2,1)S(1)}, bf16[256,512]{1,0:T(8,128)(2,1)S(1)}, u32[]{:S(2)}, u32[]{:S(2)}) %collective-permute-start.8) | collective-permute-done | bytes 262176 | tf_op jit(solution)/shard_map/ppermute | solution.py:436
  47.6 0.7 copy-done.33
  48.3 1.5 collective-permute-start.13
  49.8 4.3 %collective-permute-done.14.refs_4_.refs_12_ = bf16[256,512]{1,0:T(8,128)(2,1)S(1)} collective-permute-done((bf16[256,512]{1,0:T(8,128)(2,1)S(1)}, bf16[256,512]{1,0:T(8,128)(2,1)S(1)}, u32[]{:S(2)}, u32[]{:S(2)}) %collective-permute-start.14) | collective-permute-done | bytes 262176 | tf_op jit(solution)/shard_map/ppermute | solution.py:436
  54.2 1.3 collective-permute-start.16
  56.1 3.7 %collective-permute-done.12.refs_9_.refs_14_ = bf16[256,512]{1,0:T(8,128)(2,1)S(1)} collective-permute-done((bf16[256,512]{1,0:T(8,128)(2,1)S(1)}, bf16[256,512]{1,0:T(8,128)(2,1)S(1)}, u32[]{:S(2)}, u32[]{:S(2)}) %collective-permute-start.12) | collective-permute-done | bytes 262176 | tf_op jit(solution)/shard_map/ppermute | solution.py:436
  59.8 1.4 collective-permute-start.20
  61.9 5.9 %factor.9 = (bf16[256,512]{1,0:T(8,128)(2,1)S(1)}, bf16[256,512]{1,0:T(8,128)(2,1)S(1)}, bf16[256,512]{1,0:T(8,128)(2,1)S(1)}, bf16[256,512]{1,0:T(8,128)(2,1)S(...) custom-call(s32[32,4]{1,0:T(8,128)S(1)} %copy.69.mask, ...), custom_call_target="tpu_custom_call" | custom-call | flops 2013265920 | bytes 5242880 | tf_op jit(solution)/shard_map/factor/pallas_call | solution.py:172
  68.0 1.9 collective-permute-start.18
  69.9 1.3 collective-permute-start.19
  71.3 1.0 collective-permute-start.22
  73.0 4.9 %collective-permute-done.18.refs_2_.refs_4_ = bf16[256,512]{1,0:T(8,128)(2,1)S(1)} collective-permute-done((bf16[256,512]{1,0:T(8,128)(2,1)S(1)}, bf16[256,512]{1,0:T(8,128)(2,1)S(1)}, u32[]{:S(2)}, u32[]{:S(2)}) %collective-permute-start.18) | collective-permute-done | bytes 262176 | tf_op jit(solution)/shard_map/ppermute | solution.py:436
  78.3 1.6 collective-permute-start.24
  80.6 2.9 %collective-permute-done.22.refs_7_.refs_6_ = bf16[256,512]{1,0:T(8,128)(2,1)S(1)} collective-permute-done((bf16[256,512]{1,0:T(8,128)(2,1)S(1)}, bf16[256,512]{1,0:T(8,128)(2,1)S(1)}, u32[]{:S(2)}, u32[]{:S(2)}) %collective-permute-start.22) | collective-permute-done | bytes 262176 | tf_op jit(solution)/shard_map/ppermute | solution.py:436
  83.9 1.6 collective-permute-start.26
  86.2 3.2 %collective-permute-done.24.refs_13_.refs_8_ = bf16[256,512]{1,0:T(8,128)(2,1)S(1)} collective-permute-done((bf16[256,512]{1,0:T(8,128)(2,1)S(1)}, bf16[256,512]{1,0:T(8,128)(2,1)S(1)}, u32[]{:S(2)}, u32[]{:S(2)}) %collective-permute-start.24) | collective-permute-done | bytes 262176 | tf_op jit(solution)/shard_map/ppermute | solution.py:436
  89.5 1.6 collective-permute-start.28
  91.1 0.7 collective-permute-start.29
  91.8 3.2 %collective-permute-done.26.refs_16_.refs_10_ = bf16[256,512]{1,0:T(8,128)(2,1)S(1)} collective-permute-done((bf16[256,512]{1,0:T(8,128)(2,1)S(1)}, bf16[256,512]{1,0:T(8,128)(2,1)S(1)}, u32[]{:S(2)}, u32[]{:S(2)}) %collective-permute-start.26) | collective-permute-done | bytes 262176 | tf_op jit(solution)/shard_map/ppermute | solution.py:436
  95.1 1.6 collective-permute-start.32
  97.6 3.8 %own_panels.1 = (bf16[512,1024]{1,0:T(8,128)(2,1)S(1)}, bf16[256,1152]{1,0:T(8,128)(2,1)}) custom-call(s32[32,4]{1,0:T(8,128)S(1)} %copy.69.mask, s32[4]{0:T(128)S(1)} %bitcast.26, s32[1]{0:T(128)} %bitcast.1.me, bf16[8192,1024]{1,0:T(8,128)(2,1)} %bitcast.32, bf16[256,512]{1,0:T(8,128)(2,1)} %copy-done.5, bf16[256,512]{1,0:T(8,128)(2,1)} %copy-done.20, ...), custom_call_target="tpu_custom_call" | custom-call | flops 268435456 | bytes 2621440 | tf_op jit(solution)/shard_map/own_panels/pallas_call | solution.py:226
  101.4 5.0 %all-to-all-start = ((bf16[32,1,8,1152]{3,2,1,0:T(8,128)(2,1)}), bf16[32,1,8,1152]{3,2,1,0:T(8,128)(2,1)S(1)}, u32[]{:S(2)}, u32[]{:S(2)}) async-start(bf16[32,1,8,1152]{3,2,1,0:T(8,128)(2,1)} %bitcast.6), calls=%async_computation | async-start | bytes 1179648 | tf_op jit(solution)/shard_map/all_to_all | solution.py:472
  106.5 1.1 broadcast_select_fusion.7
  107.5 1.8 collective-permute-start.30
  109.4 1.5 collective-permute-start.31
  110.9 1.5 collective-permute-start.36
  113.0 8.3 %update.4.refs_16_ = bf16[8192,1024]{1,0:T(8,128)(2,1)} custom-call(s32[8,48]{1,0:T(8,128)S(1)} %copy-done.6, s32[32,4]{1,0:T(8,128)S(1)} %copy.69.mask, s32[1]{0:T(128)} %bitcast.1.me, bf16[512,1024]{1,0:T(8,128)(2,1)S(1)} %get-tuple-element.259.own, bf16[8192,1024]{1,0:T(8,128)(2,1)} %bitcast.33, bf16[256,512]{1,0:T(8,128)(2,1)} %copy-done.8, ...), custom_call_target="tpu_custom_call" | custom-call | flops 4294967296 | bytes 16777216 | tf_op jit(solution)/shard_map/update/pallas_call | solution.py:340
  121.3 5.4 %collective-permute-done.30.refs_0_ = bf16[256,512]{1,0:T(8,128)(2,1)S(1)} collective-permute-done((bf16[256,512]{1,0:T(8,128)(2,1)S(1)}, bf16[256,512]{1,0:T(8,128)(2,1)S(1)}, u32[]{:S(2)}, u32[]{:S(2)}) %collective-permute-start.30) | collective-permute-done | bytes 262176 | tf_op jit(solution)/shard_map/ppermute | solution.py:436
  127.3 1.4 collective-permute-start.35
  128.7 3.6 %collective-permute-done.36.refs_2_ = bf16[256,512]{1,0:T(8,128)(2,1)S(1)} collective-permute-done((bf16[256,512]{1,0:T(8,128)(2,1)S(1)}, bf16[256,512]{1,0:T(8,128)(2,1)S(1)}, u32[]{:S(2)}, u32[]{:S(2)}) %collective-permute-start.36) | collective-permute-done | bytes 262176 | tf_op jit(solution)/shard_map/ppermute | solution.py:436
  132.9 1.4 collective-permute-start.41
  134.3 9.9 %update.5.refs_12_ = bf16[8192,1024]{1,0:T(8,128)(2,1)} custom-call(s32[8,48]{1,0:T(8,128)S(1)} %copy-done.6, s32[32,4]{1,0:T(8,128)S(1)} %copy.69.mask, s32[1]{0:T(128)} %bitcast.1.me, bf16[512,1024]{1,0:T(8,128)(2,1)S(1)} %get-tuple-element.259.own, bf16[8192,1024]{1,0:T(8,128)(2,1)} %bitcast.34, ...), custom_call_target="tpu_custom_call", output_to_operand_aliasing={{}: (21, {})} | custom-call | flops 4294967296 | bytes 16777216 | tf_op jit(solution)/shard_map/update/pallas_call | solution.py:340
  144.3 1.0 broadcast_select_fusion.3
  145.3 2.1 %collective-permute-start.38 = (bf16[256,512]{1,0:T(8,128)(2,1)}, bf16[256,512]{1,0:T(8,128)(2,1)S(1)}, u32[]{:S(2)}, u32[]{:S(2)}) collective-permute-start(bf16[256,512]{1,0:T(8,128)(2,1)} %get-tuple-element.269), channel_id=1, source_target_pairs={{0,2},{1,3},{2,4},{3,5},{4,6},{5,7},{6,0},{7,1},{8,10},{9,11},{10,... | collective-permute-start | bytes 786440 | tf_op jit(solution)/shard_map/ppermute | solution.py:436
  149.3 0.9 copy.71
  150.2 3.9 %all-to-all-start.1 = ((bf16[32,4,8,256]{3,2,1,0:T(8,128)(2,1)}), bf16[32,4,8,256]{3,2,1,0:T(8,128)(2,1)S(1)}, u32[]{:S(2)}, u32[]{:S(2)}) async-start(bf16[32,4,8,256]{3,2,1,0:T(8,128)(2,1)} %bitcast.19), calls=%async_computation.1 | async-start | bytes 1048576 | tf_op jit(solution)/shard_map/all_to_all | solution.py:481
  154.2 1.8 collective-permute-start.44
  156.0 1.5 collective-permute-start.45
  157.5 0.9 broadcast_select_fusion.1
  158.4 1.5 collective-permute-start.42
  160.4 12.9 %collective-permute-done.44.refs_10_ = bf16[256,512]{1,0:T(8,128)(2,1)S(1)} collective-permute-done((bf16[256,512]{1,0:T(8,128)(2,1)S(1)}, bf16[256,512]{1,0:T(8,128)(2,1)S(1)}, u32[]{:S(2)}, u32[]{:S(2)}) %collective-permute-start.44) | collective-permute-done | bytes 262176 | tf_op jit(solution)/shard_map/ppermute | solution.py:436
  173.3 0.9 broadcast_select_fusion
  174.3 1.4 collective-permute-start.47
  175.8 6.5 %update.6.refs_4_ = bf16[8192,1024]{1,0:T(8,128)(2,1)} custom-call(s32[8,48]{1,0:T(8,128)S(1)} %copy-done.6, s32[32,4]{1,0:T(8,128)S(1)} %copy.69.mask, s32[1]{0:T(128)} %bitcast.1.me, bf16[512,1024]{1,0:T(8,128)(2,1)S(1)} %get-tuple-element.259.own, bf16[8192,1024]{1,0:T(8,128)(2,1)} %bitcast.35, ...), custom_call_target="tpu_custom_call", output_to_operand_aliasing={{}: (17, {})} | custom-call | flops 3221225472 | bytes 12582912 | tf_op jit(solution)/shard_map/update/pallas_call | solution.py:340
  182.3 5.0 %all-to-all-done.1 = bf16[32,4,8,256]{3,2,1,0:T(8,128)(2,1)S(1)} async-done(((bf16[32,4,8,256]{3,2,1,0:T(8,128)(2,1)}), bf16[32,4,8,256]{3,2,1,0:T(8,128)(2,1)S(1)}, u32[]{:S(2)}, u32[]{:S(2)}) %all-to-all-start.1) | async-done | bytes 524320 | tf_op jit(solution)/shard_map/all_to_all | solution.py:481
  187.3 1.1 copy_bitcast_fusion
  188.4 1.0 update.7
  (179 shorter events, 11.7 us)
Async XLA Ops:
  4.7 14.7 %collective-permute-start.2 = (bf16[256,512]{1,0:T(8,128)(2,1)S(1)}, bf16[256,512]{1,0:T(8,128)(2,1)S(1)}, u32[]{:S(2)}, u32[]{:S(2)}) collective-permute-start(bf16[256,512]{1,0:T(8,128)(2,1)S(1)} %get-tuple-element.147.refs_18_), channel_id=1, source_target_pairs={{0,2},{1,3},{2,4},{3,5},{4,6},{5,7},{6,0},{7,1},{8,10},{9,11},{10,... | collective-permute-start | bytes 786440 | tf_op jit(solution)/shard_map/ppermute | solution.py:436
  7.8 11.6 %collective-permute-start.3 = (bf16[256,512]{1,0:T(8,128)(2,1)S(1)}, bf16[256,512]{1,0:T(8,128)(2,1)S(1)}, u32[]{:S(2)}, u32[]{:S(2)}) collective-permute-start(bf16[256,512]{1,0:T(8,128)(2,1)S(1)} %get-tuple-element.148), channel_id=1, source_target_pairs={{0,1},{1,0},{2,3},{3,2},{4,5},{5,4},{6,7},{7,6},{8,9},{9,8},{10,11... | collective-permute-start | bytes 786440 | tf_op jit(solution)/shard_map/ppermute | solution.py:436
  12.3 10.4 %collective-permute-start = (bf16[256,512]{1,0:T(8,128)(2,1)S(1)}, bf16[256,512]{1,0:T(8,128)(2,1)S(1)}, u32[]{:S(2)}, u32[]{:S(2)}) collective-permute-start(bf16[256,512]{1,0:T(8,128)(2,1)S(1)} %get-tuple-element.153), channel_id=1, source_target_pairs={{0,2},{1,3},{2,4},{3,5},{4,6},{5,7},{6,0},{7,1},{8,10},{9,11},{10,... | collective-permute-start | bytes 786440 | tf_op jit(solution)/shard_map/ppermute | solution.py:436
  14.0 8.7 %collective-permute-start.1 = (bf16[256,512]{1,0:T(8,128)(2,1)S(1)}, bf16[256,512]{1,0:T(8,128)(2,1)S(1)}, u32[]{:S(2)}, u32[]{:S(2)}) collective-permute-start(bf16[256,512]{1,0:T(8,128)(2,1)S(1)} %get-tuple-element.154), channel_id=1, source_target_pairs={{0,1},{1,0},{2,3},{3,2},{4,5},{5,4},{6,7},{7,6},{8,9},{9,8},{10,11... | collective-permute-start | bytes 786440 | tf_op jit(solution)/shard_map/ppermute | solution.py:436
  19.4 48.4 %copy-start.8 = (bf16[256,512]{1,0:T(8,128)(2,1)}, bf16[256,512]{1,0:T(8,128)(2,1)S(1)}, u32[]{:S(2)}) copy-start(bf16[256,512]{1,0:T(8,128)(2,1)S(1)} %collective-permute-done.2.refs_19_.refs_0_) | copy-start | bytes 786436
  19.5 48.4 %copy-start.27 = (bf16[256,512]{1,0:T(8,128)(2,1)}, bf16[256,512]{1,0:T(8,128)(2,1)S(1)}, u32[]{:S(2)}) copy-start(bf16[256,512]{1,0:T(8,128)(2,1)S(1)} %collective-permute-done.3.refs_1_) | copy-start | bytes 786436
  19.5 11.1 %collective-permute-start.6 = (bf16[256,512]{1,0:T(8,128)(2,1)S(1)}, bf16[256,512]{1,0:T(8,128)(2,1)S(1)}, u32[]{:S(2)}, u32[]{:S(2)}) collective-permute-start(bf16[256,512]{1,0:T(8,128)(2,1)S(1)} %get-tuple-element.163), channel_id=1, source_target_pairs={{0,2},{1,3},{2,4},{3,5},{4,6},{5,7},{6,0},{7,1},{8,10},{9,11},{10,... | collective-permute-start | bytes 786440 | tf_op jit(solution)/shard_map/ppermute | solution.py:436
  21.2 9.5 %collective-permute-start.7 = (bf16[256,512]{1,0:T(8,128)(2,1)S(1)}, bf16[256,512]{1,0:T(8,128)(2,1)S(1)}, u32[]{:S(2)}, u32[]{:S(2)}) collective-permute-start(bf16[256,512]{1,0:T(8,128)(2,1)S(1)} %get-tuple-element.164), channel_id=1, source_target_pairs={{0,1},{1,0},{2,3},{3,2},{4,5},{5,4},{6,7},{7,6},{8,9},{9,8},{10,11... | collective-permute-start | bytes 786440 | tf_op jit(solution)/shard_map/ppermute | solution.py:436
  22.7 45.2 %copy-start.28 = (bf16[256,512]{1,0:T(8,128)(2,1)}, bf16[256,512]{1,0:T(8,128)(2,1)S(1)}, u32[]{:S(2)}) copy-start(bf16[256,512]{1,0:T(8,128)(2,1)S(1)} %collective-permute-done.refs_2_) | copy-start | bytes 786436
  22.7 45.2 %copy-start.29 = (bf16[256,512]{1,0:T(8,128)(2,1)}, bf16[256,512]{1,0:T(8,128)(2,1)S(1)}, u32[]{:S(2)}) copy-start(bf16[256,512]{1,0:T(8,128)(2,1)S(1)} %collective-permute-done.1.refs_3_) | copy-start | bytes 786436
  22.8 13.5 %collective-permute-start.4 = (bf16[256,512]{1,0:T(8,128)(2,1)S(1)}, bf16[256,512]{1,0:T(8,128)(2,1)S(1)}, u32[]{:S(2)}, u32[]{:S(2)}) collective-permute-start(bf16[256,512]{1,0:T(8,128)(2,1)S(1)} %get-tuple-element.168), channel_id=1, source_target_pairs={{0,2},{1,3},{2,4},{3,5},{4,6},{5,7},{6,0},{7,1},{8,10},{9,11},{10,... | collective-permute-start | bytes 786440 | tf_op jit(solution)/shard_map/ppermute | solution.py:436
  23.1 13.2 %collective-permute-start.5 = (bf16[256,512]{1,0:T(8,128)(2,1)S(1)}, bf16[256,512]{1,0:T(8,128)(2,1)S(1)}, u32[]{:S(2)}, u32[]{:S(2)}) collective-permute-start(bf16[256,512]{1,0:T(8,128)(2,1)S(1)} %get-tuple-element.169), channel_id=1, source_target_pairs={{0,1},{1,0},{2,3},{3,2},{4,5},{5,4},{6,7},{7,6},{8,9},{9,8},{10,11... | collective-permute-start | bytes 786440 | tf_op jit(solution)/shard_map/ppermute | solution.py:436
  30.6 37.2 %copy-start.9 = (bf16[256,512]{1,0:T(8,128)(2,1)}, bf16[256,512]{1,0:T(8,128)(2,1)S(1)}, u32[]{:S(2)}) copy-start(bf16[256,512]{1,0:T(8,128)(2,1)S(1)} %collective-permute-done.6.refs_21_.refs_4_) | copy-start | bytes 786436
  30.6 37.2 %copy-start.10 = (bf16[256,512]{1,0:T(8,128)(2,1)}, bf16[256,512]{1,0:T(8,128)(2,1)S(1)}, u32[]{:S(2)}) copy-start(bf16[256,512]{1,0:T(8,128)(2,1)S(1)} %collective-permute-done.7.refs_20_.refs_5_) | copy-start | bytes 786436
  30.7 12.2 %collective-permute-start.10 = (bf16[256,512]{1,0:T(8,128)(2,1)S(1)}, bf16[256,512]{1,0:T(8,128)(2,1)S(1)}, u32[]{:S(2)}, u32[]{:S(2)}) collective-permute-start(bf16[256,512]{1,0:T(8,128)(2,1)S(1)} %get-tuple-element.174), channel_id=1, source_target_pairs={{0,2},{1,3},{2,4},{3,5},{4,6},{5,7},{6,0},{7,1},{8,10},{9,11},{10,... | collective-permute-start | bytes 786440 | tf_op jit(solution)/shard_map/ppermute | solution.py:436
  30.8 12.2 %collective-permute-start.11 = (bf16[256,512]{1,0:T(8,128)(2,1)S(1)}, bf16[256,512]{1,0:T(8,128)(2,1)S(1)}, u32[]{:S(2)}, u32[]{:S(2)}) collective-permute-start(bf16[256,512]{1,0:T(8,128)(2,1)S(1)} %get-tuple-element.175), channel_id=1, source_target_pairs={{0,1},{1,0},{2,3},{3,2},{4,5},{5,4},{6,7},{7,6},{8,9},{9,8},{10,11... | collective-permute-start | bytes 786440 | tf_op jit(solution)/shard_map/ppermute | solution.py:436
  36.3 11.2 %collective-permute-start.8 = (bf16[256,512]{1,0:T(8,128)(2,1)S(1)}, bf16[256,512]{1,0:T(8,128)(2,1)S(1)}, u32[]{:S(2)}, u32[]{:S(2)}) collective-permute-start(bf16[256,512]{1,0:T(8,128)(2,1)S(1)} %get-tuple-element.179), channel_id=1, source_target_pairs={{0,2},{1,3},{2,4},{3,5},{4,6},{5,7},{6,0},{7,1},{8,10},{9,11},{10,... | collective-permute-start | bytes 786440 | tf_op jit(solution)/shard_map/ppermute | solution.py:436
  36.4 11.1 %collective-permute-start.9 = (bf16[256,512]{1,0:T(8,128)(2,1)S(1)}, bf16[256,512]{1,0:T(8,128)(2,1)S(1)}, u32[]{:S(2)}, u32[]{:S(2)}) collective-permute-start(bf16[256,512]{1,0:T(8,128)(2,1)S(1)} %get-tuple-element.180), channel_id=1, source_target_pairs={{0,1},{1,0},{2,3},{3,2},{4,5},{5,4},{6,7},{7,6},{8,9},{9,8},{10,11... | collective-permute-start | bytes 786440 | tf_op jit(solution)/shard_map/ppermute | solution.py:436
  42.9 54.6 %copy-start.7 = (s32[1,1,4]{2,1,0:T(1,128)S(1)}, s32[1,1,4]{2,1,0:T(1,128)}, u32[]{:S(2)}) copy-start(s32[1,1,4]{2,1,0:T(1,128)} %param.8) | copy-start | bytes 52
  43.0 54.4 %copy-start.11 = (bf16[256,512]{1,0:T(8,128)(2,1)}, bf16[256,512]{1,0:T(8,128)(2,1)S(1)}, u32[]{:S(2)}) copy-start(bf16[256,512]{1,0:T(8,128)(2,1)S(1)} %collective-permute-done.10.refs_23_.refs_8_) | copy-start | bytes 786436
  43.0 54.4 %copy-start.12 = (bf16[256,512]{1,0:T(8,128)(2,1)}, bf16[256,512]{1,0:T(8,128)(2,1)S(1)}, u32[]{:S(2)}) copy-start(bf16[256,512]{1,0:T(8,128)(2,1)S(1)} %collective-permute-done.11.refs_22_.refs_9_) | copy-start | bytes 786436
  43.1 11.0 %collective-permute-start.14 = (bf16[256,512]{1,0:T(8,128)(2,1)S(1)}, bf16[256,512]{1,0:T(8,128)(2,1)S(1)}, u32[]{:S(2)}, u32[]{:S(2)}) collective-permute-start(bf16[256,512]{1,0:T(8,128)(2,1)S(1)} %get-tuple-element.189), channel_id=1, source_target_pairs={{0,2},{1,3},{2,4},{3,5},{4,6},{5,7},{6,0},{7,1},{8,10},{9,11},{10,... | collective-permute-start | bytes 786440 | tf_op jit(solution)/shard_map/ppermute | solution.py:436
  44.6 9.5 %collective-permute-start.15 = (bf16[256,512]{1,0:T(8,128)(2,1)S(1)}, bf16[256,512]{1,0:T(8,128)(2,1)S(1)}, u32[]{:S(2)}, u32[]{:S(2)}) collective-permute-start(bf16[256,512]{1,0:T(8,128)(2,1)S(1)} %get-tuple-element.190), channel_id=1, source_target_pairs={{0,1},{1,0},{2,3},{3,2},{4,5},{5,4},{6,7},{7,6},{8,9},{9,8},{10,11... | collective-permute-start | bytes 786440 | tf_op jit(solution)/shard_map/ppermute | solution.py:436
  48.3 11.4 %collective-permute-start.12 = (bf16[256,512]{1,0:T(8,128)(2,1)S(1)}, bf16[256,512]{1,0:T(8,128)(2,1)S(1)}, u32[]{:S(2)}, u32[]{:S(2)}) collective-permute-start(bf16[256,512]{1,0:T(8,128)(2,1)S(1)} %get-tuple-element.194), channel_id=1, source_target_pairs={{0,2},{1,3},{2,4},{3,5},{4,6},{5,7},{6,0},{7,1},{8,10},{9,11},{10,... | collective-permute-start | bytes 786440 | tf_op jit(solution)/shard_map/ppermute | solution.py:436
  48.3 11.4 %collective-permute-start.13 = (bf16[256,512]{1,0:T(8,128)(2,1)S(1)}, bf16[256,512]{1,0:T(8,128)(2,1)S(1)}, u32[]{:S(2)}, u32[]{:S(2)}) collective-permute-start(bf16[256,512]{1,0:T(8,128)(2,1)S(1)} %get-tuple-element.195), channel_id=1, source_target_pairs={{0,1},{1,0},{2,3},{3,2},{4,5},{5,4},{6,7},{7,6},{8,9},{9,8},{10,11... | collective-permute-start | bytes 786440 | tf_op jit(solution)/shard_map/ppermute | solution.py:436
  54.1 43.3 %copy-start.14 = (bf16[256,512]{1,0:T(8,128)(2,1)}, bf16[256,512]{1,0:T(8,128)(2,1)S(1)}, u32[]{:S(2)}) copy-start(bf16[256,512]{1,0:T(8,128)(2,1)S(1)} %collective-permute-done.14.refs_4_.refs_12_) | copy-start | bytes 786436
  54.1 43.3 %copy-start.15 = (bf16[256,512]{1,0:T(8,128)(2,1)}, bf16[256,512]{1,0:T(8,128)(2,1)S(1)}, u32[]{:S(2)}) copy-start(bf16[256,512]{1,0:T(8,128)(2,1)S(1)} %collective-permute-done.15.refs_17_.refs_13_) | copy-start | bytes 786436
  54.2 13.7 %collective-permute-start.16 = (bf16[256,512]{1,0:T(8,128)(2,1)S(1)}, bf16[256,512]{1,0:T(8,128)(2,1)S(1)}, u32[]{:S(2)}, u32[]{:S(2)}) collective-permute-start(bf16[256,512]{1,0:T(8,128)(2,1)S(1)} %get-tuple-element.200), channel_id=1, source_target_pairs={{0,2},{1,3},{2,4},{3,5},{4,6},{5,7},{6,0},{7,1},{8,10},{9,11},{10,... | collective-permute-start | bytes 786440 | tf_op jit(solution)/shard_map/ppermute | solution.py:436
  55.4 12.5 %collective-permute-start.17 = (bf16[256,512]{1,0:T(8,128)(2,1)S(1)}, bf16[256,512]{1,0:T(8,128)(2,1)S(1)}, u32[]{:S(2)}, u32[]{:S(2)}) collective-permute-start(bf16[256,512]{1,0:T(8,128)(2,1)S(1)} %get-tuple-element.201), channel_id=1, source_target_pairs={{0,1},{1,0},{2,3},{3,2},{4,5},{5,4},{6,7},{7,6},{8,9},{9,8},{10,11... | collective-permute-start | bytes 786440 | tf_op jit(solution)/shard_map/ppermute | solution.py:436
  59.7 37.7 %copy-start.17 = (bf16[256,512]{1,0:T(8,128)(2,1)}, bf16[256,512]{1,0:T(8,128)(2,1)S(1)}, u32[]{:S(2)}) copy-start(bf16[256,512]{1,0:T(8,128)(2,1)S(1)} %collective-permute-done.12.refs_9_.refs_14_) | copy-start | bytes 786436
  59.7 37.7 %copy-start.18 = (bf16[256,512]{1,0:T(8,128)(2,1)}, bf16[256,512]{1,0:T(8,128)(2,1)S(1)}, u32[]{:S(2)}) copy-start(bf16[256,512]{1,0:T(8,128)(2,1)S(1)} %collective-permute-done.13.refs_10_.refs_15_) | copy-start | bytes 786436
  59.8 11.4 %collective-permute-start.20 = (bf16[256,512]{1,0:T(8,128)(2,1)S(1)}, bf16[256,512]{1,0:T(8,128)(2,1)S(1)}, u32[]{:S(2)}, u32[]{:S(2)}) collective-permute-start(bf16[256,512]{1,0:T(8,128)(2,1)S(1)} %get-tuple-element.205), channel_id=1, source_target_pairs={{0,2},{1,3},{2,4},{3,5},{4,6},{5,7},{6,0},{7,1},{8,10},{9,11},{10,... | collective-permute-start | bytes 786440 | tf_op jit(solution)/shard_map/ppermute | solution.py:436
  61.2 10.0 %collective-permute-start.21 = (bf16[256,512]{1,0:T(8,128)(2,1)S(1)}, bf16[256,512]{1,0:T(8,128)(2,1)S(1)}, u32[]{:S(2)}, u32[]{:S(2)}) collective-permute-start(bf16[256,512]{1,0:T(8,128)(2,1)S(1)} %get-tuple-element.206), channel_id=1, source_target_pairs={{0,1},{1,0},{2,3},{3,2},{4,5},{5,4},{6,7},{7,6},{8,9},{9,8},{10,11... | collective-permute-start | bytes 786440 | tf_op jit(solution)/shard_map/ppermute | solution.py:436
  68.0 9.8 %collective-permute-start.18 = (bf16[256,512]{1,0:T(8,128)(2,1)S(1)}, bf16[256,512]{1,0:T(8,128)(2,1)S(1)}, u32[]{:S(2)}, u32[]{:S(2)}) collective-permute-start(bf16[256,512]{1,0:T(8,128)(2,1)S(1)} %get-tuple-element.214), channel_id=1, source_target_pairs={{0,2},{1,3},{2,4},{3,5},{4,6},{5,7},{6,0},{7,1},{8,10},{9,11},{10,... | collective-permute-start | bytes 786440 | tf_op jit(solution)/shard_map/ppermute | solution.py:436
  69.9 8.3 %collective-permute-start.19 = (bf16[256,512]{1,0:T(8,128)(2,1)S(1)}, bf16[256,512]{1,0:T(8,128)(2,1)S(1)}, u32[]{:S(2)}, u32[]{:S(2)}) collective-permute-start(bf16[256,512]{1,0:T(8,128)(2,1)S(1)} %get-tuple-element.215), channel_id=1, source_target_pairs={{0,1},{1,0},{2,3},{3,2},{4,5},{5,4},{6,7},{7,6},{8,9},{9,8},{10,11... | collective-permute-start | bytes 786440 | tf_op jit(solution)/shard_map/ppermute | solution.py:436
  71.2 41.8 %copy-start.6 = (s32[8,48]{1,0:T(8,128)S(1)}, s32[8,48]{1,0:T(8,128)}, u32[]{:S(2)}) copy-start(s32[8,48]{1,0:T(8,128)} %constant.14.clone.table) | copy-start | bytes 4612
  71.3 12.2 %collective-permute-start.22 = (bf16[256,512]{1,0:T(8,128)(2,1)S(1)}, bf16[256,512]{1,0:T(8,128)(2,1)S(1)}, u32[]{:S(2)}, u32[]{:S(2)}) collective-permute-start(bf16[256,512]{1,0:T(8,128)(2,1)S(1)} %get-tuple-element.220), channel_id=1, source_target_pairs={{0,2},{1,3},{2,4},{3,5},{4,6},{5,7},{6,0},{7,1},{8,10},{9,11},{10,... | collective-permute-start | bytes 786440 | tf_op jit(solution)/shard_map/ppermute | solution.py:436
  72.3 11.6 %collective-permute-start.23 = (bf16[256,512]{1,0:T(8,128)(2,1)S(1)}, bf16[256,512]{1,0:T(8,128)(2,1)S(1)}, u32[]{:S(2)}, u32[]{:S(2)}) collective-permute-start(bf16[256,512]{1,0:T(8,128)(2,1)S(1)} %get-tuple-element.221), channel_id=1, source_target_pairs={{0,1},{1,0},{2,3},{3,2},{4,5},{5,4},{6,7},{7,6},{8,9},{9,8},{10,11... | collective-permute-start | bytes 786440 | tf_op jit(solution)/shard_map/ppermute | solution.py:436
  78.3 11.1 %collective-permute-start.24 = (bf16[256,512]{1,0:T(8,128)(2,1)S(1)}, bf16[256,512]{1,0:T(8,128)(2,1)S(1)}, u32[]{:S(2)}, u32[]{:S(2)}) collective-permute-start(bf16[256,512]{1,0:T(8,128)(2,1)S(1)} %get-tuple-element.227), channel_id=1, source_target_pairs={{0,2},{1,3},{2,4},{3,5},{4,6},{5,7},{6,0},{7,1},{8,10},{9,11},{10,... | collective-permute-start | bytes 786440 | tf_op jit(solution)/shard_map/ppermute | solution.py:436
  79.9 9.6 %collective-permute-start.25 = (bf16[256,512]{1,0:T(8,128)(2,1)S(1)}, bf16[256,512]{1,0:T(8,128)(2,1)S(1)}, u32[]{:S(2)}, u32[]{:S(2)}) collective-permute-start(bf16[256,512]{1,0:T(8,128)(2,1)S(1)} %get-tuple-element.228), channel_id=1, source_target_pairs={{0,1},{1,0},{2,3},{3,2},{4,5},{5,4},{6,7},{7,6},{8,9},{9,8},{10,11... | collective-permute-start | bytes 786440 | tf_op jit(solution)/shard_map/ppermute | solution.py:436
  83.9 11.1 %collective-permute-start.26 = (bf16[256,512]{1,0:T(8,128)(2,1)S(1)}, bf16[256,512]{1,0:T(8,128)(2,1)S(1)}, u32[]{:S(2)}, u32[]{:S(2)}) collective-permute-start(bf16[256,512]{1,0:T(8,128)(2,1)S(1)} %get-tuple-element.234), channel_id=1, source_target_pairs={{0,2},{1,3},{2,4},{3,5},{4,6},{5,7},{6,0},{7,1},{8,10},{9,11},{10,... | collective-permute-start | bytes 786440 | tf_op jit(solution)/shard_map/ppermute | solution.py:436
  85.5 9.6 %collective-permute-start.27 = (bf16[256,512]{1,0:T(8,128)(2,1)S(1)}, bf16[256,512]{1,0:T(8,128)(2,1)S(1)}, u32[]{:S(2)}, u32[]{:S(2)}) collective-permute-start(bf16[256,512]{1,0:T(8,128)(2,1)S(1)} %get-tuple-element.235), channel_id=1, source_target_pairs={{0,1},{1,0},{2,3},{3,2},{4,5},{5,4},{6,7},{7,6},{8,9},{9,8},{10,11... | collective-permute-start | bytes 786440 | tf_op jit(solution)/shard_map/ppermute | solution.py:436
  89.5 16.9 %collective-permute-start.28 = (bf16[256,512]{1,0:T(8,128)(2,1)S(1)}, bf16[256,512]{1,0:T(8,128)(2,1)}, u32[]{:S(2)}, u32[]{:S(2)}) collective-permute-start(bf16[256,512]{1,0:T(8,128)(2,1)S(1)} %get-tuple-element.239), channel_id=1, source_target_pairs={{0,2},{1,3},{2,4},{3,5},{4,6},{5,7},{6,0},{7,1},{8,10},{9,11},{10,... | collective-permute-start | bytes 786440 | tf_op jit(solution)/shard_map/ppermute | solution.py:436
  91.1 15.4 %collective-permute-start.29 = (bf16[256,512]{1,0:T(8,128)(2,1)S(1)}, bf16[256,512]{1,0:T(8,128)(2,1)}, u32[]{:S(2)}, u32[]{:S(2)}) collective-permute-start(bf16[256,512]{1,0:T(8,128)(2,1)S(1)} %get-tuple-element.240), channel_id=1, source_target_pairs={{0,1},{1,0},{2,3},{3,2},{4,5},{5,4},{6,7},{7,6},{8,9},{9,8},{10,11... | collective-permute-start | bytes 786440 | tf_op jit(solution)/shard_map/ppermute | solution.py:436
  95.1 15.7 %collective-permute-start.32 = (bf16[256,512]{1,0:T(8,128)(2,1)S(1)}, bf16[256,512]{1,0:T(8,128)(2,1)S(1)}, u32[]{:S(2)}, u32[]{:S(2)}) collective-permute-start(bf16[256,512]{1,0:T(8,128)(2,1)S(1)} %get-tuple-element.244), channel_id=1, source_target_pairs={{0,2},{1,3},{2,4},{3,5},{4,6},{5,7},{6,0},{7,1},{8,10},{9,11},{10,... | collective-permute-start | bytes 786440 | tf_op jit(solution)/shard_map/ppermute | solution.py:436
  96.7 14.1 %collective-permute-start.33 = (bf16[256,512]{1,0:T(8,128)(2,1)S(1)}, bf16[256,512]{1,0:T(8,128)(2,1)S(1)}, u32[]{:S(2)}, u32[]{:S(2)}) collective-permute-start(bf16[256,512]{1,0:T(8,128)(2,1)S(1)} %get-tuple-element.245), channel_id=1, source_target_pairs={{0,1},{1,0},{2,3},{3,2},{4,5},{5,4},{6,7},{7,6},{8,9},{9,8},{10,11... | collective-permute-start | bytes 786440 | tf_op jit(solution)/shard_map/ppermute | solution.py:436
  101.4 46.6 %all-to-all-start = ((bf16[32,1,8,1152]{3,2,1,0:T(8,128)(2,1)}), bf16[32,1,8,1152]{3,2,1,0:T(8,128)(2,1)S(1)}, u32[]{:S(2)}, u32[]{:S(2)}) async-start(bf16[32,1,8,1152]{3,2,1,0:T(8,128)(2,1)} %bitcast.6), calls=%async_computation | async-start | bytes 1179648 | tf_op jit(solution)/shard_map/all_to_all | solution.py:472
  107.5 19.2 %collective-permute-start.30 = (bf16[256,512]{1,0:T(8,128)(2,1)S(1)}, bf16[256,512]{1,0:T(8,128)(2,1)S(1)}, u32[]{:S(2)}, u32[]{:S(2)}) collective-permute-start(bf16[256,512]{1,0:T(8,128)(2,1)S(1)} %get-tuple-element.248), channel_id=1, source_target_pairs={{0,2},{1,3},{2,4},{3,5},{4,6},{5,7},{6,0},{7,1},{8,10},{9,11},{10,... | collective-permute-start | bytes 786440 | tf_op jit(solution)/shard_map/ppermute | solution.py:436
  109.4 17.4 %collective-permute-start.31 = (bf16[256,512]{1,0:T(8,128)(2,1)S(1)}, bf16[256,512]{1,0:T(8,128)(2,1)S(1)}, u32[]{:S(2)}, u32[]{:S(2)}) collective-permute-start(bf16[256,512]{1,0:T(8,128)(2,1)S(1)} %get-tuple-element.249), channel_id=1, source_target_pairs={{0,1},{1,0},{2,3},{3,2},{4,5},{5,4},{6,7},{7,6},{8,9},{9,8},{10,11... | collective-permute-start | bytes 786440 | tf_op jit(solution)/shard_map/ppermute | solution.py:436
  110.9 21.4 %collective-permute-start.36 = (bf16[256,512]{1,0:T(8,128)(2,1)S(1)}, bf16[256,512]{1,0:T(8,128)(2,1)S(1)}, u32[]{:S(2)}, u32[]{:S(2)}) collective-permute-start(bf16[256,512]{1,0:T(8,128)(2,1)S(1)} %get-tuple-element.252), channel_id=1, source_target_pairs={{0,2},{1,3},{2,4},{3,5},{4,6},{5,7},{6,0},{7,1},{8,10},{9,11},{10,... | collective-permute-start | bytes 786440 | tf_op jit(solution)/shard_map/ppermute | solution.py:436
  112.4 19.9 %collective-permute-start.37 = (bf16[256,512]{1,0:T(8,128)(2,1)S(1)}, bf16[256,512]{1,0:T(8,128)(2,1)S(1)}, u32[]{:S(2)}, u32[]{:S(2)}) collective-permute-start(bf16[256,512]{1,0:T(8,128)(2,1)S(1)} %get-tuple-element.253), channel_id=1, source_target_pairs={{0,1},{1,0},{2,3},{3,2},{4,5},{5,4},{6,7},{7,6},{8,9},{9,8},{10,11... | collective-permute-start | bytes 786440 | tf_op jit(solution)/shard_map/ppermute | solution.py:436
  126.8 17.5 %collective-permute-start.34 = (bf16[256,512]{1,0:T(8,128)(2,1)S(1)}, bf16[256,512]{1,0:T(8,128)(2,1)S(1)}, u32[]{:S(2)}, u32[]{:S(2)}) collective-permute-start(bf16[256,512]{1,0:T(8,128)(2,1)S(1)} %get-tuple-element.256), channel_id=1, source_target_pairs={{0,2},{1,3},{2,4},{3,5},{4,6},{5,7},{6,0},{7,1},{8,10},{9,11},{10,... | collective-permute-start | bytes 786440 | tf_op jit(solution)/shard_map/ppermute | solution.py:436
  127.3 17.0 %collective-permute-start.35 = (bf16[256,512]{1,0:T(8,128)(2,1)S(1)}, bf16[256,512]{1,0:T(8,128)(2,1)S(1)}, u32[]{:S(2)}, u32[]{:S(2)}) collective-permute-start(bf16[256,512]{1,0:T(8,128)(2,1)S(1)} %get-tuple-element.257), channel_id=1, source_target_pairs={{0,1},{1,0},{2,3},{3,2},{4,5},{5,4},{6,7},{7,6},{8,9},{9,8},{10,11... | collective-permute-start | bytes 786440 | tf_op jit(solution)/shard_map/ppermute | solution.py:436
  132.4 15.6 %collective-permute-start.40 = (bf16[256,512]{1,0:T(8,128)(2,1)S(1)}, bf16[256,512]{1,0:T(8,128)(2,1)S(1)}, u32[]{:S(2)}, u32[]{:S(2)}) collective-permute-start(bf16[256,512]{1,0:T(8,128)(2,1)S(1)} %get-tuple-element.265), channel_id=1, source_target_pairs={{0,2},{1,3},{2,4},{3,5},{4,6},{5,7},{6,0},{7,1},{8,10},{9,11},{10,... | collective-permute-start | bytes 786440 | tf_op jit(solution)/shard_map/ppermute | solution.py:436
  132.9 15.1 %collective-permute-start.41 = (bf16[256,512]{1,0:T(8,128)(2,1)S(1)}, bf16[256,512]{1,0:T(8,128)(2,1)S(1)}, u32[]{:S(2)}, u32[]{:S(2)}) collective-permute-start(bf16[256,512]{1,0:T(8,128)(2,1)S(1)} %get-tuple-element.266), channel_id=1, source_target_pairs={{0,1},{1,0},{2,3},{3,2},{4,5},{5,4},{6,7},{7,6},{8,9},{9,8},{10,11... | collective-permute-start | bytes 786440 | tf_op jit(solution)/shard_map/ppermute | solution.py:436
  145.3 12.1 %collective-permute-start.38 = (bf16[256,512]{1,0:T(8,128)(2,1)}, bf16[256,512]{1,0:T(8,128)(2,1)S(1)}, u32[]{:S(2)}, u32[]{:S(2)}) collective-permute-start(bf16[256,512]{1,0:T(8,128)(2,1)} %get-tuple-element.269), channel_id=1, source_target_pairs={{0,2},{1,3},{2,4},{3,5},{4,6},{5,7},{6,0},{7,1},{8,10},{9,11},{10,... | collective-permute-start | bytes 786440 | tf_op jit(solution)/shard_map/ppermute | solution.py:436
  147.4 10.1 %collective-permute-start.39 = (bf16[256,512]{1,0:T(8,128)(2,1)}, bf16[256,512]{1,0:T(8,128)(2,1)S(1)}, u32[]{:S(2)}, u32[]{:S(2)}) collective-permute-start(bf16[256,512]{1,0:T(8,128)(2,1)} %get-tuple-element.270), channel_id=1, source_target_pairs={{0,1},{1,0},{2,3},{3,2},{4,5},{5,4},{6,7},{7,6},{8,9},{9,8},{10,11... | collective-permute-start | bytes 786440 | tf_op jit(solution)/shard_map/ppermute | solution.py:436
  150.2 37.1 %all-to-all-start.1 = ((bf16[32,4,8,256]{3,2,1,0:T(8,128)(2,1)}), bf16[32,4,8,256]{3,2,1,0:T(8,128)(2,1)S(1)}, u32[]{:S(2)}, u32[]{:S(2)}) async-start(bf16[32,4,8,256]{3,2,1,0:T(8,128)(2,1)} %bitcast.19), calls=%async_computation.1 | async-start | bytes 1048576 | tf_op jit(solution)/shard_map/all_to_all | solution.py:481
  154.2 19.2 %collective-permute-start.44 = (bf16[256,512]{1,0:T(8,128)(2,1)S(1)}, bf16[256,512]{1,0:T(8,128)(2,1)S(1)}, u32[]{:S(2)}, u32[]{:S(2)}) collective-permute-start(bf16[256,512]{1,0:T(8,128)(2,1)S(1)} %get-tuple-element.273), channel_id=1, source_target_pairs={{0,2},{1,3},{2,4},{3,5},{4,6},{5,7},{6,0},{7,1},{8,10},{9,11},{10,... | collective-permute-start | bytes 786440 | tf_op jit(solution)/shard_map/ppermute | solution.py:436
  156.0 17.4 %collective-permute-start.45 = (bf16[256,512]{1,0:T(8,128)(2,1)S(1)}, bf16[256,512]{1,0:T(8,128)(2,1)S(1)}, u32[]{:S(2)}, u32[]{:S(2)}) collective-permute-start(bf16[256,512]{1,0:T(8,128)(2,1)S(1)} %get-tuple-element.274), channel_id=1, source_target_pairs={{0,1},{1,0},{2,3},{3,2},{4,5},{5,4},{6,7},{7,6},{8,9},{9,8},{10,11... | collective-permute-start | bytes 786440 | tf_op jit(solution)/shard_map/ppermute | solution.py:436
  158.4 30.0 %collective-permute-start.42 = (bf16[256,512]{1,0:T(8,128)(2,1)}, bf16[256,512]{1,0:T(8,128)(2,1)}, u32[]{:S(2)}, u32[]{:S(2)}) collective-permute-start(bf16[256,512]{1,0:T(8,128)(2,1)} %get-tuple-element.277), channel_id=1, source_target_pairs={{0,2},{1,3},{2,4},{3,5},{4,6},{5,7},{6,0},{7,1},{8,10},{9,11},{10,... | collective-permute-start | bytes 786440 | tf_op jit(solution)/shard_map/ppermute | solution.py:436
  159.9 28.5 %collective-permute-start.43 = (bf16[256,512]{1,0:T(8,128)(2,1)}, bf16[256,512]{1,0:T(8,128)(2,1)}, u32[]{:S(2)}, u32[]{:S(2)}) collective-permute-start(bf16[256,512]{1,0:T(8,128)(2,1)} %get-tuple-element.278), channel_id=1, source_target_pairs={{0,1},{1,0},{2,3},{3,2},{4,5},{5,4},{6,7},{7,6},{8,9},{9,8},{10,11... | collective-permute-start | bytes 786440 | tf_op jit(solution)/shard_map/ppermute | solution.py:436
  174.2 14.1 %collective-permute-start.46 = (bf16[256,512]{1,0:T(8,128)(2,1)}, bf16[256,512]{1,0:T(8,128)(2,1)}, u32[]{:S(2)}, u32[]{:S(2)}) collective-permute-start(bf16[256,512]{1,0:T(8,128)(2,1)} %get-tuple-element.281), channel_id=1, source_target_pairs={{0,2},{1,3},{2,4},{3,5},{4,6},{5,7},{6,0},{7,1},{8,10},{9,11},{10,... | collective-permute-start | bytes 786440 | tf_op jit(solution)/shard_map/ppermute | solution.py:436
  174.3 14.1 %collective-permute-start.47 = (bf16[256,512]{1,0:T(8,128)(2,1)}, bf16[256,512]{1,0:T(8,128)(2,1)}, u32[]{:S(2)}, u32[]{:S(2)}) collective-permute-start(bf16[256,512]{1,0:T(8,128)(2,1)} %get-tuple-element.282), channel_id=1, source_target_pairs={{0,1},{1,0},{2,3},{3,2},{4,5},{5,4},{6,7},{7,6},{8,9},{9,8},{10,11... | collective-permute-start | bytes 786440 | tf_op jit(solution)/shard_map/ppermute | solution.py:436
  (36 other events, 610.6 us)
where the time goes:
time: 191 us; the launch traced here: 190 us
  starting transfers between devices  64 us (34%)
  waiting for transfers between devices  62.4 us (33%)
  Pallas kernels  50.7 us (27%)
  other arithmetic  6.1 us (3%)
  local copies, waits for them, and re-layouts  4.34 us (2%)
    ppermute x48, waiting for transfers between devices, shards(): held.append([lax.ppermute(turn[s], 'grp', perms[s]) for s in (0, 1)])  57.4 us
    ppermute x48, starting transfers between devices, shards(): held.append([lax.ppermute(turn[s], 'grp', perms[s]) for s in (0, 1)])  55.1 us
    pallas_call x4, Pallas kernels, update(): pl.pallas_call(functools.partial(update_kernel, tuple(numbers), width //...  25.8 us
    pallas_call x5, Pallas kernels, factor(): pl.pallas_call(functools.partial(factor_kernel, tuple(tiles), head), out_...  21.1 us
    all_to_all x1, starting transfers between devices, shards(): lax.all_to_all(pieces, ('front', 'grp'), split_axis=0, concat_axis=0, til...  5.04 us
    all_to_all x1, waiting for transfers between devices, parents(): lax.all_to_all(sums.reshape(n_dev, slots_dev, piece, TILE), ('front', 'gr...  4.99 us
    select_n x9, other arithmetic, shards(): value = jnp.where(others[s], held[e - CHAINS][1 - rules[s][0]], value)  4.05 us
    all_to_all x1, starting transfers between devices, parents(): lax.all_to_all(sums.reshape(n_dev, slots_dev, piece, TILE), ('front', 'gr...  3.87 us
  transfers between devices with their start and end apart: 50, of which 17 were waited for; matrix products, arithmetic and copies ran while one was open for 4% of the time, Pallas kernels for 25%

commit v1 on v0

--- a/solution.py
+++ b/solution.py
@@ -9,6 +9,7 @@
 
 TILE = 256
 CHAINS = 2
+SUM_AFTER = 3
 VMEM_LIMIT = 16 * 1024 * 1024
 UPDATE_LIMIT = 32 * 1024 * 1024
 HBM = pl.BlockSpec(memory_space=pltpu.HBM)
@@ -112,7 +113,10 @@
 def factor_kernel(tiles, head, mask, front, *refs):
     count = len(tiles)
     if head:
-        inverse, outs, (parts, one, blocks, sems, top, top_sem) = refs[0], refs[1 : count + 1], refs[count + 1 :]
+        source, outs, rest = refs[0], refs[1 : count + 1], refs[count + 1 :]
+        parts, one, blocks, sems, top, top_sem, inverse, inverse_sem = rest
+        inverse_copy = pltpu.make_async_copy(source, inverse, inverse_sem)
+        inverse_copy.start()
     else:
         parts, one, outs, (blocks, sems) = refs[0], refs[1], refs[2 : count + 2], refs[count + 2 :]
     copies = [
@@ -131,6 +135,7 @@
         return (dot(x, parts[1]) + dot(x, parts[0])).astype(jnp.bfloat16)
 
     if head:
+        inverse_copy.wait()
         for which in range(2):
             hi, low = split2(inverse[which].T)
             parts[2 * which] = hi
@@ -168,11 +173,12 @@
             jax.ShapeDtypeStruct((TILE, TILE), jnp.bfloat16),
         ]
         scratch += [pltpu.VMEM((TILE, TILE), jnp.bfloat16), pltpu.SemaphoreType.DMA(())]
-    operands = (inverse,) if head else parts
+        scratch += [pltpu.VMEM((2, TILE, TILE), jnp.float32), pltpu.SemaphoreType.DMA(())]
+    operands = (in_hbm(inverse),) if head else parts
     return pl.pallas_call(
         functools.partial(factor_kernel, tuple(tiles), head),
         out_shape=out_shape,
-        in_specs=[VMEM, HBM] + [VMEM] * len(operands),
+        in_specs=[VMEM, HBM] + [HBM if head else VMEM] * len(operands),
         out_specs=[VMEM] * len(out_shape),
         scratch_shapes=scratch,
         compiler_params=pltpu.CompilerParams(vmem_limit_bytes=VMEM_LIMIT),
@@ -271,7 +277,7 @@
         def begin(n=n, row=row, spot=spot):
             listed[spot] = row
             fetch(n, spot).start()
-            load(row, spot).start()
+            pl.when(spot < 4)(lambda: load(row, spot).start())
 
         pl.when(row > 0)(begin)
         spot = spot + (row > 0).astype(jnp.int32)
@@ -294,6 +300,8 @@
             fetch(0, spot).wait()
             load(0, spot).wait()
 
+        for ahead in (first + 4, first + 5):
+            pl.when(ahead < total)(lambda ahead=ahead: load(listed[ahead], ahead).start())
         ready(first)
         pl.when(both)(lambda: ready(first + 1))
         panel = panels[pl.ds(first, 2)].reshape(2 * TILE, 2 * TILE)
@@ -395,14 +403,14 @@
     longest = max(len(lists[0]), len(lists[1]))
 
     order = [(e, lists[s][e]) for e in range(longest) for s in (0, 1) if e < len(lists[s])] + [(longest, 0)]
-    cuts = [0, 2, 6] + list(range(14, len(order) - 2, 8)) + [len(order)]
+    cuts = [0, 4, 8] + list(range(16, len(order) - 2, 8)) + [len(order)]
     made, parts, where_made = [], None, {}
 
     def make(e, turn):
         nonlocal parts
         while len(made) < len(cuts) - 1:
             begin, end = cuts[len(made)], cuts[len(made) + 1]
-            if order[begin][0] > max(e + 1, e + 2 if begin > 2 else 0):
+            if order[begin][0] > max(0, e + 1 if begin < 8 else e + 2):
                 break
             names = [tile for _, tile in order[begin:end]]
             for n, tile in enumerate(names):
@@ -418,7 +426,69 @@
     odd = [[n for n in range(n_grp) if rules[s][n] != rules[s][0]] for s in (0, 1)]
     others = [one_of(g, odd[s]) if odd[s] else None for s in (0, 1)]
     scalars = [value for value in (root, *others) if value is not None]
-    held, turns, turn = [], [], ()
+    table = []
+    for n in range(n_grp):
+        line = []
+        for now in got:
+            for arrival in now:
+                line.append(arrival[n] if arrival[n] not in line else 0)
+        table.append(line)
+    rows = jnp.asarray(table, jnp.int32)
+    used = [[any(line[2 * e + s] for line in table) for s in (0, 1)] for e in range(events)]
+    for e in reversed(range(events - CHAINS)):
+        for s in (0, 1):
+            used[e][s] = used[e][s] or any(used[e + CHAINS])
+
+    needed = [
+        [n * cols_dev + c for c in range(cols_dev)] + [tiles - rows_out + r for r in range(rows_out)]
+        for n in range(n_grp)
+    ]
+    ready = max(table[n].index(tile) // 2 for n in range(1, n_grp) for tile in needed[n])
+
+    def own_part():
+        blocks, names = [], {}
+
+        def choice(tile, n):
+            if n == 0:
+                name = (-1, tile)
+                which, place = where_made[tile]
+                block = made[which][place]
+            else:
+                name = divmod(table[n].index(tile), 2)
+                block = held[name[0]][name[1]]
+            if name not in names:
+                names[name] = len(blocks)
+                blocks.append(block)
+            return names[name]
+
+        choices = [[choice(needed[n][part], n) for n in range(n_grp)] for part in range(cols_dev + rows_out)]
+        return own_panels(mask, targets, me, front, blocks, choices, rows_out)
+
+    piece = TILE // n_dev
+
+    def exchange(blocks):
+        return lax.all_to_all(blocks, ("front", "grp"), split_axis=0, concat_axis=0, tiled=True)
+
+    def sums_of(arrived):
+        digits = arrived[:, 0, 0, width : width + 2 * contrib].astype(jnp.int32).reshape(n_dev * contrib, 2)
+        labels = digits[:, 0] * 32 + digits[:, 1]
+        blocks = arrived[..., :width].reshape(n_dev, rows_out, piece, cols_dev, TILE)
+        blocks = jnp.transpose(blocks, (0, 3, 1, 2, 4)).reshape(n_dev * contrib, piece * TILE)
+        picker = labels[None, :] == jnp.arange(n_dev * slots_dev, dtype=jnp.int32)[:, None]
+        sums = dot(picker.astype(jnp.bfloat16), blocks).astype(jnp.bfloat16)
+        return sums.reshape(n_dev, slots_dev, piece, TILE)
+
+    held, turn, result, done = [], (), None, 0
+
+    def step(limit, at_hand, *waits):
+        nonlocal result, done
+        numbers = list(range(done, min(done + limit, at_hand)))
+        done += len(numbers)
+        here = after((me,), *waits)[0]
+        blocks = [held[n // 2][n % 2] for n in numbers]
+        if numbers:
+            result = update(rows, mask, here, own, front, numbers, blocks, base=result)
+
     for e in range(events):
         values = []
         for s in (0, 1):
@@ -432,72 +502,27 @@
                 value = made[which][n] if value is None else jnp.where(root, made[which][n], value)
             values.append(value)
         turn = after(values, *turn, *(scalars if e == 0 else ()))
-        turns.append(turn)
-        held.append([lax.ppermute(turn[s], "grp", perms[s]) for s in (0, 1)])
+        held.append([lax.ppermute(turn[s], "grp", perms[s]) if used[e][s] else turn[s] for s in (0, 1)])
         make(e, turn)
-        if e + 1 < events and e + 1 >= CHAINS:
+        if CHAINS <= e + 1 < events:
             held[e + 1 - CHAINS] = list(after(held[e + 1 - CHAINS], *turn))
-    table = []
-    for n in range(n_grp):
-        line = []
-        for now in got:
-            for arrival in now:
-                line.append(arrival[n] if arrival[n] not in line else 0)
-        table.append(line)
-    rows = jnp.asarray(table, jnp.int32)
-
-    blocks, names, ready = [], {}, 0
-
-    def choice(tile, n):
-        nonlocal ready
-        if n == 0:
-            name = (-1, tile)
-            which, place = where_made[tile]
-            block = made[which][place]
-        else:
-            name = divmod(table[n].index(tile), 2)
-            ready = max(ready, name[0])
-            block = held[name[0]][name[1]]
-        if name not in names:
-            names[name] = len(blocks)
-            blocks.append(block)
-        return names[name]
-
-    choices = [[choice(n * cols_dev + c, n) for n in range(n_grp)] for c in range(cols_dev)]
-    choices += [[choice(tiles - rows_out + r, n) for n in range(n_grp)] for r in range(rows_out)]
-    own, bottom = own_panels(mask, targets, me, front, blocks, choices, rows_out)
-
-    piece = TILE // n_dev
-    pieces = jnp.transpose(bottom.reshape(rows_out, n_dev, piece, width + 128), (1, 0, 2, 3))
-    arrived = lax.all_to_all(pieces, ("front", "grp"), split_axis=0, concat_axis=0, tiled=True)
-
-    def parents(arrived):
-        digits = arrived[:, 0, 0, width : width + 2 * contrib].astype(jnp.int32).reshape(n_dev * contrib, 2)
-        labels = digits[:, 0] * 32 + digits[:, 1]
-        blocks = arrived[..., :width].reshape(n_dev, rows_out, piece, cols_dev, TILE)
-        blocks = jnp.transpose(blocks, (0, 3, 1, 2, 4)).reshape(n_dev * contrib, piece * TILE)
-        picker = labels[None, :] == jnp.arange(n_dev * slots_dev, dtype=jnp.int32)[:, None]
-        sums = dot(picker.astype(jnp.bfloat16), blocks).astype(jnp.bfloat16)
-        sums = lax.all_to_all(
-            sums.reshape(n_dev, slots_dev, piece, TILE), ("front", "grp"), split_axis=0, concat_axis=0, tiled=True
-        )
-        return jnp.transpose(sums, (1, 0, 2, 3)).reshape(slots_dev, TILE, TILE).astype(jnp.float32)
-
-    result, parent_tiles = None, None
-    done, e = 0, ready + CHAINS + 1
+        late = e - ready - CHAINS
+        if late == 0:
+            own, bottom = own_part()
+            pieces = jnp.transpose(bottom.reshape(rows_out, n_dev, piece, width + 128), (1, 0, 2, 3))
+            arrived = exchange(pieces)
+        if late == SUM_AFTER:
+            sums = sums_of(after((arrived,), *turn)[0])
+            parent_pieces = exchange(sums)
+            turn = (*turn, sums)
+        if late >= 2 and late % 2 == 0:
+            step(12, 2 * (e - CHAINS + 1), *turn)
+            turn = (*turn, result)
+    parent_tiles = jnp.transpose(parent_pieces, (1, 0, 2, 3)).reshape(slots_dev, TILE, TILE).astype(jnp.float32)
+    if done < 2 * (events - CHAINS):
+        step(12, 2 * (events - CHAINS), *turn)
     while done < 2 * events:
-        at_hand = 2 * min(e - CHAINS + 1, events)
-        take = min(at_hand - done, 16)
-        if e < events - 1 and take < 16:
-            e += 1
-            continue
-        numbers = list(range(done, done + take))
-        done += take
-        if e >= events - 1 and parent_tiles is None:
-            parent_tiles = parents(after((arrived,), result)[0])
-        here = after((me,), *(turns[e] if e < events else (parent_tiles,)))[0]
-        result = update(rows, mask, here, own, front, numbers, [held[n // 2][n % 2] for n in numbers], base=result)
-        e = min(e + 2, events - 1) if e < events - 1 else e + CHAINS
+        step(12, 2 * events, parent_tiles)
     return (result[None], parent_tiles)
 
 

time: 191 us -> 194 us (1.016)
  waiting for transfers between devices: 62.4 us -> 58.4 us
  Pallas kernels: 50.7 us -> 53.7 us
  other arithmetic: 6.1 us -> 8.77 us
    ppermute x48 -> x47, waiting for transfers between devices: 57.4 us -> 43.4 us  [shards(): lax.ppermute(turn[s], 'grp', perms[s])]
    all_to_all x2, waiting for transfers between devices: 5 us -> 15 us  [exchange(): lax.all_to_all(blocks, ('front', 'grp'), split_axis=0, concat_axis=0, til...]
    pallas_call x4 -> x5, Pallas kernels: 25.8 us -> 28.3 us  [update(): pl.pallas_call(functools.partial(update_kernel, tuple(numbers), width //...]
    all_to_all x2, starting transfers between devices: 8.91 us -> 11 us  [exchange(): lax.all_to_all(blocks, ('front', 'grp'), split_axis=0, concat_axis=0, til...]
    ppermute x48 -> x47, starting transfers between devices: 55.1 us -> 53.6 us  [shards(): lax.ppermute(turn[s], 'grp', perms[s])]
  transfers between devices with their start and end apart: 50 -> 49, of which waited for: 17 -> 19; matrix products, arithmetic and copies ran while one was open for 4% -> 6% of each run, Pallas kernels for 25% -> 25%
where the time goes in v1:
time: 194 us; the launch traced here: 192 us
  starting transfers between devices  64.7 us (33%)
  waiting for transfers between devices  58.4 us (30%)
  Pallas kernels  53.7 us (28%)
  other arithmetic  8.77 us (5%)
  local copies, waits for them, and re-layouts  4.78 us (2%)
    ppermute x47, starting transfers between devices, shards(): lax.ppermute(turn[s], 'grp', perms[s])  53.6 us
    ppermute x47, waiting for transfers between devices, shards(): lax.ppermute(turn[s], 'grp', perms[s])  43.4 us
    pallas_call x5, Pallas kernels, update(): pl.pallas_call(functools.partial(update_kernel, tuple(numbers), width //...  28.3 us
    pallas_call x5, Pallas kernels, factor(): pl.pallas_call(functools.partial(factor_kernel, tuple(tiles), head), out_...  21.6 us
    all_to_all x2, waiting for transfers between devices, exchange(): lax.all_to_all(blocks, ('front', 'grp'), split_axis=0, concat_axis=0, til...  15 us
    all_to_all x2, starting transfers between devices, exchange(): lax.all_to_all(blocks, ('front', 'grp'), split_axis=0, concat_axis=0, til...  11 us
    select_n x9, other arithmetic, shards(): value = jnp.where(others[s], held[e - CHAINS][1 - rules[s][0]], value)  5.9 us
  transfers between devices with their start and end apart: 49, of which 19 were waited for; matrix products, arithmetic and copies ran while one was open for 6% of the time, Pallas kernels for 25%

profile of v1, /device:TPU:0, one launch (start us, length us, event | category | flops | bytes accessed | tf_op | source)
XLA Modules:
  0.0 192.2 jit_solution(13003957118622718346)
XLA Ops:
  1.4 3.8 %factor.5 = (bf16[256,512]{1,0:T(8,128)(2,1)S(1)}, bf16[256,512]{1,0:T(8,128)(2,1)S(1)}, bf16[256,512]{1,0:T(8,128)(2,1)S(1)}, bf16[256,512]{1,0:T(8,128)(2,1)S(...) custom-call(s32[32,4]{1,0:T(8,128)S(1)} %copy.75.mask, bf16[8192,1024]{1,0:T(8,128)(2,1)} %bitcast.26, ...), custom_call_target="tpu_custom_call" | custom-call | flops 805306368 | bytes 2097152 | tf_op jit(solution)/shard_map/factor/pallas_call | solution.py:178
  5.2 3.1 %collective-permute-start = (bf16[256,512]{1,0:T(8,128)(2,1)S(1)}, bf16[256,512]{1,0:T(8,128)(2,1)S(1)}, u32[]{:S(2)}, u32[]{:S(2)}) collective-permute-start(bf16[256,512]{1,0:T(8,128)(2,1)S(1)} %get-tuple-element.150.refs_18_), channel_id=1, source_target_pairs={{0,2},{1,3},{2,4},{3,5},{4,6},{5,7},{6,0},{7,1},{8,10},{9,11},{10,... | collective-permute-start | bytes 786440 | tf_op jit(solution)/shard_map/ppermute | solution.py:505
  8.3 1.5 collective-permute-start.1
  9.8 1.6 collective-permute-start.4
  11.9 3.0 %factor.6 = (bf16[256,512]{1,0:T(8,128)(2,1)S(1)}, bf16[256,512]{1,0:T(8,128)(2,1)S(1)}, bf16[256,512]{1,0:T(8,128)(2,1)S(1)}, bf16[256,512]{1,0:T(8,128)(2,1)S(1)}) custom-call(s32[32,4]{1,0:T(8,128)S(1)} %copy.75.mask, bf16[8192,1024]{1,0:T(8,128)(2,1)} %bitcast.27, bf16[4,256,256]{2,1,0:T(8,128)(2,1)S(1)} %get-tuple-element.214.refs_0_, ...), custom_call_target="tpu_custom_call" | custom-call | flops 805306368 | bytes 2097152 | tf_op jit(solution)/shard_map/factor/pallas_call | solution.py:178
  14.9 2.6 %collective-permute-done.refs_19_.refs_0_ = bf16[256,512]{1,0:T(8,128)(2,1)S(1)} collective-permute-done((bf16[256,512]{1,0:T(8,128)(2,1)S(1)}, bf16[256,512]{1,0:T(8,128)(2,1)S(1)}, u32[]{:S(2)}, u32[]{:S(2)}) %collective-permute-start) | collective-permute-done | bytes 262176 | tf_op jit(solution)/shard_map/ppermute | solution.py:505
  17.6 1.6 collective-permute-start.2
  19.2 1.5 collective-permute-start.3
  20.7 2.3 %collective-permute-done.4.refs_2_ = bf16[256,512]{1,0:T(8,128)(2,1)S(1)} collective-permute-done((bf16[256,512]{1,0:T(8,128)(2,1)S(1)}, bf16[256,512]{1,0:T(8,128)(2,1)S(1)}, u32[]{:S(2)}, u32[]{:S(2)}) %collective-permute-start.4) | collective-permute-done | bytes 262176 | tf_op jit(solution)/shard_map/ppermute | solution.py:505
  23.2 1.6 collective-permute-start.8
  24.8 1.6 collective-permute-start.9
  26.4 4.9 %factor.7 = (bf16[256,512]{1,0:T(8,128)(2,1)S(1)}, bf16[256,512]{1,0:T(8,128)(2,1)S(1)}, bf16[256,512]{1,0:T(8,128)(2,1)S(1)}, bf16[256,512]{1,0:T(8,128)(2,1)S(...) custom-call(s32[32,4]{1,0:T(8,128)S(1)} %copy.75.mask, ...), custom_call_target="tpu_custom_call" | custom-call | flops 1610612736 | bytes 4194304 | tf_op jit(solution)/shard_map/factor/pallas_call | solution.py:178
  31.5 1.6 collective-permute-start.6
  34.0 2.0 %collective-permute-start.12 = (bf16[256,512]{1,0:T(8,128)(2,1)S(1)}, bf16[256,512]{1,0:T(8,128)(2,1)S(1)}, u32[]{:S(2)}, u32[]{:S(2)}) collective-permute-start(bf16[256,512]{1,0:T(8,128)(2,1)S(1)} %get-tuple-element.181), channel_id=1, source_target_pairs={{0,2},{1,3},{2,4},{3,5},{4,6},{5,7},{6,0},{7,1},{8,10},{9,11},{10,... | collective-permute-start | bytes 786440 | tf_op jit(solution)/shard_map/ppermute | solution.py:505
  36.0 1.5 collective-permute-start.13
  37.6 4.7 %collective-permute-done.6.refs_23_.refs_8_ = bf16[256,512]{1,0:T(8,128)(2,1)S(1)} collective-permute-done((bf16[256,512]{1,0:T(8,128)(2,1)S(1)}, bf16[256,512]{1,0:T(8,128)(2,1)S(1)}, u32[]{:S(2)}, u32[]{:S(2)}) %collective-permute-start.6) | collective-permute-done | bytes 262176 | tf_op jit(solution)/shard_map/ppermute | solution.py:505
  43.5 4.4 %collective-permute-done.12.refs_10_ = bf16[256,512]{1,0:T(8,128)(2,1)S(1)} collective-permute-done((bf16[256,512]{1,0:T(8,128)(2,1)S(1)}, bf16[256,512]{1,0:T(8,128)(2,1)S(1)}, u32[]{:S(2)}, u32[]{:S(2)}) %collective-permute-start.12) | collective-permute-done | bytes 262176 | tf_op jit(solution)/shard_map/ppermute | solution.py:505
  49.7 4.9 %factor.8 = (bf16[256,512]{1,0:T(8,128)(2,1)S(1)}, bf16[256,512]{1,0:T(8,128)(2,1)S(1)}, bf16[256,512]{1,0:T(8,128)(2,1)S(1)}, bf16[256,512]{1,0:T(8,128)(2,1)S(...) custom-call(s32[32,4]{1,0:T(8,128)S(1)} %copy.75.mask, ...), custom_call_target="tpu_custom_call" | custom-call | flops 1610612736 | bytes 4194304 | tf_op jit(solution)/shard_map/factor/pallas_call | solution.py:178
  54.8 1.3 collective-permute-start.14
  56.1 1.7 collective-permute-start.15
  59.2 1.1 collective-permute-start.21
  60.4 5.5 %collective-permute-done.14.refs_3_.refs_4_ = bf16[256,512]{1,0:T(8,128)(2,1)S(1)} collective-permute-done((bf16[256,512]{1,0:T(8,128)(2,1)S(1)}, bf16[256,512]{1,0:T(8,128)(2,1)S(1)}, u32[]{:S(2)}, u32[]{:S(2)}) %collective-permute-start.14) | collective-permute-done | bytes 262176 | tf_op jit(solution)/shard_map/ppermute | solution.py:505
  66.5 1.9 collective-permute-start.19
  68.4 3.1 %collective-permute-done.20.refs_8_.refs_6_ = bf16[256,512]{1,0:T(8,128)(2,1)S(1)} collective-permute-done((bf16[256,512]{1,0:T(8,128)(2,1)S(1)}, bf16[256,512]{1,0:T(8,128)(2,1)S(1)}, u32[]{:S(2)}, u32[]{:S(2)}) %collective-permute-start.20) | collective-permute-done | bytes 262176 | tf_op jit(solution)/shard_map/ppermute | solution.py:505
  72.3 1.9 collective-permute-start.23
  74.2 5.0 %factor.9 = (bf16[256,512]{1,0:T(8,128)(2,1)S(1)}, bf16[256,512]{1,0:T(8,128)(2,1)S(1)}, bf16[256,512]{1,0:T(8,128)(2,1)S(1)}, bf16[256,512]{1,0:T(8,128)(2,1)S(...) custom-call(s32[32,4]{1,0:T(8,128)S(1)} %copy.75.mask, ...), custom_call_target="tpu_custom_call" | custom-call | flops 1610612736 | bytes 4194304 | tf_op jit(solution)/shard_map/factor/pallas_call | solution.py:178
  79.4 1.8 collective-permute-start.24
  81.7 1.2 collective-permute-done.22.refs_7_.refs_10_
  82.9 0.8 collective-permute-start.26
  83.8 1.5 collective-permute-start.27
  85.3 3.1 %collective-permute-done.24.refs_13_.refs_0_ = bf16[256,512]{1,0:T(8,128)(2,1)S(1)} collective-permute-done((bf16[256,512]{1,0:T(8,128)(2,1)S(1)}, bf16[256,512]{1,0:T(8,128)(2,1)S(1)}, u32[]{:S(2)}, u32[]{:S(2)}) %collective-permute-start.24) | collective-permute-done | bytes 262176 | tf_op jit(solution)/shard_map/ppermute | solution.py:505
  88.4 1.6 collective-permute-done.25.refs_12_.refs_1_
  89.9 0.9 select_select_fusion.1
  91.3 2.7 %collective-permute-done.26.refs_16_.refs_2_ = bf16[256,512]{1,0:T(8,128)(2,1)S(1)} collective-permute-done((bf16[256,512]{1,0:T(8,128)(2,1)S(1)}, bf16[256,512]{1,0:T(8,128)(2,1)S(1)}, u32[]{:S(2)}, u32[]{:S(2)}) %collective-permute-start.26) | collective-permute-done | bytes 262176 | tf_op jit(solution)/shard_map/ppermute | solution.py:505
  94.0 1.6 collective-permute-done.27.refs_15_.refs_3_
  95.6 0.9 broadcast_select_fusion.8
  97.1 3.8 %own_panels.1 = (bf16[512,1024]{1,0:T(8,128)(2,1)S(1)}, bf16[256,1152]{1,0:T(8,128)(2,1)}) custom-call(s32[32,4]{1,0:T(8,128)S(1)} %copy.75.mask, s32[4]{0:T(128)S(1)} %bitcast.25, s32[1]{0:T(128)} %bitcast.1.me, bf16[8192,1024]{1,0:T(8,128)(2,1)} %bitcast.31, bf16[256,512]{1,0:T(8,128)(2,1)} %copy-done.4, bf16[256,512]{1,0:T(8,128)(2,1)} %copy-done.19, ...), custom_call_target="tpu_custom_call" | custom-call | flops 268435456 | bytes 2621440 | tf_op jit(solution)/shard_map/own_panels/pallas_call | solution.py:232
  100.9 6.2 %all-to-all-start = ((bf16[32,1,8,1152]{3,2,1,0:T(8,128)(2,1)}), bf16[32,1,8,1152]{3,2,1,0:T(8,128)(2,1)S(1)}, u32[]{:S(2)}, u32[]{:S(2)}) async-start(bf16[32,1,8,1152]{3,2,1,0:T(8,128)(2,1)} %bitcast.6), calls=%async_computation | async-start | bytes 1179648 | tf_op jit(solution)/shard_map/all_to_all | solution.py:470
  107.2 1.1 broadcast_select_fusion.7
  108.3 1.8 collective-permute-start.30
  110.1 1.5 collective-permute-start.31
  111.5 1.1 broadcast_select_fusion.6
  112.6 1.5 collective-permute-start.36
  114.7 5.7 %update.5.refs_12_ = bf16[8192,1024]{1,0:T(8,128)(2,1)} custom-call(s32[8,48]{1,0:T(8,128)S(1)} %copy-done.5, s32[32,4]{1,0:T(8,128)S(1)} %copy.75.mask, s32[1]{0:T(128)} %bitcast.1.me, bf16[512,1024]{1,0:T(8,128)(2,1)S(1)} %get-tuple-element.258.own, bf16[8192,1024]{1,0:T(8,128)(2,1)} %bitcast.32, bf16[256,512]{1,0:T(8,128)(2,1)} %copy-done.7, ...), custom_call_target="tpu_custom_call" | custom-call | flops 3221225472 | bytes 12582912 | tf_op jit(solution)/shard_map/update/pallas_call | solution.py:348
  120.4 7.0 %collective-permute-done.30.refs_8_ = bf16[256,512]{1,0:T(8,128)(2,1)S(1)} collective-permute-done((bf16[256,512]{1,0:T(8,128)(2,1)S(1)}, bf16[256,512]{1,0:T(8,128)(2,1)S(1)}, u32[]{:S(2)}, u32[]{:S(2)}) %collective-permute-start.30) | collective-permute-done | bytes 262176 | tf_op jit(solution)/shard_map/ppermute | solution.py:505
  127.5 1.0 broadcast_select_fusion.5
  128.9 1.4 collective-permute-start.35
  130.3 2.6 %collective-permute-done.36.refs_10_ = bf16[256,512]{1,0:T(8,128)(2,1)S(1)} collective-permute-done((bf16[256,512]{1,0:T(8,128)(2,1)S(1)}, bf16[256,512]{1,0:T(8,128)(2,1)S(1)}, u32[]{:S(2)}, u32[]{:S(2)}) %collective-permute-start.36) | collective-permute-done | bytes 262176 | tf_op jit(solution)/shard_map/ppermute | solution.py:505
  132.9 0.9 broadcast_select_fusion.4
  133.8 7.9 %all-to-all-done = bf16[32,1,8,1152]{3,2,1,0:T(8,128)(2,1)S(1)} async-done(((bf16[32,1,8,1152]{3,2,1,0:T(8,128)(2,1)}), bf16[32,1,8,1152]{3,2,1,0:T(8,128)(2,1)S(1)}, u32[]{:S(2)}, u32[]{:S(2)}) %all-to-all-start) | async-done | bytes 589856 | tf_op jit(solution)/shard_map/all_to_all | solution.py:470
  143.1 0.9 copy.77
  144.8 4.8 %all-to-all-start.1 = ((bf16[32,4,8,256]{3,2,1,0:T(8,128)(2,1)}), bf16[32,4,8,256]{3,2,1,0:T(8,128)(2,1)S(1)}, u32[]{:S(2)}, u32[]{:S(2)}) async-start(bf16[32,4,8,256]{3,2,1,0:T(8,128)(2,1)} %bitcast.19), calls=%async_computation.1 | async-start | bytes 1048576 | tf_op jit(solution)/shard_map/all_to_all | solution.py:470
  149.6 8.4 %update.6.refs_12_ = bf16[8192,1024]{1,0:T(8,128)(2,1)} custom-call(s32[8,48]{1,0:T(8,128)S(1)} %copy-done.5, s32[32,4]{1,0:T(8,128)S(1)} %copy.75.mask, s32[1]{0:T(128)} %bitcast.1.me, bf16[512,1024]{1,0:T(8,128)(2,1)S(1)} %get-tuple-element.258.own, bf16[8192,1024]{1,0:T(8,128)(2,1)} %bitcast.33, ...), custom_call_target="tpu_custom_call", output_to_operand_aliasing={{}: (17, {})} | custom-call | flops 3221225472 | bytes 12582912 | tf_op jit(solution)/shard_map/update/pallas_call | solution.py:348
  158.1 1.6 collective-permute-start.38
  159.8 1.5 collective-permute-start.39
  161.3 1.5 collective-permute-start.44
  163.4 8.2 %update.7.refs_8_ = bf16[8192,1024]{1,0:T(8,128)(2,1)} custom-call(s32[8,48]{1,0:T(8,128)S(1)} %copy-done.5, s32[32,4]{1,0:T(8,128)S(1)} %copy.75.mask, s32[1]{0:T(128)} %bitcast.1.me, bf16[512,1024]{1,0:T(8,128)(2,1)S(1)} %get-tuple-element.258.own, bf16[8192,1024]{1,0:T(8,128)(2,1)} %bitcast.34, ...), custom_call_target="tpu_custom_call", output_to_operand_aliasing={{}: (17, {})} | custom-call | flops 3221225472 | bytes 12582912 | tf_op jit(solution)/shard_map/update/pallas_call | solution.py:348
  172.0 2.6 %collective-permute-start.43 = (bf16[256,512]{1,0:T(8,128)(2,1)S(1)}, bf16[256,512]{1,0:T(8,128)(2,1)S(1)}, u32[]{:S(2)}, u32[]{:S(2)}) collective-permute-start(bf16[256,512]{1,0:T(8,128)(2,1)S(1)} %get-tuple-element.280), channel_id=1, source_target_pairs={{0,1},{1,0},{2,3},{3,2},{4,5},{5,4},{6,7},{7,6},{8,9},{9,8},{10,11... | collective-permute-start | bytes 786440 | tf_op jit(solution)/shard_map/ppermute | solution.py:505
  174.6 0.9 broadcast_select_fusion
  175.5 0.8 collective-permute-start.46
  176.3 5.0 %update.8.refs_4_ = bf16[8192,1024]{1,0:T(8,128)(2,1)} custom-call(s32[8,48]{1,0:T(8,128)S(1)} %copy-done.5, s32[32,4]{1,0:T(8,128)S(1)} %copy.75.mask, s32[1]{0:T(128)} %bitcast.1.me, bf16[512,1024]{1,0:T(8,128)(2,1)S(1)} %get-tuple-element.258.own, bf16[8192,1024]{1,0:T(8,128)(2,1)} %bitcast.35, ...), custom_call_target="tpu_custom_call", output_to_operand_aliasing={{}: (13, {})} | custom-call | flops 2147483648 | bytes 8388608 | tf_op jit(solution)/shard_map/update/pallas_call | solution.py:348
  181.3 7.1 %all-to-all-done.1 = bf16[32,4,8,256]{3,2,1,0:T(8,128)(2,1)S(1)} async-done(((bf16[32,4,8,256]{3,2,1,0:T(8,128)(2,1)}), bf16[32,4,8,256]{3,2,1,0:T(8,128)(2,1)S(1)}, u32[]{:S(2)}, u32[]{:S(2)}) %all-to-all-start.1) | async-done | bytes 524320 | tf_op jit(solution)/shard_map/all_to_all | solution.py:470
  188.4 1.1 copy_bitcast_fusion
  191.0 1.0 update.9
  (178 shorter events, 15.9 us)
Async XLA Ops:
  5.2 26.2 %copy-start.3 = (bf16[256,512]{1,0:T(8,128)(2,1)}, bf16[256,512]{1,0:T(8,128)(2,1)S(1)}, u32[]{:S(2)}) copy-start(bf16[256,512]{1,0:T(8,128)(2,1)S(1)} %get-tuple-element.150.refs_18_) | copy-start | bytes 786436
  5.2 12.2 %collective-permute-start = (bf16[256,512]{1,0:T(8,128)(2,1)S(1)}, bf16[256,512]{1,0:T(8,128)(2,1)S(1)}, u32[]{:S(2)}, u32[]{:S(2)}) collective-permute-start(bf16[256,512]{1,0:T(8,128)(2,1)S(1)} %get-tuple-element.150.refs_18_), channel_id=1, source_target_pairs={{0,2},{1,3},{2,4},{3,5},{4,6},{5,7},{6,0},{7,1},{8,10},{9,11},{10,... | collective-permute-start | bytes 786440 | tf_op jit(solution)/shard_map/ppermute | solution.py:505
  8.3 9.2 %collective-permute-start.1 = (bf16[256,512]{1,0:T(8,128)(2,1)S(1)}, bf16[256,512]{1,0:T(8,128)(2,1)S(1)}, u32[]{:S(2)}, u32[]{:S(2)}) collective-permute-start(bf16[256,512]{1,0:T(8,128)(2,1)S(1)} %get-tuple-element.151), channel_id=1, source_target_pairs={{0,1},{1,0},{2,3},{3,2},{4,5},{5,4},{6,7},{7,6},{8,9},{9,8},{10,11... | collective-permute-start | bytes 786440 | tf_op jit(solution)/shard_map/ppermute | solution.py:505
  9.8 13.3 %collective-permute-start.4 = (bf16[256,512]{1,0:T(8,128)(2,1)S(1)}, bf16[256,512]{1,0:T(8,128)(2,1)S(1)}, u32[]{:S(2)}, u32[]{:S(2)}) collective-permute-start(bf16[256,512]{1,0:T(8,128)(2,1)S(1)} %get-tuple-element.152), channel_id=1, source_target_pairs={{0,2},{1,3},{2,4},{3,5},{4,6},{5,7},{6,0},{7,1},{8,10},{9,11},{10,... | collective-permute-start | bytes 786440 | tf_op jit(solution)/shard_map/ppermute | solution.py:505
  11.4 11.8 %collective-permute-start.5 = (bf16[256,512]{1,0:T(8,128)(2,1)S(1)}, bf16[256,512]{1,0:T(8,128)(2,1)S(1)}, u32[]{:S(2)}, u32[]{:S(2)}) collective-permute-start(bf16[256,512]{1,0:T(8,128)(2,1)S(1)} %get-tuple-element.153), channel_id=1, source_target_pairs={{0,1},{1,0},{2,3},{3,2},{4,5},{5,4},{6,7},{7,6},{8,9},{9,8},{10,11... | collective-permute-start | bytes 786440 | tf_op jit(solution)/shard_map/ppermute | solution.py:505
  17.4 37.2 %copy-start.7 = (bf16[256,512]{1,0:T(8,128)(2,1)}, bf16[256,512]{1,0:T(8,128)(2,1)S(1)}, u32[]{:S(2)}) copy-start(bf16[256,512]{1,0:T(8,128)(2,1)S(1)} %collective-permute-done.refs_19_.refs_0_) | copy-start | bytes 786436
  17.6 13.8 %collective-permute-start.2 = (bf16[256,512]{1,0:T(8,128)(2,1)S(1)}, bf16[256,512]{1,0:T(8,128)(2,1)S(1)}, u32[]{:S(2)}, u32[]{:S(2)}) collective-permute-start(bf16[256,512]{1,0:T(8,128)(2,1)S(1)} %get-tuple-element.160), channel_id=1, source_target_pairs={{0,2},{1,3},{2,4},{3,5},{4,6},{5,7},{6,0},{7,1},{8,10},{9,11},{10,... | collective-permute-start | bytes 786440 | tf_op jit(solution)/shard_map/ppermute | solution.py:505
  19.2 12.2 %collective-permute-start.3 = (bf16[256,512]{1,0:T(8,128)(2,1)S(1)}, bf16[256,512]{1,0:T(8,128)(2,1)S(1)}, u32[]{:S(2)}, u32[]{:S(2)}) collective-permute-start(bf16[256,512]{1,0:T(8,128)(2,1)S(1)} %get-tuple-element.161), channel_id=1, source_target_pairs={{0,1},{1,0},{2,3},{3,2},{4,5},{5,4},{6,7},{7,6},{8,9},{9,8},{10,11... | collective-permute-start | bytes 786440 | tf_op jit(solution)/shard_map/ppermute | solution.py:505
  23.2 10.8 %collective-permute-start.8 = (bf16[256,512]{1,0:T(8,128)(2,1)S(1)}, bf16[256,512]{1,0:T(8,128)(2,1)S(1)}, u32[]{:S(2)}, u32[]{:S(2)}) collective-permute-start(bf16[256,512]{1,0:T(8,128)(2,1)S(1)} %get-tuple-element.170), channel_id=1, source_target_pairs={{0,2},{1,3},{2,4},{3,5},{4,6},{5,7},{6,0},{7,1},{8,10},{9,11},{10,... | collective-permute-start | bytes 786440 | tf_op jit(solution)/shard_map/ppermute | solution.py:505
  24.8 9.2 %collective-permute-start.9 = (bf16[256,512]{1,0:T(8,128)(2,1)S(1)}, bf16[256,512]{1,0:T(8,128)(2,1)S(1)}, u32[]{:S(2)}, u32[]{:S(2)}) collective-permute-start(bf16[256,512]{1,0:T(8,128)(2,1)S(1)} %get-tuple-element.171), channel_id=1, source_target_pairs={{0,1},{1,0},{2,3},{3,2},{4,5},{5,4},{6,7},{7,6},{8,9},{9,8},{10,11... | collective-permute-start | bytes 786440 | tf_op jit(solution)/shard_map/ppermute | solution.py:505
  31.4 47.8 %copy-start.8 = (bf16[256,512]{1,0:T(8,128)(2,1)}, bf16[256,512]{1,0:T(8,128)(2,1)S(1)}, u32[]{:S(2)}) copy-start(bf16[256,512]{1,0:T(8,128)(2,1)S(1)} %collective-permute-done.2.refs_21_.refs_4_) | copy-start | bytes 786436
  31.4 47.8 %copy-start.9 = (bf16[256,512]{1,0:T(8,128)(2,1)}, bf16[256,512]{1,0:T(8,128)(2,1)S(1)}, u32[]{:S(2)}) copy-start(bf16[256,512]{1,0:T(8,128)(2,1)S(1)} %collective-permute-done.3.refs_20_.refs_5_) | copy-start | bytes 786436
  31.5 10.8 %collective-permute-start.6 = (bf16[256,512]{1,0:T(8,128)(2,1)S(1)}, bf16[256,512]{1,0:T(8,128)(2,1)S(1)}, u32[]{:S(2)}, u32[]{:S(2)}) collective-permute-start(bf16[256,512]{1,0:T(8,128)(2,1)S(1)} %get-tuple-element.175), channel_id=1, source_target_pairs={{0,2},{1,3},{2,4},{3,5},{4,6},{5,7},{6,0},{7,1},{8,10},{9,11},{10,... | collective-permute-start | bytes 786440 | tf_op jit(solution)/shard_map/ppermute | solution.py:505
  33.1 9.1 %collective-permute-start.7 = (bf16[256,512]{1,0:T(8,128)(2,1)S(1)}, bf16[256,512]{1,0:T(8,128)(2,1)S(1)}, u32[]{:S(2)}, u32[]{:S(2)}) collective-permute-start(bf16[256,512]{1,0:T(8,128)(2,1)S(1)} %get-tuple-element.176), channel_id=1, source_target_pairs={{0,1},{1,0},{2,3},{3,2},{4,5},{5,4},{6,7},{7,6},{8,9},{9,8},{10,11... | collective-permute-start | bytes 786440 | tf_op jit(solution)/shard_map/ppermute | solution.py:505
  34.0 13.8 %collective-permute-start.12 = (bf16[256,512]{1,0:T(8,128)(2,1)S(1)}, bf16[256,512]{1,0:T(8,128)(2,1)S(1)}, u32[]{:S(2)}, u32[]{:S(2)}) collective-permute-start(bf16[256,512]{1,0:T(8,128)(2,1)S(1)} %get-tuple-element.181), channel_id=1, source_target_pairs={{0,2},{1,3},{2,4},{3,5},{4,6},{5,7},{6,0},{7,1},{8,10},{9,11},{10,... | collective-permute-start | bytes 786440 | tf_op jit(solution)/shard_map/ppermute | solution.py:505
  36.0 11.8 %collective-permute-start.13 = (bf16[256,512]{1,0:T(8,128)(2,1)S(1)}, bf16[256,512]{1,0:T(8,128)(2,1)S(1)}, u32[]{:S(2)}, u32[]{:S(2)}) collective-permute-start(bf16[256,512]{1,0:T(8,128)(2,1)S(1)} %get-tuple-element.182), channel_id=1, source_target_pairs={{0,1},{1,0},{2,3},{3,2},{4,5},{5,4},{6,7},{7,6},{8,9},{9,8},{10,11... | collective-permute-start | bytes 786440 | tf_op jit(solution)/shard_map/ppermute | solution.py:505
  42.2 37.0 %copy-start.14 = (bf16[256,512]{1,0:T(8,128)(2,1)}, bf16[256,512]{1,0:T(8,128)(2,1)S(1)}, u32[]{:S(2)}) copy-start(bf16[256,512]{1,0:T(8,128)(2,1)S(1)} %collective-permute-done.6.refs_23_.refs_8_) | copy-start | bytes 786436
  42.2 37.0 %copy-start.15 = (bf16[256,512]{1,0:T(8,128)(2,1)}, bf16[256,512]{1,0:T(8,128)(2,1)S(1)}, u32[]{:S(2)}) copy-start(bf16[256,512]{1,0:T(8,128)(2,1)S(1)} %collective-permute-done.7.refs_22_.refs_9_) | copy-start | bytes 786436
  42.3 12.4 %collective-permute-start.10 = (bf16[256,512]{1,0:T(8,128)(2,1)S(1)}, bf16[256,512]{1,0:T(8,128)(2,1)S(1)}, u32[]{:S(2)}, u32[]{:S(2)}) collective-permute-start(bf16[256,512]{1,0:T(8,128)(2,1)S(1)} %get-tuple-element.186), channel_id=1, source_target_pairs={{0,2},{1,3},{2,4},{3,5},{4,6},{5,7},{6,0},{7,1},{8,10},{9,11},{10,... | collective-permute-start | bytes 786440 | tf_op jit(solution)/shard_map/ppermute | solution.py:505
  43.0 11.7 %collective-permute-start.11 = (bf16[256,512]{1,0:T(8,128)(2,1)S(1)}, bf16[256,512]{1,0:T(8,128)(2,1)S(1)}, u32[]{:S(2)}, u32[]{:S(2)}) collective-permute-start(bf16[256,512]{1,0:T(8,128)(2,1)S(1)} %get-tuple-element.187), channel_id=1, source_target_pairs={{0,1},{1,0},{2,3},{3,2},{4,5},{5,4},{6,7},{7,6},{8,9},{9,8},{10,11... | collective-permute-start | bytes 786440 | tf_op jit(solution)/shard_map/ppermute | solution.py:505
  48.6 9.7 %collective-permute-start.16 = (bf16[256,512]{1,0:T(8,128)(2,1)S(1)}, bf16[256,512]{1,0:T(8,128)(2,1)S(1)}, u32[]{:S(2)}, u32[]{:S(2)}) collective-permute-start(bf16[256,512]{1,0:T(8,128)(2,1)S(1)} %get-tuple-element.196), channel_id=1, source_target_pairs={{0,2},{1,3},{2,4},{3,5},{4,6},{5,7},{6,0},{7,1},{8,10},{9,11},{10,... | collective-permute-start | bytes 786440 | tf_op jit(solution)/shard_map/ppermute | solution.py:505
  49.2 9.2 %collective-permute-start.17 = (bf16[256,512]{1,0:T(8,128)(2,1)S(1)}, bf16[256,512]{1,0:T(8,128)(2,1)S(1)}, u32[]{:S(2)}, u32[]{:S(2)}) collective-permute-start(bf16[256,512]{1,0:T(8,128)(2,1)S(1)} %get-tuple-element.197), channel_id=1, source_target_pairs={{0,1},{1,0},{2,3},{3,2},{4,5},{5,4},{6,7},{7,6},{8,9},{9,8},{10,11... | collective-permute-start | bytes 786440 | tf_op jit(solution)/shard_map/ppermute | solution.py:505
  54.7 42.5 %copy-start.6 = (s32[1,1,4]{2,1,0:T(1,128)S(1)}, s32[1,1,4]{2,1,0:T(1,128)}, u32[]{:S(2)}) copy-start(s32[1,1,4]{2,1,0:T(1,128)} %param.8) | copy-start | bytes 52
  54.7 42.3 %copy-start.10 = (bf16[256,512]{1,0:T(8,128)(2,1)}, bf16[256,512]{1,0:T(8,128)(2,1)S(1)}, u32[]{:S(2)}) copy-start(bf16[256,512]{1,0:T(8,128)(2,1)S(1)} %collective-permute-done.10.refs_4_.refs_0_) | copy-start | bytes 786436
  54.7 42.3 %copy-start.11 = (bf16[256,512]{1,0:T(8,128)(2,1)}, bf16[256,512]{1,0:T(8,128)(2,1)S(1)}, u32[]{:S(2)}) copy-start(bf16[256,512]{1,0:T(8,128)(2,1)S(1)} %collective-permute-done.11.refs_17_.refs_1_) | copy-start | bytes 786436
  54.8 11.1 %collective-permute-start.14 = (bf16[256,512]{1,0:T(8,128)(2,1)S(1)}, bf16[256,512]{1,0:T(8,128)(2,1)S(1)}, u32[]{:S(2)}, u32[]{:S(2)}) collective-permute-start(bf16[256,512]{1,0:T(8,128)(2,1)S(1)} %get-tuple-element.201), channel_id=1, source_target_pairs={{0,2},{1,3},{2,4},{3,5},{4,6},{5,7},{6,0},{7,1},{8,10},{9,11},{10,... | collective-permute-start | bytes 786440 | tf_op jit(solution)/shard_map/ppermute | solution.py:505
  56.1 9.8 %collective-permute-start.15 = (bf16[256,512]{1,0:T(8,128)(2,1)S(1)}, bf16[256,512]{1,0:T(8,128)(2,1)S(1)}, u32[]{:S(2)}, u32[]{:S(2)}) collective-permute-start(bf16[256,512]{1,0:T(8,128)(2,1)S(1)} %get-tuple-element.202), channel_id=1, source_target_pairs={{0,1},{1,0},{2,3},{3,2},{4,5},{5,4},{6,7},{7,6},{8,9},{9,8},{10,11... | collective-permute-start | bytes 786440 | tf_op jit(solution)/shard_map/ppermute | solution.py:505
  58.4 38.6 %copy-start.12 = (bf16[256,512]{1,0:T(8,128)(2,1)}, bf16[256,512]{1,0:T(8,128)(2,1)S(1)}, u32[]{:S(2)}) copy-start(bf16[256,512]{1,0:T(8,128)(2,1)S(1)} %collective-permute-done.16.refs_9_.refs_2_) | copy-start | bytes 786436
  58.4 38.6 %copy-start.13 = (bf16[256,512]{1,0:T(8,128)(2,1)}, bf16[256,512]{1,0:T(8,128)(2,1)S(1)}, u32[]{:S(2)}) copy-start(bf16[256,512]{1,0:T(8,128)(2,1)S(1)} %collective-permute-done.17.refs_10_.refs_3_) | copy-start | bytes 786436
  58.5 13.0 %collective-permute-start.20 = (bf16[256,512]{1,0:T(8,128)(2,1)S(1)}, bf16[256,512]{1,0:T(8,128)(2,1)S(1)}, u32[]{:S(2)}, u32[]{:S(2)}) collective-permute-start(bf16[256,512]{1,0:T(8,128)(2,1)S(1)} %get-tuple-element.207), channel_id=1, source_target_pairs={{0,2},{1,3},{2,4},{3,5},{4,6},{5,7},{6,0},{7,1},{8,10},{9,11},{10,... | collective-permute-start | bytes 786440 | tf_op jit(solution)/shard_map/ppermute | solution.py:505
  59.2 12.3 %collective-permute-start.21 = (bf16[256,512]{1,0:T(8,128)(2,1)S(1)}, bf16[256,512]{1,0:T(8,128)(2,1)S(1)}, u32[]{:S(2)}, u32[]{:S(2)}) collective-permute-start(bf16[256,512]{1,0:T(8,128)(2,1)S(1)} %get-tuple-element.208), channel_id=1, source_target_pairs={{0,1},{1,0},{2,3},{3,2},{4,5},{5,4},{6,7},{7,6},{8,9},{9,8},{10,11... | collective-permute-start | bytes 786440 | tf_op jit(solution)/shard_map/ppermute | solution.py:505
  65.9 31.1 %copy-start.16 = (bf16[256,512]{1,0:T(8,128)(2,1)}, bf16[256,512]{1,0:T(8,128)(2,1)S(1)}, u32[]{:S(2)}) copy-start(bf16[256,512]{1,0:T(8,128)(2,1)S(1)} %collective-permute-done.14.refs_3_.refs_4_) | copy-start | bytes 786436
  66.0 13.3 %collective-permute-start.18 = (bf16[256,512]{1,0:T(8,128)(2,1)S(1)}, bf16[256,512]{1,0:T(8,128)(2,1)S(1)}, u32[]{:S(2)}, u32[]{:S(2)}) collective-permute-start(bf16[256,512]{1,0:T(8,128)(2,1)S(1)} %get-tuple-element.212), channel_id=1, source_target_pairs={{0,2},{1,3},{2,4},{3,5},{4,6},{5,7},{6,0},{7,1},{8,10},{9,11},{10,... | collective-permute-start | bytes 786440 | tf_op jit(solution)/shard_map/ppermute | solution.py:505
  66.5 12.8 %collective-permute-start.19 = (bf16[256,512]{1,0:T(8,128)(2,1)S(1)}, bf16[256,512]{1,0:T(8,128)(2,1)S(1)}, u32[]{:S(2)}, u32[]{:S(2)}) collective-permute-start(bf16[256,512]{1,0:T(8,128)(2,1)S(1)} %get-tuple-element.213), channel_id=1, source_target_pairs={{0,1},{1,0},{2,3},{3,2},{4,5},{5,4},{6,7},{7,6},{8,9},{9,8},{10,11... | collective-permute-start | bytes 786440 | tf_op jit(solution)/shard_map/ppermute | solution.py:505
  71.6 11.3 %collective-permute-start.22 = (bf16[256,512]{1,0:T(8,128)(2,1)S(1)}, bf16[256,512]{1,0:T(8,128)(2,1)S(1)}, u32[]{:S(2)}, u32[]{:S(2)}) collective-permute-start(bf16[256,512]{1,0:T(8,128)(2,1)S(1)} %get-tuple-element.221), channel_id=1, source_target_pairs={{0,2},{1,3},{2,4},{3,5},{4,6},{5,7},{6,0},{7,1},{8,10},{9,11},{10,... | collective-permute-start | bytes 786440 | tf_op jit(solution)/shard_map/ppermute | solution.py:505
  72.3 10.5 %collective-permute-start.23 = (bf16[256,512]{1,0:T(8,128)(2,1)S(1)}, bf16[256,512]{1,0:T(8,128)(2,1)S(1)}, u32[]{:S(2)}, u32[]{:S(2)}) collective-permute-start(bf16[256,512]{1,0:T(8,128)(2,1)S(1)} %get-tuple-element.222), channel_id=1, source_target_pairs={{0,1},{1,0},{2,3},{3,2},{4,5},{5,4},{6,7},{7,6},{8,9},{9,8},{10,11... | collective-permute-start | bytes 786440 | tf_op jit(solution)/shard_map/ppermute | solution.py:505
  79.3 35.4 %copy-start.5 = (s32[8,48]{1,0:T(8,128)S(1)}, s32[8,48]{1,0:T(8,128)}, u32[]{:S(2)}) copy-start(s32[8,48]{1,0:T(8,128)} %constant.14.clone.table) | copy-start | bytes 4612
  79.4 9.0 %collective-permute-start.24 = (bf16[256,512]{1,0:T(8,128)(2,1)S(1)}, bf16[256,512]{1,0:T(8,128)(2,1)S(1)}, u32[]{:S(2)}, u32[]{:S(2)}) collective-permute-start(bf16[256,512]{1,0:T(8,128)(2,1)S(1)} %get-tuple-element.228), channel_id=1, source_target_pairs={{0,2},{1,3},{2,4},{3,5},{4,6},{5,7},{6,0},{7,1},{8,10},{9,11},{10,... | collective-permute-start | bytes 786440 | tf_op jit(solution)/shard_map/ppermute | solution.py:505
  81.1 8.8 %collective-permute-start.25 = (bf16[256,512]{1,0:T(8,128)(2,1)S(1)}, bf16[256,512]{1,0:T(8,128)(2,1)S(1)}, u32[]{:S(2)}, u32[]{:S(2)}) collective-permute-start(bf16[256,512]{1,0:T(8,128)(2,1)S(1)} %get-tuple-element.229), channel_id=1, source_target_pairs={{0,1},{1,0},{2,3},{3,2},{4,5},{5,4},{6,7},{7,6},{8,9},{9,8},{10,11... | collective-permute-start | bytes 786440 | tf_op jit(solution)/shard_map/ppermute | solution.py:505
  82.9 11.1 %collective-permute-start.26 = (bf16[256,512]{1,0:T(8,128)(2,1)S(1)}, bf16[256,512]{1,0:T(8,128)(2,1)S(1)}, u32[]{:S(2)}, u32[]{:S(2)}) collective-permute-start(bf16[256,512]{1,0:T(8,128)(2,1)S(1)} %get-tuple-element.235), channel_id=1, source_target_pairs={{0,2},{1,3},{2,4},{3,5},{4,6},{5,7},{6,0},{7,1},{8,10},{9,11},{10,... | collective-permute-start | bytes 786440 | tf_op jit(solution)/shard_map/ppermute | solution.py:505
  83.8 11.8 %collective-permute-start.27 = (bf16[256,512]{1,0:T(8,128)(2,1)S(1)}, bf16[256,512]{1,0:T(8,128)(2,1)S(1)}, u32[]{:S(2)}, u32[]{:S(2)}) collective-permute-start(bf16[256,512]{1,0:T(8,128)(2,1)S(1)} %get-tuple-element.236), channel_id=1, source_target_pairs={{0,1},{1,0},{2,3},{3,2},{4,5},{5,4},{6,7},{7,6},{8,9},{9,8},{10,11... | collective-permute-start | bytes 786440 | tf_op jit(solution)/shard_map/ppermute | solution.py:505
  90.8 16.3 %collective-permute-start.28 = (bf16[256,512]{1,0:T(8,128)(2,1)}, bf16[256,512]{1,0:T(8,128)(2,1)}, u32[]{:S(2)}, u32[]{:S(2)}) collective-permute-start(bf16[256,512]{1,0:T(8,128)(2,1)} %get-tuple-element.240), channel_id=1, source_target_pairs={{0,2},{1,3},{2,4},{3,5},{4,6},{5,7},{6,0},{7,1},{8,10},{9,11},{10,... | collective-permute-start | bytes 786440 | tf_op jit(solution)/shard_map/ppermute | solution.py:505
  90.8 16.4 %collective-permute-start.29 = (bf16[256,512]{1,0:T(8,128)(2,1)}, bf16[256,512]{1,0:T(8,128)(2,1)}, u32[]{:S(2)}, u32[]{:S(2)}) collective-permute-start(bf16[256,512]{1,0:T(8,128)(2,1)} %get-tuple-element.241), channel_id=1, source_target_pairs={{0,1},{1,0},{2,3},{3,2},{4,5},{5,4},{6,7},{7,6},{8,9},{9,8},{10,11... | collective-permute-start | bytes 786440 | tf_op jit(solution)/shard_map/ppermute | solution.py:505
  96.5 15.1 %collective-permute-start.32 = (bf16[256,512]{1,0:T(8,128)(2,1)}, bf16[256,512]{1,0:T(8,128)(2,1)}, u32[]{:S(2)}, u32[]{:S(2)}) collective-permute-start(bf16[256,512]{1,0:T(8,128)(2,1)} %get-tuple-element.245), channel_id=1, source_target_pairs={{0,2},{1,3},{2,4},{3,5},{4,6},{5,7},{6,0},{7,1},{8,10},{9,11},{10,... | collective-permute-start | bytes 786440 | tf_op jit(solution)/shard_map/ppermute | solution.py:505
  96.5 15.1 %collective-permute-start.33 = (bf16[256,512]{1,0:T(8,128)(2,1)}, bf16[256,512]{1,0:T(8,128)(2,1)}, u32[]{:S(2)}, u32[]{:S(2)}) collective-permute-start(bf16[256,512]{1,0:T(8,128)(2,1)} %get-tuple-element.246), channel_id=1, source_target_pairs={{0,1},{1,0},{2,3},{3,2},{4,5},{5,4},{6,7},{7,6},{8,9},{9,8},{10,11... | collective-permute-start | bytes 786440 | tf_op jit(solution)/shard_map/ppermute | solution.py:505
  100.9 40.8 %all-to-all-start = ((bf16[32,1,8,1152]{3,2,1,0:T(8,128)(2,1)}), bf16[32,1,8,1152]{3,2,1,0:T(8,128)(2,1)S(1)}, u32[]{:S(2)}, u32[]{:S(2)}) async-start(bf16[32,1,8,1152]{3,2,1,0:T(8,128)(2,1)} %bitcast.6), calls=%async_computation | async-start | bytes 1179648 | tf_op jit(solution)/shard_map/all_to_all | solution.py:470
  108.3 19.2 %collective-permute-start.30 = (bf16[256,512]{1,0:T(8,128)(2,1)S(1)}, bf16[256,512]{1,0:T(8,128)(2,1)S(1)}, u32[]{:S(2)}, u32[]{:S(2)}) collective-permute-start(bf16[256,512]{1,0:T(8,128)(2,1)S(1)} %get-tuple-element.249), channel_id=1, source_target_pairs={{0,2},{1,3},{2,4},{3,5},{4,6},{5,7},{6,0},{7,1},{8,10},{9,11},{10,... | collective-permute-start | bytes 786440 | tf_op jit(solution)/shard_map/ppermute | solution.py:505
  110.1 17.4 %collective-permute-start.31 = (bf16[256,512]{1,0:T(8,128)(2,1)S(1)}, bf16[256,512]{1,0:T(8,128)(2,1)S(1)}, u32[]{:S(2)}, u32[]{:S(2)}) collective-permute-start(bf16[256,512]{1,0:T(8,128)(2,1)S(1)} %get-tuple-element.250), channel_id=1, source_target_pairs={{0,1},{1,0},{2,3},{3,2},{4,5},{5,4},{6,7},{7,6},{8,9},{9,8},{10,11... | collective-permute-start | bytes 786440 | tf_op jit(solution)/shard_map/ppermute | solution.py:505
  112.6 20.3 %collective-permute-start.36 = (bf16[256,512]{1,0:T(8,128)(2,1)S(1)}, bf16[256,512]{1,0:T(8,128)(2,1)S(1)}, u32[]{:S(2)}, u32[]{:S(2)}) collective-permute-start(bf16[256,512]{1,0:T(8,128)(2,1)S(1)} %get-tuple-element.253), channel_id=1, source_target_pairs={{0,2},{1,3},{2,4},{3,5},{4,6},{5,7},{6,0},{7,1},{8,10},{9,11},{10,... | collective-permute-start | bytes 786440 | tf_op jit(solution)/shard_map/ppermute | solution.py:505
  114.2 18.8 %collective-permute-start.37 = (bf16[256,512]{1,0:T(8,128)(2,1)S(1)}, bf16[256,512]{1,0:T(8,128)(2,1)S(1)}, u32[]{:S(2)}, u32[]{:S(2)}) collective-permute-start(bf16[256,512]{1,0:T(8,128)(2,1)S(1)} %get-tuple-element.254), channel_id=1, source_target_pairs={{0,1},{1,0},{2,3},{3,2},{4,5},{5,4},{6,7},{7,6},{8,9},{9,8},{10,11... | collective-permute-start | bytes 786440 | tf_op jit(solution)/shard_map/ppermute | solution.py:505
  127.4 30.6 %copy-start.35 = (bf16[256,512]{1,0:T(8,128)(2,1)}, bf16[256,512]{1,0:T(8,128)(2,1)S(1)}, u32[]{:S(2)}) copy-start(bf16[256,512]{1,0:T(8,128)(2,1)S(1)} %collective-permute-done.30.refs_8_) | copy-start | bytes 786436
  127.4 30.6 %copy-start.36 = (bf16[256,512]{1,0:T(8,128)(2,1)}, bf16[256,512]{1,0:T(8,128)(2,1)S(1)}, u32[]{:S(2)}) copy-start(bf16[256,512]{1,0:T(8,128)(2,1)S(1)} %collective-permute-done.31.refs_9_) | copy-start | bytes 786436
  128.4 29.7 %collective-permute-start.34 = (bf16[256,512]{1,0:T(8,128)(2,1)}, bf16[256,512]{1,0:T(8,128)(2,1)S(1)}, u32[]{:S(2)}, u32[]{:S(2)}) collective-permute-start(bf16[256,512]{1,0:T(8,128)(2,1)} %get-tuple-element.259), channel_id=1, source_target_pairs={{0,2},{1,3},{2,4},{3,5},{4,6},{5,7},{6,0},{7,1},{8,10},{9,11},{10,... | collective-permute-start | bytes 786440 | tf_op jit(solution)/shard_map/ppermute | solution.py:505
  128.9 29.2 %collective-permute-start.35 = (bf16[256,512]{1,0:T(8,128)(2,1)}, bf16[256,512]{1,0:T(8,128)(2,1)S(1)}, u32[]{:S(2)}, u32[]{:S(2)}) collective-permute-start(bf16[256,512]{1,0:T(8,128)(2,1)} %get-tuple-element.260), channel_id=1, source_target_pairs={{0,1},{1,0},{2,3},{3,2},{4,5},{5,4},{6,7},{7,6},{8,9},{9,8},{10,11... | collective-permute-start | bytes 786440 | tf_op jit(solution)/shard_map/ppermute | solution.py:505
  144.0 17.3 %collective-permute-start.40 = (bf16[256,512]{1,0:T(8,128)(2,1)}, bf16[256,512]{1,0:T(8,128)(2,1)S(1)}, u32[]{:S(2)}, u32[]{:S(2)}) collective-permute-start(bf16[256,512]{1,0:T(8,128)(2,1)} %get-tuple-element.265), channel_id=1, source_target_pairs={{0,2},{1,3},{2,4},{3,5},{4,6},{5,7},{6,0},{7,1},{8,10},{9,11},{10,... | collective-permute-start | bytes 786440 | tf_op jit(solution)/shard_map/ppermute | solution.py:505
  144.6 16.6 %collective-permute-start.41 = (bf16[256,512]{1,0:T(8,128)(2,1)}, bf16[256,512]{1,0:T(8,128)(2,1)S(1)}, u32[]{:S(2)}, u32[]{:S(2)}) collective-permute-start(bf16[256,512]{1,0:T(8,128)(2,1)} %get-tuple-element.266), channel_id=1, source_target_pairs={{0,1},{1,0},{2,3},{3,2},{4,5},{5,4},{6,7},{7,6},{8,9},{9,8},{10,11... | collective-permute-start | bytes 786440 | tf_op jit(solution)/shard_map/ppermute | solution.py:505
  144.8 43.7 %all-to-all-start.1 = ((bf16[32,4,8,256]{3,2,1,0:T(8,128)(2,1)}), bf16[32,4,8,256]{3,2,1,0:T(8,128)(2,1)S(1)}, u32[]{:S(2)}, u32[]{:S(2)}) async-start(bf16[32,4,8,256]{3,2,1,0:T(8,128)(2,1)} %bitcast.19), calls=%async_computation.1 | async-start | bytes 1048576 | tf_op jit(solution)/shard_map/all_to_all | solution.py:470
  158.1 13.5 %collective-permute-start.38 = (bf16[256,512]{1,0:T(8,128)(2,1)S(1)}, bf16[256,512]{1,0:T(8,128)(2,1)S(1)}, u32[]{:S(2)}, u32[]{:S(2)}) collective-permute-start(bf16[256,512]{1,0:T(8,128)(2,1)S(1)} %get-tuple-element.270), channel_id=1, source_target_pairs={{0,2},{1,3},{2,4},{3,5},{4,6},{5,7},{6,0},{7,1},{8,10},{9,11},{10,... | collective-permute-start | bytes 786440 | tf_op jit(solution)/shard_map/ppermute | solution.py:505
  159.8 11.9 %collective-permute-start.39 = (bf16[256,512]{1,0:T(8,128)(2,1)S(1)}, bf16[256,512]{1,0:T(8,128)(2,1)S(1)}, u32[]{:S(2)}, u32[]{:S(2)}) collective-permute-start(bf16[256,512]{1,0:T(8,128)(2,1)S(1)} %get-tuple-element.271), channel_id=1, source_target_pairs={{0,1},{1,0},{2,3},{3,2},{4,5},{5,4},{6,7},{7,6},{8,9},{9,8},{10,11... | collective-permute-start | bytes 786440 | tf_op jit(solution)/shard_map/ppermute | solution.py:505
  161.3 13.3 %collective-permute-start.44 = (bf16[256,512]{1,0:T(8,128)(2,1)S(1)}, bf16[256,512]{1,0:T(8,128)(2,1)S(1)}, u32[]{:S(2)}, u32[]{:S(2)}) collective-permute-start(bf16[256,512]{1,0:T(8,128)(2,1)S(1)} %get-tuple-element.274), channel_id=1, source_target_pairs={{0,2},{1,3},{2,4},{3,5},{4,6},{5,7},{6,0},{7,1},{8,10},{9,11},{10,... | collective-permute-start | bytes 786440 | tf_op jit(solution)/shard_map/ppermute | solution.py:505
  162.9 11.8 %collective-permute-start.45 = (bf16[256,512]{1,0:T(8,128)(2,1)S(1)}, bf16[256,512]{1,0:T(8,128)(2,1)S(1)}, u32[]{:S(2)}, u32[]{:S(2)}) collective-permute-start(bf16[256,512]{1,0:T(8,128)(2,1)S(1)} %get-tuple-element.275), channel_id=1, source_target_pairs={{0,1},{1,0},{2,3},{3,2},{4,5},{5,4},{6,7},{7,6},{8,9},{9,8},{10,11... | collective-permute-start | bytes 786440 | tf_op jit(solution)/shard_map/ppermute | solution.py:505
  171.7 17.8 %collective-permute-start.42 = (bf16[256,512]{1,0:T(8,128)(2,1)S(1)}, bf16[256,512]{1,0:T(8,128)(2,1)S(1)}, u32[]{:S(2)}, u32[]{:S(2)}) collective-permute-start(bf16[256,512]{1,0:T(8,128)(2,1)S(1)} %get-tuple-element.279), channel_id=1, source_target_pairs={{0,2},{1,3},{2,4},{3,5},{4,6},{5,7},{6,0},{7,1},{8,10},{9,11},{10,... | collective-permute-start | bytes 786440 | tf_op jit(solution)/shard_map/ppermute | solution.py:505
  172.0 17.5 %collective-permute-start.43 = (bf16[256,512]{1,0:T(8,128)(2,1)S(1)}, bf16[256,512]{1,0:T(8,128)(2,1)S(1)}, u32[]{:S(2)}, u32[]{:S(2)}) collective-permute-start(bf16[256,512]{1,0:T(8,128)(2,1)S(1)} %get-tuple-element.280), channel_id=1, source_target_pairs={{0,1},{1,0},{2,3},{3,2},{4,5},{5,4},{6,7},{7,6},{8,9},{9,8},{10,11... | collective-permute-start | bytes 786440 | tf_op jit(solution)/shard_map/ppermute | solution.py:505
  175.5 14.0 %collective-permute-start.46 = (bf16[256,512]{1,0:T(8,128)(2,1)}, bf16[256,512]{1,0:T(8,128)(2,1)S(1)}, u32[]{:S(2)}, u32[]{:S(2)}) collective-permute-start(bf16[256,512]{1,0:T(8,128)(2,1)} %get-tuple-element.283), channel_id=1, source_target_pairs={{0,2},{1,3},{2,4},{3,5},{4,6},{5,7},{6,0},{7,1},{8,10},{9,11},{10,... | collective-permute-start | bytes 786440 | tf_op jit(solution)/shard_map/ppermute | solution.py:505
  (35 other events, 329.8 us)

commit v2 on v1

--- a/solution.py
+++ b/solution.py
@@ -1,4 +1,5 @@
 import functools
+import itertools
 
 import jax
 import jax.numpy as jnp
@@ -9,7 +10,7 @@
 
 TILE = 256
 CHAINS = 2
-SUM_AFTER = 3
+SUM_AFTER = 4
 VMEM_LIMIT = 16 * 1024 * 1024
 UPDATE_LIMIT = 32 * 1024 * 1024
 HBM = pl.BlockSpec(memory_space=pltpu.HBM)
@@ -43,7 +44,7 @@
 
 def travel(perms, rules, lists, n_grp, tiles):
     got = []
-    missing = {(g, tile) for g in range(n_grp) for tile in range(1, tiles)}
+    missing = {(g, tile) for g in range(1, n_grp) for tile in range(1, tiles)}
     while missing:
         e = len(got)
         now = []
@@ -95,6 +96,36 @@
         if g == 0:
             picks[shorter()].append((g, tile))
     return [heads[s] + [tile for _, tile in picks[s]] for s in (0, 1)]
+
+
+def live_pairs(perms, rules, lists, got, table, n_grp):
+    width = max(n_grp // 4, 1)
+    live = [[set(), set()] for _ in got]
+    result = [[[], []] for _ in got]
+    for e in reversed(range(len(got))):
+        for s in (0, 1):
+            for g, target in perms[s]:
+                needed = target and table[target][2 * e + s]
+                later = e + CHAINS
+                if target and later < len(got):
+                    needed = needed or any(rules[t][target] == s and target in live[later][t] for t in (0, 1))
+                if needed:
+                    live[e][s].add(g)
+            if not live[e][s]:
+                continue
+            pairs = [(g, target) for g, target in perms[s] if g in live[e][s]]
+            sources = set(range(n_grp)) - {g for g, _ in pairs}
+            targets = set(range(n_grp)) - {target for _, target in pairs}
+            pairs += [(g, g) for g in sorted(sources & targets)]
+            sources, targets = sorted(sources - targets, reverse=True), sorted(targets - sources)
+            best = list(zip(sources, targets))
+            if len(sources) <= 4:
+                best = min(
+                    (list(zip(sources, order)) for order in itertools.permutations(targets)),
+                    key=lambda some: sum(max(0, v // width - u // width) for u, v in some),
+                )
+            result[e][s] = pairs + best
+    return result
 
 
 def in_hbm(x):
@@ -253,7 +284,7 @@
     )(mask, targets, me, in_hbm(front), *[in_hbm(block) for block in blocks])
 
 
-def update_kernel(numbers, cols_dev, start, table, mask, me, own, front, *refs):
+def update_kernel(numbers, room, cols_dev, start, table, mask, me, own, front, *refs):
     count = len(numbers)
     blocks = refs[:count]
     out, panels, old, new, listed, panel_sems, in_sems, out_sems = refs[-8:]
@@ -285,8 +316,8 @@
     listed[total] = 0
     if start:
         here = pl.ds(0, TILE)
-        top_in = pltpu.make_async_copy(front.at[here], new.at[count], in_sems.at[count])
-        top_out = pltpu.make_async_copy(new.at[count], out.at[here], out_sems.at[count])
+        top_in = pltpu.make_async_copy(front.at[here], new.at[room], in_sems.at[room])
+        top_out = pltpu.make_async_copy(new.at[room], out.at[here], out_sems.at[room])
         top_in.start()
         top_in.wait()
         top_out.start()
@@ -334,10 +365,9 @@
         top_out.wait()
 
 
-def update(table, mask, me, own, front, numbers, blocks, base=None):
+def update(table, mask, me, own, front, numbers, blocks, room, base=None):
     width = front.shape[1]
     count = len(numbers)
-    room = count + count % 2
     operands = [table, mask, me, own, in_hbm(front), *[in_hbm(block) for block in blocks]]
     in_specs = [SMEM, SMEM, SMEM, VMEM, HBM] + [HBM] * count
     aliases = {}
@@ -346,7 +376,7 @@
         operands.append(in_hbm(base))
         in_specs.append(HBM)
     return pl.pallas_call(
-        functools.partial(update_kernel, tuple(numbers), width // TILE, base is None),
+        functools.partial(update_kernel, tuple(numbers), room, width // TILE, base is None),
         out_shape=jax.ShapeDtypeStruct(front.shape, jnp.bfloat16),
         in_specs=in_specs,
         out_specs=HBM,
@@ -362,7 +392,7 @@
         input_output_aliases=aliases,
         compiler_params=pltpu.CompilerParams(vmem_limit_bytes=UPDATE_LIMIT),
         cost_estimate=pl.CostEstimate(
-            flops=2 * count * TILE * width * 2 * TILE, bytes_accessed=4 * count * TILE * width, transcendentals=0
+            flops=2 * room * TILE * width * 2 * TILE, bytes_accessed=4 * room * TILE * width, transcendentals=0
         ),
         name="update",
     )(*operands)
@@ -431,13 +461,17 @@
         line = []
         for now in got:
             for arrival in now:
-                line.append(arrival[n] if arrival[n] not in line else 0)
+                line.append(arrival[n] if n and arrival[n] not in line else 0)
         table.append(line)
+    pairs = live_pairs(perms, rules, lists, got, table, n_grp)
+    numbers_at = [[2 * e, 2 * e + 1] for e in range(events)]
+    made_at = {}
+    for e, tile in order[:-1]:
+        made_at[len(table[0])] = tile
+        numbers_at[e].append(len(table[0]))
+        for n in range(n_grp):
+            table[n].append(0 if n else tile)
     rows = jnp.asarray(table, jnp.int32)
-    used = [[any(line[2 * e + s] for line in table) for s in (0, 1)] for e in range(events)]
-    for e in reversed(range(events - CHAINS)):
-        for s in (0, 1):
-            used[e][s] = used[e][s] or any(used[e + CHAINS])
 
     needed = [
         [n * cols_dev + c for c in range(cols_dev)] + [tiles - rows_out + r for r in range(rows_out)]
@@ -480,14 +514,20 @@
 
     held, turn, result, done = [], (), None, 0
 
-    def step(limit, at_hand, *waits):
+    def block_of(number):
+        if number in made_at:
+            which, place = where_made[made_at[number]]
+            return made[which][place]
+        return held[number // 2][number % 2]
+
+    def step(count, *waits):
         nonlocal result, done
-        numbers = list(range(done, min(done + limit, at_hand)))
-        done += len(numbers)
+        numbers = [number for e in range(done, done + count) for number in numbers_at[e]]
+        numbers = [number for number in numbers if any(line[number] for line in table)]
+        done += count
         here = after((me,), *waits)[0]
-        blocks = [held[n // 2][n % 2] for n in numbers]
-        if numbers:
-            result = update(rows, mask, here, own, front, numbers, blocks, base=result)
+        blocks = [block_of(number) for number in numbers]
+        result = update(rows, mask, here, own, front, numbers, blocks, 2 * count, base=result)
 
     for e in range(events):
         values = []
@@ -502,7 +542,7 @@
                 value = made[which][n] if value is None else jnp.where(root, made[which][n], value)
             values.append(value)
         turn = after(values, *turn, *(scalars if e == 0 else ()))
-        held.append([lax.ppermute(turn[s], "grp", perms[s]) if used[e][s] else turn[s] for s in (0, 1)])
+        held.append([lax.ppermute(turn[s], "grp", pairs[e][s]) if pairs[e][s] else turn[s] for s in (0, 1)])
         make(e, turn)
         if CHAINS <= e + 1 < events:
             held[e + 1 - CHAINS] = list(after(held[e + 1 - CHAINS], *turn))
@@ -510,19 +550,19 @@
         if late == 0:
             own, bottom = own_part()
             pieces = jnp.transpose(bottom.reshape(rows_out, n_dev, piece, width + 128), (1, 0, 2, 3))
-            arrived = exchange(pieces)
+        if late == 1:
+            arrived = exchange(after((pieces,), *turn)[0])
         if late == SUM_AFTER:
             sums = sums_of(after((arrived,), *turn)[0])
             parent_pieces = exchange(sums)
             turn = (*turn, sums)
-        if late >= 2 and late % 2 == 0:
-            step(12, 2 * (e - CHAINS + 1), *turn)
+        elif late >= 2 and e < events - 2:
+            step(min(4, e - CHAINS + 1 - done), *turn)
             turn = (*turn, result)
     parent_tiles = jnp.transpose(parent_pieces, (1, 0, 2, 3)).reshape(slots_dev, TILE, TILE).astype(jnp.float32)
-    if done < 2 * (events - CHAINS):
-        step(12, 2 * (events - CHAINS), *turn)
-    while done < 2 * events:
-        step(12, 2 * events, parent_tiles)
+    while done < events - CHAINS:
+        step(min(6, events - CHAINS - done), *turn)
+    step(CHAINS, parent_tiles)
     return (result[None], parent_tiles)
 
 

time: 194 us -> 222 us (1.14)
  the two profiles are of different devices: /device:TPU:0 before, /device:TPU:24 now
where the time goes in v2:
time: 222 us; the launch traced here: 220 us
  starting transfers between devices  131 us (59%)
  Pallas kernels  57.5 us (26%)
  waiting for transfers between devices  15.5 us (7%)
  other arithmetic  8.49 us (4%)
  local copies, waits for them, and re-layouts  4.87 us (2%)
  between operations  2.55 us (1%)
    ppermute x47, starting transfers between devices, shards(): lax.ppermute(turn[s], 'grp', pairs[e][s])  118 us
    pallas_call x6, Pallas kernels, update(): pl.pallas_call(functools.partial(update_kernel, tuple(numbers), room, wid...  32.1 us
    pallas_call x5, Pallas kernels, factor(): pl.pallas_call(functools.partial(factor_kernel, tuple(tiles), head), out_...  21.6 us
    ppermute x47, waiting for transfers between devices, shards(): lax.ppermute(turn[s], 'grp', pairs[e][s])  15.5 us
    all_to_all x2, starting transfers between devices, exchange(): lax.all_to_all(blocks, ('front', 'grp'), split_axis=0, concat_axis=0, til...  13 us
    select_n x9, other arithmetic, shards(): value = jnp.where(others[s], held[e - CHAINS][1 - rules[s][0]], value)  6.43 us
  transfers between devices with their start and end apart: 49, of which 9 were waited for; matrix products, arithmetic and copies ran while one was open for 5% of the time, Pallas kernels for 23%

profile of v2, /device:TPU:24, one launch (start us, length us, event | category | flops | bytes accessed | tf_op | source)
XLA Modules:
  0.0 220.5 jit_solution(8126359454654548592)
XLA Ops:
  0.6 0.8 copy.81.mask
  1.4 3.8 %factor.5 = (bf16[256,512]{1,0:T(8,128)(2,1)S(1)}, bf16[256,512]{1,0:T(8,128)(2,1)S(1)}, bf16[256,512]{1,0:T(8,128)(2,1)S(1)}, bf16[256,512]{1,0:T(8,128)(2,1)S(...) custom-call(s32[32,4]{1,0:T(8,128)S(1)} %copy.81.mask, bf16[8192,1024]{1,0:T(8,128)(2,1)} %bitcast.25, ...), custom_call_target="tpu_custom_call" | custom-call | flops 805306368 | bytes 2097152 | tf_op jit(solution)/shard_map/factor/pallas_call | solution.py:209
  7.3 0.7 collective-permute-start.5
  8.0 3.0 %factor.6 = (bf16[256,512]{1,0:T(8,128)(2,1)S(1)}, bf16[256,512]{1,0:T(8,128)(2,1)S(1)}, bf16[256,512]{1,0:T(8,128)(2,1)S(1)}, bf16[256,512]{1,0:T(8,128)(2,1)S(1)}) custom-call(s32[32,4]{1,0:T(8,128)S(1)} %copy.81.mask, bf16[8192,1024]{1,0:T(8,128)(2,1)} %bitcast.26, bf16[4,256,256]{2,1,0:T(8,128)(2,1)S(1)} %get-tuple-element.215.refs_0_, ...), custom_call_target="tpu_custom_call" | custom-call | flops 805306368 | bytes 2097152 | tf_op jit(solution)/shard_map/factor/pallas_call | solution.py:209
  12.6 0.7 collective-permute-start.8
  13.3 0.7 collective-permute-start.9
  14.0 5.0 %factor.7 = (bf16[256,512]{1,0:T(8,128)(2,1)S(1)}, bf16[256,512]{1,0:T(8,128)(2,1)S(1)}, bf16[256,512]{1,0:T(8,128)(2,1)S(1)}, bf16[256,512]{1,0:T(8,128)(2,1)S(...) custom-call(s32[32,4]{1,0:T(8,128)S(1)} %copy.81.mask, ...), custom_call_target="tpu_custom_call" | custom-call | flops 1610612736 | bytes 4194304 | tf_op jit(solution)/shard_map/factor/pallas_call | solution.py:209
  19.2 17.9 %collective-permute-start.6 = (bf16[256,512]{1,0:T(8,128)(2,1)S(1)}, bf16[256,512]{1,0:T(8,128)(2,1)S(1)}, u32[]{:S(2)}, u32[]{:S(2)}) collective-permute-start(bf16[256,512]{1,0:T(8,128)(2,1)S(1)} %get-tuple-element.176), channel_id=1, source_target_pairs={{0,2},{1,3},{2,4},{3,5},{4,6},{7,7},{6,0},{5,1},{8,10},{9,11},{10,... | collective-permute-start | bytes 786440 | tf_op jit(solution)/shard_map/ppermute | solution.py:545
  37.9 5.4 %collective-permute-start.12 = (bf16[256,512]{1,0:T(8,128)(2,1)S(1)}, bf16[256,512]{1,0:T(8,128)(2,1)S(1)}, u32[]{:S(2)}, u32[]{:S(2)}) collective-permute-start(bf16[256,512]{1,0:T(8,128)(2,1)S(1)} %get-tuple-element.182), channel_id=1, source_target_pairs={{0,2},{1,3},{2,4},{3,5},{4,6},{7,7},{6,0},{5,1},{8,10},{9,11},{10,... | collective-permute-start | bytes 786440 | tf_op jit(solution)/shard_map/ppermute | solution.py:545
  44.0 7.5 %collective-permute-start.10 = (bf16[256,512]{1,0:T(8,128)(2,1)S(1)}, bf16[256,512]{1,0:T(8,128)(2,1)S(1)}, u32[]{:S(2)}, u32[]{:S(2)}) collective-permute-start(bf16[256,512]{1,0:T(8,128)(2,1)S(1)} %get-tuple-element.187), channel_id=1, source_target_pairs={{0,2},{1,3},{2,4},{3,5},{4,6},{5,7},{7,0},{6,1},{8,10},{9,11},{10,... | collective-permute-start | bytes 786440 | tf_op jit(solution)/shard_map/ppermute | solution.py:545
  51.5 2.5 %collective-permute-start.11 = (bf16[256,512]{1,0:T(8,128)(2,1)S(1)}, bf16[256,512]{1,0:T(8,128)(2,1)S(1)}, u32[]{:S(2)}, u32[]{:S(2)}) collective-permute-start(bf16[256,512]{1,0:T(8,128)(2,1)S(1)} %get-tuple-element.188), channel_id=1, source_target_pairs={{0,1},{2,3},{3,2},{4,5},{5,4},{6,7},{7,6},{1,0},{8,9},{10,11},{11,... | collective-permute-start | bytes 786440 | tf_op jit(solution)/shard_map/ppermute | solution.py:545
  54.1 9.6 %collective-permute-start.16 = (bf16[256,512]{1,0:T(8,128)(2,1)S(1)}, bf16[256,512]{1,0:T(8,128)(2,1)S(1)}, u32[]{:S(2)}, u32[]{:S(2)}) collective-permute-start(bf16[256,512]{1,0:T(8,128)(2,1)S(1)} %get-tuple-element.197), channel_id=1, source_target_pairs={{0,2},{1,3},{2,4},{3,5},{4,6},{5,7},{7,0},{6,1},{8,10},{9,11},{10,... | collective-permute-start | bytes 786440 | tf_op jit(solution)/shard_map/ppermute | solution.py:545
  63.9 5.0 %factor.8 = (bf16[256,512]{1,0:T(8,128)(2,1)S(1)}, bf16[256,512]{1,0:T(8,128)(2,1)S(1)}, bf16[256,512]{1,0:T(8,128)(2,1)S(1)}, bf16[256,512]{1,0:T(8,128)(2,1)S(...) custom-call(s32[32,4]{1,0:T(8,128)S(1)} %copy.81.mask, ...), custom_call_target="tpu_custom_call" | custom-call | flops 1610612736 | bytes 4194304 | tf_op jit(solution)/shard_map/factor/pallas_call | solution.py:209
  69.1 3.1 %collective-permute-start.14 = (bf16[256,512]{1,0:T(8,128)(2,1)S(1)}, bf16[256,512]{1,0:T(8,128)(2,1)S(1)}, u32[]{:S(2)}, u32[]{:S(2)}) collective-permute-start(bf16[256,512]{1,0:T(8,128)(2,1)S(1)} %get-tuple-element.202), channel_id=1, source_target_pairs={{0,2},{1,3},{2,4},{3,5},{4,6},{5,7},{7,1},{6,0},{8,10},{9,11},{10,... | collective-permute-start | bytes 786440 | tf_op jit(solution)/shard_map/ppermute | solution.py:545
  72.3 5.5 %collective-permute-start.20 = (bf16[256,512]{1,0:T(8,128)(2,1)S(1)}, bf16[256,512]{1,0:T(8,128)(2,1)S(1)}, u32[]{:S(2)}, u32[]{:S(2)}) collective-permute-start(bf16[256,512]{1,0:T(8,128)(2,1)S(1)} %get-tuple-element.208), channel_id=1, source_target_pairs={{0,2},{1,3},{2,4},{3,5},{4,6},{5,7},{7,1},{6,0},{8,10},{9,11},{10,... | collective-permute-start | bytes 786440 | tf_op jit(solution)/shard_map/ppermute | solution.py:545
  77.9 0.7 collective-permute-done.14.refs_3_.refs_0_
  78.6 2.7 %collective-permute-done.15.refs_1_ = bf16[256,512]{1,0:T(8,128)(2,1)S(1)} collective-permute-done((bf16[256,512]{1,0:T(8,128)(2,1)S(1)}, bf16[256,512]{1,0:T(8,128)(2,1)S(1)}, u32[]{:S(2)}, u32[]{:S(2)}) %collective-permute-start.15) | collective-permute-done | bytes 262176 | tf_op jit(solution)/shard_map/ppermute | solution.py:545
  81.4 2.0 collective-permute-start.18
  84.2 2.8 %collective-permute-done.21.refs_5_ = bf16[256,512]{1,0:T(8,128)(2,1)S(1)} collective-permute-done((bf16[256,512]{1,0:T(8,128)(2,1)S(1)}, bf16[256,512]{1,0:T(8,128)(2,1)S(1)}, u32[]{:S(2)}, u32[]{:S(2)}) %collective-permute-start.21) | collective-permute-done | bytes 262176 | tf_op jit(solution)/shard_map/ppermute | solution.py:545
  87.0 2.2 collective-permute-start.22
  89.5 5.0 %factor.9 = (bf16[256,512]{1,0:T(8,128)(2,1)S(1)}, bf16[256,512]{1,0:T(8,128)(2,1)S(1)}, bf16[256,512]{1,0:T(8,128)(2,1)S(1)}, bf16[256,512]{1,0:T(8,128)(2,1)S(...) custom-call(s32[32,4]{1,0:T(8,128)S(1)} %copy.81.mask, ...), custom_call_target="tpu_custom_call" | custom-call | flops 1610612736 | bytes 4194304 | tf_op jit(solution)/shard_map/factor/pallas_call | solution.py:209
  95.0 1.9 collective-permute-start.25
  96.9 1.6 collective-permute-done.23.refs_6_.refs_13_
  98.6 1.7 collective-permute-start.26
  100.4 2.4 %collective-permute-done.24.refs_13_.refs_0_ = bf16[256,512]{1,0:T(8,128)(2,1)S(1)} collective-permute-done((bf16[256,512]{1,0:T(8,128)(2,1)S(1)}, bf16[256,512]{1,0:T(8,128)(2,1)S(1)}, u32[]{:S(2)}, u32[]{:S(2)}) %collective-permute-start.24) | collective-permute-done | bytes 262176 | tf_op jit(solution)/shard_map/ppermute | solution.py:545
  102.8 1.5 collective-permute-done.25.refs_12_.refs_1_
  104.3 1.7 collective-permute-start.28
  106.6 1.8 collective-permute-done.26.refs_16_.refs_4_
  108.4 1.3 collective-permute-done.27.refs_15_.refs_5_
  109.8 1.8 collective-permute-start.30
  111.6 2.6 %collective-permute-start.31 = (bf16[256,512]{1,0:T(8,128)(2,1)S(1)}, bf16[256,512]{1,0:T(8,128)(2,1)S(1)}, u32[]{:S(2)}, u32[]{:S(2)}) collective-permute-start(bf16[256,512]{1,0:T(8,128)(2,1)S(1)} %get-tuple-element.247), channel_id=1, source_target_pairs={{2,3},{3,2},{4,5},{5,4},{6,7},{7,6},{0,0},{1,1},{10,11},{11,10},{1... | collective-permute-start | bytes 786440 | tf_op jit(solution)/shard_map/ppermute | solution.py:545
  114.3 3.8 %own_panels.1 = (bf16[512,1024]{1,0:T(8,128)(2,1)S(1)}, bf16[256,1152]{1,0:T(8,128)(2,1)}) custom-call(s32[32,4]{1,0:T(8,128)S(1)} %copy.81.mask, s32[4]{0:T(128)S(1)} %bitcast.24, s32[1]{0:T(128)} %bitcast.1.me, bf16[8192,1024]{1,0:T(8,128)(2,1)} %bitcast.30, bf16[256,512]{1,0:T(8,128)(2,1)} %copy-done.31, bf16[256,512]{1,0:T(8,128)(2,1)} %copy-done.42, ...), custom_call_target="tpu_custom_call" | custom-call | flops 268435456 | bytes 2621440 | tf_op jit(solution)/shard_map/own_panels/pallas_call | solution.py:263
  118.2 0.7 copy-done.62
  118.9 0.9 broadcast_select_fusion.6
  119.8 1.9 collective-permute-start.34
  121.7 3.4 %collective-permute-start.35 = (bf16[256,512]{1,0:T(8,128)(2,1)}, bf16[256,512]{1,0:T(8,128)(2,1)S(1)}, u32[]{:S(2)}, u32[]{:S(2)}) collective-permute-start(bf16[256,512]{1,0:T(8,128)(2,1)} %get-tuple-element.251), channel_id=1, source_target_pairs={{2,3},{3,2},{4,5},{5,4},{6,7},{7,6},{0,0},{1,1},{10,11},{11,10},{1... | collective-permute-start | bytes 786440 | tf_op jit(solution)/shard_map/ppermute | solution.py:545
  125.9 0.9 broadcast_select_fusion.5
  126.8 3.5 %collective-permute-start.32 = (bf16[256,512]{1,0:T(8,128)(2,1)}, bf16[256,512]{1,0:T(8,128)(2,1)}, u32[]{:S(2)}, u32[]{:S(2)}) collective-permute-start(bf16[256,512]{1,0:T(8,128)(2,1)} %get-tuple-element.255), channel_id=1, source_target_pairs={{2,4},{3,5},{4,6},{5,7},{7,1},{0,0},{6,2},{1,3},{10,12},{11,13},{1... | collective-permute-start | bytes 786440 | tf_op jit(solution)/shard_map/ppermute | solution.py:545
  130.3 1.9 collective-permute-start.33
  132.2 6.4 %all-to-all-start = ((bf16[32,1,8,1152]{3,2,1,0:T(8,128)(2,1)}), bf16[32,1,8,1152]{3,2,1,0:T(8,128)(2,1)S(1)}, u32[]{:S(2)}, u32[]{:S(2)}) async-start(bf16[32,1,8,1152]{3,2,1,0:T(8,128)(2,1)} %bitcast.6), calls=%async_computation | async-start | bytes 1179648 | tf_op jit(solution)/shard_map/all_to_all | solution.py:504
  138.6 3.1 %update.6.refs_16_ = bf16[8192,1024]{1,0:T(8,128)(2,1)} custom-call(s32[8,79]{1,0:T(8,128)S(1)} %copy-done.32, s32[32,4]{1,0:T(8,128)S(1)} %copy.81.mask, s32[1]{0:T(128)} %bitcast.1.me, bf16[512,1024]{1,0:T(8,128)(2,1)S(1)} %get-tuple-element.260.own, bf16[8192,1024]{1,0:T(8,128)(2,1)} %bitcast.31, bf16[256,512]{1,0:T(8,128)(2,1)} %copy-done.34, ...), custom_call_target="tpu_custom_call" | custom-call | flops 2147483648 | bytes 8388608 | tf_op jit(solution)/shard_map/update/pallas_call | solution.py:378
  141.8 3.8 %collective-permute-start.36 = (bf16[256,512]{1,0:T(8,128)(2,1)S(1)}, bf16[256,512]{1,0:T(8,128)(2,1)S(1)}, u32[]{:S(2)}, u32[]{:S(2)}) collective-permute-start(bf16[256,512]{1,0:T(8,128)(2,1)S(1)} %get-tuple-element.261), channel_id=1, source_target_pairs={{3,5},{4,6},{5,7},{7,1},{0,0},{2,2},{6,4},{1,3},{11,13},{12,14},{1... | collective-permute-start | bytes 786440 | tf_op jit(solution)/shard_map/ppermute | solution.py:545
  145.5 4.5 %collective-permute-start.37 = (bf16[256,512]{1,0:T(8,128)(2,1)S(1)}, bf16[256,512]{1,0:T(8,128)(2,1)S(1)}, u32[]{:S(2)}, u32[]{:S(2)}) collective-permute-start(bf16[256,512]{1,0:T(8,128)(2,1)S(1)} %get-tuple-element.262), channel_id=1, source_target_pairs={{3,2},{4,5},{5,4},{6,7},{7,6},{0,0},{1,1},{2,3},{11,10},{12,13},{1... | collective-permute-start | bytes 786440 | tf_op jit(solution)/shard_map/ppermute | solution.py:545
  150.1 4.9 %update.7.refs_16_ = bf16[8192,1024]{1,0:T(8,128)(2,1)} custom-call(s32[8,79]{1,0:T(8,128)S(1)} %copy-done.32, s32[32,4]{1,0:T(8,128)S(1)} %copy.81.mask, s32[1]{0:T(128)} %bitcast.1.me, bf16[512,1024]{1,0:T(8,128)(2,1)S(1)} %get-tuple-element.260.own, bf16[8192,1024]{1,0:T(8,128)(2,1)} %bitcast.32, ...), custom_call_target="tpu_custom_call", output_to_operand_aliasing={{}: (21, {})} | custom-call | flops 2147483648 | bytes 8388608 | tf_op jit(solution)/shard_map/update/pallas_call | solution.py:378
  155.0 1.9 broadcast_select_fusion.3
  156.9 1.9 collective-permute-start.40
  158.8 2.2 collective-permute-start.41
  161.0 0.9 broadcast_select_fusion.2
  163.2 0.9 copy.83
  164.1 6.6 %all-to-all-start.1 = ((bf16[32,4,8,256]{3,2,1,0:T(8,128)(2,1)}), bf16[32,4,8,256]{3,2,1,0:T(8,128)(2,1)S(1)}, u32[]{:S(2)}, u32[]{:S(2)}) async-start(bf16[32,4,8,256]{3,2,1,0:T(8,128)(2,1)} %bitcast.18), calls=%async_computation.1 | async-start | bytes 1048576 | tf_op jit(solution)/shard_map/all_to_all | solution.py:504
  170.8 1.6 collective-permute-start.38
  172.4 4.2 %collective-permute-start.39 = (bf16[256,512]{1,0:T(8,128)(2,1)}, bf16[256,512]{1,0:T(8,128)(2,1)S(1)}, u32[]{:S(2)}, u32[]{:S(2)}) collective-permute-start(bf16[256,512]{1,0:T(8,128)(2,1)} %get-tuple-element.273), channel_id=1, source_target_pairs={{5,4},{6,7},{7,6},{0,0},{1,1},{2,2},{3,3},{4,5},{13,12},{14,15},{1... | collective-permute-start | bytes 786440 | tf_op jit(solution)/shard_map/ppermute | solution.py:545
  176.7 6.6 %update.8.refs_15_ = bf16[8192,1024]{1,0:T(8,128)(2,1)} custom-call(s32[8,79]{1,0:T(8,128)S(1)} %copy-done.32, s32[32,4]{1,0:T(8,128)S(1)} %copy.81.mask, s32[1]{0:T(128)} %bitcast.1.me, bf16[512,1024]{1,0:T(8,128)(2,1)S(1)} %get-tuple-element.260.own, bf16[8192,1024]{1,0:T(8,128)(2,1)} %bitcast.33, ...), custom_call_target="tpu_custom_call", output_to_operand_aliasing={{}: (21, {})} | custom-call | flops 2147483648 | bytes 8388608 | tf_op jit(solution)/shard_map/update/pallas_call | solution.py:378
  184.0 5.2 %collective-permute-start.45 = (bf16[256,512]{1,0:T(8,128)(2,1)S(1)}, bf16[256,512]{1,0:T(8,128)(2,1)S(1)}, u32[]{:S(2)}, u32[]{:S(2)}) collective-permute-start(bf16[256,512]{1,0:T(8,128)(2,1)S(1)} %get-tuple-element.278), channel_id=1, source_target_pairs={{6,7},{7,6},{0,0},{1,1},{2,2},{3,3},{4,4},{5,5},{14,15},{15,14},{8... | collective-permute-start | bytes 786440 | tf_op jit(solution)/shard_map/ppermute | solution.py:545
  189.2 6.6 %update.9.refs_12_ = bf16[8192,1024]{1,0:T(8,128)(2,1)} custom-call(s32[8,79]{1,0:T(8,128)S(1)} %copy-done.32, s32[32,4]{1,0:T(8,128)S(1)} %copy.81.mask, s32[1]{0:T(128)} %bitcast.1.me, bf16[512,1024]{1,0:T(8,128)(2,1)S(1)} %get-tuple-element.260.own, bf16[8192,1024]{1,0:T(8,128)(2,1)} %bitcast.34, ...), custom_call_target="tpu_custom_call", output_to_operand_aliasing={{}: (20, {})} | custom-call | flops 2147483648 | bytes 8388608 | tf_op jit(solution)/shard_map/update/pallas_call | solution.py:378
  195.8 0.9 broadcast_select_fusion
  196.7 0.8 broadcast_select_fusion.8
  197.5 1.6 collective-permute-start.46
  199.1 1.6 collective-permute-start.42
  200.7 6.6 %collective-permute-start.43 = (bf16[256,512]{1,0:T(8,128)(2,1)}, bf16[256,512]{1,0:T(8,128)(2,1)}, u32[]{:S(2)}, u32[]{:S(2)}) collective-permute-start(bf16[256,512]{1,0:T(8,128)(2,1)} %get-tuple-element.283), channel_id=1, source_target_pairs={{7,6},{0,0},{1,1},{2,2},{3,3},{4,4},{5,5},{6,7},{15,14},{8,8},{9,9... | collective-permute-start | bytes 786440 | tf_op jit(solution)/shard_map/ppermute | solution.py:545
  207.3 7.4 %update.10.refs_3_ = bf16[8192,1024]{1,0:T(8,128)(2,1)} custom-call(s32[8,79]{1,0:T(8,128)S(1)} %copy-done.32, s32[32,4]{1,0:T(8,128)S(1)} %copy.81.mask, s32[1]{0:T(128)} %bitcast.1.me, bf16[512,1024]{1,0:T(8,128)(2,1)S(1)} %get-tuple-element.260.own, bf16[8192,1024]{1,0:T(8,128)(2,1)} %bitcast.35, ...), custom_call_target="tpu_custom_call", output_to_operand_aliasing={{}: (17, {})} | custom-call | flops 3221225472 | bytes 12582912 | tf_op jit(solution)/shard_map/update/pallas_call | solution.py:378
  214.8 1.1 copy_bitcast_fusion
  215.9 0.7 copy-done.76
  216.7 3.6 %update.11 = bf16[8192,1024]{1,0:T(8,128)(2,1)} custom-call(s32[8,79]{1,0:T(8,128)S(1)} %copy-done.32, s32[32,4]{1,0:T(8,128)S(1)} %copy.81.mask, s32[1]{0:T(128)} %bitcast.1.me, bf16[512,1024]{1,0:T(8,128)(2,1)S(1)} %get-tuple-element.260.own, bf16[8192,1024]{1,0:T(8,128)(2,1)} %bitcast.36, ...), custom_call_target="tpu_custom_call", output_to_operand_aliasing={{}: (8, {})} | custom-call | flops 1073741824 | bytes 4194304 | tf_op jit(solution)/shard_map/update/pallas_call | solution.py:378
  (235 shorter events, 11.0 us)
Async XLA Ops:
  5.2 5.8 %collective-permute-start = (bf16[256,512]{1,0:T(8,128)(2,1)S(1)}, bf16[256,512]{1,0:T(8,128)(2,1)S(1)}, u32[]{:S(2)}, u32[]{:S(2)}) collective-permute-start(bf16[256,512]{1,0:T(8,128)(2,1)S(1)} %get-tuple-element.151.refs_18_.refs_2_), channel_id=1, source_target_pairs={{0,2},{1,1},{3,3},{4,4},{5,5},{6,6},{7,7},{2,0},{8,10},{9,9},{11,1... | collective-permute-start | bytes 786440 | tf_op jit(solution)/shard_map/ppermute | solution.py:545
  5.9 5.1 %collective-permute-start.1 = (bf16[256,512]{1,0:T(8,128)(2,1)S(1)}, bf16[256,512]{1,0:T(8,128)(2,1)S(1)}, u32[]{:S(2)}, u32[]{:S(2)}) collective-permute-start(bf16[256,512]{1,0:T(8,128)(2,1)S(1)} %get-tuple-element.152.refs_3_), channel_id=1, source_target_pairs={{0,1},{2,2},{3,3},{4,4},{5,5},{6,6},{7,7},{1,0},{8,9},{10,10},{11,... | collective-permute-start | bytes 786440 | tf_op jit(solution)/shard_map/ppermute | solution.py:545
  6.6 5.9 %collective-permute-start.4 = (bf16[256,512]{1,0:T(8,128)(2,1)S(1)}, bf16[256,512]{1,0:T(8,128)(2,1)S(1)}, u32[]{:S(2)}, u32[]{:S(2)}) collective-permute-start(bf16[256,512]{1,0:T(8,128)(2,1)S(1)} %get-tuple-element.153.refs_6_), channel_id=1, source_target_pairs={{0,2},{1,1},{3,3},{4,4},{5,5},{6,6},{7,7},{2,0},{8,10},{9,9},{11,1... | collective-permute-start | bytes 786440 | tf_op jit(solution)/shard_map/ppermute | solution.py:545
  7.3 5.2 %collective-permute-start.5 = (bf16[256,512]{1,0:T(8,128)(2,1)S(1)}, bf16[256,512]{1,0:T(8,128)(2,1)S(1)}, u32[]{:S(2)}, u32[]{:S(2)}) collective-permute-start(bf16[256,512]{1,0:T(8,128)(2,1)S(1)} %get-tuple-element.154.refs_7_), channel_id=1, source_target_pairs={{0,1},{2,2},{3,3},{4,4},{5,5},{6,6},{7,7},{1,0},{8,9},{10,10},{11,... | collective-permute-start | bytes 786440 | tf_op jit(solution)/shard_map/ppermute | solution.py:545
  11.0 57.9 %copy-start.4 = (bf16[256,512]{1,0:T(8,128)(2,1)}, bf16[256,512]{1,0:T(8,128)(2,1)S(1)}, u32[]{:S(2)}) copy-start(bf16[256,512]{1,0:T(8,128)(2,1)S(1)} %get-tuple-element.157.refs_10_) | copy-start | bytes 786436
  11.0 57.9 %copy-start.5 = (bf16[256,512]{1,0:T(8,128)(2,1)}, bf16[256,512]{1,0:T(8,128)(2,1)S(1)}, u32[]{:S(2)}) copy-start(bf16[256,512]{1,0:T(8,128)(2,1)S(1)} %get-tuple-element.160.refs_11_) | copy-start | bytes 786436
  11.0 57.9 %copy-start.6 = (bf16[256,512]{1,0:T(8,128)(2,1)}, bf16[256,512]{1,0:T(8,128)(2,1)S(1)}, u32[]{:S(2)}) copy-start(bf16[256,512]{1,0:T(8,128)(2,1)S(1)} %get-tuple-element.167.refs_14_) | copy-start | bytes 786436
  11.0 57.9 %copy-start.7 = (bf16[256,512]{1,0:T(8,128)(2,1)}, bf16[256,512]{1,0:T(8,128)(2,1)S(1)}, u32[]{:S(2)}) copy-start(bf16[256,512]{1,0:T(8,128)(2,1)S(1)} %get-tuple-element.170.refs_15_) | copy-start | bytes 786436
  11.0 57.8 %copy-start.34 = (bf16[256,512]{1,0:T(8,128)(2,1)}, bf16[256,512]{1,0:T(8,128)(2,1)S(1)}, u32[]{:S(2)}) copy-start(bf16[256,512]{1,0:T(8,128)(2,1)S(1)} %collective-permute-done.refs_19_.refs_0_) | copy-start | bytes 786436
  11.1 8.0 %collective-permute-start.2 = (bf16[256,512]{1,0:T(8,128)(2,1)S(1)}, bf16[256,512]{1,0:T(8,128)(2,1)S(1)}, u32[]{:S(2)}, u32[]{:S(2)}) collective-permute-start(bf16[256,512]{1,0:T(8,128)(2,1)S(1)} %get-tuple-element.161), channel_id=1, source_target_pairs={{0,2},{1,3},{2,4},{5,5},{6,6},{7,7},{4,0},{3,1},{8,10},{9,11},{10,... | collective-permute-start | bytes 786440 | tf_op jit(solution)/shard_map/ppermute | solution.py:545
  11.8 7.3 %collective-permute-start.3 = (bf16[256,512]{1,0:T(8,128)(2,1)S(1)}, bf16[256,512]{1,0:T(8,128)(2,1)S(1)}, u32[]{:S(2)}, u32[]{:S(2)}) collective-permute-start(bf16[256,512]{1,0:T(8,128)(2,1)S(1)} %get-tuple-element.162), channel_id=1, source_target_pairs={{0,1},{2,3},{4,4},{5,5},{6,6},{7,7},{3,2},{1,0},{8,9},{10,11},{12,... | collective-permute-start | bytes 786440 | tf_op jit(solution)/shard_map/ppermute | solution.py:545
  12.5 51.2 %copy-start.54 = (bf16[256,512]{1,0:T(8,128)(2,1)}, bf16[256,512]{1,0:T(8,128)(2,1)S(1)}, u32[]{:S(2)}) copy-start(bf16[256,512]{1,0:T(8,128)(2,1)S(1)} %collective-permute-done.4.refs_4_) | copy-start | bytes 786436
  12.6 25.2 %collective-permute-start.8 = (bf16[256,512]{1,0:T(8,128)(2,1)S(1)}, bf16[256,512]{1,0:T(8,128)(2,1)S(1)}, u32[]{:S(2)}, u32[]{:S(2)}) collective-permute-start(bf16[256,512]{1,0:T(8,128)(2,1)S(1)} %get-tuple-element.171), channel_id=1, source_target_pairs={{0,2},{1,3},{2,4},{5,5},{6,6},{7,7},{4,0},{3,1},{8,10},{9,11},{10,... | collective-permute-start | bytes 786440 | tf_op jit(solution)/shard_map/ppermute | solution.py:545
  13.3 24.5 %collective-permute-start.9 = (bf16[256,512]{1,0:T(8,128)(2,1)S(1)}, bf16[256,512]{1,0:T(8,128)(2,1)S(1)}, u32[]{:S(2)}, u32[]{:S(2)}) collective-permute-start(bf16[256,512]{1,0:T(8,128)(2,1)S(1)} %get-tuple-element.172), channel_id=1, source_target_pairs={{0,1},{2,3},{4,4},{5,5},{6,6},{7,7},{3,2},{1,0},{8,9},{10,11},{12,... | collective-permute-start | bytes 786440 | tf_op jit(solution)/shard_map/ppermute | solution.py:545
  19.0 70.2 %copy-start.22 = (bf16[256,512]{1,0:T(8,128)(2,1)}, bf16[256,512]{1,0:T(8,128)(2,1)S(1)}, u32[]{:S(2)}) copy-start(bf16[256,512]{1,0:T(8,128)(2,1)S(1)} %get-tuple-element.193.refs_14_) | copy-start | bytes 786436
  19.1 70.2 %copy-start.23 = (bf16[256,512]{1,0:T(8,128)(2,1)}, bf16[256,512]{1,0:T(8,128)(2,1)S(1)}, u32[]{:S(2)}) copy-start(bf16[256,512]{1,0:T(8,128)(2,1)S(1)} %get-tuple-element.196.refs_15_) | copy-start | bytes 786436
  19.1 75.4 %copy-start.35 = (bf16[256,512]{1,0:T(8,128)(2,1)}, bf16[256,512]{1,0:T(8,128)(2,1)S(1)}, u32[]{:S(2)}) copy-start(bf16[256,512]{1,0:T(8,128)(2,1)S(1)} %collective-permute-done.2.refs_21_.refs_8_) | copy-start | bytes 786436
  19.1 75.4 %copy-start.36 = (bf16[256,512]{1,0:T(8,128)(2,1)}, bf16[256,512]{1,0:T(8,128)(2,1)S(1)}, u32[]{:S(2)}) copy-start(bf16[256,512]{1,0:T(8,128)(2,1)S(1)} %collective-permute-done.3.refs_20_.refs_9_) | copy-start | bytes 786436
  19.2 24.8 %collective-permute-start.6 = (bf16[256,512]{1,0:T(8,128)(2,1)S(1)}, bf16[256,512]{1,0:T(8,128)(2,1)S(1)}, u32[]{:S(2)}, u32[]{:S(2)}) collective-permute-start(bf16[256,512]{1,0:T(8,128)(2,1)S(1)} %get-tuple-element.176), channel_id=1, source_target_pairs={{0,2},{1,3},{2,4},{3,5},{4,6},{7,7},{6,0},{5,1},{8,10},{9,11},{10,... | collective-permute-start | bytes 786440 | tf_op jit(solution)/shard_map/ppermute | solution.py:545
  37.1 6.9 %collective-permute-start.7 = (bf16[256,512]{1,0:T(8,128)(2,1)S(1)}, bf16[256,512]{1,0:T(8,128)(2,1)S(1)}, u32[]{:S(2)}, u32[]{:S(2)}) collective-permute-start(bf16[256,512]{1,0:T(8,128)(2,1)S(1)} %get-tuple-element.177), channel_id=1, source_target_pairs={{0,1},{2,3},{3,2},{4,5},{6,6},{7,7},{5,4},{1,0},{8,9},{10,11},{11,... | collective-permute-start | bytes 786440 | tf_op jit(solution)/shard_map/ppermute | solution.py:545
  37.9 16.1 %collective-permute-start.12 = (bf16[256,512]{1,0:T(8,128)(2,1)S(1)}, bf16[256,512]{1,0:T(8,128)(2,1)S(1)}, u32[]{:S(2)}, u32[]{:S(2)}) collective-permute-start(bf16[256,512]{1,0:T(8,128)(2,1)S(1)} %get-tuple-element.182), channel_id=1, source_target_pairs={{0,2},{1,3},{2,4},{3,5},{4,6},{7,7},{6,0},{5,1},{8,10},{9,11},{10,... | collective-permute-start | bytes 786440 | tf_op jit(solution)/shard_map/ppermute | solution.py:545
  43.2 10.8 %collective-permute-start.13 = (bf16[256,512]{1,0:T(8,128)(2,1)S(1)}, bf16[256,512]{1,0:T(8,128)(2,1)S(1)}, u32[]{:S(2)}, u32[]{:S(2)}) collective-permute-start(bf16[256,512]{1,0:T(8,128)(2,1)S(1)} %get-tuple-element.183), channel_id=1, source_target_pairs={{0,1},{2,3},{3,2},{4,5},{6,6},{7,7},{5,4},{1,0},{8,9},{10,11},{11,... | collective-permute-start | bytes 786440 | tf_op jit(solution)/shard_map/ppermute | solution.py:545
  43.9 50.5 %copy-start.38 = (bf16[256,512]{1,0:T(8,128)(2,1)}, bf16[256,512]{1,0:T(8,128)(2,1)S(1)}, u32[]{:S(2)}) copy-start(bf16[256,512]{1,0:T(8,128)(2,1)S(1)} %collective-permute-done.6.refs_23_.refs_0_) | copy-start | bytes 786436
  44.0 50.5 %copy-start.39 = (bf16[256,512]{1,0:T(8,128)(2,1)}, bf16[256,512]{1,0:T(8,128)(2,1)S(1)}, u32[]{:S(2)}) copy-start(bf16[256,512]{1,0:T(8,128)(2,1)S(1)} %collective-permute-done.7.refs_22_.refs_1_) | copy-start | bytes 786436
  44.0 24.9 %collective-permute-start.10 = (bf16[256,512]{1,0:T(8,128)(2,1)S(1)}, bf16[256,512]{1,0:T(8,128)(2,1)S(1)}, u32[]{:S(2)}, u32[]{:S(2)}) collective-permute-start(bf16[256,512]{1,0:T(8,128)(2,1)S(1)} %get-tuple-element.187), channel_id=1, source_target_pairs={{0,2},{1,3},{2,4},{3,5},{4,6},{5,7},{7,0},{6,1},{8,10},{9,11},{10,... | collective-permute-start | bytes 786440 | tf_op jit(solution)/shard_map/ppermute | solution.py:545
  51.5 17.5 %collective-permute-start.11 = (bf16[256,512]{1,0:T(8,128)(2,1)S(1)}, bf16[256,512]{1,0:T(8,128)(2,1)S(1)}, u32[]{:S(2)}, u32[]{:S(2)}) collective-permute-start(bf16[256,512]{1,0:T(8,128)(2,1)S(1)} %get-tuple-element.188), channel_id=1, source_target_pairs={{0,1},{2,3},{3,2},{4,5},{5,4},{6,7},{7,6},{1,0},{8,9},{10,11},{11,... | collective-permute-start | bytes 786440 | tf_op jit(solution)/shard_map/ppermute | solution.py:545
  54.1 18.1 %collective-permute-start.16 = (bf16[256,512]{1,0:T(8,128)(2,1)S(1)}, bf16[256,512]{1,0:T(8,128)(2,1)S(1)}, u32[]{:S(2)}, u32[]{:S(2)}) collective-permute-start(bf16[256,512]{1,0:T(8,128)(2,1)S(1)} %get-tuple-element.197), channel_id=1, source_target_pairs={{0,2},{1,3},{2,4},{3,5},{4,6},{5,7},{7,0},{6,1},{8,10},{9,11},{10,... | collective-permute-start | bytes 786440 | tf_op jit(solution)/shard_map/ppermute | solution.py:545
  63.8 8.4 %collective-permute-start.17 = (bf16[256,512]{1,0:T(8,128)(2,1)S(1)}, bf16[256,512]{1,0:T(8,128)(2,1)S(1)}, u32[]{:S(2)}, u32[]{:S(2)}) collective-permute-start(bf16[256,512]{1,0:T(8,128)(2,1)S(1)} %get-tuple-element.198), channel_id=1, source_target_pairs={{0,1},{2,3},{3,2},{4,5},{5,4},{6,7},{7,6},{1,0},{8,9},{10,11},{11,... | collective-permute-start | bytes 786440 | tf_op jit(solution)/shard_map/ppermute | solution.py:545
  68.9 49.2 %copy-start.8 = (bf16[256,512]{1,0:T(8,128)(2,1)}, bf16[256,512]{1,0:T(8,128)(2,1)S(1)}, u32[]{:S(2)}) copy-start(bf16[256,512]{1,0:T(8,128)(2,1)S(1)} %get-tuple-element.192.refs_2_) | copy-start | bytes 786436
  68.9 49.2 %copy-start.9 = (bf16[256,512]{1,0:T(8,128)(2,1)}, bf16[256,512]{1,0:T(8,128)(2,1)S(1)}, u32[]{:S(2)}) copy-start(bf16[256,512]{1,0:T(8,128)(2,1)S(1)} %get-tuple-element.201.refs_3_) | copy-start | bytes 786436
  68.9 49.2 %copy-start.14 = (bf16[256,512]{1,0:T(8,128)(2,1)}, bf16[256,512]{1,0:T(8,128)(2,1)S(1)}, u32[]{:S(2)}) copy-start(bf16[256,512]{1,0:T(8,128)(2,1)S(1)} %get-tuple-element.218.refs_14_) | copy-start | bytes 786436
  69.1 9.6 %collective-permute-start.14 = (bf16[256,512]{1,0:T(8,128)(2,1)S(1)}, bf16[256,512]{1,0:T(8,128)(2,1)S(1)}, u32[]{:S(2)}, u32[]{:S(2)}) collective-permute-start(bf16[256,512]{1,0:T(8,128)(2,1)S(1)} %get-tuple-element.202), channel_id=1, source_target_pairs={{0,2},{1,3},{2,4},{3,5},{4,6},{5,7},{7,1},{6,0},{8,10},{9,11},{10,... | collective-permute-start | bytes 786440 | tf_op jit(solution)/shard_map/ppermute | solution.py:545
  72.2 9.2 %collective-permute-start.15 = (bf16[256,512]{1,0:T(8,128)(2,1)S(1)}, bf16[256,512]{1,0:T(8,128)(2,1)S(1)}, u32[]{:S(2)}, u32[]{:S(2)}) collective-permute-start(bf16[256,512]{1,0:T(8,128)(2,1)S(1)} %get-tuple-element.203), channel_id=1, source_target_pairs={{0,1},{2,3},{3,2},{4,5},{5,4},{6,7},{7,6},{1,0},{8,9},{10,11},{11,... | collective-permute-start | bytes 786440 | tf_op jit(solution)/shard_map/ppermute | solution.py:545
  72.3 11.9 %collective-permute-start.20 = (bf16[256,512]{1,0:T(8,128)(2,1)S(1)}, bf16[256,512]{1,0:T(8,128)(2,1)S(1)}, u32[]{:S(2)}, u32[]{:S(2)}) collective-permute-start(bf16[256,512]{1,0:T(8,128)(2,1)S(1)} %get-tuple-element.208), channel_id=1, source_target_pairs={{0,2},{1,3},{2,4},{3,5},{4,6},{5,7},{7,1},{6,0},{8,10},{9,11},{10,... | collective-permute-start | bytes 786440 | tf_op jit(solution)/shard_map/ppermute | solution.py:545
  77.8 9.2 %collective-permute-start.21 = (bf16[256,512]{1,0:T(8,128)(2,1)S(1)}, bf16[256,512]{1,0:T(8,128)(2,1)S(1)}, u32[]{:S(2)}, u32[]{:S(2)}) collective-permute-start(bf16[256,512]{1,0:T(8,128)(2,1)S(1)} %get-tuple-element.209), channel_id=1, source_target_pairs={{0,1},{2,3},{3,2},{4,5},{5,4},{6,7},{7,6},{1,0},{8,9},{10,11},{11,... | collective-permute-start | bytes 786440 | tf_op jit(solution)/shard_map/ppermute | solution.py:545
  81.4 13.1 %collective-permute-start.18 = (bf16[256,512]{1,0:T(8,128)(2,1)S(1)}, bf16[256,512]{1,0:T(8,128)(2,1)S(1)}, u32[]{:S(2)}, u32[]{:S(2)}) collective-permute-start(bf16[256,512]{1,0:T(8,128)(2,1)S(1)} %get-tuple-element.213), channel_id=1, source_target_pairs={{0,2},{1,3},{2,4},{3,5},{4,6},{5,7},{7,1},{6,0},{8,10},{9,11},{10,... | collective-permute-start | bytes 786440 | tf_op jit(solution)/shard_map/ppermute | solution.py:545
  83.5 11.1 %collective-permute-start.19 = (bf16[256,512]{1,0:T(8,128)(2,1)S(1)}, bf16[256,512]{1,0:T(8,128)(2,1)S(1)}, u32[]{:S(2)}, u32[]{:S(2)}) collective-permute-start(bf16[256,512]{1,0:T(8,128)(2,1)S(1)} %get-tuple-element.214), channel_id=1, source_target_pairs={{0,1},{2,3},{3,2},{4,5},{5,4},{6,7},{7,6},{1,0},{8,9},{10,11},{11,... | collective-permute-start | bytes 786440 | tf_op jit(solution)/shard_map/ppermute | solution.py:545
  87.0 9.9 %collective-permute-start.22 = (bf16[256,512]{1,0:T(8,128)(2,1)S(1)}, bf16[256,512]{1,0:T(8,128)(2,1)S(1)}, u32[]{:S(2)}, u32[]{:S(2)}) collective-permute-start(bf16[256,512]{1,0:T(8,128)(2,1)S(1)} %get-tuple-element.222), channel_id=1, source_target_pairs={{0,2},{1,3},{2,4},{3,5},{4,6},{5,7},{7,1},{6,0},{8,10},{9,11},{10,... | collective-permute-start | bytes 786440 | tf_op jit(solution)/shard_map/ppermute | solution.py:545
  89.3 9.2 %collective-permute-start.23 = (bf16[256,512]{1,0:T(8,128)(2,1)S(1)}, bf16[256,512]{1,0:T(8,128)(2,1)S(1)}, u32[]{:S(2)}, u32[]{:S(2)}) collective-permute-start(bf16[256,512]{1,0:T(8,128)(2,1)S(1)} %get-tuple-element.223), channel_id=1, source_target_pairs={{0,1},{2,3},{3,2},{4,5},{5,4},{6,7},{7,6},{1,0},{8,9},{10,11},{11,... | collective-permute-start | bytes 786440 | tf_op jit(solution)/shard_map/ppermute | solution.py:545
  94.7 8.1 %collective-permute-start.24 = (bf16[256,512]{1,0:T(8,128)(2,1)S(1)}, bf16[256,512]{1,0:T(8,128)(2,1)S(1)}, u32[]{:S(2)}, u32[]{:S(2)}) collective-permute-start(bf16[256,512]{1,0:T(8,128)(2,1)S(1)} %get-tuple-element.229), channel_id=1, source_target_pairs={{0,2},{1,3},{2,4},{3,5},{4,6},{5,7},{7,1},{6,0},{8,10},{9,11},{10,... | collective-permute-start | bytes 786440 | tf_op jit(solution)/shard_map/ppermute | solution.py:545
  95.0 9.2 %collective-permute-start.25 = (bf16[256,512]{1,0:T(8,128)(2,1)S(1)}, bf16[256,512]{1,0:T(8,128)(2,1)S(1)}, u32[]{:S(2)}, u32[]{:S(2)}) collective-permute-start(bf16[256,512]{1,0:T(8,128)(2,1)S(1)} %get-tuple-element.230), channel_id=1, source_target_pairs={{0,1},{2,3},{3,2},{4,5},{5,4},{6,7},{7,6},{1,0},{8,9},{10,11},{11,... | collective-permute-start | bytes 786440 | tf_op jit(solution)/shard_map/ppermute | solution.py:545
  98.6 9.8 %collective-permute-start.26 = (bf16[256,512]{1,0:T(8,128)(2,1)S(1)}, bf16[256,512]{1,0:T(8,128)(2,1)S(1)}, u32[]{:S(2)}, u32[]{:S(2)}) collective-permute-start(bf16[256,512]{1,0:T(8,128)(2,1)S(1)} %get-tuple-element.236), channel_id=1, source_target_pairs={{0,2},{1,3},{2,4},{3,5},{4,6},{5,7},{7,1},{6,0},{8,10},{9,11},{10,... | collective-permute-start | bytes 786440 | tf_op jit(solution)/shard_map/ppermute | solution.py:545
  100.3 9.4 %collective-permute-start.27 = (bf16[256,512]{1,0:T(8,128)(2,1)S(1)}, bf16[256,512]{1,0:T(8,128)(2,1)S(1)}, u32[]{:S(2)}, u32[]{:S(2)}) collective-permute-start(bf16[256,512]{1,0:T(8,128)(2,1)S(1)} %get-tuple-element.237), channel_id=1, source_target_pairs={{0,1},{2,3},{3,2},{4,5},{5,4},{6,7},{7,6},{1,0},{8,9},{10,11},{11,... | collective-permute-start | bytes 786440 | tf_op jit(solution)/shard_map/ppermute | solution.py:545
  104.3 13.8 %collective-permute-start.28 = (bf16[256,512]{1,0:T(8,128)(2,1)S(1)}, bf16[256,512]{1,0:T(8,128)(2,1)S(1)}, u32[]{:S(2)}, u32[]{:S(2)}) collective-permute-start(bf16[256,512]{1,0:T(8,128)(2,1)S(1)} %get-tuple-element.241), channel_id=1, source_target_pairs={{0,2},{1,3},{2,4},{3,5},{4,6},{5,7},{7,1},{6,0},{8,10},{9,11},{10,... | collective-permute-start | bytes 786440 | tf_op jit(solution)/shard_map/ppermute | solution.py:545
  106.0 12.2 %collective-permute-start.29 = (bf16[256,512]{1,0:T(8,128)(2,1)S(1)}, bf16[256,512]{1,0:T(8,128)(2,1)S(1)}, u32[]{:S(2)}, u32[]{:S(2)}) collective-permute-start(bf16[256,512]{1,0:T(8,128)(2,1)S(1)} %get-tuple-element.242), channel_id=1, source_target_pairs={{0,1},{2,3},{3,2},{4,5},{5,4},{6,7},{7,6},{1,0},{8,9},{10,11},{11,... | collective-permute-start | bytes 786440 | tf_op jit(solution)/shard_map/ppermute | solution.py:545
  109.8 15.4 %collective-permute-start.30 = (bf16[256,512]{1,0:T(8,128)(2,1)S(1)}, bf16[256,512]{1,0:T(8,128)(2,1)S(1)}, u32[]{:S(2)}, u32[]{:S(2)}) collective-permute-start(bf16[256,512]{1,0:T(8,128)(2,1)S(1)} %get-tuple-element.246), channel_id=1, source_target_pairs={{0,2},{1,3},{2,4},{3,5},{4,6},{5,7},{7,1},{6,0},{8,10},{9,11},{10,... | collective-permute-start | bytes 786440 | tf_op jit(solution)/shard_map/ppermute | solution.py:545
  111.6 13.6 %collective-permute-start.31 = (bf16[256,512]{1,0:T(8,128)(2,1)S(1)}, bf16[256,512]{1,0:T(8,128)(2,1)S(1)}, u32[]{:S(2)}, u32[]{:S(2)}) collective-permute-start(bf16[256,512]{1,0:T(8,128)(2,1)S(1)} %get-tuple-element.247), channel_id=1, source_target_pairs={{2,3},{3,2},{4,5},{5,4},{6,7},{7,6},{0,0},{1,1},{10,11},{11,10},{1... | collective-permute-start | bytes 786440 | tf_op jit(solution)/shard_map/ppermute | solution.py:545
  119.8 21.9 %collective-permute-start.34 = (bf16[256,512]{1,0:T(8,128)(2,1)}, bf16[256,512]{1,0:T(8,128)(2,1)S(1)}, u32[]{:S(2)}, u32[]{:S(2)}) collective-permute-start(bf16[256,512]{1,0:T(8,128)(2,1)} %get-tuple-element.250), channel_id=1, source_target_pairs={{1,3},{2,4},{3,5},{4,6},{5,7},{7,1},{0,0},{6,2},{9,11},{10,12},{11... | collective-permute-start | bytes 786440 | tf_op jit(solution)/shard_map/ppermute | solution.py:545
  121.7 20.0 %collective-permute-start.35 = (bf16[256,512]{1,0:T(8,128)(2,1)}, bf16[256,512]{1,0:T(8,128)(2,1)S(1)}, u32[]{:S(2)}, u32[]{:S(2)}) collective-permute-start(bf16[256,512]{1,0:T(8,128)(2,1)} %get-tuple-element.251), channel_id=1, source_target_pairs={{2,3},{3,2},{4,5},{5,4},{6,7},{7,6},{0,0},{1,1},{10,11},{11,10},{1... | collective-permute-start | bytes 786440 | tf_op jit(solution)/shard_map/ppermute | solution.py:545
  126.8 28.2 %collective-permute-start.32 = (bf16[256,512]{1,0:T(8,128)(2,1)}, bf16[256,512]{1,0:T(8,128)(2,1)}, u32[]{:S(2)}, u32[]{:S(2)}) collective-permute-start(bf16[256,512]{1,0:T(8,128)(2,1)} %get-tuple-element.255), channel_id=1, source_target_pairs={{2,4},{3,5},{4,6},{5,7},{7,1},{0,0},{6,2},{1,3},{10,12},{11,13},{1... | collective-permute-start | bytes 786440 | tf_op jit(solution)/shard_map/ppermute | solution.py:545
  130.3 24.8 %collective-permute-start.33 = (bf16[256,512]{1,0:T(8,128)(2,1)}, bf16[256,512]{1,0:T(8,128)(2,1)}, u32[]{:S(2)}, u32[]{:S(2)}) collective-permute-start(bf16[256,512]{1,0:T(8,128)(2,1)} %get-tuple-element.256), channel_id=1, source_target_pairs={{2,3},{3,2},{4,5},{5,4},{6,7},{7,6},{0,0},{1,1},{10,11},{11,10},{1... | collective-permute-start | bytes 786440 | tf_op jit(solution)/shard_map/ppermute | solution.py:545
  132.2 29.7 %all-to-all-start = ((bf16[32,1,8,1152]{3,2,1,0:T(8,128)(2,1)}), bf16[32,1,8,1152]{3,2,1,0:T(8,128)(2,1)S(1)}, u32[]{:S(2)}, u32[]{:S(2)}) async-start(bf16[32,1,8,1152]{3,2,1,0:T(8,128)(2,1)} %bitcast.6), calls=%async_computation | async-start | bytes 1179648 | tf_op jit(solution)/shard_map/all_to_all | solution.py:504
  141.8 19.2 %collective-permute-start.36 = (bf16[256,512]{1,0:T(8,128)(2,1)S(1)}, bf16[256,512]{1,0:T(8,128)(2,1)S(1)}, u32[]{:S(2)}, u32[]{:S(2)}) collective-permute-start(bf16[256,512]{1,0:T(8,128)(2,1)S(1)} %get-tuple-element.261), channel_id=1, source_target_pairs={{3,5},{4,6},{5,7},{7,1},{0,0},{2,2},{6,4},{1,3},{11,13},{12,14},{1... | collective-permute-start | bytes 786440 | tf_op jit(solution)/shard_map/ppermute | solution.py:545
  145.5 15.5 %collective-permute-start.37 = (bf16[256,512]{1,0:T(8,128)(2,1)S(1)}, bf16[256,512]{1,0:T(8,128)(2,1)S(1)}, u32[]{:S(2)}, u32[]{:S(2)}) collective-permute-start(bf16[256,512]{1,0:T(8,128)(2,1)S(1)} %get-tuple-element.262), channel_id=1, source_target_pairs={{3,2},{4,5},{5,4},{6,7},{7,6},{0,0},{1,1},{2,3},{11,10},{12,13},{1... | collective-permute-start | bytes 786440 | tf_op jit(solution)/shard_map/ppermute | solution.py:545
  156.9 19.7 %collective-permute-start.40 = (bf16[256,512]{1,0:T(8,128)(2,1)}, bf16[256,512]{1,0:T(8,128)(2,1)S(1)}, u32[]{:S(2)}, u32[]{:S(2)}) collective-permute-start(bf16[256,512]{1,0:T(8,128)(2,1)} %get-tuple-element.266), channel_id=1, source_target_pairs={{4,6},{5,7},{7,1},{0,0},{2,2},{3,3},{6,4},{1,5},{12,14},{13,15},{1... | collective-permute-start | bytes 786440 | tf_op jit(solution)/shard_map/ppermute | solution.py:545
  158.8 17.8 %collective-permute-start.41 = (bf16[256,512]{1,0:T(8,128)(2,1)}, bf16[256,512]{1,0:T(8,128)(2,1)S(1)}, u32[]{:S(2)}, u32[]{:S(2)}) collective-permute-start(bf16[256,512]{1,0:T(8,128)(2,1)} %get-tuple-element.267), channel_id=1, source_target_pairs={{4,5},{5,4},{6,7},{7,6},{0,0},{1,1},{2,2},{3,3},{12,13},{13,12},{1... | collective-permute-start | bytes 786440 | tf_op jit(solution)/shard_map/ppermute | solution.py:545
  164.1 50.6 %all-to-all-start.1 = ((bf16[32,4,8,256]{3,2,1,0:T(8,128)(2,1)}), bf16[32,4,8,256]{3,2,1,0:T(8,128)(2,1)S(1)}, u32[]{:S(2)}, u32[]{:S(2)}) async-start(bf16[32,4,8,256]{3,2,1,0:T(8,128)(2,1)} %bitcast.18), calls=%async_computation.1 | async-start | bytes 1048576 | tf_op jit(solution)/shard_map/all_to_all | solution.py:504
  170.8 24.9 %collective-permute-start.38 = (bf16[256,512]{1,0:T(8,128)(2,1)}, bf16[256,512]{1,0:T(8,128)(2,1)S(1)}, u32[]{:S(2)}, u32[]{:S(2)}) collective-permute-start(bf16[256,512]{1,0:T(8,128)(2,1)} %get-tuple-element.272), channel_id=1, source_target_pairs={{5,7},{7,1},{0,0},{2,2},{3,3},{4,4},{6,6},{1,5},{13,15},{15,9},{8,... | collective-permute-start | bytes 786440 | tf_op jit(solution)/shard_map/ppermute | solution.py:545
  172.4 23.4 %collective-permute-start.39 = (bf16[256,512]{1,0:T(8,128)(2,1)}, bf16[256,512]{1,0:T(8,128)(2,1)S(1)}, u32[]{:S(2)}, u32[]{:S(2)}) collective-permute-start(bf16[256,512]{1,0:T(8,128)(2,1)} %get-tuple-element.273), channel_id=1, source_target_pairs={{5,4},{6,7},{7,6},{0,0},{1,1},{2,2},{3,3},{4,5},{13,12},{14,15},{1... | collective-permute-start | bytes 786440 | tf_op jit(solution)/shard_map/ppermute | solution.py:545
  183.3 13.4 %collective-permute-start.44 = (bf16[256,512]{1,0:T(8,128)(2,1)S(1)}, bf16[256,512]{1,0:T(8,128)(2,1)S(1)}, u32[]{:S(2)}, u32[]{:S(2)}) collective-permute-start(bf16[256,512]{1,0:T(8,128)(2,1)S(1)} %get-tuple-element.277), channel_id=1, source_target_pairs={{7,1},{0,0},{2,2},{3,3},{4,4},{5,5},{6,6},{1,7},{15,9},{8,8},{10,1... | collective-permute-start | bytes 786440 | tf_op jit(solution)/shard_map/ppermute | solution.py:545
  184.0 12.7 %collective-permute-start.45 = (bf16[256,512]{1,0:T(8,128)(2,1)S(1)}, bf16[256,512]{1,0:T(8,128)(2,1)S(1)}, u32[]{:S(2)}, u32[]{:S(2)}) collective-permute-start(bf16[256,512]{1,0:T(8,128)(2,1)S(1)} %get-tuple-element.278), channel_id=1, source_target_pairs={{6,7},{7,6},{0,0},{1,1},{2,2},{3,3},{4,4},{5,5},{14,15},{15,14},{8... | collective-permute-start | bytes 786440 | tf_op jit(solution)/shard_map/ppermute | solution.py:545
  197.5 18.3 %collective-permute-start.46 = (bf16[256,512]{1,0:T(8,128)(2,1)}, bf16[256,512]{1,0:T(8,128)(2,1)S(1)}, u32[]{:S(2)}, u32[]{:S(2)}) collective-permute-start(bf16[256,512]{1,0:T(8,128)(2,1)} %broadcast_select_fusion.8), channel_id=1, source_target_pairs={{7,1},{0,0},{2,2},{3,3},{4,4},{5,5},{6,6},{1,7},{15,9},{8,8},{10,1... | collective-permute-start | bytes 786440 | tf_op jit(solution)/shard_map/ppermute | solution.py:545
  199.1 16.7 %collective-permute-start.42 = (bf16[256,512]{1,0:T(8,128)(2,1)}, bf16[256,512]{1,0:T(8,128)(2,1)S(1)}, u32[]{:S(2)}, u32[]{:S(2)}) collective-permute-start(bf16[256,512]{1,0:T(8,128)(2,1)} %get-tuple-element.282), channel_id=1, source_target_pairs={{7,1},{0,0},{2,2},{3,3},{4,4},{5,5},{6,6},{1,7},{15,9},{8,8},{10,1... | collective-permute-start | bytes 786440 | tf_op jit(solution)/shard_map/ppermute | solution.py:545
  200.7 15.2 %collective-permute-start.43 = (bf16[256,512]{1,0:T(8,128)(2,1)}, bf16[256,512]{1,0:T(8,128)(2,1)}, u32[]{:S(2)}, u32[]{:S(2)}) collective-permute-start(bf16[256,512]{1,0:T(8,128)(2,1)} %get-tuple-element.283), channel_id=1, source_target_pairs={{7,6},{0,0},{1,1},{2,2},{3,3},{4,4},{5,5},{6,7},{15,14},{8,8},{9,9... | collective-permute-start | bytes 786440 | tf_op jit(solution)/shard_map/ppermute | solution.py:545
  (63 other events, 1398.7 us)

commit v3 on v1

--- a/solution.py
+++ b/solution.py
@@ -9,7 +9,8 @@
 
 TILE = 256
 CHAINS = 2
-SUM_AFTER = 3
+RELAY_AFTER = 3
+LABEL_ROWS = 16
 VMEM_LIMIT = 16 * 1024 * 1024
 UPDATE_LIMIT = 32 * 1024 * 1024
 HBM = pl.BlockSpec(memory_space=pltpu.HBM)
@@ -189,10 +190,9 @@
     )(mask, in_hbm(front), *operands)
 
 
-def own_kernel(choices, sources, cols_dev, rows_out, mask, targets, me, front, *refs):
-    blocks, (own, bottom, panels, old, sems, old_sem) = refs[:sources], refs[sources:]
+def own_kernel(choices, sources, cols_dev, rows_out, span_front, mask, targets, me, front, *refs):
+    blocks, (own, sends, panels, old, sems, old_sem) = refs[:sources], refs[sources:]
     tiles = front.shape[0] // TILE
-    width = front.shape[1]
 
     def copy(part, source):
         return pltpu.make_async_copy(blocks[source], panels.at[part], sems.at[part])
@@ -202,38 +202,45 @@
     for part, options in enumerate(choices):
         for g, source in enumerate(options):
             pl.when(me[0] == g)(lambda part=part, source=source: copy(part, source).start())
-    lane = lax.broadcasted_iota(jnp.int32, (rows_out * TILE, 128), 1)
-    digits = jnp.zeros((rows_out * TILE, 128), jnp.int32)
-    for number in range(cols_dev * rows_out):
-        target = targets[number]
-        digits = jnp.where(lane == 2 * number, target >> 5, digits)
-        digits = jnp.where(lane == 2 * number + 1, target & 31, digits)
-    bottom[:, width:] = digits.astype(jnp.float32).astype(jnp.bfloat16)
+    sends[...] = jnp.zeros_like(sends)
+    lane = lax.broadcasted_iota(jnp.int32, (LABEL_ROWS, TILE), 1)
+    count = cols_dev * rows_out
+    labels = [targets[number] + 1 for number in range(count)]
+    parents = [targets[number] // span_front for number in range(count)]
+    ranks = [sum([(parents[m] == parents[n]).astype(jnp.int32) for m in range(n)], jnp.int32(0)) for n in range(count)]
+    for parent in range(sends.shape[0]):
+        digits = jnp.zeros((LABEL_ROWS, TILE), jnp.int32)
+        for n in range(count):
+            spot = jnp.where(parents[n] == parent, 2 * ranks[n], -2)
+            digits = jnp.where(lane == spot, labels[n] // 32, digits)
+            digits = jnp.where(lane == spot + 1, labels[n] % 32, digits)
+        sends[parent, 2 * TILE :, :] = digits.astype(jnp.float32).astype(jnp.bfloat16)
     for part, options in enumerate(choices):
         copy(part, options[0]).wait()
     for c in range(cols_dev):
         own[:, c * TILE : (c + 1) * TILE] = panels[c].astype(jnp.float32).T.astype(jnp.bfloat16)
     old_copy.wait()
-    for r in range(rows_out):
-        row, rows, panel = tiles - rows_out + r, slice(r * TILE, (r + 1) * TILE), panels.at[cols_dev + r]
-        for c in range(cols_dev):
+    for c in range(cols_dev):
+        for r in range(rows_out):
+            row, rows, panel = tiles - rows_out + r, slice(r * TILE, (r + 1) * TILE), panels.at[cols_dev + r]
             span = slice(c * TILE, (c + 1) * TILE)
             change = jnp.where(mask[row, c] > 0, dot(panel[...], own[:, span]), 0.0)
-            bottom[rows, span] = (old[rows, span].astype(jnp.float32) - change).astype(jnp.bfloat16)
-
-        @pl.when(me[0] == 0)
-        def _():
-            bottom[rows, : 2 * TILE] = panel[...]
-
-
-def own_panels(mask, targets, me, front, blocks, choices, rows_out):
+            tile = (old[rows, span].astype(jnp.float32) - change).astype(jnp.bfloat16)
+            if c < 2:
+                tile = jnp.where(me[0] == 0, panel[:, span], tile)
+            number = c * rows_out + r
+            place = pl.ds(pl.multiple_of(ranks[number] * TILE, TILE), TILE)
+            sends[parents[number], place, :] = tile
+
+
+def own_panels(mask, targets, me, front, blocks, choices, rows_out, n_front, span_front):
     width = front.shape[1]
     parts = len(choices)
     return pl.pallas_call(
-        functools.partial(own_kernel, choices, len(blocks), width // TILE, rows_out),
+        functools.partial(own_kernel, choices, len(blocks), width // TILE, rows_out, span_front),
         out_shape=[
             jax.ShapeDtypeStruct((2 * TILE, width), jnp.bfloat16),
-            jax.ShapeDtypeStruct((rows_out * TILE, width + 128), jnp.bfloat16),
+            jax.ShapeDtypeStruct((n_front, 2 * TILE + LABEL_ROWS, TILE), jnp.bfloat16),
         ],
         in_specs=[SMEM, SMEM, SMEM, HBM] + [HBM] * len(blocks),
         out_specs=[VMEM, VMEM],
@@ -253,7 +260,57 @@
     )(mask, targets, me, in_hbm(front), *[in_hbm(block) for block in blocks])
 
 
-def update_kernel(numbers, cols_dev, start, table, mask, me, own, front, *refs):
+def relay_kernel(slots, labels, arrived, sends):
+    n_grp = sends.shape[0]
+    sends[...] = jnp.zeros_like(sends)
+    for source in range(arrived.shape[0]):
+        for rank in range(2):
+            label = labels[source, rank]
+
+            @pl.when(label > 0)
+            def _():
+                owner = (label - 1) // slots % n_grp
+                slot = ((label - 1) % slots + 1).astype(jnp.float32)
+                sends[owner, :TILE, :] = arrived[source, rank * TILE : (rank + 1) * TILE, :]
+                sends[owner, TILE:, :] = jnp.full((LABEL_ROWS, TILE), slot, jnp.float32).astype(jnp.bfloat16)
+
+
+def relay(labels, arrived, slots, n_grp):
+    return pl.pallas_call(
+        functools.partial(relay_kernel, slots),
+        out_shape=jax.ShapeDtypeStruct((n_grp, TILE + LABEL_ROWS, TILE), jnp.bfloat16),
+        in_specs=[SMEM, VMEM],
+        out_specs=VMEM,
+        compiler_params=pltpu.CompilerParams(vmem_limit_bytes=VMEM_LIMIT),
+        cost_estimate=pl.CostEstimate(flops=0, bytes_accessed=4 * n_grp * TILE * TILE, transcendentals=0),
+        name="relay",
+    )(labels, arrived)
+
+
+def sum_kernel(labels, arrived, out):
+    out[...] = jnp.zeros_like(out)
+    for source in range(arrived.shape[0]):
+        label = labels[source]
+
+        @pl.when(label > 0)
+        def _():
+            slot = label - 1
+            out[slot] = out[slot] + arrived[source, :TILE, :].astype(jnp.float32)
+
+
+def sum_parents(labels, arrived, slots):
+    return pl.pallas_call(
+        sum_kernel,
+        out_shape=jax.ShapeDtypeStruct((slots, TILE, TILE), jnp.float32),
+        in_specs=[SMEM, VMEM],
+        out_specs=VMEM,
+        compiler_params=pltpu.CompilerParams(vmem_limit_bytes=VMEM_LIMIT),
+        cost_estimate=pl.CostEstimate(flops=0, bytes_accessed=8 * slots * TILE * TILE, transcendentals=0),
+        name="sum_parents",
+    )(labels, arrived)
+
+
+def update_kernel(numbers, room, cols_dev, start, table, mask, me, own, front, *refs):
     count = len(numbers)
     blocks = refs[:count]
     out, panels, old, new, listed, panel_sems, in_sems, out_sems = refs[-8:]
@@ -285,8 +342,8 @@
     listed[total] = 0
     if start:
         here = pl.ds(0, TILE)
-        top_in = pltpu.make_async_copy(front.at[here], new.at[count], in_sems.at[count])
-        top_out = pltpu.make_async_copy(new.at[count], out.at[here], out_sems.at[count])
+        top_in = pltpu.make_async_copy(front.at[here], new.at[room], in_sems.at[room])
+        top_out = pltpu.make_async_copy(new.at[room], out.at[here], out_sems.at[room])
         top_in.start()
         top_in.wait()
         top_out.start()
@@ -334,10 +391,9 @@
         top_out.wait()
 
 
-def update(table, mask, me, own, front, numbers, blocks, base=None):
+def update(table, mask, me, own, front, numbers, blocks, room, base=None):
     width = front.shape[1]
     count = len(numbers)
-    room = count + count % 2
     operands = [table, mask, me, own, in_hbm(front), *[in_hbm(block) for block in blocks]]
     in_specs = [SMEM, SMEM, SMEM, VMEM, HBM] + [HBM] * count
     aliases = {}
@@ -346,7 +402,7 @@
         operands.append(in_hbm(base))
         in_specs.append(HBM)
     return pl.pallas_call(
-        functools.partial(update_kernel, tuple(numbers), width // TILE, base is None),
+        functools.partial(update_kernel, tuple(numbers), room, width // TILE, base is None),
         out_shape=jax.ShapeDtypeStruct(front.shape, jnp.bfloat16),
         in_specs=in_specs,
         out_specs=HBM,
@@ -362,7 +418,7 @@
         input_output_aliases=aliases,
         compiler_params=pltpu.CompilerParams(vmem_limit_bytes=UPDATE_LIMIT),
         cost_estimate=pl.CostEstimate(
-            flops=2 * count * TILE * width * 2 * TILE, bytes_accessed=4 * count * TILE * width, transcendentals=0
+            flops=2 * room * TILE * width * 2 * TILE, bytes_accessed=4 * room * TILE * width, transcendentals=0
         ),
         name="update",
     )(*operands)
@@ -390,7 +446,7 @@
     contrib = targets.shape[0]
     rows_out = contrib // cols_dev
     n_grp = lax.axis_size("grp")
-    n_dev = n_grp * lax.axis_size("front")
+    n_front = lax.axis_size("front")
     slots_dev = n_grp // 2
     g = lax.axis_index("grp")
     me = jnp.reshape(g, (1,)).astype(jnp.int32)
@@ -398,11 +454,15 @@
 
     perms, rules = routes(n_grp)
     lists = stream_plan(perms, rules, n_grp, tiles, cols_dev, rows_out)
+    if n_grp == 8:
+        lists[1] += lists[0][-2 * CHAINS :]
     got = travel(perms, rules, lists, n_grp, tiles)
     events = len(got)
     longest = max(len(lists[0]), len(lists[1]))
 
-    order = [(e, lists[s][e]) for e in range(longest) for s in (0, 1) if e < len(lists[s])] + [(longest, 0)]
+    order = [(e, lists[s][e]) for e in range(longest) for s in (0, 1) if e < len(lists[s])]
+    order = [(e, tile) for n, (e, tile) in enumerate(order) if tile not in [other for _, other in order[:n]]]
+    order.append((longest, 0))
     cuts = [0, 4, 8] + list(range(16, len(order) - 2, 8)) + [len(order)]
     made, parts, where_made = [], None, {}
 
@@ -462,32 +522,24 @@
             return names[name]
 
         choices = [[choice(needed[n][part], n) for n in range(n_grp)] for part in range(cols_dev + rows_out)]
-        return own_panels(mask, targets, me, front, blocks, choices, rows_out)
-
-    piece = TILE // n_dev
-
-    def exchange(blocks):
-        return lax.all_to_all(blocks, ("front", "grp"), split_axis=0, concat_axis=0, tiled=True)
-
-    def sums_of(arrived):
-        digits = arrived[:, 0, 0, width : width + 2 * contrib].astype(jnp.int32).reshape(n_dev * contrib, 2)
-        labels = digits[:, 0] * 32 + digits[:, 1]
-        blocks = arrived[..., :width].reshape(n_dev, rows_out, piece, cols_dev, TILE)
-        blocks = jnp.transpose(blocks, (0, 3, 1, 2, 4)).reshape(n_dev * contrib, piece * TILE)
-        picker = labels[None, :] == jnp.arange(n_dev * slots_dev, dtype=jnp.int32)[:, None]
-        sums = dot(picker.astype(jnp.bfloat16), blocks).astype(jnp.bfloat16)
-        return sums.reshape(n_dev, slots_dev, piece, TILE)
+        return own_panels(mask, targets, me, front, blocks, choices, rows_out, n_front, n_grp * slots_dev)
+
+    def exchange(blocks, axis):
+        return lax.all_to_all(blocks, axis, split_axis=0, concat_axis=0, tiled=True)
+
+    def relayed(arrived):
+        digits = arrived[:, 2 * TILE, :4].astype(jnp.int32).reshape(n_front, 2, 2)
+        return exchange(relay(digits[..., 0] * 32 + digits[..., 1], arrived, slots_dev, n_grp), "grp")
 
     held, turn, result, done = [], (), None, 0
 
-    def step(limit, at_hand, *waits):
+    def step(count, *waits):
         nonlocal result, done
-        numbers = list(range(done, min(done + limit, at_hand)))
-        done += len(numbers)
+        numbers = [n for n in range(2 * done, 2 * (done + count)) if any(line[n] for line in table)]
+        done += count
         here = after((me,), *waits)[0]
         blocks = [held[n // 2][n % 2] for n in numbers]
-        if numbers:
-            result = update(rows, mask, here, own, front, numbers, blocks, base=result)
+        result = update(rows, mask, here, own, front, numbers, blocks, 2 * count, base=result)
 
     for e in range(events):
         values = []
@@ -508,21 +560,19 @@
             held[e + 1 - CHAINS] = list(after(held[e + 1 - CHAINS], *turn))
         late = e - ready - CHAINS
         if late == 0:
-            own, bottom = own_part()
-            pieces = jnp.transpose(bottom.reshape(rows_out, n_dev, piece, width + 128), (1, 0, 2, 3))
-            arrived = exchange(pieces)
-        if late == SUM_AFTER:
-            sums = sums_of(after((arrived,), *turn)[0])
-            parent_pieces = exchange(sums)
-            turn = (*turn, sums)
-        if late >= 2 and late % 2 == 0:
-            step(12, 2 * (e - CHAINS + 1), *turn)
+            own, sends = own_part()
+        if late == 1:
+            arrived = exchange(after((sends,), *turn)[0], "front")
+        if late == RELAY_AFTER:
+            arrived = relayed(after((arrived,), *turn)[0])
+        if late >= 2 and late != RELAY_AFTER and e < events - 1:
+            step(min(4, e - CHAINS + 1 - done), *turn)
             turn = (*turn, result)
-    parent_tiles = jnp.transpose(parent_pieces, (1, 0, 2, 3)).reshape(slots_dev, TILE, TILE).astype(jnp.float32)
-    if done < 2 * (events - CHAINS):
-        step(12, 2 * (events - CHAINS), *turn)
-    while done < 2 * events:
-        step(12, 2 * events, parent_tiles)
+    while done < events - CHAINS:
+        step(min(6, events - CHAINS - done), *turn)
+    slots_here = after((arrived,), result)[0]
+    parent_tiles = sum_parents(slots_here[:, TILE, 0].astype(jnp.int32), slots_here, slots_dev)
+    step(CHAINS, parent_tiles)
     return (result[None], parent_tiles)
 
 

time: 194 us -> 190 us (0.979)
  Pallas kernels: 53.7 us -> 60 us
  other arithmetic: 8.77 us -> 5.97 us
  waiting for transfers between devices: 58.4 us -> 56 us
  local copies, waits for them, and re-layouts: 4.78 us -> 2.67 us
    all_to_all x2, waiting for transfers between devices: 15 us -> 2.67 us  [exchange(): return lax.all_to_all(blocks, axis, split_axis=0, concat_axis=0, tiled=True)]
    ppermute x47 -> x44, waiting for transfers between devices: 43.4 us -> 53.3 us  [shards(): lax.ppermute(turn[s], 'grp', perms[s])]
    pallas_call x5 -> x8, Pallas kernels: 28.3 us -> 34.4 us  [the longest x6 31 us: update(): pl.pallas_call(functools.partial(update_kernel, tuple(numbers), room, wid...]
    select_n x9 -> x4, other arithmetic: 5.9 us -> 0.15 us  [shards(): value = jnp.where(others[s], held[e - CHAINS][1 - rules[s][0]], value)]
    select_n x13 -> x17, other arithmetic: 1.58 us -> 5.57 us  [shards(): jnp.where(root, made[which][n], value)]
    all_to_all x2, starting transfers between devices: 11 us -> 9.02 us  [exchange(): return lax.all_to_all(blocks, axis, split_axis=0, concat_axis=0, tiled=True)]
    ppermute x47 -> x44, starting transfers between devices: 53.6 us -> 54.2 us  [shards(): lax.ppermute(turn[s], 'grp', perms[s])]
  transfers between devices with their start and end apart: 49 -> 46, of which waited for: 19 -> 18; matrix products, arithmetic and copies ran while one was open for 6% -> 3% of each run, Pallas kernels for 25% -> 29%
where the time goes in v3:
time: 190 us; the launch traced here: 189 us
  starting transfers between devices  63.2 us (33%)
  Pallas kernels  60 us (32%)
  waiting for transfers between devices  56 us (29%)
  other arithmetic  5.97 us (3%)
  local copies, waits for them, and re-layouts  2.67 us (1%)
    ppermute x44, starting transfers between devices, shards(): lax.ppermute(turn[s], 'grp', perms[s])  54.2 us
    ppermute x44, waiting for transfers between devices, shards(): lax.ppermute(turn[s], 'grp', perms[s])  53.3 us
    pallas_call x6, Pallas kernels, update(): pl.pallas_call(functools.partial(update_kernel, tuple(numbers), room, wid...  31 us
    pallas_call x5, Pallas kernels, factor(): pl.pallas_call(functools.partial(factor_kernel, tuple(tiles), head), out_...  21.6 us
    all_to_all x2, starting transfers between devices, exchange(): return lax.all_to_all(blocks, axis, split_axis=0, concat_axis=0, tiled=True)  9.02 us
    select_n x17, other arithmetic, shards(): jnp.where(root, made[which][n], value)  5.57 us
    pallas_call x1, Pallas kernels, own_panels(): pl.pallas_call(functools.partial(own_kernel, choices, len(blocks), width...  4 us
  transfers between devices with their start and end apart: 46, of which 18 were waited for; matrix products, arithmetic and copies ran while one was open for 3% of the time, Pallas kernels for 29%

profile of v3, /device:TPU:0, one launch (start us, length us, event | category | flops | bytes accessed | tf_op | source)
XLA Modules:
  0.0 189.4 jit_solution(15801134217677450776)
XLA Ops:
  1.4 3.8 %factor.5 = (bf16[256,512]{1,0:T(8,128)(2,1)S(1)}, bf16[256,512]{1,0:T(8,128)(2,1)S(1)}, bf16[256,512]{1,0:T(8,128)(2,1)S(1)}, bf16[256,512]{1,0:T(8,128)(2,1)S(...) custom-call(s32[32,4]{1,0:T(8,128)S(1)} %copy.53.mask, bf16[8192,1024]{1,0:T(8,128)(2,1)} %bitcast.9, ...), custom_call_target="tpu_custom_call" | custom-call | flops 805306368 | bytes 2097152 | tf_op jit(solution)/shard_map/factor/pallas_call | solution.py:179
  5.2 3.1 %collective-permute-start = (bf16[256,512]{1,0:T(8,128)(2,1)S(1)}, bf16[256,512]{1,0:T(8,128)(2,1)S(1)}, u32[]{:S(2)}, u32[]{:S(2)}) collective-permute-start(bf16[256,512]{1,0:T(8,128)(2,1)S(1)} %get-tuple-element.148.refs_18_), channel_id=1, source_target_pairs={{0,2},{1,3},{2,4},{3,5},{4,6},{5,7},{6,0},{7,1},{8,10},{9,11},{10,... | collective-permute-start | bytes 786440 | tf_op jit(solution)/shard_map/ppermute | solution.py:557
  8.3 1.5 collective-permute-start.1
  9.8 1.6 collective-permute-start.4
  11.9 3.0 %factor.6 = (bf16[256,512]{1,0:T(8,128)(2,1)S(1)}, bf16[256,512]{1,0:T(8,128)(2,1)S(1)}, bf16[256,512]{1,0:T(8,128)(2,1)S(1)}, bf16[256,512]{1,0:T(8,128)(2,1)S(1)}) custom-call(s32[32,4]{1,0:T(8,128)S(1)} %copy.53.mask, bf16[8192,1024]{1,0:T(8,128)(2,1)} %bitcast.10, bf16[4,256,256]{2,1,0:T(8,128)(2,1)S(1)} %get-tuple-element.212.refs_0_, ...), custom_call_target="tpu_custom_call" | custom-call | flops 805306368 | bytes 2097152 | tf_op jit(solution)/shard_map/factor/pallas_call | solution.py:179
  14.9 2.6 %collective-permute-done.refs_19_.refs_0_ = bf16[256,512]{1,0:T(8,128)(2,1)S(1)} collective-permute-done((bf16[256,512]{1,0:T(8,128)(2,1)S(1)}, bf16[256,512]{1,0:T(8,128)(2,1)S(1)}, u32[]{:S(2)}, u32[]{:S(2)}) %collective-permute-start) | collective-permute-done | bytes 262176 | tf_op jit(solution)/shard_map/ppermute | solution.py:557
  17.6 1.6 collective-permute-start.2
  19.2 1.5 collective-permute-start.3
  20.7 2.3 %collective-permute-done.4.refs_2_ = bf16[256,512]{1,0:T(8,128)(2,1)S(1)} collective-permute-done((bf16[256,512]{1,0:T(8,128)(2,1)S(1)}, bf16[256,512]{1,0:T(8,128)(2,1)S(1)}, u32[]{:S(2)}, u32[]{:S(2)}) %collective-permute-start.4) | collective-permute-done | bytes 262176 | tf_op jit(solution)/shard_map/ppermute | solution.py:557
  23.2 1.6 collective-permute-start.8
  24.8 1.5 collective-permute-start.9
  26.3 4.9 %factor.7 = (bf16[256,512]{1,0:T(8,128)(2,1)S(1)}, bf16[256,512]{1,0:T(8,128)(2,1)S(1)}, bf16[256,512]{1,0:T(8,128)(2,1)S(1)}, bf16[256,512]{1,0:T(8,128)(2,1)S(...) custom-call(s32[32,4]{1,0:T(8,128)S(1)} %copy.53.mask, ...), custom_call_target="tpu_custom_call" | custom-call | flops 1610612736 | bytes 4194304 | tf_op jit(solution)/shard_map/factor/pallas_call | solution.py:179
  31.4 1.6 collective-permute-start.6
  34.4 1.7 collective-permute-start.12
  36.0 1.5 collective-permute-start.13
  37.6 4.6 %collective-permute-done.6.refs_23_.refs_0_ = bf16[256,512]{1,0:T(8,128)(2,1)S(1)} collective-permute-done((bf16[256,512]{1,0:T(8,128)(2,1)S(1)}, bf16[256,512]{1,0:T(8,128)(2,1)S(1)}, u32[]{:S(2)}, u32[]{:S(2)}) %collective-permute-start.6) | collective-permute-done | bytes 262176 | tf_op jit(solution)/shard_map/ppermute | solution.py:557
  43.2 4.6 %collective-permute-done.12.refs_2_ = bf16[256,512]{1,0:T(8,128)(2,1)S(1)} collective-permute-done((bf16[256,512]{1,0:T(8,128)(2,1)S(1)}, bf16[256,512]{1,0:T(8,128)(2,1)S(1)}, u32[]{:S(2)}, u32[]{:S(2)}) %collective-permute-start.12) | collective-permute-done | bytes 262176 | tf_op jit(solution)/shard_map/ppermute | solution.py:557
  49.4 4.9 %factor.8 = (bf16[256,512]{1,0:T(8,128)(2,1)S(1)}, bf16[256,512]{1,0:T(8,128)(2,1)S(1)}, bf16[256,512]{1,0:T(8,128)(2,1)S(1)}, bf16[256,512]{1,0:T(8,128)(2,1)S(...) custom-call(s32[32,4]{1,0:T(8,128)S(1)} %copy.53.mask, ...), custom_call_target="tpu_custom_call" | custom-call | flops 1610612736 | bytes 4194304 | tf_op jit(solution)/shard_map/factor/pallas_call | solution.py:179
  54.5 1.6 collective-permute-start.14
  56.1 1.7 collective-permute-start.15
  57.9 1.3 collective-permute-start.20
  59.2 1.1 collective-permute-start.21
  60.4 5.3 %collective-permute-done.14.refs_3_.refs_0_ = bf16[256,512]{1,0:T(8,128)(2,1)S(1)} collective-permute-done((bf16[256,512]{1,0:T(8,128)(2,1)S(1)}, bf16[256,512]{1,0:T(8,128)(2,1)S(1)}, u32[]{:S(2)}, u32[]{:S(2)}) %collective-permute-start.14) | collective-permute-done | bytes 262176 | tf_op jit(solution)/shard_map/ppermute | solution.py:557
  66.6 1.9 collective-permute-start.19
  68.4 2.8 %collective-permute-done.20.refs_8_.refs_2_ = bf16[256,512]{1,0:T(8,128)(2,1)S(1)} collective-permute-done((bf16[256,512]{1,0:T(8,128)(2,1)S(1)}, bf16[256,512]{1,0:T(8,128)(2,1)S(1)}, u32[]{:S(2)}, u32[]{:S(2)}) %collective-permute-start.20) | collective-permute-done | bytes 262176 | tf_op jit(solution)/shard_map/ppermute | solution.py:557
  71.3 1.0 collective-permute-start.22
  72.4 1.9 collective-permute-start.23
  74.2 5.0 %factor.9 = (bf16[256,512]{1,0:T(8,128)(2,1)S(1)}, bf16[256,512]{1,0:T(8,128)(2,1)S(1)}, bf16[256,512]{1,0:T(8,128)(2,1)S(1)}, bf16[256,512]{1,0:T(8,128)(2,1)S(...) custom-call(s32[32,4]{1,0:T(8,128)S(1)} %copy.53.mask, ...), custom_call_target="tpu_custom_call" | custom-call | flops 1610612736 | bytes 4194304 | tf_op jit(solution)/shard_map/factor/pallas_call | solution.py:179
  79.4 1.7 collective-permute-start.24
  81.7 0.9 collective-permute-done.22.refs_7_.refs_6_
  82.7 1.2 collective-permute-start.26
  83.8 1.5 collective-permute-start.27
  85.3 3.8 %collective-permute-done.24.refs_13_.refs_0_ = bf16[256,512]{1,0:T(8,128)(2,1)S(1)} collective-permute-done((bf16[256,512]{1,0:T(8,128)(2,1)S(1)}, bf16[256,512]{1,0:T(8,128)(2,1)S(1)}, u32[]{:S(2)}, u32[]{:S(2)}) %collective-permute-start.24) | collective-permute-done | bytes 262176 | tf_op jit(solution)/shard_map/ppermute | solution.py:557
  89.1 1.2 collective-permute-done.25.refs_12_.refs_1_
  90.5 0.9 collective-permute-start.29
  91.4 3.3 %collective-permute-done.26.refs_16_.refs_2_ = bf16[256,512]{1,0:T(8,128)(2,1)S(1)} collective-permute-done((bf16[256,512]{1,0:T(8,128)(2,1)S(1)}, bf16[256,512]{1,0:T(8,128)(2,1)S(1)}, u32[]{:S(2)}, u32[]{:S(2)}) %collective-permute-start.26) | collective-permute-done | bytes 262176 | tf_op jit(solution)/shard_map/ppermute | solution.py:557
  94.7 0.9 collective-permute-done.27.refs_15_.refs_3_
  95.6 0.9 select_select_fusion.3
  96.8 1.0 collective-permute-start.33
  98.0 4.0 %own_panels.1 = (bf16[512,1024]{1,0:T(8,128)(2,1)S(1)}, bf16[4,528,256]{2,1,0:T(8,128)(2,1)}) custom-call(s32[32,4]{1,0:T(8,128)S(1)} %copy.53.mask, s32[4]{0:T(128)S(1)} %bitcast.8, s32[1]{0:T(128)} %bitcast.1.me, bf16[8192,1024]{1,0:T(8,128)(2,1)} %bitcast.14, bf16[256,512]{1,0:T(8,128)(2,1)} %copy-done.5, bf16[256,512]{1,0:T(8,128)(2,1)} %copy-done.20, ...), custom_call_target="tpu_custom_call" | custom-call | flops 268435456 | bytes 2621440 | tf_op jit(solution)/shard_map/own_panels/pallas_call | solution.py:239
  102.0 0.9 select_select_fusion.2
  103.0 3.5 %all-to-all-start = ((bf16[4,528,256]{2,1,0:T(8,128)(2,1)}), bf16[4,528,256]{2,1,0:T(8,128)(2,1)S(1)}, u32[]{:S(2)}, u32[]{:S(2)}) async-start(bf16[4,528,256]{2,1,0:T(8,128)(2,1)} %get-tuple-element.249), calls=%async_computation | async-start | bytes 2162688 | tf_op jit(solution)/shard_map/all_to_all | solution.py:528
  106.5 1.8 collective-permute-start.30
  108.3 1.1 collective-permute-start.31
  109.4 1.9 select_select_fusion.1
  112.5 4.4 %update.6.refs_8_ = bf16[8192,1024]{1,0:T(8,128)(2,1)} custom-call(s32[8,46]{1,0:T(8,128)S(1)} %copy-done.6, s32[32,4]{1,0:T(8,128)S(1)} %copy.53.mask, s32[1]{0:T(128)} %bitcast.1.me, bf16[512,1024]{1,0:T(8,128)(2,1)S(1)} %get-tuple-element.257.own, bf16[8192,1024]{1,0:T(8,128)(2,1)} %bitcast.15, bf16[256,512]{1,0:T(8,128)(2,1)} %copy-done.8, ...), custom_call_target="tpu_custom_call" | custom-call | flops 2147483648 | bytes 8388608 | tf_op jit(solution)/shard_map/update/pallas_call | solution.py:404
  117.7 0.9 select_select_fusion
  118.6 2.7 %all-to-all-done.arrived = bf16[4,528,256]{2,1,0:T(8,128)(2,1)S(1)} async-done(((bf16[4,528,256]{2,1,0:T(8,128)(2,1)}), bf16[4,528,256]{2,1,0:T(8,128)(2,1)S(1)}, u32[]{:S(2)}, u32[]{:S(2)}) %all-to-all-start) | async-done | bytes 1081376 | tf_op jit(solution)/shard_map/all_to_all | solution.py:528
  121.5 1.8 relay.1
  123.2 5.5 %all-to-all-start.1 = ((bf16[8,272,256]{2,1,0:T(8,128)(2,1)}), bf16[8,272,256]{2,1,0:T(8,128)(2,1)S(1)}, u32[]{:S(2)}, u32[]{:S(2)}) async-start(bf16[8,272,256]{2,1,0:T(8,128)(2,1)} %relay.1), calls=%async_computation.1 | async-start | bytes 2228224 | tf_op jit(solution)/shard_map/all_to_all | solution.py:528
  128.7 2.0 %collective-permute-start.34 = (bf16[256,512]{1,0:T(8,128)(2,1)}, bf16[256,512]{1,0:T(8,128)(2,1)S(1)}, u32[]{:S(2)}, u32[]{:S(2)}) collective-permute-start(bf16[256,512]{1,0:T(8,128)(2,1)} %get-tuple-element.258), channel_id=1, source_target_pairs={{0,2},{1,3},{2,4},{3,5},{4,6},{5,7},{6,0},{7,1},{8,10},{9,11},{10,... | collective-permute-start | bytes 786440 | tf_op jit(solution)/shard_map/ppermute | solution.py:557
  130.8 1.5 collective-permute-start.35
  132.3 1.5 collective-permute-start.40
  134.4 5.8 %update.7.refs_8_ = bf16[8192,1024]{1,0:T(8,128)(2,1)} custom-call(s32[8,46]{1,0:T(8,128)S(1)} %copy-done.6, s32[32,4]{1,0:T(8,128)S(1)} %copy.53.mask, s32[1]{0:T(128)} %bitcast.1.me, bf16[512,1024]{1,0:T(8,128)(2,1)S(1)} %get-tuple-element.257.own, bf16[8192,1024]{1,0:T(8,128)(2,1)} %bitcast.16, ...), custom_call_target="tpu_custom_call", output_to_operand_aliasing={{}: (13, {})} | custom-call | flops 2147483648 | bytes 8388608 | tf_op jit(solution)/shard_map/update/pallas_call | solution.py:404
  140.2 17.7 %collective-permute-done.34.refs_4_ = bf16[256,512]{1,0:T(8,128)(2,1)S(1)} collective-permute-done((bf16[256,512]{1,0:T(8,128)(2,1)}, bf16[256,512]{1,0:T(8,128)(2,1)S(1)}, u32[]{:S(2)}, u32[]{:S(2)}) %collective-permute-start.34) | collective-permute-done | bytes 262176 | tf_op jit(solution)/shard_map/ppermute | solution.py:557
  158.0 2.1 %collective-permute-start.38 = (bf16[256,512]{1,0:T(8,128)(2,1)S(1)}, bf16[256,512]{1,0:T(8,128)(2,1)S(1)}, u32[]{:S(2)}, u32[]{:S(2)}) collective-permute-start(bf16[256,512]{1,0:T(8,128)(2,1)S(1)} %get-tuple-element.268), channel_id=1, source_target_pairs={{0,2},{1,3},{2,4},{3,5},{4,6},{5,7},{6,0},{7,1},{8,10},{9,11},{10,... | collective-permute-start | bytes 786440 | tf_op jit(solution)/shard_map/ppermute | solution.py:557
  160.1 1.7 collective-permute-start.39
  161.8 1.7 collective-permute-done.40.refs_6_
  163.6 6.7 %update.8.refs_8_ = bf16[8192,1024]{1,0:T(8,128)(2,1)} custom-call(s32[8,46]{1,0:T(8,128)S(1)} %copy-done.6, s32[32,4]{1,0:T(8,128)S(1)} %copy.53.mask, s32[1]{0:T(128)} %bitcast.1.me, bf16[512,1024]{1,0:T(8,128)(2,1)S(1)} %get-tuple-element.257.own, bf16[8192,1024]{1,0:T(8,128)(2,1)} %bitcast.17, ...), custom_call_target="tpu_custom_call", output_to_operand_aliasing={{}: (13, {})} | custom-call | flops 2147483648 | bytes 8388608 | tf_op jit(solution)/shard_map/update/pallas_call | solution.py:404
  170.3 1.4 collective-permute-start.42
  171.7 6.6 %update.9.refs_10_ = bf16[8192,1024]{1,0:T(8,128)(2,1)} custom-call(s32[8,46]{1,0:T(8,128)S(1)} %copy-done.6, s32[32,4]{1,0:T(8,128)S(1)} %copy.53.mask, s32[1]{0:T(128)} %bitcast.1.me, bf16[512,1024]{1,0:T(8,128)(2,1)S(1)} %get-tuple-element.257.own, bf16[8192,1024]{1,0:T(8,128)(2,1)} %bitcast.18, ...), custom_call_target="tpu_custom_call", output_to_operand_aliasing={{}: (13, {})} | custom-call | flops 2147483648 | bytes 8388608 | tf_op jit(solution)/shard_map/update/pallas_call | solution.py:404
  179.2 6.4 %update.10.refs_2_ = bf16[8192,1024]{1,0:T(8,128)(2,1)} custom-call(s32[8,46]{1,0:T(8,128)S(1)} %copy-done.6, s32[32,4]{1,0:T(8,128)S(1)} %copy.53.mask, s32[1]{0:T(128)} %bitcast.1.me, bf16[512,1024]{1,0:T(8,128)(2,1)S(1)} %get-tuple-element.257.own, bf16[8192,1024]{1,0:T(8,128)(2,1)} %bitcast.19, ...), custom_call_target="tpu_custom_call", output_to_operand_aliasing={{}: (15, {})} | custom-call | flops 2684354560 | bytes 10485760 | tf_op jit(solution)/shard_map/update/pallas_call | solution.py:404
  185.9 1.7 sum_parents.1
  188.3 1.0 update.11
  (167 shorter events, 12.6 us)
Async XLA Ops:
  5.2 26.1 %copy-start.4 = (bf16[256,512]{1,0:T(8,128)(2,1)}, bf16[256,512]{1,0:T(8,128)(2,1)S(1)}, u32[]{:S(2)}) copy-start(bf16[256,512]{1,0:T(8,128)(2,1)S(1)} %get-tuple-element.148.refs_18_) | copy-start | bytes 786436
  5.2 12.2 %collective-permute-start = (bf16[256,512]{1,0:T(8,128)(2,1)S(1)}, bf16[256,512]{1,0:T(8,128)(2,1)S(1)}, u32[]{:S(2)}, u32[]{:S(2)}) collective-permute-start(bf16[256,512]{1,0:T(8,128)(2,1)S(1)} %get-tuple-element.148.refs_18_), channel_id=1, source_target_pairs={{0,2},{1,3},{2,4},{3,5},{4,6},{5,7},{6,0},{7,1},{8,10},{9,11},{10,... | collective-permute-start | bytes 786440 | tf_op jit(solution)/shard_map/ppermute | solution.py:557
  8.3 9.2 %collective-permute-start.1 = (bf16[256,512]{1,0:T(8,128)(2,1)S(1)}, bf16[256,512]{1,0:T(8,128)(2,1)S(1)}, u32[]{:S(2)}, u32[]{:S(2)}) collective-permute-start(bf16[256,512]{1,0:T(8,128)(2,1)S(1)} %get-tuple-element.149), channel_id=1, source_target_pairs={{0,1},{1,0},{2,3},{3,2},{4,5},{5,4},{6,7},{7,6},{8,9},{9,8},{10,11... | collective-permute-start | bytes 786440 | tf_op jit(solution)/shard_map/ppermute | solution.py:557
  9.8 13.3 %collective-permute-start.4 = (bf16[256,512]{1,0:T(8,128)(2,1)S(1)}, bf16[256,512]{1,0:T(8,128)(2,1)S(1)}, u32[]{:S(2)}, u32[]{:S(2)}) collective-permute-start(bf16[256,512]{1,0:T(8,128)(2,1)S(1)} %get-tuple-element.150), channel_id=1, source_target_pairs={{0,2},{1,3},{2,4},{3,5},{4,6},{5,7},{6,0},{7,1},{8,10},{9,11},{10,... | collective-permute-start | bytes 786440 | tf_op jit(solution)/shard_map/ppermute | solution.py:557
  11.4 11.8 %collective-permute-start.5 = (bf16[256,512]{1,0:T(8,128)(2,1)S(1)}, bf16[256,512]{1,0:T(8,128)(2,1)S(1)}, u32[]{:S(2)}, u32[]{:S(2)}) collective-permute-start(bf16[256,512]{1,0:T(8,128)(2,1)S(1)} %get-tuple-element.151), channel_id=1, source_target_pairs={{0,1},{1,0},{2,3},{3,2},{4,5},{5,4},{6,7},{7,6},{8,9},{9,8},{10,11... | collective-permute-start | bytes 786440 | tf_op jit(solution)/shard_map/ppermute | solution.py:557
  17.4 36.9 %copy-start.8 = (bf16[256,512]{1,0:T(8,128)(2,1)}, bf16[256,512]{1,0:T(8,128)(2,1)S(1)}, u32[]{:S(2)}) copy-start(bf16[256,512]{1,0:T(8,128)(2,1)S(1)} %collective-permute-done.refs_19_.refs_0_) | copy-start | bytes 786436
  17.6 13.7 %collective-permute-start.2 = (bf16[256,512]{1,0:T(8,128)(2,1)S(1)}, bf16[256,512]{1,0:T(8,128)(2,1)S(1)}, u32[]{:S(2)}, u32[]{:S(2)}) collective-permute-start(bf16[256,512]{1,0:T(8,128)(2,1)S(1)} %get-tuple-element.158), channel_id=1, source_target_pairs={{0,2},{1,3},{2,4},{3,5},{4,6},{5,7},{6,0},{7,1},{8,10},{9,11},{10,... | collective-permute-start | bytes 786440 | tf_op jit(solution)/shard_map/ppermute | solution.py:557
  19.2 12.1 %collective-permute-start.3 = (bf16[256,512]{1,0:T(8,128)(2,1)S(1)}, bf16[256,512]{1,0:T(8,128)(2,1)S(1)}, u32[]{:S(2)}, u32[]{:S(2)}) collective-permute-start(bf16[256,512]{1,0:T(8,128)(2,1)S(1)} %get-tuple-element.159), channel_id=1, source_target_pairs={{0,1},{1,0},{2,3},{3,2},{4,5},{5,4},{6,7},{7,6},{8,9},{9,8},{10,11... | collective-permute-start | bytes 786440 | tf_op jit(solution)/shard_map/ppermute | solution.py:557
  23.0 31.3 %copy-start.28 = (bf16[256,512]{1,0:T(8,128)(2,1)}, bf16[256,512]{1,0:T(8,128)(2,1)S(1)}, u32[]{:S(2)}) copy-start(bf16[256,512]{1,0:T(8,128)(2,1)S(1)} %collective-permute-done.4.refs_2_) | copy-start | bytes 786436
  23.1 31.2 %copy-start.29 = (bf16[256,512]{1,0:T(8,128)(2,1)}, bf16[256,512]{1,0:T(8,128)(2,1)S(1)}, u32[]{:S(2)}) copy-start(bf16[256,512]{1,0:T(8,128)(2,1)S(1)} %collective-permute-done.5.refs_3_) | copy-start | bytes 786436
  23.2 11.1 %collective-permute-start.8 = (bf16[256,512]{1,0:T(8,128)(2,1)S(1)}, bf16[256,512]{1,0:T(8,128)(2,1)S(1)}, u32[]{:S(2)}, u32[]{:S(2)}) collective-permute-start(bf16[256,512]{1,0:T(8,128)(2,1)S(1)} %get-tuple-element.168), channel_id=1, source_target_pairs={{0,2},{1,3},{2,4},{3,5},{4,6},{5,7},{6,0},{7,1},{8,10},{9,11},{10,... | collective-permute-start | bytes 786440 | tf_op jit(solution)/shard_map/ppermute | solution.py:557
  24.8 9.5 %collective-permute-start.9 = (bf16[256,512]{1,0:T(8,128)(2,1)S(1)}, bf16[256,512]{1,0:T(8,128)(2,1)S(1)}, u32[]{:S(2)}, u32[]{:S(2)}) collective-permute-start(bf16[256,512]{1,0:T(8,128)(2,1)S(1)} %get-tuple-element.169), channel_id=1, source_target_pairs={{0,1},{1,0},{2,3},{3,2},{4,5},{5,4},{6,7},{7,6},{8,9},{9,8},{10,11... | collective-permute-start | bytes 786440 | tf_op jit(solution)/shard_map/ppermute | solution.py:557
  31.3 47.9 %copy-start.11 = (bf16[256,512]{1,0:T(8,128)(2,1)}, bf16[256,512]{1,0:T(8,128)(2,1)S(1)}, u32[]{:S(2)}) copy-start(bf16[256,512]{1,0:T(8,128)(2,1)S(1)} %collective-permute-done.2.refs_21_.refs_4_) | copy-start | bytes 786436
  31.3 47.9 %copy-start.12 = (bf16[256,512]{1,0:T(8,128)(2,1)}, bf16[256,512]{1,0:T(8,128)(2,1)S(1)}, u32[]{:S(2)}) copy-start(bf16[256,512]{1,0:T(8,128)(2,1)S(1)} %collective-permute-done.3.refs_20_.refs_5_) | copy-start | bytes 786436
  31.4 10.7 %collective-permute-start.6 = (bf16[256,512]{1,0:T(8,128)(2,1)S(1)}, bf16[256,512]{1,0:T(8,128)(2,1)S(1)}, u32[]{:S(2)}, u32[]{:S(2)}) collective-permute-start(bf16[256,512]{1,0:T(8,128)(2,1)S(1)} %get-tuple-element.173), channel_id=1, source_target_pairs={{0,2},{1,3},{2,4},{3,5},{4,6},{5,7},{6,0},{7,1},{8,10},{9,11},{10,... | collective-permute-start | bytes 786440 | tf_op jit(solution)/shard_map/ppermute | solution.py:557
  33.1 9.1 %collective-permute-start.7 = (bf16[256,512]{1,0:T(8,128)(2,1)S(1)}, bf16[256,512]{1,0:T(8,128)(2,1)S(1)}, u32[]{:S(2)}, u32[]{:S(2)}) collective-permute-start(bf16[256,512]{1,0:T(8,128)(2,1)S(1)} %get-tuple-element.174), channel_id=1, source_target_pairs={{0,1},{1,0},{2,3},{3,2},{4,5},{5,4},{6,7},{7,6},{8,9},{9,8},{10,11... | collective-permute-start | bytes 786440 | tf_op jit(solution)/shard_map/ppermute | solution.py:557
  34.3 31.4 %copy-start.32 = (bf16[256,512]{1,0:T(8,128)(2,1)}, bf16[256,512]{1,0:T(8,128)(2,1)S(1)}, u32[]{:S(2)}) copy-start(bf16[256,512]{1,0:T(8,128)(2,1)S(1)} %collective-permute-done.8.refs_6_) | copy-start | bytes 786436
  34.3 31.4 %copy-start.33 = (bf16[256,512]{1,0:T(8,128)(2,1)}, bf16[256,512]{1,0:T(8,128)(2,1)S(1)}, u32[]{:S(2)}) copy-start(bf16[256,512]{1,0:T(8,128)(2,1)S(1)} %collective-permute-done.9.refs_7_) | copy-start | bytes 786436
  34.4 13.4 %collective-permute-start.12 = (bf16[256,512]{1,0:T(8,128)(2,1)S(1)}, bf16[256,512]{1,0:T(8,128)(2,1)S(1)}, u32[]{:S(2)}, u32[]{:S(2)}) collective-permute-start(bf16[256,512]{1,0:T(8,128)(2,1)S(1)} %get-tuple-element.179), channel_id=1, source_target_pairs={{0,2},{1,3},{2,4},{3,5},{4,6},{5,7},{6,0},{7,1},{8,10},{9,11},{10,... | collective-permute-start | bytes 786440 | tf_op jit(solution)/shard_map/ppermute | solution.py:557
  36.0 11.7 %collective-permute-start.13 = (bf16[256,512]{1,0:T(8,128)(2,1)S(1)}, bf16[256,512]{1,0:T(8,128)(2,1)S(1)}, u32[]{:S(2)}, u32[]{:S(2)}) collective-permute-start(bf16[256,512]{1,0:T(8,128)(2,1)S(1)} %get-tuple-element.180), channel_id=1, source_target_pairs={{0,1},{1,0},{2,3},{3,2},{4,5},{5,4},{6,7},{7,6},{8,9},{9,8},{10,11... | collective-permute-start | bytes 786440 | tf_op jit(solution)/shard_map/ppermute | solution.py:557
  42.2 37.1 %copy-start.9 = (bf16[256,512]{1,0:T(8,128)(2,1)}, bf16[256,512]{1,0:T(8,128)(2,1)S(1)}, u32[]{:S(2)}) copy-start(bf16[256,512]{1,0:T(8,128)(2,1)S(1)} %collective-permute-done.6.refs_23_.refs_0_) | copy-start | bytes 786436
  42.2 37.1 %copy-start.10 = (bf16[256,512]{1,0:T(8,128)(2,1)}, bf16[256,512]{1,0:T(8,128)(2,1)S(1)}, u32[]{:S(2)}) copy-start(bf16[256,512]{1,0:T(8,128)(2,1)S(1)} %collective-permute-done.7.refs_22_.refs_1_) | copy-start | bytes 786436
  42.2 12.1 %collective-permute-start.10 = (bf16[256,512]{1,0:T(8,128)(2,1)S(1)}, bf16[256,512]{1,0:T(8,128)(2,1)S(1)}, u32[]{:S(2)}, u32[]{:S(2)}) collective-permute-start(bf16[256,512]{1,0:T(8,128)(2,1)S(1)} %get-tuple-element.184), channel_id=1, source_target_pairs={{0,2},{1,3},{2,4},{3,5},{4,6},{5,7},{6,0},{7,1},{8,10},{9,11},{10,... | collective-permute-start | bytes 786440 | tf_op jit(solution)/shard_map/ppermute | solution.py:557
  42.6 11.8 %collective-permute-start.11 = (bf16[256,512]{1,0:T(8,128)(2,1)S(1)}, bf16[256,512]{1,0:T(8,128)(2,1)S(1)}, u32[]{:S(2)}, u32[]{:S(2)}) collective-permute-start(bf16[256,512]{1,0:T(8,128)(2,1)S(1)} %get-tuple-element.185), channel_id=1, source_target_pairs={{0,1},{1,0},{2,3},{3,2},{4,5},{5,4},{6,7},{7,6},{8,9},{9,8},{10,11... | collective-permute-start | bytes 786440 | tf_op jit(solution)/shard_map/ppermute | solution.py:557
  48.6 9.3 %collective-permute-start.16 = (bf16[256,512]{1,0:T(8,128)(2,1)S(1)}, bf16[256,512]{1,0:T(8,128)(2,1)S(1)}, u32[]{:S(2)}, u32[]{:S(2)}) collective-permute-start(bf16[256,512]{1,0:T(8,128)(2,1)S(1)} %get-tuple-element.194), channel_id=1, source_target_pairs={{0,2},{1,3},{2,4},{3,5},{4,6},{5,7},{6,0},{7,1},{8,10},{9,11},{10,... | collective-permute-start | bytes 786440 | tf_op jit(solution)/shard_map/ppermute | solution.py:557
  48.8 9.0 %collective-permute-start.17 = (bf16[256,512]{1,0:T(8,128)(2,1)S(1)}, bf16[256,512]{1,0:T(8,128)(2,1)S(1)}, u32[]{:S(2)}, u32[]{:S(2)}) collective-permute-start(bf16[256,512]{1,0:T(8,128)(2,1)S(1)} %get-tuple-element.195), channel_id=1, source_target_pairs={{0,1},{1,0},{2,3},{3,2},{4,5},{5,4},{6,7},{7,6},{8,9},{9,8},{10,11... | collective-permute-start | bytes 786440 | tf_op jit(solution)/shard_map/ppermute | solution.py:557
  54.4 43.6 %copy-start.7 = (s32[1,1,4]{2,1,0:T(1,128)S(1)}, s32[1,1,4]{2,1,0:T(1,128)}, u32[]{:S(2)}) copy-start(s32[1,1,4]{2,1,0:T(1,128)} %param.8) | copy-start | bytes 52
  54.4 43.4 %copy-start.13 = (bf16[256,512]{1,0:T(8,128)(2,1)}, bf16[256,512]{1,0:T(8,128)(2,1)S(1)}, u32[]{:S(2)}) copy-start(bf16[256,512]{1,0:T(8,128)(2,1)S(1)} %collective-permute-done.10.refs_4_) | copy-start | bytes 786436
  54.4 43.4 %copy-start.14 = (bf16[256,512]{1,0:T(8,128)(2,1)}, bf16[256,512]{1,0:T(8,128)(2,1)S(1)}, u32[]{:S(2)}) copy-start(bf16[256,512]{1,0:T(8,128)(2,1)S(1)} %collective-permute-done.11.refs_17_.refs_5_) | copy-start | bytes 786436
  54.5 11.1 %collective-permute-start.14 = (bf16[256,512]{1,0:T(8,128)(2,1)S(1)}, bf16[256,512]{1,0:T(8,128)(2,1)S(1)}, u32[]{:S(2)}, u32[]{:S(2)}) collective-permute-start(bf16[256,512]{1,0:T(8,128)(2,1)S(1)} %get-tuple-element.199), channel_id=1, source_target_pairs={{0,2},{1,3},{2,4},{3,5},{4,6},{5,7},{6,0},{7,1},{8,10},{9,11},{10,... | collective-permute-start | bytes 786440 | tf_op jit(solution)/shard_map/ppermute | solution.py:557
  56.1 9.5 %collective-permute-start.15 = (bf16[256,512]{1,0:T(8,128)(2,1)S(1)}, bf16[256,512]{1,0:T(8,128)(2,1)S(1)}, u32[]{:S(2)}, u32[]{:S(2)}) collective-permute-start(bf16[256,512]{1,0:T(8,128)(2,1)S(1)} %get-tuple-element.200), channel_id=1, source_target_pairs={{0,1},{1,0},{2,3},{3,2},{4,5},{5,4},{6,7},{7,6},{8,9},{9,8},{10,11... | collective-permute-start | bytes 786440 | tf_op jit(solution)/shard_map/ppermute | solution.py:557
  57.8 40.0 %copy-start.16 = (bf16[256,512]{1,0:T(8,128)(2,1)}, bf16[256,512]{1,0:T(8,128)(2,1)S(1)}, u32[]{:S(2)}) copy-start(bf16[256,512]{1,0:T(8,128)(2,1)S(1)} %collective-permute-done.16.refs_9_.refs_6_) | copy-start | bytes 786436
  57.8 40.0 %copy-start.17 = (bf16[256,512]{1,0:T(8,128)(2,1)}, bf16[256,512]{1,0:T(8,128)(2,1)S(1)}, u32[]{:S(2)}) copy-start(bf16[256,512]{1,0:T(8,128)(2,1)S(1)} %collective-permute-done.17.refs_10_.refs_7_) | copy-start | bytes 786436
  57.9 13.3 %collective-permute-start.20 = (bf16[256,512]{1,0:T(8,128)(2,1)S(1)}, bf16[256,512]{1,0:T(8,128)(2,1)S(1)}, u32[]{:S(2)}, u32[]{:S(2)}) collective-permute-start(bf16[256,512]{1,0:T(8,128)(2,1)S(1)} %get-tuple-element.205), channel_id=1, source_target_pairs={{0,2},{1,3},{2,4},{3,5},{4,6},{5,7},{6,0},{7,1},{8,10},{9,11},{10,... | collective-permute-start | bytes 786440 | tf_op jit(solution)/shard_map/ppermute | solution.py:557
  59.2 12.0 %collective-permute-start.21 = (bf16[256,512]{1,0:T(8,128)(2,1)S(1)}, bf16[256,512]{1,0:T(8,128)(2,1)S(1)}, u32[]{:S(2)}, u32[]{:S(2)}) collective-permute-start(bf16[256,512]{1,0:T(8,128)(2,1)S(1)} %get-tuple-element.206), channel_id=1, source_target_pairs={{0,1},{1,0},{2,3},{3,2},{4,5},{5,4},{6,7},{7,6},{8,9},{9,8},{10,11... | collective-permute-start | bytes 786440 | tf_op jit(solution)/shard_map/ppermute | solution.py:557
  65.6 32.2 %copy-start.15 = (bf16[256,512]{1,0:T(8,128)(2,1)}, bf16[256,512]{1,0:T(8,128)(2,1)S(1)}, u32[]{:S(2)}) copy-start(bf16[256,512]{1,0:T(8,128)(2,1)S(1)} %collective-permute-done.14.refs_3_.refs_0_) | copy-start | bytes 786436
  65.7 13.6 %collective-permute-start.18 = (bf16[256,512]{1,0:T(8,128)(2,1)S(1)}, bf16[256,512]{1,0:T(8,128)(2,1)S(1)}, u32[]{:S(2)}, u32[]{:S(2)}) collective-permute-start(bf16[256,512]{1,0:T(8,128)(2,1)S(1)} %get-tuple-element.210), channel_id=1, source_target_pairs={{0,2},{1,3},{2,4},{3,5},{4,6},{5,7},{6,0},{7,1},{8,10},{9,11},{10,... | collective-permute-start | bytes 786440 | tf_op jit(solution)/shard_map/ppermute | solution.py:557
  66.6 12.7 %collective-permute-start.19 = (bf16[256,512]{1,0:T(8,128)(2,1)S(1)}, bf16[256,512]{1,0:T(8,128)(2,1)S(1)}, u32[]{:S(2)}, u32[]{:S(2)}) collective-permute-start(bf16[256,512]{1,0:T(8,128)(2,1)S(1)} %get-tuple-element.211), channel_id=1, source_target_pairs={{0,1},{1,0},{2,3},{3,2},{4,5},{5,4},{6,7},{7,6},{8,9},{9,8},{10,11... | collective-permute-start | bytes 786440 | tf_op jit(solution)/shard_map/ppermute | solution.py:557
  71.2 26.6 %copy-start.18 = (bf16[256,512]{1,0:T(8,128)(2,1)}, bf16[256,512]{1,0:T(8,128)(2,1)S(1)}, u32[]{:S(2)}) copy-start(bf16[256,512]{1,0:T(8,128)(2,1)S(1)} %collective-permute-done.20.refs_8_.refs_2_) | copy-start | bytes 786436
  71.3 11.3 %collective-permute-start.22 = (bf16[256,512]{1,0:T(8,128)(2,1)S(1)}, bf16[256,512]{1,0:T(8,128)(2,1)S(1)}, u32[]{:S(2)}, u32[]{:S(2)}) collective-permute-start(bf16[256,512]{1,0:T(8,128)(2,1)S(1)} %get-tuple-element.219), channel_id=1, source_target_pairs={{0,2},{1,3},{2,4},{3,5},{4,6},{5,7},{6,0},{7,1},{8,10},{9,11},{10,... | collective-permute-start | bytes 786440 | tf_op jit(solution)/shard_map/ppermute | solution.py:557
  72.4 10.2 %collective-permute-start.23 = (bf16[256,512]{1,0:T(8,128)(2,1)S(1)}, bf16[256,512]{1,0:T(8,128)(2,1)S(1)}, u32[]{:S(2)}, u32[]{:S(2)}) collective-permute-start(bf16[256,512]{1,0:T(8,128)(2,1)S(1)} %get-tuple-element.220), channel_id=1, source_target_pairs={{0,1},{1,0},{2,3},{3,2},{4,5},{5,4},{6,7},{7,6},{8,9},{9,8},{10,11... | collective-permute-start | bytes 786440 | tf_op jit(solution)/shard_map/ppermute | solution.py:557
  79.3 33.2 %copy-start.6 = (s32[8,46]{1,0:T(8,128)S(1)}, s32[8,46]{1,0:T(8,128)}, u32[]{:S(2)}) copy-start(s32[8,46]{1,0:T(8,128)} %constant.14.clone.table) | copy-start | bytes 4420
  79.4 9.7 %collective-permute-start.24 = (bf16[256,512]{1,0:T(8,128)(2,1)S(1)}, bf16[256,512]{1,0:T(8,128)(2,1)S(1)}, u32[]{:S(2)}, u32[]{:S(2)}) collective-permute-start(bf16[256,512]{1,0:T(8,128)(2,1)S(1)} %get-tuple-element.226), channel_id=1, source_target_pairs={{0,2},{1,3},{2,4},{3,5},{4,6},{5,7},{6,0},{7,1},{8,10},{9,11},{10,... | collective-permute-start | bytes 786440 | tf_op jit(solution)/shard_map/ppermute | solution.py:557
  81.1 9.2 %collective-permute-start.25 = (bf16[256,512]{1,0:T(8,128)(2,1)S(1)}, bf16[256,512]{1,0:T(8,128)(2,1)S(1)}, u32[]{:S(2)}, u32[]{:S(2)}) collective-permute-start(bf16[256,512]{1,0:T(8,128)(2,1)S(1)} %get-tuple-element.227), channel_id=1, source_target_pairs={{0,1},{1,0},{2,3},{3,2},{4,5},{5,4},{6,7},{7,6},{8,9},{9,8},{10,11... | collective-permute-start | bytes 786440 | tf_op jit(solution)/shard_map/ppermute | solution.py:557
  82.7 12.1 %collective-permute-start.26 = (bf16[256,512]{1,0:T(8,128)(2,1)S(1)}, bf16[256,512]{1,0:T(8,128)(2,1)S(1)}, u32[]{:S(2)}, u32[]{:S(2)}) collective-permute-start(bf16[256,512]{1,0:T(8,128)(2,1)S(1)} %get-tuple-element.233), channel_id=1, source_target_pairs={{0,2},{1,3},{2,4},{3,5},{4,6},{5,7},{6,0},{7,1},{8,10},{9,11},{10,... | collective-permute-start | bytes 786440 | tf_op jit(solution)/shard_map/ppermute | solution.py:557
  83.8 11.8 %collective-permute-start.27 = (bf16[256,512]{1,0:T(8,128)(2,1)S(1)}, bf16[256,512]{1,0:T(8,128)(2,1)S(1)}, u32[]{:S(2)}, u32[]{:S(2)}) collective-permute-start(bf16[256,512]{1,0:T(8,128)(2,1)S(1)} %get-tuple-element.234), channel_id=1, source_target_pairs={{0,1},{1,0},{2,3},{3,2},{4,5},{5,4},{6,7},{7,6},{8,9},{9,8},{10,11... | collective-permute-start | bytes 786440 | tf_op jit(solution)/shard_map/ppermute | solution.py:557
  90.4 11.5 %collective-permute-start.28 = (bf16[256,512]{1,0:T(8,128)(2,1)S(1)}, bf16[256,512]{1,0:T(8,128)(2,1)S(1)}, u32[]{:S(2)}, u32[]{:S(2)}) collective-permute-start(bf16[256,512]{1,0:T(8,128)(2,1)S(1)} %get-tuple-element.238), channel_id=1, source_target_pairs={{0,2},{1,3},{2,4},{3,5},{4,6},{5,7},{6,0},{7,1},{8,10},{9,11},{10,... | collective-permute-start | bytes 786440 | tf_op jit(solution)/shard_map/ppermute | solution.py:557
  90.5 11.5 %collective-permute-start.29 = (bf16[256,512]{1,0:T(8,128)(2,1)S(1)}, bf16[256,512]{1,0:T(8,128)(2,1)S(1)}, u32[]{:S(2)}, u32[]{:S(2)}) collective-permute-start(bf16[256,512]{1,0:T(8,128)(2,1)S(1)} %get-tuple-element.239), channel_id=1, source_target_pairs={{0,1},{1,0},{2,3},{3,2},{4,5},{5,4},{6,7},{7,6},{8,9},{9,8},{10,11... | collective-permute-start | bytes 786440 | tf_op jit(solution)/shard_map/ppermute | solution.py:557
  96.5 12.8 %collective-permute-start.32 = (bf16[256,512]{1,0:T(8,128)(2,1)}, bf16[256,512]{1,0:T(8,128)(2,1)}, u32[]{:S(2)}, u32[]{:S(2)}) collective-permute-start(bf16[256,512]{1,0:T(8,128)(2,1)} %get-tuple-element.243), channel_id=1, source_target_pairs={{0,2},{1,3},{2,4},{3,5},{4,6},{5,7},{6,0},{7,1},{8,10},{9,11},{10,... | collective-permute-start | bytes 786440 | tf_op jit(solution)/shard_map/ppermute | solution.py:557
  96.8 12.6 %collective-permute-start.33 = (bf16[256,512]{1,0:T(8,128)(2,1)}, bf16[256,512]{1,0:T(8,128)(2,1)}, u32[]{:S(2)}, u32[]{:S(2)}) collective-permute-start(bf16[256,512]{1,0:T(8,128)(2,1)} %get-tuple-element.244), channel_id=1, source_target_pairs={{0,1},{1,0},{2,3},{3,2},{4,5},{5,4},{6,7},{7,6},{8,9},{9,8},{10,11... | collective-permute-start | bytes 786440 | tf_op jit(solution)/shard_map/ppermute | solution.py:557
  103.0 18.3 %all-to-all-start = ((bf16[4,528,256]{2,1,0:T(8,128)(2,1)}), bf16[4,528,256]{2,1,0:T(8,128)(2,1)S(1)}, u32[]{:S(2)}, u32[]{:S(2)}) async-start(bf16[4,528,256]{2,1,0:T(8,128)(2,1)} %get-tuple-element.249), calls=%async_computation | async-start | bytes 2162688 | tf_op jit(solution)/shard_map/all_to_all | solution.py:528
  106.5 11.2 %collective-permute-start.30 = (bf16[256,512]{1,0:T(8,128)(2,1)}, bf16[256,512]{1,0:T(8,128)(2,1)S(1)}, u32[]{:S(2)}, u32[]{:S(2)}) collective-permute-start(bf16[256,512]{1,0:T(8,128)(2,1)} %get-tuple-element.247), channel_id=1, source_target_pairs={{0,2},{1,3},{2,4},{3,5},{4,6},{5,7},{6,0},{7,1},{8,10},{9,11},{10,... | collective-permute-start | bytes 786440 | tf_op jit(solution)/shard_map/ppermute | solution.py:557
  108.3 9.4 %collective-permute-start.31 = (bf16[256,512]{1,0:T(8,128)(2,1)}, bf16[256,512]{1,0:T(8,128)(2,1)S(1)}, u32[]{:S(2)}, u32[]{:S(2)}) collective-permute-start(bf16[256,512]{1,0:T(8,128)(2,1)} %get-tuple-element.248), channel_id=1, source_target_pairs={{0,1},{1,0},{2,3},{3,2},{4,5},{5,4},{6,7},{7,6},{8,9},{9,8},{10,11... | collective-permute-start | bytes 786440 | tf_op jit(solution)/shard_map/ppermute | solution.py:557
  111.2 21.0 %collective-permute-start.36 = (bf16[256,512]{1,0:T(8,128)(2,1)}, bf16[256,512]{1,0:T(8,128)(2,1)S(1)}, u32[]{:S(2)}, u32[]{:S(2)}) collective-permute-start(bf16[256,512]{1,0:T(8,128)(2,1)} %get-tuple-element.252), channel_id=1, source_target_pairs={{0,2},{1,3},{2,4},{3,5},{4,6},{5,7},{6,0},{7,1},{8,10},{9,11},{10,... | collective-permute-start | bytes 786440 | tf_op jit(solution)/shard_map/ppermute | solution.py:557
  111.7 20.5 %collective-permute-start.37 = (bf16[256,512]{1,0:T(8,128)(2,1)S(1)}, bf16[256,512]{1,0:T(8,128)(2,1)S(1)}, u32[]{:S(2)}, u32[]{:S(2)}) collective-permute-start(bf16[256,512]{1,0:T(8,128)(2,1)S(1)} %get-tuple-element.253), channel_id=1, source_target_pairs={{0,1},{1,0},{2,3},{3,2},{4,5},{5,4},{6,7},{7,6},{8,9},{9,8},{10,11... | collective-permute-start | bytes 786440 | tf_op jit(solution)/shard_map/ppermute | solution.py:557
  123.2 62.4 %all-to-all-start.1 = ((bf16[8,272,256]{2,1,0:T(8,128)(2,1)}), bf16[8,272,256]{2,1,0:T(8,128)(2,1)S(1)}, u32[]{:S(2)}, u32[]{:S(2)}) async-start(bf16[8,272,256]{2,1,0:T(8,128)(2,1)} %relay.1), calls=%async_computation.1 | async-start | bytes 2228224 | tf_op jit(solution)/shard_map/all_to_all | solution.py:528
  128.7 29.2 %collective-permute-start.34 = (bf16[256,512]{1,0:T(8,128)(2,1)}, bf16[256,512]{1,0:T(8,128)(2,1)S(1)}, u32[]{:S(2)}, u32[]{:S(2)}) collective-permute-start(bf16[256,512]{1,0:T(8,128)(2,1)} %get-tuple-element.258), channel_id=1, source_target_pairs={{0,2},{1,3},{2,4},{3,5},{4,6},{5,7},{6,0},{7,1},{8,10},{9,11},{10,... | collective-permute-start | bytes 786440 | tf_op jit(solution)/shard_map/ppermute | solution.py:557
  130.8 27.1 %collective-permute-start.35 = (bf16[256,512]{1,0:T(8,128)(2,1)}, bf16[256,512]{1,0:T(8,128)(2,1)S(1)}, u32[]{:S(2)}, u32[]{:S(2)}) collective-permute-start(bf16[256,512]{1,0:T(8,128)(2,1)} %get-tuple-element.259), channel_id=1, source_target_pairs={{0,1},{1,0},{2,3},{3,2},{4,5},{5,4},{6,7},{7,6},{8,9},{9,8},{10,11... | collective-permute-start | bytes 786440 | tf_op jit(solution)/shard_map/ppermute | solution.py:557
  132.3 31.2 %collective-permute-start.40 = (bf16[256,512]{1,0:T(8,128)(2,1)S(1)}, bf16[256,512]{1,0:T(8,128)(2,1)S(1)}, u32[]{:S(2)}, u32[]{:S(2)}) collective-permute-start(bf16[256,512]{1,0:T(8,128)(2,1)S(1)} %get-tuple-element.263), channel_id=1, source_target_pairs={{0,2},{1,3},{2,4},{3,5},{4,6},{5,7},{6,0},{7,1},{8,10},{9,11},{10,... | collective-permute-start | bytes 786440 | tf_op jit(solution)/shard_map/ppermute | solution.py:557
  133.8 29.7 %collective-permute-start.41 = (bf16[256,512]{1,0:T(8,128)(2,1)S(1)}, bf16[256,512]{1,0:T(8,128)(2,1)S(1)}, u32[]{:S(2)}, u32[]{:S(2)}) collective-permute-start(bf16[256,512]{1,0:T(8,128)(2,1)S(1)} %get-tuple-element.264), channel_id=1, source_target_pairs={{0,1},{1,0},{2,3},{3,2},{4,5},{5,4},{6,7},{7,6},{8,9},{9,8},{10,11... | collective-permute-start | bytes 786440 | tf_op jit(solution)/shard_map/ppermute | solution.py:557
  158.0 20.4 %collective-permute-start.38 = (bf16[256,512]{1,0:T(8,128)(2,1)S(1)}, bf16[256,512]{1,0:T(8,128)(2,1)S(1)}, u32[]{:S(2)}, u32[]{:S(2)}) collective-permute-start(bf16[256,512]{1,0:T(8,128)(2,1)S(1)} %get-tuple-element.268), channel_id=1, source_target_pairs={{0,2},{1,3},{2,4},{3,5},{4,6},{5,7},{6,0},{7,1},{8,10},{9,11},{10,... | collective-permute-start | bytes 786440 | tf_op jit(solution)/shard_map/ppermute | solution.py:557
  160.1 18.3 %collective-permute-start.39 = (bf16[256,512]{1,0:T(8,128)(2,1)S(1)}, bf16[256,512]{1,0:T(8,128)(2,1)S(1)}, u32[]{:S(2)}, u32[]{:S(2)}) collective-permute-start(bf16[256,512]{1,0:T(8,128)(2,1)S(1)} %get-tuple-element.269), channel_id=1, source_target_pairs={{0,1},{1,0},{2,3},{3,2},{4,5},{5,4},{6,7},{7,6},{8,9},{9,8},{10,11... | collective-permute-start | bytes 786440 | tf_op jit(solution)/shard_map/ppermute | solution.py:557
  170.3 17.3 %collective-permute-start.42 = (bf16[256,512]{1,0:T(8,128)(2,1)S(1)}, bf16[256,512]{1,0:T(8,128)(2,1)S(1)}, u32[]{:S(2)}, u32[]{:S(2)}) collective-permute-start(bf16[256,512]{1,0:T(8,128)(2,1)S(1)} %broadcast_select_fusion.1), channel_id=1, source_target_pairs={{0,1},{1,0},{2,3},{3,2},{4,5},{5,4},{6,7},{7,6},{8,9},{9,8},{10,11... | collective-permute-start | bytes 786440 | tf_op jit(solution)/shard_map/ppermute | solution.py:557
  178.4 9.1 %collective-permute-start.43 = (bf16[256,512]{1,0:T(8,128)(2,1)S(1)}, bf16[256,512]{1,0:T(8,128)(2,1)}, u32[]{:S(2)}, u32[]{:S(2)}) collective-permute-start(bf16[256,512]{1,0:T(8,128)(2,1)S(1)} %broadcast_select_fusion), channel_id=1, source_target_pairs={{0,1},{1,0},{2,3},{3,2},{4,5},{5,4},{6,7},{7,6},{8,9},{9,8},{10,11... | collective-permute-start | bytes 786440 | tf_op jit(solution)/shard_map/ppermute | solution.py:557
  (31 other events, 289.1 us)

commit v4 on v3

--- a/solution.py
+++ b/solution.py
@@ -9,7 +9,7 @@
 
 TILE = 256
 CHAINS = 2
-RELAY_AFTER = 3
+RELAY_AFTER = 6
 LABEL_ROWS = 16
 VMEM_LIMIT = 16 * 1024 * 1024
 UPDATE_LIMIT = 32 * 1024 * 1024
@@ -463,7 +463,7 @@
     order = [(e, lists[s][e]) for e in range(longest) for s in (0, 1) if e < len(lists[s])]
     order = [(e, tile) for n, (e, tile) in enumerate(order) if tile not in [other for _, other in order[:n]]]
     order.append((longest, 0))
-    cuts = [0, 4, 8] + list(range(16, len(order) - 2, 8)) + [len(order)]
+    cuts = list(range(0, len(order) - 2, 4)) + [len(order)]
     made, parts, where_made = [], None, {}
 
     def make(e, turn):
@@ -537,10 +537,11 @@
         nonlocal result, done
         numbers = [n for n in range(2 * done, 2 * (done + count)) if any(line[n] for line in table)]
         done += count
-        here = after((me,), *waits)[0]
+        here = after((me,), *waits)[0] if waits else me
         blocks = [held[n // 2][n % 2] for n in numbers]
         result = update(rows, mask, here, own, front, numbers, blocks, 2 * count, base=result)
 
+    relay_after = min(RELAY_AFTER, events - 1 - ready - CHAINS)
     for e in range(events):
         values = []
         for s in (0, 1):
@@ -563,16 +564,16 @@
             own, sends = own_part()
         if late == 1:
             arrived = exchange(after((sends,), *turn)[0], "front")
-        if late == RELAY_AFTER:
+        if late == relay_after:
             arrived = relayed(after((arrived,), *turn)[0])
-        if late >= 2 and late != RELAY_AFTER and e < events - 1:
-            step(min(4, e - CHAINS + 1 - done), *turn)
+        elif late >= 2 and late % 2 == 0 and e < events - 1:
+            step(min(8, e - CHAINS + 1 - done), *turn)
             turn = (*turn, result)
     while done < events - CHAINS:
-        step(min(6, events - CHAINS - done), *turn)
+        step(min(8, events - CHAINS - done), *turn)
+    step(CHAINS)
     slots_here = after((arrived,), result)[0]
     parent_tiles = sum_parents(slots_here[:, TILE, 0].astype(jnp.int32), slots_here, slots_dev)
-    step(CHAINS, parent_tiles)
     return (result[None], parent_tiles)
 
 

time: 190 us -> 184 us (0.968)
  waiting for transfers between devices: 56 us -> 50.5 us
  local copies, waits for them, and re-layouts: 2.67 us -> 5.3 us
  Pallas kernels: 60 us -> 57.6 us
  other arithmetic: 5.97 us -> 3.64 us
    pallas_call x6 -> x4, Pallas kernels: 31 us -> 25.4 us  [update(): pl.pallas_call(functools.partial(update_kernel, tuple(numbers), room, wid...]
    pallas_call x5 -> x8, Pallas kernels: 21.6 us -> 24.7 us  [factor(): pl.pallas_call(functools.partial(factor_kernel, tuple(tiles), head), out_...]
    select_n x17, other arithmetic: 5.57 us -> 2.55 us  [shards(): jnp.where(root, made[which][n], value)]
    ppermute x44, waiting for transfers between devices: 53.3 us -> 50.5 us  [shards(): lax.ppermute(turn[s], 'grp', perms[s])]
    all_to_all x2, waiting for transfers between devices: 2.67 us -> 0.01 us  [exchange(): return lax.all_to_all(blocks, axis, split_axis=0, concat_axis=0, tiled=True)]
    unnamed x98 -> x106, local copies, waits for them, and re-layouts: 1.72 us -> 4.35 us
    ppermute x44, starting transfers between devices: 54.2 us -> 56.2 us  [shards(): lax.ppermute(turn[s], 'grp', perms[s])]
  transfers between devices with their start and end apart: 46 -> 46, of which waited for: 18 -> 18; matrix products, arithmetic and copies ran while one was open for 3% -> 2% of each run, Pallas kernels for 29% -> 28%
where the time goes in v4:
time: 184 us; the launch traced here: 182 us
  starting transfers between devices  63.5 us (35%)
  Pallas kernels  57.6 us (31%)
  waiting for transfers between devices  50.5 us (27%)
  local copies, waits for them, and re-layouts  5.3 us (3%)
  other arithmetic  3.64 us (2%)
    ppermute x44, starting transfers between devices, shards(): lax.ppermute(turn[s], 'grp', perms[s])  56.2 us
    ppermute x44, waiting for transfers between devices, shards(): lax.ppermute(turn[s], 'grp', perms[s])  50.5 us
    pallas_call x4, Pallas kernels, update(): pl.pallas_call(functools.partial(update_kernel, tuple(numbers), room, wid...  25.4 us
    pallas_call x8, Pallas kernels, factor(): pl.pallas_call(functools.partial(factor_kernel, tuple(tiles), head), out_...  24.7 us
    all_to_all x2, starting transfers between devices, exchange(): return lax.all_to_all(blocks, axis, split_axis=0, concat_axis=0, tiled=True)  7.29 us
    unnamed x106, local copies, waits for them, and re-layouts  4.35 us
    pallas_call x1, Pallas kernels, own_panels(): pl.pallas_call(functools.partial(own_kernel, choices, len(blocks), width...  4 us
  transfers between devices with their start and end apart: 46, of which 18 were waited for; matrix products, arithmetic and copies ran while one was open for 2% of the time, Pallas kernels for 28%

profile of v4, /device:TPU:0, one launch (start us, length us, event | category | flops | bytes accessed | tf_op | source)
XLA Modules:
  0.0 182.0 jit_solution(5566587396901029031)
XLA Ops:
  1.4 3.8 %factor.8 = (bf16[256,512]{1,0:T(8,128)(2,1)S(1)}, bf16[256,512]{1,0:T(8,128)(2,1)S(1)}, bf16[256,512]{1,0:T(8,128)(2,1)S(1)}, bf16[256,512]{1,0:T(8,128)(2,1)S(...) custom-call(s32[32,4]{1,0:T(8,128)S(1)} %copy.52.mask, bf16[8192,1024]{1,0:T(8,128)(2,1)} %bitcast.9, ...), custom_call_target="tpu_custom_call" | custom-call | flops 805306368 | bytes 2097152 | tf_op jit(solution)/shard_map/factor/pallas_call | solution.py:179
  5.2 3.1 %collective-permute-start = (bf16[256,512]{1,0:T(8,128)(2,1)S(1)}, bf16[256,512]{1,0:T(8,128)(2,1)S(1)}, u32[]{:S(2)}, u32[]{:S(2)}) collective-permute-start(bf16[256,512]{1,0:T(8,128)(2,1)S(1)} %get-tuple-element.151.refs_18_), channel_id=1, source_target_pairs={{0,2},{1,3},{2,4},{3,5},{4,6},{5,7},{6,0},{7,1},{8,10},{9,11},{10,... | collective-permute-start | bytes 786440 | tf_op jit(solution)/shard_map/ppermute | solution.py:558
  8.3 1.5 collective-permute-start.1
  9.8 1.6 collective-permute-start.4
  11.9 3.0 %factor.9 = (bf16[256,512]{1,0:T(8,128)(2,1)S(1)}, bf16[256,512]{1,0:T(8,128)(2,1)S(1)}, bf16[256,512]{1,0:T(8,128)(2,1)S(1)}, bf16[256,512]{1,0:T(8,128)(2,1)S(1)}) custom-call(s32[32,4]{1,0:T(8,128)S(1)} %copy.52.mask, bf16[8192,1024]{1,0:T(8,128)(2,1)} %bitcast.10, bf16[4,256,256]{2,1,0:T(8,128)(2,1)S(1)} %get-tuple-element.233.refs_0_, ...), custom_call_target="tpu_custom_call" | custom-call | flops 805306368 | bytes 2097152 | tf_op jit(solution)/shard_map/factor/pallas_call | solution.py:179
  14.9 2.6 %collective-permute-done.refs_19_.refs_0_ = bf16[256,512]{1,0:T(8,128)(2,1)S(1)} collective-permute-done((bf16[256,512]{1,0:T(8,128)(2,1)S(1)}, bf16[256,512]{1,0:T(8,128)(2,1)S(1)}, u32[]{:S(2)}, u32[]{:S(2)}) %collective-permute-start) | collective-permute-done | bytes 262176 | tf_op jit(solution)/shard_map/ppermute | solution.py:558
  17.6 1.6 collective-permute-start.2
  19.2 1.5 collective-permute-start.3
  20.7 2.3 %collective-permute-done.4.refs_2_ = bf16[256,512]{1,0:T(8,128)(2,1)S(1)} collective-permute-done((bf16[256,512]{1,0:T(8,128)(2,1)S(1)}, bf16[256,512]{1,0:T(8,128)(2,1)S(1)}, u32[]{:S(2)}, u32[]{:S(2)}) %collective-permute-start.4) | collective-permute-done | bytes 262176 | tf_op jit(solution)/shard_map/ppermute | solution.py:558
  23.2 1.6 collective-permute-start.8
  24.8 1.5 collective-permute-start.9
  26.3 3.0 %factor.10 = (bf16[256,512]{1,0:T(8,128)(2,1)S(1)}, bf16[256,512]{1,0:T(8,128)(2,1)S(1)}, bf16[256,512]{1,0:T(8,128)(2,1)S(1)}, bf16[256,512]{1,0:T(8,128)(2,1)S(1)}) custom-call(s32[32,4]{1,0:T(8,128)S(1)} %copy.52.mask, bf16[8192,1024]{1,0:T(8,128)(2,1)} %bitcast.11, bf16[4,256,256]{2,1,0:T(8,128)(2,1)S(1)} %get-tuple-element.233.refs_0_, ...), custom_call_target="tpu_custom_call" | custom-call | flops 805306368 | bytes 2097152 | tf_op jit(solution)/shard_map/factor/pallas_call | solution.py:179
  29.5 1.6 collective-permute-start.6
  31.1 0.8 collective-permute-start.7
  31.9 2.3 %collective-permute-done.8.refs_6_ = bf16[256,512]{1,0:T(8,128)(2,1)S(1)} collective-permute-done((bf16[256,512]{1,0:T(8,128)(2,1)S(1)}, bf16[256,512]{1,0:T(8,128)(2,1)S(1)}, u32[]{:S(2)}, u32[]{:S(2)}) %collective-permute-start.8) | collective-permute-done | bytes 262176 | tf_op jit(solution)/shard_map/ppermute | solution.py:558
  34.4 1.6 collective-permute-start.12
  36.1 1.5 collective-permute-start.13
  37.6 3.0 %factor.11 = (bf16[256,512]{1,0:T(8,128)(2,1)S(1)}, bf16[256,512]{1,0:T(8,128)(2,1)S(1)}, bf16[256,512]{1,0:T(8,128)(2,1)S(1)}, bf16[256,512]{1,0:T(8,128)(2,1)S(1)}) custom-call(s32[32,4]{1,0:T(8,128)S(1)} %copy.52.mask, bf16[8192,1024]{1,0:T(8,128)(2,1)} %bitcast.12, bf16[4,256,256]{2,1,0:T(8,128)(2,1)S(1)} %get-tuple-element.233.refs_0_, ...), custom_call_target="tpu_custom_call" | custom-call | flops 805306368 | bytes 2097152 | tf_op jit(solution)/shard_map/factor/pallas_call | solution.py:179
  40.7 1.6 collective-permute-start.10
  42.3 0.8 collective-permute-start.11
  43.2 3.0 %collective-permute-done.12.refs_10_ = bf16[256,512]{1,0:T(8,128)(2,1)S(1)} collective-permute-done((bf16[256,512]{1,0:T(8,128)(2,1)S(1)}, bf16[256,512]{1,0:T(8,128)(2,1)S(1)}, u32[]{:S(2)}, u32[]{:S(2)}) %collective-permute-start.12) | collective-permute-done | bytes 262176 | tf_op jit(solution)/shard_map/ppermute | solution.py:558
  46.9 0.9 collective-permute-start.16
  47.9 1.5 collective-permute-start.17
  49.4 3.0 %factor.12 = (bf16[256,512]{1,0:T(8,128)(2,1)S(1)}, bf16[256,512]{1,0:T(8,128)(2,1)S(1)}, bf16[256,512]{1,0:T(8,128)(2,1)S(1)}, bf16[256,512]{1,0:T(8,128)(2,1)S(1)}) custom-call(s32[32,4]{1,0:T(8,128)S(1)} %copy.52.mask, bf16[8192,1024]{1,0:T(8,128)(2,1)} %bitcast.13, bf16[4,256,256]{2,1,0:T(8,128)(2,1)S(1)} %get-tuple-element.233.refs_0_, ...), custom_call_target="tpu_custom_call" | custom-call | flops 805306368 | bytes 2097152 | tf_op jit(solution)/shard_map/factor/pallas_call | solution.py:179
  52.5 1.6 collective-permute-start.14
  54.6 3.3 %collective-permute-done.16.refs_9_.refs_14_ = bf16[256,512]{1,0:T(8,128)(2,1)S(1)} collective-permute-done((bf16[256,512]{1,0:T(8,128)(2,1)S(1)}, bf16[256,512]{1,0:T(8,128)(2,1)S(1)}, u32[]{:S(2)}, u32[]{:S(2)}) %collective-permute-start.16) | collective-permute-done | bytes 262176 | tf_op jit(solution)/shard_map/ppermute | solution.py:558
  58.8 1.5 collective-permute-start.21
  60.4 3.0 %factor.13 = (bf16[256,512]{1,0:T(8,128)(2,1)S(1)}, bf16[256,512]{1,0:T(8,128)(2,1)S(1)}, bf16[256,512]{1,0:T(8,128)(2,1)S(1)}, bf16[256,512]{1,0:T(8,128)(2,1)S(1)}) custom-call(s32[32,4]{1,0:T(8,128)S(1)} %copy.52.mask, bf16[8192,1024]{1,0:T(8,128)(2,1)} %bitcast.14, bf16[4,256,256]{2,1,0:T(8,128)(2,1)S(1)} %get-tuple-element.233.refs_0_, ...), custom_call_target="tpu_custom_call" | custom-call | flops 805306368 | bytes 2097152 | tf_op jit(solution)/shard_map/factor/pallas_call | solution.py:179
  63.7 1.2 collective-permute-start.18
  64.8 1.1 collective-permute-start.19
  65.9 3.3 %collective-permute-done.20.refs_8_.refs_2_ = bf16[256,512]{1,0:T(8,128)(2,1)S(1)} collective-permute-done((bf16[256,512]{1,0:T(8,128)(2,1)S(1)}, bf16[256,512]{1,0:T(8,128)(2,1)S(1)}, u32[]{:S(2)}, u32[]{:S(2)}) %collective-permute-start.20) | collective-permute-done | bytes 262176 | tf_op jit(solution)/shard_map/ppermute | solution.py:558
  69.3 0.9 collective-permute-start.22
  70.2 1.5 collective-permute-start.23
  71.8 3.0 %factor.14 = (bf16[256,512]{1,0:T(8,128)(2,1)S(1)}, bf16[256,512]{1,0:T(8,128)(2,1)S(1)}, bf16[256,512]{1,0:T(8,128)(2,1)S(1)}, bf16[256,512]{1,0:T(8,128)(2,1)S(1)}) custom-call(s32[32,4]{1,0:T(8,128)S(1)} %copy.52.mask, bf16[8192,1024]{1,0:T(8,128)(2,1)} %bitcast.15, bf16[4,256,256]{2,1,0:T(8,128)(2,1)S(1)} %get-tuple-element.233.refs_0_, ...), custom_call_target="tpu_custom_call" | custom-call | flops 805306368 | bytes 2097152 | tf_op jit(solution)/shard_map/factor/pallas_call | solution.py:179
  74.9 1.3 collective-permute-start.24
  76.2 1.0 collective-permute-start.25
  77.2 3.4 %collective-permute-done.22.refs_7_.refs_6_ = bf16[256,512]{1,0:T(8,128)(2,1)S(1)} collective-permute-done((bf16[256,512]{1,0:T(8,128)(2,1)S(1)}, bf16[256,512]{1,0:T(8,128)(2,1)S(1)}, u32[]{:S(2)}, u32[]{:S(2)}) %collective-permute-start.22) | collective-permute-done | bytes 262176 | tf_op jit(solution)/shard_map/ppermute | solution.py:558
  81.3 1.5 collective-permute-start.27
  82.8 3.0 %factor.15 = (bf16[256,512]{1,0:T(8,128)(2,1)S(1)}, bf16[256,512]{1,0:T(8,128)(2,1)S(1)}, bf16[256,512]{1,0:T(8,128)(2,1)S(1)}, bf16[256,512]{1,0:T(8,128)(2,1)S(1)}) custom-call(s32[32,4]{1,0:T(8,128)S(1)} %copy.52.mask, bf16[8192,1024]{1,0:T(8,128)(2,1)} %bitcast.16, bf16[4,256,256]{2,1,0:T(8,128)(2,1)S(1)} %get-tuple-element.233.refs_0_, ...), custom_call_target="tpu_custom_call" | custom-call | flops 805306368 | bytes 2097152 | tf_op jit(solution)/shard_map/factor/pallas_call | solution.py:179
  86.3 1.1 collective-permute-start.30
  87.4 1.1 collective-permute-start.31
  88.4 3.4 %collective-permute-done.26.refs_16_.refs_10_ = bf16[256,512]{1,0:T(8,128)(2,1)S(1)} collective-permute-done((bf16[256,512]{1,0:T(8,128)(2,1)S(1)}, bf16[256,512]{1,0:T(8,128)(2,1)S(1)}, u32[]{:S(2)}, u32[]{:S(2)}) %collective-permute-start.26) | collective-permute-done | bytes 262176 | tf_op jit(solution)/shard_map/ppermute | solution.py:558
  92.6 1.5 collective-permute-start.29
  94.1 4.0 %own_panels.1 = (bf16[512,1024]{1,0:T(8,128)(2,1)S(1)}, bf16[4,528,256]{2,1,0:T(8,128)(2,1)}) custom-call(s32[32,4]{1,0:T(8,128)S(1)} %copy.52.mask, s32[4]{0:T(128)S(1)} %bitcast.8, s32[1]{0:T(128)} %bitcast.1.me, bf16[8192,1024]{1,0:T(8,128)(2,1)} %bitcast.17, bf16[256,512]{1,0:T(8,128)(2,1)} %copy-done.6, bf16[256,512]{1,0:T(8,128)(2,1)} %copy-done.21, ...), custom_call_target="tpu_custom_call" | custom-call | flops 268435456 | bytes 2621440 | tf_op jit(solution)/shard_map/own_panels/pallas_call | solution.py:239
  98.9 1.3 collective-permute-start.34
  100.7 1.4 collective-permute-done.28.refs_14_
  102.8 0.9 select_select_fusion.1
  103.7 0.9 collective-permute-start.32
  104.6 1.5 collective-permute-start.33
  106.1 3.5 %all-to-all-start = ((bf16[4,528,256]{2,1,0:T(8,128)(2,1)}), bf16[4,528,256]{2,1,0:T(8,128)(2,1)S(1)}, u32[]{:S(2)}, u32[]{:S(2)}) async-start(bf16[4,528,256]{2,1,0:T(8,128)(2,1)} %get-tuple-element.285), calls=%async_computation | async-start | bytes 2162688 | tf_op jit(solution)/shard_map/all_to_all | solution.py:528
  109.6 7.8 %update.4.refs_16_ = bf16[8192,1024]{1,0:T(8,128)(2,1)} custom-call(s32[8,46]{1,0:T(8,128)S(1)} %copy-done.7, s32[32,4]{1,0:T(8,128)S(1)} %copy.52.mask, s32[1]{0:T(128)} %bitcast.1.me, bf16[512,1024]{1,0:T(8,128)(2,1)S(1)} %get-tuple-element.251.own, bf16[8192,1024]{1,0:T(8,128)(2,1)} %bitcast.18, bf16[256,512]{1,0:T(8,128)(2,1)} %copy-done.9, ...), custom_call_target="tpu_custom_call" | custom-call | flops 4294967296 | bytes 16777216 | tf_op jit(solution)/shard_map/update/pallas_call | solution.py:404
  118.2 3.0 %collective-permute-start.38 = (bf16[256,512]{1,0:T(8,128)(2,1)S(1)}, bf16[256,512]{1,0:T(8,128)(2,1)S(1)}, u32[]{:S(2)}, u32[]{:S(2)}) collective-permute-start(bf16[256,512]{1,0:T(8,128)(2,1)S(1)} %get-tuple-element.265), channel_id=1, source_target_pairs={{0,2},{1,3},{2,4},{3,5},{4,6},{5,7},{6,0},{7,1},{8,10},{9,11},{10,... | collective-permute-start | bytes 786440 | tf_op jit(solution)/shard_map/ppermute | solution.py:558
  121.9 1.6 collective-permute-start.37
  123.4 10.2 %update.5.refs_10_ = bf16[8192,1024]{1,0:T(8,128)(2,1)} custom-call(s32[8,46]{1,0:T(8,128)S(1)} %copy-done.7, s32[32,4]{1,0:T(8,128)S(1)} %copy.52.mask, s32[1]{0:T(128)} %bitcast.1.me, bf16[512,1024]{1,0:T(8,128)(2,1)S(1)} %get-tuple-element.251.own, bf16[8192,1024]{1,0:T(8,128)(2,1)} %bitcast.19, ...), custom_call_target="tpu_custom_call", output_to_operand_aliasing={{}: (21, {})} | custom-call | flops 4294967296 | bytes 16777216 | tf_op jit(solution)/shard_map/update/pallas_call | solution.py:404
  134.3 0.9 collective-permute-done.37.refs_7_
  136.8 1.8 relay.1
  138.6 3.8 %all-to-all-start.1 = ((bf16[8,272,256]{2,1,0:T(8,128)(2,1)}), bf16[8,272,256]{2,1,0:T(8,128)(2,1)S(1)}, u32[]{:S(2)}, u32[]{:S(2)}) async-start(bf16[8,272,256]{2,1,0:T(8,128)(2,1)} %relay.1), calls=%async_computation.1 | async-start | bytes 2228224 | tf_op jit(solution)/shard_map/all_to_all | solution.py:528
  142.4 2.0 %collective-permute-start.41 = (bf16[256,512]{1,0:T(8,128)(2,1)S(1)}, bf16[256,512]{1,0:T(8,128)(2,1)S(1)}, u32[]{:S(2)}, u32[]{:S(2)}) collective-permute-start(bf16[256,512]{1,0:T(8,128)(2,1)S(1)} %get-tuple-element.274), channel_id=1, source_target_pairs={{0,2},{1,3},{2,4},{3,5},{4,6},{5,7},{6,0},{7,1},{8,10},{9,11},{10,... | collective-permute-start | bytes 786440 | tf_op jit(solution)/shard_map/ppermute | solution.py:558
  144.4 1.5 collective-permute-start.42
  146.4 23.3 %collective-permute-done.41.refs_8_ = bf16[256,512]{1,0:T(8,128)(2,1)S(1)} collective-permute-done((bf16[256,512]{1,0:T(8,128)(2,1)S(1)}, bf16[256,512]{1,0:T(8,128)(2,1)S(1)}, u32[]{:S(2)}, u32[]{:S(2)}) %collective-permute-start.41) | collective-permute-done | bytes 262176 | tf_op jit(solution)/shard_map/ppermute | solution.py:558
  169.8 1.5 collective-permute-start.43
  171.3 6.4 %update.6.refs_2_ = bf16[8192,1024]{1,0:T(8,128)(2,1)} custom-call(s32[8,46]{1,0:T(8,128)S(1)} %copy-done.7, s32[32,4]{1,0:T(8,128)S(1)} %copy.52.mask, s32[1]{0:T(128)} %bitcast.1.me, bf16[512,1024]{1,0:T(8,128)(2,1)S(1)} %get-tuple-element.251.own, bf16[8192,1024]{1,0:T(8,128)(2,1)} %bitcast.20, ...), custom_call_target="tpu_custom_call", output_to_operand_aliasing={{}: (15, {})} | custom-call | flops 2684354560 | bytes 10485760 | tf_op jit(solution)/shard_map/update/pallas_call | solution.py:404
  179.1 1.0 update.7
  180.4 1.7 sum_parents.1
  (176 shorter events, 14.1 us)
Async XLA Ops:
  5.2 9.7 %copy-start.5 = (bf16[256,512]{1,0:T(8,128)(2,1)}, bf16[256,512]{1,0:T(8,128)(2,1)S(1)}, u32[]{:S(2)}) copy-start(bf16[256,512]{1,0:T(8,128)(2,1)S(1)} %get-tuple-element.151.refs_18_) | copy-start | bytes 786436
  5.2 12.2 %collective-permute-start = (bf16[256,512]{1,0:T(8,128)(2,1)S(1)}, bf16[256,512]{1,0:T(8,128)(2,1)S(1)}, u32[]{:S(2)}, u32[]{:S(2)}) collective-permute-start(bf16[256,512]{1,0:T(8,128)(2,1)S(1)} %get-tuple-element.151.refs_18_), channel_id=1, source_target_pairs={{0,2},{1,3},{2,4},{3,5},{4,6},{5,7},{6,0},{7,1},{8,10},{9,11},{10,... | collective-permute-start | bytes 786440 | tf_op jit(solution)/shard_map/ppermute | solution.py:558
  8.3 9.2 %collective-permute-start.1 = (bf16[256,512]{1,0:T(8,128)(2,1)S(1)}, bf16[256,512]{1,0:T(8,128)(2,1)S(1)}, u32[]{:S(2)}, u32[]{:S(2)}) collective-permute-start(bf16[256,512]{1,0:T(8,128)(2,1)S(1)} %get-tuple-element.152), channel_id=1, source_target_pairs={{0,1},{1,0},{2,3},{3,2},{4,5},{5,4},{6,7},{7,6},{8,9},{9,8},{10,11... | collective-permute-start | bytes 786440 | tf_op jit(solution)/shard_map/ppermute | solution.py:558
  9.8 13.3 %collective-permute-start.4 = (bf16[256,512]{1,0:T(8,128)(2,1)S(1)}, bf16[256,512]{1,0:T(8,128)(2,1)S(1)}, u32[]{:S(2)}, u32[]{:S(2)}) collective-permute-start(bf16[256,512]{1,0:T(8,128)(2,1)S(1)} %get-tuple-element.153), channel_id=1, source_target_pairs={{0,2},{1,3},{2,4},{3,5},{4,6},{5,7},{6,0},{7,1},{8,10},{9,11},{10,... | collective-permute-start | bytes 786440 | tf_op jit(solution)/shard_map/ppermute | solution.py:558
  11.4 11.8 %collective-permute-start.5 = (bf16[256,512]{1,0:T(8,128)(2,1)S(1)}, bf16[256,512]{1,0:T(8,128)(2,1)S(1)}, u32[]{:S(2)}, u32[]{:S(2)}) collective-permute-start(bf16[256,512]{1,0:T(8,128)(2,1)S(1)} %get-tuple-element.154), channel_id=1, source_target_pairs={{0,1},{1,0},{2,3},{3,2},{4,5},{5,4},{6,7},{7,6},{8,9},{9,8},{10,11... | collective-permute-start | bytes 786440 | tf_op jit(solution)/shard_map/ppermute | solution.py:558
  17.4 5.7 %copy-start.9 = (bf16[256,512]{1,0:T(8,128)(2,1)}, bf16[256,512]{1,0:T(8,128)(2,1)S(1)}, u32[]{:S(2)}) copy-start(bf16[256,512]{1,0:T(8,128)(2,1)S(1)} %collective-permute-done.refs_19_.refs_0_) | copy-start | bytes 786436
  17.6 11.8 %collective-permute-start.2 = (bf16[256,512]{1,0:T(8,128)(2,1)S(1)}, bf16[256,512]{1,0:T(8,128)(2,1)S(1)}, u32[]{:S(2)}, u32[]{:S(2)}) collective-permute-start(bf16[256,512]{1,0:T(8,128)(2,1)S(1)} %get-tuple-element.161), channel_id=1, source_target_pairs={{0,2},{1,3},{2,4},{3,5},{4,6},{5,7},{6,0},{7,1},{8,10},{9,11},{10,... | collective-permute-start | bytes 786440 | tf_op jit(solution)/shard_map/ppermute | solution.py:558
  19.2 10.2 %collective-permute-start.3 = (bf16[256,512]{1,0:T(8,128)(2,1)S(1)}, bf16[256,512]{1,0:T(8,128)(2,1)S(1)}, u32[]{:S(2)}, u32[]{:S(2)}) collective-permute-start(bf16[256,512]{1,0:T(8,128)(2,1)S(1)} %get-tuple-element.162), channel_id=1, source_target_pairs={{0,1},{1,0},{2,3},{3,2},{4,5},{5,4},{6,7},{7,6},{8,9},{9,8},{10,11... | collective-permute-start | bytes 786440 | tf_op jit(solution)/shard_map/ppermute | solution.py:558
  23.0 6.3 %copy-start.29 = (bf16[256,512]{1,0:T(8,128)(2,1)}, bf16[256,512]{1,0:T(8,128)(2,1)S(1)}, u32[]{:S(2)}) copy-start(bf16[256,512]{1,0:T(8,128)(2,1)S(1)} %collective-permute-done.4.refs_2_) | copy-start | bytes 786436
  23.1 6.2 %copy-start.30 = (bf16[256,512]{1,0:T(8,128)(2,1)}, bf16[256,512]{1,0:T(8,128)(2,1)S(1)}, u32[]{:S(2)}) copy-start(bf16[256,512]{1,0:T(8,128)(2,1)S(1)} %collective-permute-done.5.refs_3_) | copy-start | bytes 786436
  23.2 11.1 %collective-permute-start.8 = (bf16[256,512]{1,0:T(8,128)(2,1)S(1)}, bf16[256,512]{1,0:T(8,128)(2,1)S(1)}, u32[]{:S(2)}, u32[]{:S(2)}) collective-permute-start(bf16[256,512]{1,0:T(8,128)(2,1)S(1)} %get-tuple-element.170), channel_id=1, source_target_pairs={{0,2},{1,3},{2,4},{3,5},{4,6},{5,7},{6,0},{7,1},{8,10},{9,11},{10,... | collective-permute-start | bytes 786440 | tf_op jit(solution)/shard_map/ppermute | solution.py:558
  24.8 9.5 %collective-permute-start.9 = (bf16[256,512]{1,0:T(8,128)(2,1)S(1)}, bf16[256,512]{1,0:T(8,128)(2,1)S(1)}, u32[]{:S(2)}, u32[]{:S(2)}) collective-permute-start(bf16[256,512]{1,0:T(8,128)(2,1)S(1)} %get-tuple-element.171), channel_id=1, source_target_pairs={{0,1},{1,0},{2,3},{3,2},{4,5},{5,4},{6,7},{7,6},{8,9},{9,8},{10,11... | collective-permute-start | bytes 786440 | tf_op jit(solution)/shard_map/ppermute | solution.py:558
  29.5 11.1 %collective-permute-start.6 = (bf16[256,512]{1,0:T(8,128)(2,1)S(1)}, bf16[256,512]{1,0:T(8,128)(2,1)S(1)}, u32[]{:S(2)}, u32[]{:S(2)}) collective-permute-start(bf16[256,512]{1,0:T(8,128)(2,1)S(1)} %get-tuple-element.175), channel_id=1, source_target_pairs={{0,2},{1,3},{2,4},{3,5},{4,6},{5,7},{6,0},{7,1},{8,10},{9,11},{10,... | collective-permute-start | bytes 786440 | tf_op jit(solution)/shard_map/ppermute | solution.py:558
  31.1 9.5 %collective-permute-start.7 = (bf16[256,512]{1,0:T(8,128)(2,1)S(1)}, bf16[256,512]{1,0:T(8,128)(2,1)S(1)}, u32[]{:S(2)}, u32[]{:S(2)}) collective-permute-start(bf16[256,512]{1,0:T(8,128)(2,1)S(1)} %get-tuple-element.176), channel_id=1, source_target_pairs={{0,1},{1,0},{2,3},{3,2},{4,5},{5,4},{6,7},{7,6},{8,9},{9,8},{10,11... | collective-permute-start | bytes 786440 | tf_op jit(solution)/shard_map/ppermute | solution.py:558
  34.3 6.3 %copy-start.31 = (bf16[256,512]{1,0:T(8,128)(2,1)}, bf16[256,512]{1,0:T(8,128)(2,1)S(1)}, u32[]{:S(2)}) copy-start(bf16[256,512]{1,0:T(8,128)(2,1)S(1)} %collective-permute-done.8.refs_6_) | copy-start | bytes 786436
  34.4 6.2 %copy-start.32 = (bf16[256,512]{1,0:T(8,128)(2,1)}, bf16[256,512]{1,0:T(8,128)(2,1)S(1)}, u32[]{:S(2)}) copy-start(bf16[256,512]{1,0:T(8,128)(2,1)S(1)} %collective-permute-done.9.refs_7_) | copy-start | bytes 786436
  34.4 11.7 %collective-permute-start.12 = (bf16[256,512]{1,0:T(8,128)(2,1)S(1)}, bf16[256,512]{1,0:T(8,128)(2,1)S(1)}, u32[]{:S(2)}, u32[]{:S(2)}) collective-permute-start(bf16[256,512]{1,0:T(8,128)(2,1)S(1)} %get-tuple-element.184), channel_id=1, source_target_pairs={{0,2},{1,3},{2,4},{3,5},{4,6},{5,7},{6,0},{7,1},{8,10},{9,11},{10,... | collective-permute-start | bytes 786440 | tf_op jit(solution)/shard_map/ppermute | solution.py:558
  36.1 10.1 %collective-permute-start.13 = (bf16[256,512]{1,0:T(8,128)(2,1)S(1)}, bf16[256,512]{1,0:T(8,128)(2,1)S(1)}, u32[]{:S(2)}, u32[]{:S(2)}) collective-permute-start(bf16[256,512]{1,0:T(8,128)(2,1)S(1)} %get-tuple-element.185), channel_id=1, source_target_pairs={{0,1},{1,0},{2,3},{3,2},{4,5},{5,4},{6,7},{7,6},{8,9},{9,8},{10,11... | collective-permute-start | bytes 786440 | tf_op jit(solution)/shard_map/ppermute | solution.py:558
  40.7 11.7 %collective-permute-start.10 = (bf16[256,512]{1,0:T(8,128)(2,1)S(1)}, bf16[256,512]{1,0:T(8,128)(2,1)S(1)}, u32[]{:S(2)}, u32[]{:S(2)}) collective-permute-start(bf16[256,512]{1,0:T(8,128)(2,1)S(1)} %get-tuple-element.189), channel_id=1, source_target_pairs={{0,2},{1,3},{2,4},{3,5},{4,6},{5,7},{6,0},{7,1},{8,10},{9,11},{10,... | collective-permute-start | bytes 786440 | tf_op jit(solution)/shard_map/ppermute | solution.py:558
  42.3 10.1 %collective-permute-start.11 = (bf16[256,512]{1,0:T(8,128)(2,1)S(1)}, bf16[256,512]{1,0:T(8,128)(2,1)S(1)}, u32[]{:S(2)}, u32[]{:S(2)}) collective-permute-start(bf16[256,512]{1,0:T(8,128)(2,1)S(1)} %get-tuple-element.190), channel_id=1, source_target_pairs={{0,1},{1,0},{2,3},{3,2},{4,5},{5,4},{6,7},{7,6},{8,9},{9,8},{10,11... | collective-permute-start | bytes 786440 | tf_op jit(solution)/shard_map/ppermute | solution.py:558
  46.2 6.2 %copy-start.33 = (bf16[256,512]{1,0:T(8,128)(2,1)}, bf16[256,512]{1,0:T(8,128)(2,1)S(1)}, u32[]{:S(2)}) copy-start(bf16[256,512]{1,0:T(8,128)(2,1)S(1)} %collective-permute-done.12.refs_10_) | copy-start | bytes 786436
  46.9 11.0 %collective-permute-start.16 = (bf16[256,512]{1,0:T(8,128)(2,1)S(1)}, bf16[256,512]{1,0:T(8,128)(2,1)S(1)}, u32[]{:S(2)}, u32[]{:S(2)}) collective-permute-start(bf16[256,512]{1,0:T(8,128)(2,1)S(1)} %get-tuple-element.198), channel_id=1, source_target_pairs={{0,2},{1,3},{2,4},{3,5},{4,6},{5,7},{6,0},{7,1},{8,10},{9,11},{10,... | collective-permute-start | bytes 786440 | tf_op jit(solution)/shard_map/ppermute | solution.py:558
  47.9 10.1 %collective-permute-start.17 = (bf16[256,512]{1,0:T(8,128)(2,1)S(1)}, bf16[256,512]{1,0:T(8,128)(2,1)S(1)}, u32[]{:S(2)}, u32[]{:S(2)}) collective-permute-start(bf16[256,512]{1,0:T(8,128)(2,1)S(1)} %get-tuple-element.199), channel_id=1, source_target_pairs={{0,1},{1,0},{2,3},{3,2},{4,5},{5,4},{6,7},{7,6},{8,9},{9,8},{10,11... | collective-permute-start | bytes 786440 | tf_op jit(solution)/shard_map/ppermute | solution.py:558
  52.5 11.1 %collective-permute-start.14 = (bf16[256,512]{1,0:T(8,128)(2,1)S(1)}, bf16[256,512]{1,0:T(8,128)(2,1)S(1)}, u32[]{:S(2)}, u32[]{:S(2)}) collective-permute-start(bf16[256,512]{1,0:T(8,128)(2,1)S(1)} %get-tuple-element.203), channel_id=1, source_target_pairs={{0,2},{1,3},{2,4},{3,5},{4,6},{5,7},{6,0},{7,1},{8,10},{9,11},{10,... | collective-permute-start | bytes 786440 | tf_op jit(solution)/shard_map/ppermute | solution.py:558
  54.1 9.5 %collective-permute-start.15 = (bf16[256,512]{1,0:T(8,128)(2,1)S(1)}, bf16[256,512]{1,0:T(8,128)(2,1)S(1)}, u32[]{:S(2)}, u32[]{:S(2)}) collective-permute-start(bf16[256,512]{1,0:T(8,128)(2,1)S(1)} %get-tuple-element.204), channel_id=1, source_target_pairs={{0,1},{1,0},{2,3},{3,2},{4,5},{5,4},{6,7},{7,6},{8,9},{9,8},{10,11... | collective-permute-start | bytes 786440 | tf_op jit(solution)/shard_map/ppermute | solution.py:558
  58.1 11.1 %collective-permute-start.20 = (bf16[256,512]{1,0:T(8,128)(2,1)S(1)}, bf16[256,512]{1,0:T(8,128)(2,1)S(1)}, u32[]{:S(2)}, u32[]{:S(2)}) collective-permute-start(bf16[256,512]{1,0:T(8,128)(2,1)S(1)} %get-tuple-element.212), channel_id=1, source_target_pairs={{0,2},{1,3},{2,4},{3,5},{4,6},{5,7},{6,0},{7,1},{8,10},{9,11},{10,... | collective-permute-start | bytes 786440 | tf_op jit(solution)/shard_map/ppermute | solution.py:558
  58.8 10.4 %collective-permute-start.21 = (bf16[256,512]{1,0:T(8,128)(2,1)S(1)}, bf16[256,512]{1,0:T(8,128)(2,1)S(1)}, u32[]{:S(2)}, u32[]{:S(2)}) collective-permute-start(bf16[256,512]{1,0:T(8,128)(2,1)S(1)} %get-tuple-element.213), channel_id=1, source_target_pairs={{0,1},{1,0},{2,3},{3,2},{4,5},{5,4},{6,7},{7,6},{8,9},{9,8},{10,11... | collective-permute-start | bytes 786440 | tf_op jit(solution)/shard_map/ppermute | solution.py:558
  63.7 11.2 %collective-permute-start.18 = (bf16[256,512]{1,0:T(8,128)(2,1)S(1)}, bf16[256,512]{1,0:T(8,128)(2,1)S(1)}, u32[]{:S(2)}, u32[]{:S(2)}) collective-permute-start(bf16[256,512]{1,0:T(8,128)(2,1)S(1)} %get-tuple-element.217), channel_id=1, source_target_pairs={{0,2},{1,3},{2,4},{3,5},{4,6},{5,7},{6,0},{7,1},{8,10},{9,11},{10,... | collective-permute-start | bytes 786440 | tf_op jit(solution)/shard_map/ppermute | solution.py:558
  64.8 10.0 %collective-permute-start.19 = (bf16[256,512]{1,0:T(8,128)(2,1)S(1)}, bf16[256,512]{1,0:T(8,128)(2,1)S(1)}, u32[]{:S(2)}, u32[]{:S(2)}) collective-permute-start(bf16[256,512]{1,0:T(8,128)(2,1)S(1)} %get-tuple-element.218), channel_id=1, source_target_pairs={{0,1},{1,0},{2,3},{3,2},{4,5},{5,4},{6,7},{7,6},{8,9},{9,8},{10,11... | collective-permute-start | bytes 786440 | tf_op jit(solution)/shard_map/ppermute | solution.py:558
  69.3 11.3 %collective-permute-start.22 = (bf16[256,512]{1,0:T(8,128)(2,1)S(1)}, bf16[256,512]{1,0:T(8,128)(2,1)S(1)}, u32[]{:S(2)}, u32[]{:S(2)}) collective-permute-start(bf16[256,512]{1,0:T(8,128)(2,1)S(1)} %get-tuple-element.226), channel_id=1, source_target_pairs={{0,2},{1,3},{2,4},{3,5},{4,6},{5,7},{6,0},{7,1},{8,10},{9,11},{10,... | collective-permute-start | bytes 786440 | tf_op jit(solution)/shard_map/ppermute | solution.py:558
  70.2 10.3 %collective-permute-start.23 = (bf16[256,512]{1,0:T(8,128)(2,1)S(1)}, bf16[256,512]{1,0:T(8,128)(2,1)S(1)}, u32[]{:S(2)}, u32[]{:S(2)}) collective-permute-start(bf16[256,512]{1,0:T(8,128)(2,1)S(1)} %get-tuple-element.227), channel_id=1, source_target_pairs={{0,1},{1,0},{2,3},{3,2},{4,5},{5,4},{6,7},{7,6},{8,9},{9,8},{10,11... | collective-permute-start | bytes 786440 | tf_op jit(solution)/shard_map/ppermute | solution.py:558
  74.8 5.8 %copy-start.20 = (bf16[256,512]{1,0:T(8,128)(2,1)}, bf16[256,512]{1,0:T(8,128)(2,1)S(1)}, u32[]{:S(2)}) copy-start(bf16[256,512]{1,0:T(8,128)(2,1)S(1)} %collective-permute-done.18.refs_2_.refs_4_) | copy-start | bytes 786436
  74.8 5.8 %copy-start.21 = (bf16[256,512]{1,0:T(8,128)(2,1)}, bf16[256,512]{1,0:T(8,128)(2,1)S(1)}, u32[]{:S(2)}) copy-start(bf16[256,512]{1,0:T(8,128)(2,1)S(1)} %collective-permute-done.19.refs_1_.refs_5_) | copy-start | bytes 786436
  74.9 11.3 %collective-permute-start.24 = (bf16[256,512]{1,0:T(8,128)(2,1)S(1)}, bf16[256,512]{1,0:T(8,128)(2,1)S(1)}, u32[]{:S(2)}, u32[]{:S(2)}) collective-permute-start(bf16[256,512]{1,0:T(8,128)(2,1)S(1)} %get-tuple-element.231), channel_id=1, source_target_pairs={{0,2},{1,3},{2,4},{3,5},{4,6},{5,7},{6,0},{7,1},{8,10},{9,11},{10,... | collective-permute-start | bytes 786440 | tf_op jit(solution)/shard_map/ppermute | solution.py:558
  76.2 10.0 %collective-permute-start.25 = (bf16[256,512]{1,0:T(8,128)(2,1)S(1)}, bf16[256,512]{1,0:T(8,128)(2,1)S(1)}, u32[]{:S(2)}, u32[]{:S(2)}) collective-permute-start(bf16[256,512]{1,0:T(8,128)(2,1)S(1)} %get-tuple-element.232), channel_id=1, source_target_pairs={{0,1},{1,0},{2,3},{3,2},{4,5},{5,4},{6,7},{7,6},{8,9},{9,8},{10,11... | collective-permute-start | bytes 786440 | tf_op jit(solution)/shard_map/ppermute | solution.py:558
  80.7 11.1 %collective-permute-start.26 = (bf16[256,512]{1,0:T(8,128)(2,1)S(1)}, bf16[256,512]{1,0:T(8,128)(2,1)S(1)}, u32[]{:S(2)}, u32[]{:S(2)}) collective-permute-start(bf16[256,512]{1,0:T(8,128)(2,1)S(1)} %get-tuple-element.242), channel_id=1, source_target_pairs={{0,2},{1,3},{2,4},{3,5},{4,6},{5,7},{6,0},{7,1},{8,10},{9,11},{10,... | collective-permute-start | bytes 786440 | tf_op jit(solution)/shard_map/ppermute | solution.py:558
  81.3 10.5 %collective-permute-start.27 = (bf16[256,512]{1,0:T(8,128)(2,1)S(1)}, bf16[256,512]{1,0:T(8,128)(2,1)S(1)}, u32[]{:S(2)}, u32[]{:S(2)}) collective-permute-start(bf16[256,512]{1,0:T(8,128)(2,1)S(1)} %get-tuple-element.243), channel_id=1, source_target_pairs={{0,1},{1,0},{2,3},{3,2},{4,5},{5,4},{6,7},{7,6},{8,9},{9,8},{10,11... | collective-permute-start | bytes 786440 | tf_op jit(solution)/shard_map/ppermute | solution.py:558
  85.9 6.0 %copy-start = (bf16[256,512]{1,0:T(8,128)(2,1)}, bf16[256,512]{1,0:T(8,128)(2,1)S(1)}, u32[]{:S(2)}) copy-start(bf16[256,512]{1,0:T(8,128)(2,1)S(1)} %get-tuple-element.246.refs_14_) | copy-start | bytes 786436
  85.9 6.0 %copy-start.2 = (bf16[256,512]{1,0:T(8,128)(2,1)}, bf16[256,512]{1,0:T(8,128)(2,1)S(1)}, u32[]{:S(2)}) copy-start(bf16[256,512]{1,0:T(8,128)(2,1)S(1)} %get-tuple-element.236.refs_5_) | copy-start | bytes 786436
  85.9 6.0 %copy-start.4 = (bf16[256,512]{1,0:T(8,128)(2,1)}, bf16[256,512]{1,0:T(8,128)(2,1)S(1)}, u32[]{:S(2)}) copy-start(bf16[256,512]{1,0:T(8,128)(2,1)S(1)} %get-tuple-element.239.refs_11_) | copy-start | bytes 786436
  85.9 6.0 %copy-start.6 = (bf16[256,512]{1,0:T(8,128)(2,1)}, bf16[256,512]{1,0:T(8,128)(2,1)S(1)}, u32[]{:S(2)}) copy-start(bf16[256,512]{1,0:T(8,128)(2,1)S(1)} %get-tuple-element.235.refs_0_) | copy-start | bytes 786436
  86.3 7.8 %copy-start.8 = (s32[1,1,4]{2,1,0:T(1,128)S(1)}, s32[1,1,4]{2,1,0:T(1,128)}, u32[]{:S(2)}) copy-start(s32[1,1,4]{2,1,0:T(1,128)} %param.8) | copy-start | bytes 52
  86.3 11.8 %collective-permute-start.30 = (bf16[256,512]{1,0:T(8,128)(2,1)S(1)}, bf16[256,512]{1,0:T(8,128)(2,1)S(1)}, u32[]{:S(2)}, u32[]{:S(2)}) collective-permute-start(bf16[256,512]{1,0:T(8,128)(2,1)S(1)} %get-tuple-element.247), channel_id=1, source_target_pairs={{0,2},{1,3},{2,4},{3,5},{4,6},{5,7},{6,0},{7,1},{8,10},{9,11},{10,... | collective-permute-start | bytes 786440 | tf_op jit(solution)/shard_map/ppermute | solution.py:558
  87.4 10.8 %collective-permute-start.31 = (bf16[256,512]{1,0:T(8,128)(2,1)S(1)}, bf16[256,512]{1,0:T(8,128)(2,1)S(1)}, u32[]{:S(2)}, u32[]{:S(2)}) collective-permute-start(bf16[256,512]{1,0:T(8,128)(2,1)S(1)} %get-tuple-element.248), channel_id=1, source_target_pairs={{0,1},{1,0},{2,3},{3,2},{4,5},{5,4},{6,7},{7,6},{8,9},{9,8},{10,11... | collective-permute-start | bytes 786440 | tf_op jit(solution)/shard_map/ppermute | solution.py:558
  91.9 10.2 %collective-permute-start.28 = (bf16[256,512]{1,0:T(8,128)(2,1)S(1)}, bf16[256,512]{1,0:T(8,128)(2,1)S(1)}, u32[]{:S(2)}, u32[]{:S(2)}) collective-permute-start(bf16[256,512]{1,0:T(8,128)(2,1)S(1)} %get-tuple-element.252), channel_id=1, source_target_pairs={{0,2},{1,3},{2,4},{3,5},{4,6},{5,7},{6,0},{7,1},{8,10},{9,11},{10,... | collective-permute-start | bytes 786440 | tf_op jit(solution)/shard_map/ppermute | solution.py:558
  92.6 9.5 %collective-permute-start.29 = (bf16[256,512]{1,0:T(8,128)(2,1)S(1)}, bf16[256,512]{1,0:T(8,128)(2,1)S(1)}, u32[]{:S(2)}, u32[]{:S(2)}) collective-permute-start(bf16[256,512]{1,0:T(8,128)(2,1)S(1)} %get-tuple-element.253), channel_id=1, source_target_pairs={{0,1},{1,0},{2,3},{3,2},{4,5},{5,4},{6,7},{7,6},{8,9},{9,8},{10,11... | collective-permute-start | bytes 786440 | tf_op jit(solution)/shard_map/ppermute | solution.py:558
  98.9 18.5 %collective-permute-start.34 = (bf16[256,512]{1,0:T(8,128)(2,1)}, bf16[256,512]{1,0:T(8,128)(2,1)S(1)}, u32[]{:S(2)}, u32[]{:S(2)}) collective-permute-start(bf16[256,512]{1,0:T(8,128)(2,1)} %get-tuple-element.256), channel_id=1, source_target_pairs={{0,2},{1,3},{2,4},{3,5},{4,6},{5,7},{6,0},{7,1},{8,10},{9,11},{10,... | collective-permute-start | bytes 786440 | tf_op jit(solution)/shard_map/ppermute | solution.py:558
  100.2 17.3 %collective-permute-start.35 = (bf16[256,512]{1,0:T(8,128)(2,1)S(1)}, bf16[256,512]{1,0:T(8,128)(2,1)S(1)}, u32[]{:S(2)}, u32[]{:S(2)}) collective-permute-start(bf16[256,512]{1,0:T(8,128)(2,1)S(1)} %get-tuple-element.257), channel_id=1, source_target_pairs={{0,1},{1,0},{2,3},{3,2},{4,5},{5,4},{6,7},{7,6},{8,9},{9,8},{10,11... | collective-permute-start | bytes 786440 | tf_op jit(solution)/shard_map/ppermute | solution.py:558
  103.7 5.9 %copy-start.7 = (s32[8,46]{1,0:T(8,128)S(1)}, s32[8,46]{1,0:T(8,128)}, u32[]{:S(2)}) copy-start(s32[8,46]{1,0:T(8,128)} %constant.14.clone.table) | copy-start | bytes 4420
  103.7 18.0 %collective-permute-start.32 = (bf16[256,512]{1,0:T(8,128)(2,1)}, bf16[256,512]{1,0:T(8,128)(2,1)S(1)}, u32[]{:S(2)}, u32[]{:S(2)}) collective-permute-start(bf16[256,512]{1,0:T(8,128)(2,1)} %get-tuple-element.260), channel_id=1, source_target_pairs={{0,2},{1,3},{2,4},{3,5},{4,6},{5,7},{6,0},{7,1},{8,10},{9,11},{10,... | collective-permute-start | bytes 786440 | tf_op jit(solution)/shard_map/ppermute | solution.py:558
  104.6 17.1 %collective-permute-start.33 = (bf16[256,512]{1,0:T(8,128)(2,1)}, bf16[256,512]{1,0:T(8,128)(2,1)S(1)}, u32[]{:S(2)}, u32[]{:S(2)}) collective-permute-start(bf16[256,512]{1,0:T(8,128)(2,1)} %get-tuple-element.261), channel_id=1, source_target_pairs={{0,1},{1,0},{2,3},{3,2},{4,5},{5,4},{6,7},{7,6},{8,9},{9,8},{10,11... | collective-permute-start | bytes 786440 | tf_op jit(solution)/shard_map/ppermute | solution.py:558
  106.1 30.5 %all-to-all-start = ((bf16[4,528,256]{2,1,0:T(8,128)(2,1)}), bf16[4,528,256]{2,1,0:T(8,128)(2,1)S(1)}, u32[]{:S(2)}, u32[]{:S(2)}) async-start(bf16[4,528,256]{2,1,0:T(8,128)(2,1)} %get-tuple-element.285), calls=%async_computation | async-start | bytes 2162688 | tf_op jit(solution)/shard_map/all_to_all | solution.py:528
  109.6 7.8 %copy-start.1 = (bf16[256,512]{1,0:T(8,128)(2,1)S(1)}, bf16[256,512]{1,0:T(8,128)(2,1)}, u32[]{:S(2)}) copy-start(bf16[256,512]{1,0:T(8,128)(2,1)} %copy-done) | copy-start | bytes 786436
  118.2 15.5 %collective-permute-start.38 = (bf16[256,512]{1,0:T(8,128)(2,1)S(1)}, bf16[256,512]{1,0:T(8,128)(2,1)S(1)}, u32[]{:S(2)}, u32[]{:S(2)}) collective-permute-start(bf16[256,512]{1,0:T(8,128)(2,1)S(1)} %get-tuple-element.265), channel_id=1, source_target_pairs={{0,2},{1,3},{2,4},{3,5},{4,6},{5,7},{6,0},{7,1},{8,10},{9,11},{10,... | collective-permute-start | bytes 786440 | tf_op jit(solution)/shard_map/ppermute | solution.py:558
  121.2 12.5 %collective-permute-start.39 = (bf16[256,512]{1,0:T(8,128)(2,1)S(1)}, bf16[256,512]{1,0:T(8,128)(2,1)S(1)}, u32[]{:S(2)}, u32[]{:S(2)}) collective-permute-start(bf16[256,512]{1,0:T(8,128)(2,1)S(1)} %get-tuple-element.266), channel_id=1, source_target_pairs={{0,1},{1,0},{2,3},{3,2},{4,5},{5,4},{6,7},{7,6},{8,9},{9,8},{10,11... | collective-permute-start | bytes 786440 | tf_op jit(solution)/shard_map/ppermute | solution.py:558
  121.7 12.0 %copy-start.37 = (bf16[256,512]{1,0:T(8,128)(2,1)}, bf16[256,512]{1,0:T(8,128)(2,1)S(1)}, u32[]{:S(2)}) copy-start(bf16[256,512]{1,0:T(8,128)(2,1)S(1)} %collective-permute-done.32.refs_2_) | copy-start | bytes 786436
  121.7 12.0 %copy-start.38 = (bf16[256,512]{1,0:T(8,128)(2,1)}, bf16[256,512]{1,0:T(8,128)(2,1)S(1)}, u32[]{:S(2)}) copy-start(bf16[256,512]{1,0:T(8,128)(2,1)S(1)} %collective-permute-done.33.refs_3_) | copy-start | bytes 786436
  121.8 12.5 %collective-permute-start.36 = (bf16[256,512]{1,0:T(8,128)(2,1)S(1)}, bf16[256,512]{1,0:T(8,128)(2,1)S(1)}, u32[]{:S(2)}, u32[]{:S(2)}) collective-permute-start(bf16[256,512]{1,0:T(8,128)(2,1)S(1)} %get-tuple-element.269), channel_id=1, source_target_pairs={{0,2},{1,3},{2,4},{3,5},{4,6},{5,7},{6,0},{7,1},{8,10},{9,11},{10,... | collective-permute-start | bytes 786440 | tf_op jit(solution)/shard_map/ppermute | solution.py:558
  121.9 13.3 %collective-permute-start.37 = (bf16[256,512]{1,0:T(8,128)(2,1)S(1)}, bf16[256,512]{1,0:T(8,128)(2,1)S(1)}, u32[]{:S(2)}, u32[]{:S(2)}) collective-permute-start(bf16[256,512]{1,0:T(8,128)(2,1)S(1)} %get-tuple-element.270), channel_id=1, source_target_pairs={{0,1},{1,0},{2,3},{3,2},{4,5},{5,4},{6,7},{7,6},{8,9},{9,8},{10,11... | collective-permute-start | bytes 786440 | tf_op jit(solution)/shard_map/ppermute | solution.py:558
  138.6 41.5 %all-to-all-start.1 = ((bf16[8,272,256]{2,1,0:T(8,128)(2,1)}), bf16[8,272,256]{2,1,0:T(8,128)(2,1)S(1)}, u32[]{:S(2)}, u32[]{:S(2)}) async-start(bf16[8,272,256]{2,1,0:T(8,128)(2,1)} %relay.1), calls=%async_computation.1 | async-start | bytes 2228224 | tf_op jit(solution)/shard_map/all_to_all | solution.py:528
  142.4 27.4 %collective-permute-start.41 = (bf16[256,512]{1,0:T(8,128)(2,1)S(1)}, bf16[256,512]{1,0:T(8,128)(2,1)S(1)}, u32[]{:S(2)}, u32[]{:S(2)}) collective-permute-start(bf16[256,512]{1,0:T(8,128)(2,1)S(1)} %get-tuple-element.274), channel_id=1, source_target_pairs={{0,2},{1,3},{2,4},{3,5},{4,6},{5,7},{6,0},{7,1},{8,10},{9,11},{10,... | collective-permute-start | bytes 786440 | tf_op jit(solution)/shard_map/ppermute | solution.py:558
  144.4 25.3 %collective-permute-start.42 = (bf16[256,512]{1,0:T(8,128)(2,1)S(1)}, bf16[256,512]{1,0:T(8,128)(2,1)S(1)}, u32[]{:S(2)}, u32[]{:S(2)}) collective-permute-start(bf16[256,512]{1,0:T(8,128)(2,1)S(1)} %get-tuple-element.275), channel_id=1, source_target_pairs={{0,1},{1,0},{2,3},{3,2},{4,5},{5,4},{6,7},{7,6},{8,9},{9,8},{10,11... | collective-permute-start | bytes 786440 | tf_op jit(solution)/shard_map/ppermute | solution.py:558
  145.9 31.8 %collective-permute-start.40 = (bf16[256,512]{1,0:T(8,128)(2,1)}, bf16[256,512]{1,0:T(8,128)(2,1)S(1)}, u32[]{:S(2)}, u32[]{:S(2)}) collective-permute-start(bf16[256,512]{1,0:T(8,128)(2,1)} %broadcast_select_fusion.1), channel_id=1, source_target_pairs={{0,1},{1,0},{2,3},{3,2},{4,5},{5,4},{6,7},{7,6},{8,9},{9,8},{10,11... | collective-permute-start | bytes 786440 | tf_op jit(solution)/shard_map/ppermute | solution.py:558
  169.8 7.9 %collective-permute-start.43 = (bf16[256,512]{1,0:T(8,128)(2,1)S(1)}, bf16[256,512]{1,0:T(8,128)(2,1)S(1)}, u32[]{:S(2)}, u32[]{:S(2)}) collective-permute-start(bf16[256,512]{1,0:T(8,128)(2,1)S(1)} %broadcast_select_fusion), channel_id=1, source_target_pairs={{0,1},{1,0},{2,3},{3,2},{4,5},{5,4},{6,7},{7,6},{8,9},{9,8},{10,11... | collective-permute-start | bytes 786440 | tf_op jit(solution)/shard_map/ppermute | solution.py:558
  (35 other events, 138.7 us)

commit v5 on v4

--- a/solution.py
+++ b/solution.py
@@ -9,7 +9,7 @@
 
 TILE = 256
 CHAINS = 2
-RELAY_AFTER = 6
+RELAY_AFTER = 7
 LABEL_ROWS = 16
 VMEM_LIMIT = 16 * 1024 * 1024
 UPDATE_LIMIT = 32 * 1024 * 1024
@@ -566,12 +566,11 @@
             arrived = exchange(after((sends,), *turn)[0], "front")
         if late == relay_after:
             arrived = relayed(after((arrived,), *turn)[0])
-        elif late >= 2 and late % 2 == 0 and e < events - 1:
+        elif late == 2 or late > RELAY_AFTER and e % 4 == 0:
             step(min(8, e - CHAINS + 1 - done), *turn)
             turn = (*turn, result)
-    while done < events - CHAINS:
-        step(min(8, events - CHAINS - done), *turn)
-    step(CHAINS)
+    while done < events:
+        step(min(8, events - done), *turn)
     slots_here = after((arrived,), result)[0]
     parent_tiles = sum_parents(slots_here[:, TILE, 0].astype(jnp.int32), slots_here, slots_dev)
     return (result[None], parent_tiles)

time: 184 us -> 181 us (0.984)
  local copies, waits for them, and re-layouts: 5.3 us -> 3.28 us
    unnamed x106 -> x108, local copies, waits for them, and re-layouts: 4.35 us -> 2.32 us
    pallas_call x4 -> x3, Pallas kernels: 25.4 us -> 24.5 us  [update(): pl.pallas_call(functools.partial(update_kernel, tuple(numbers), room, wid...]
  transfers between devices with their start and end apart: 46 -> 46, of which waited for: 18 -> 18; matrix products, arithmetic and copies ran while one was open for 2% -> 2% of each run, Pallas kernels for 28% -> 27%
where the time goes in v5:
time: 181 us; the launch traced here: 180 us
  starting transfers between devices  63.3 us (35%)
  Pallas kernels  56.7 us (31%)
  waiting for transfers between devices  51.3 us (28%)
  other arithmetic  4.02 us (2%)
  local copies, waits for them, and re-layouts  3.28 us (2%)
    ppermute x44, starting transfers between devices, shards(): lax.ppermute(turn[s], 'grp', perms[s])  56.1 us
    ppermute x44, waiting for transfers between devices, shards(): lax.ppermute(turn[s], 'grp', perms[s])  51.3 us
    pallas_call x8, Pallas kernels, factor(): pl.pallas_call(functools.partial(factor_kernel, tuple(tiles), head), out_...  24.7 us
    pallas_call x3, Pallas kernels, update(): pl.pallas_call(functools.partial(update_kernel, tuple(numbers), room, wid...  24.5 us
    all_to_all x2, starting transfers between devices, exchange(): return lax.all_to_all(blocks, axis, split_axis=0, concat_axis=0, tiled=True)  7.21 us
    pallas_call x1, Pallas kernels, own_panels(): pl.pallas_call(functools.partial(own_kernel, choices, len(blocks), width...  4 us
  transfers between devices with their start and end apart: 46, of which 18 were waited for; matrix products, arithmetic and copies ran while one was open for 2% of the time, Pallas kernels for 27%

profile of v5, /device:TPU:0, one launch (start us, length us, event | category | flops | bytes accessed | tf_op | source)
XLA Modules:
  0.0 180.1 jit_solution(6534763655507886153)
XLA Ops:
  1.4 3.8 %factor.8 = (bf16[256,512]{1,0:T(8,128)(2,1)S(1)}, bf16[256,512]{1,0:T(8,128)(2,1)S(1)}, bf16[256,512]{1,0:T(8,128)(2,1)S(1)}, bf16[256,512]{1,0:T(8,128)(2,1)S(...) custom-call(s32[32,4]{1,0:T(8,128)S(1)} %copy.48.mask, bf16[8192,1024]{1,0:T(8,128)(2,1)} %bitcast.9, ...), custom_call_target="tpu_custom_call" | custom-call | flops 805306368 | bytes 2097152 | tf_op jit(solution)/shard_map/factor/pallas_call | solution.py:179
  5.2 3.1 %collective-permute-start = (bf16[256,512]{1,0:T(8,128)(2,1)S(1)}, bf16[256,512]{1,0:T(8,128)(2,1)S(1)}, u32[]{:S(2)}, u32[]{:S(2)}) collective-permute-start(bf16[256,512]{1,0:T(8,128)(2,1)S(1)} %get-tuple-element.151.refs_18_), channel_id=1, source_target_pairs={{0,2},{1,3},{2,4},{3,5},{4,6},{5,7},{6,0},{7,1},{8,10},{9,11},{10,... | collective-permute-start | bytes 786440 | tf_op jit(solution)/shard_map/ppermute | solution.py:558
  8.3 1.5 collective-permute-start.1
  9.8 1.6 collective-permute-start.4
  11.9 3.0 %factor.9 = (bf16[256,512]{1,0:T(8,128)(2,1)S(1)}, bf16[256,512]{1,0:T(8,128)(2,1)S(1)}, bf16[256,512]{1,0:T(8,128)(2,1)S(1)}, bf16[256,512]{1,0:T(8,128)(2,1)S(1)}) custom-call(s32[32,4]{1,0:T(8,128)S(1)} %copy.48.mask, bf16[8192,1024]{1,0:T(8,128)(2,1)} %bitcast.10, bf16[4,256,256]{2,1,0:T(8,128)(2,1)S(1)} %get-tuple-element.233.refs_0_, ...), custom_call_target="tpu_custom_call" | custom-call | flops 805306368 | bytes 2097152 | tf_op jit(solution)/shard_map/factor/pallas_call | solution.py:179
  14.9 2.6 %collective-permute-done.refs_19_.refs_0_ = bf16[256,512]{1,0:T(8,128)(2,1)S(1)} collective-permute-done((bf16[256,512]{1,0:T(8,128)(2,1)S(1)}, bf16[256,512]{1,0:T(8,128)(2,1)S(1)}, u32[]{:S(2)}, u32[]{:S(2)}) %collective-permute-start) | collective-permute-done | bytes 262176 | tf_op jit(solution)/shard_map/ppermute | solution.py:558
  17.6 1.6 collective-permute-start.2
  19.2 1.5 collective-permute-start.3
  20.7 2.3 %collective-permute-done.4.refs_2_ = bf16[256,512]{1,0:T(8,128)(2,1)S(1)} collective-permute-done((bf16[256,512]{1,0:T(8,128)(2,1)S(1)}, bf16[256,512]{1,0:T(8,128)(2,1)S(1)}, u32[]{:S(2)}, u32[]{:S(2)}) %collective-permute-start.4) | collective-permute-done | bytes 262176 | tf_op jit(solution)/shard_map/ppermute | solution.py:558
  23.2 1.6 collective-permute-start.8
  24.8 1.5 collective-permute-start.9
  26.3 3.0 %factor.10 = (bf16[256,512]{1,0:T(8,128)(2,1)S(1)}, bf16[256,512]{1,0:T(8,128)(2,1)S(1)}, bf16[256,512]{1,0:T(8,128)(2,1)S(1)}, bf16[256,512]{1,0:T(8,128)(2,1)S(1)}) custom-call(s32[32,4]{1,0:T(8,128)S(1)} %copy.48.mask, bf16[8192,1024]{1,0:T(8,128)(2,1)} %bitcast.11, bf16[4,256,256]{2,1,0:T(8,128)(2,1)S(1)} %get-tuple-element.233.refs_0_, ...), custom_call_target="tpu_custom_call" | custom-call | flops 805306368 | bytes 2097152 | tf_op jit(solution)/shard_map/factor/pallas_call | solution.py:179
  29.5 1.6 collective-permute-start.6
  31.9 2.3 %collective-permute-done.8.refs_6_ = bf16[256,512]{1,0:T(8,128)(2,1)S(1)} collective-permute-done((bf16[256,512]{1,0:T(8,128)(2,1)S(1)}, bf16[256,512]{1,0:T(8,128)(2,1)S(1)}, u32[]{:S(2)}, u32[]{:S(2)}) %collective-permute-start.8) | collective-permute-done | bytes 262176 | tf_op jit(solution)/shard_map/ppermute | solution.py:558
  34.4 1.6 collective-permute-start.12
  36.1 1.5 collective-permute-start.13
  37.6 3.0 %factor.11 = (bf16[256,512]{1,0:T(8,128)(2,1)S(1)}, bf16[256,512]{1,0:T(8,128)(2,1)S(1)}, bf16[256,512]{1,0:T(8,128)(2,1)S(1)}, bf16[256,512]{1,0:T(8,128)(2,1)S(1)}) custom-call(s32[32,4]{1,0:T(8,128)S(1)} %copy.48.mask, bf16[8192,1024]{1,0:T(8,128)(2,1)} %bitcast.12, bf16[4,256,256]{2,1,0:T(8,128)(2,1)S(1)} %get-tuple-element.233.refs_0_, ...), custom_call_target="tpu_custom_call" | custom-call | flops 805306368 | bytes 2097152 | tf_op jit(solution)/shard_map/factor/pallas_call | solution.py:179
  40.7 1.6 collective-permute-start.10
  42.3 0.8 collective-permute-start.11
  43.2 3.0 %collective-permute-done.12.refs_10_ = bf16[256,512]{1,0:T(8,128)(2,1)S(1)} collective-permute-done((bf16[256,512]{1,0:T(8,128)(2,1)S(1)}, bf16[256,512]{1,0:T(8,128)(2,1)S(1)}, u32[]{:S(2)}, u32[]{:S(2)}) %collective-permute-start.12) | collective-permute-done | bytes 262176 | tf_op jit(solution)/shard_map/ppermute | solution.py:558
  46.3 1.0 collective-permute-start.16
  47.3 1.5 collective-permute-start.17
  48.8 3.0 %factor.12 = (bf16[256,512]{1,0:T(8,128)(2,1)S(1)}, bf16[256,512]{1,0:T(8,128)(2,1)S(1)}, bf16[256,512]{1,0:T(8,128)(2,1)S(1)}, bf16[256,512]{1,0:T(8,128)(2,1)S(1)}) custom-call(s32[32,4]{1,0:T(8,128)S(1)} %copy.48.mask, bf16[8192,1024]{1,0:T(8,128)(2,1)} %bitcast.13, bf16[4,256,256]{2,1,0:T(8,128)(2,1)S(1)} %get-tuple-element.233.refs_0_, ...), custom_call_target="tpu_custom_call" | custom-call | flops 805306368 | bytes 2097152 | tf_op jit(solution)/shard_map/factor/pallas_call | solution.py:179
  51.9 1.6 collective-permute-start.14
  53.6 0.8 collective-permute-start.15
  54.4 3.0 %collective-permute-done.16.refs_9_.refs_14_ = bf16[256,512]{1,0:T(8,128)(2,1)S(1)} collective-permute-done((bf16[256,512]{1,0:T(8,128)(2,1)S(1)}, bf16[256,512]{1,0:T(8,128)(2,1)S(1)}, u32[]{:S(2)}, u32[]{:S(2)}) %collective-permute-start.16) | collective-permute-done | bytes 262176 | tf_op jit(solution)/shard_map/ppermute | solution.py:558
  57.5 1.0 collective-permute-start.20
  58.5 1.5 collective-permute-start.21
  60.1 3.0 %factor.13 = (bf16[256,512]{1,0:T(8,128)(2,1)S(1)}, bf16[256,512]{1,0:T(8,128)(2,1)S(1)}, bf16[256,512]{1,0:T(8,128)(2,1)S(1)}, bf16[256,512]{1,0:T(8,128)(2,1)S(1)}) custom-call(s32[32,4]{1,0:T(8,128)S(1)} %copy.48.mask, bf16[8192,1024]{1,0:T(8,128)(2,1)} %bitcast.14, bf16[4,256,256]{2,1,0:T(8,128)(2,1)S(1)} %get-tuple-element.233.refs_0_, ...), custom_call_target="tpu_custom_call" | custom-call | flops 805306368 | bytes 2097152 | tf_op jit(solution)/shard_map/factor/pallas_call | solution.py:179
  63.2 1.6 collective-permute-start.18
  65.7 3.0 %collective-permute-done.20.refs_8_.refs_2_ = bf16[256,512]{1,0:T(8,128)(2,1)S(1)} collective-permute-done((bf16[256,512]{1,0:T(8,128)(2,1)S(1)}, bf16[256,512]{1,0:T(8,128)(2,1)S(1)}, u32[]{:S(2)}, u32[]{:S(2)}) %collective-permute-start.20) | collective-permute-done | bytes 262176 | tf_op jit(solution)/shard_map/ppermute | solution.py:558
  68.7 1.2 collective-permute-start.24
  70.0 1.5 collective-permute-start.25
  71.5 3.0 %factor.14 = (bf16[256,512]{1,0:T(8,128)(2,1)S(1)}, bf16[256,512]{1,0:T(8,128)(2,1)S(1)}, bf16[256,512]{1,0:T(8,128)(2,1)S(1)}, bf16[256,512]{1,0:T(8,128)(2,1)S(1)}) custom-call(s32[32,4]{1,0:T(8,128)S(1)} %copy.48.mask, bf16[8192,1024]{1,0:T(8,128)(2,1)} %bitcast.15, bf16[4,256,256]{2,1,0:T(8,128)(2,1)S(1)} %get-tuple-element.233.refs_0_, ...), custom_call_target="tpu_custom_call" | custom-call | flops 805306368 | bytes 2097152 | tf_op jit(solution)/shard_map/factor/pallas_call | solution.py:179
  74.6 1.6 collective-permute-start.22
  76.9 3.1 %collective-permute-done.24.refs_7_.refs_6_ = bf16[256,512]{1,0:T(8,128)(2,1)S(1)} collective-permute-done((bf16[256,512]{1,0:T(8,128)(2,1)S(1)}, bf16[256,512]{1,0:T(8,128)(2,1)S(1)}, u32[]{:S(2)}, u32[]{:S(2)}) %collective-permute-start.24) | collective-permute-done | bytes 262176 | tf_op jit(solution)/shard_map/ppermute | solution.py:558
  80.1 0.9 collective-permute-start.28
  81.0 1.5 collective-permute-start.29
  82.5 3.0 %factor.15 = (bf16[256,512]{1,0:T(8,128)(2,1)S(1)}, bf16[256,512]{1,0:T(8,128)(2,1)S(1)}, bf16[256,512]{1,0:T(8,128)(2,1)S(1)}, bf16[256,512]{1,0:T(8,128)(2,1)S(1)}) custom-call(s32[32,4]{1,0:T(8,128)S(1)} %copy.48.mask, bf16[8192,1024]{1,0:T(8,128)(2,1)} %bitcast.16, bf16[4,256,256]{2,1,0:T(8,128)(2,1)S(1)} %get-tuple-element.233.refs_0_, ...), custom_call_target="tpu_custom_call" | custom-call | flops 805306368 | bytes 2097152 | tf_op jit(solution)/shard_map/factor/pallas_call | solution.py:179
  85.7 1.6 collective-permute-start.26
  88.2 3.1 %collective-permute-done.28.refs_16_.refs_10_ = bf16[256,512]{1,0:T(8,128)(2,1)S(1)} collective-permute-done((bf16[256,512]{1,0:T(8,128)(2,1)S(1)}, bf16[256,512]{1,0:T(8,128)(2,1)S(1)}, u32[]{:S(2)}, u32[]{:S(2)}) %collective-permute-start.28) | collective-permute-done | bytes 262176 | tf_op jit(solution)/shard_map/ppermute | solution.py:558
  91.4 0.9 collective-permute-start.32
  92.3 1.5 collective-permute-start.33
  93.8 4.0 %own_panels.1 = (bf16[512,1024]{1,0:T(8,128)(2,1)S(1)}, bf16[4,528,256]{2,1,0:T(8,128)(2,1)}) custom-call(s32[32,4]{1,0:T(8,128)S(1)} %copy.48.mask, s32[4]{0:T(128)S(1)} %bitcast.8, s32[1]{0:T(128)} %bitcast.1.me, bf16[8192,1024]{1,0:T(8,128)(2,1)} %bitcast.17, bf16[256,512]{1,0:T(8,128)(2,1)} %copy-done.6, bf16[256,512]{1,0:T(8,128)(2,1)} %copy-done.17, ...), custom_call_target="tpu_custom_call" | custom-call | flops 268435456 | bytes 2621440 | tf_op jit(solution)/shard_map/own_panels/pallas_call | solution.py:239
  98.0 1.6 collective-permute-start.30
  100.1 2.4 %collective-permute-done.32.refs_14_ = bf16[256,512]{1,0:T(8,128)(2,1)S(1)} collective-permute-done((bf16[256,512]{1,0:T(8,128)(2,1)S(1)}, bf16[256,512]{1,0:T(8,128)(2,1)S(1)}, u32[]{:S(2)}, u32[]{:S(2)}) %collective-permute-start.32) | collective-permute-done | bytes 262176 | tf_op jit(solution)/shard_map/ppermute | solution.py:558
  102.5 0.9 select_select_fusion.1
  103.4 0.9 collective-permute-start.36
  104.3 1.5 collective-permute-start.37
  105.8 7.8 %update.3.refs_16_ = bf16[8192,1024]{1,0:T(8,128)(2,1)} custom-call(s32[8,46]{1,0:T(8,128)S(1)} %copy-done.7, s32[32,4]{1,0:T(8,128)S(1)} %copy.48.mask, s32[1]{0:T(128)} %bitcast.1.me, bf16[512,1024]{1,0:T(8,128)(2,1)S(1)} %get-tuple-element.264.own, bf16[8192,1024]{1,0:T(8,128)(2,1)} %bitcast.18, bf16[256,512]{1,0:T(8,128)(2,1)} %copy-done.9, ...), custom_call_target="tpu_custom_call" | custom-call | flops 4294967296 | bytes 16777216 | tf_op jit(solution)/shard_map/update/pallas_call | solution.py:404
  113.7 0.9 select_select_fusion
  114.6 3.3 %collective-permute-start.34 = (bf16[256,512]{1,0:T(8,128)(2,1)}, bf16[256,512]{1,0:T(8,128)(2,1)S(1)}, u32[]{:S(2)}, u32[]{:S(2)}) collective-permute-start(bf16[256,512]{1,0:T(8,128)(2,1)} %get-tuple-element.265), channel_id=1, source_target_pairs={{0,2},{1,3},{2,4},{3,5},{4,6},{5,7},{6,0},{7,1},{8,10},{9,11},{10,... | collective-permute-start | bytes 786440 | tf_op jit(solution)/shard_map/ppermute | solution.py:558
  118.4 3.5 %all-to-all-start = ((bf16[4,528,256]{2,1,0:T(8,128)(2,1)}), bf16[4,528,256]{2,1,0:T(8,128)(2,1)S(1)}, u32[]{:S(2)}, u32[]{:S(2)}) async-start(bf16[4,528,256]{2,1,0:T(8,128)(2,1)} %get-tuple-element.285), calls=%async_computation | async-start | bytes 2162688 | tf_op jit(solution)/shard_map/all_to_all | solution.py:528
  122.1 1.6 collective-permute-start.41
  125.1 7.8 %collective-permute-done.40.refs_6_ = bf16[256,512]{1,0:T(8,128)(2,1)S(1)} collective-permute-done((bf16[256,512]{1,0:T(8,128)(2,1)S(1)}, bf16[256,512]{1,0:T(8,128)(2,1)S(1)}, u32[]{:S(2)}, u32[]{:S(2)}) %collective-permute-start.40) | collective-permute-done | bytes 262176 | tf_op jit(solution)/shard_map/ppermute | solution.py:558
  133.8 4.3 %collective-permute-done.38.refs_8_ = bf16[256,512]{1,0:T(8,128)(2,1)S(1)} collective-permute-done((bf16[256,512]{1,0:T(8,128)(2,1)S(1)}, bf16[256,512]{1,0:T(8,128)(2,1)S(1)}, u32[]{:S(2)}, u32[]{:S(2)}) %collective-permute-start.38) | collective-permute-done | bytes 262176 | tf_op jit(solution)/shard_map/ppermute | solution.py:558
  139.8 1.8 %relay.1 = bf16[8,272,256]{2,1,0:T(8,128)(2,1)} custom-call(s32[4,2]{1,0:T(4,128)S(1)} %copy.50.labels, bf16[4,528,256]{2,1,0:T(8,128)(2,1)S(1)} %all-to-all-done.arrived), custom_call_target="tpu_custom_call" | custom-call | bytes 2097152 | tf_op jit(solution)/shard_map/relay/pallas_call | solution.py:279
  141.6 3.7 %all-to-all-start.1 = ((bf16[8,272,256]{2,1,0:T(8,128)(2,1)}), bf16[8,272,256]{2,1,0:T(8,128)(2,1)S(1)}, u32[]{:S(2)}, u32[]{:S(2)}) async-start(bf16[8,272,256]{2,1,0:T(8,128)(2,1)} %relay.1), calls=%async_computation.1 | async-start | bytes 2228224 | tf_op jit(solution)/shard_map/all_to_all | solution.py:528
  145.3 1.9 %collective-permute-start.42 = (bf16[256,512]{1,0:T(8,128)(2,1)S(1)}, bf16[256,512]{1,0:T(8,128)(2,1)S(1)}, u32[]{:S(2)}, u32[]{:S(2)}) collective-permute-start(bf16[256,512]{1,0:T(8,128)(2,1)S(1)} %copy-done.53), channel_id=1, source_target_pairs={{0,1},{1,0},{2,3},{3,2},{4,5},{5,4},{6,7},{7,6},{8,9},{9,8},{10,11... | collective-permute-start | bytes 786440 | tf_op jit(solution)/shard_map/ppermute | solution.py:558
  147.4 10.2 %update.4.refs_12_ = bf16[8192,1024]{1,0:T(8,128)(2,1)} custom-call(s32[8,46]{1,0:T(8,128)S(1)} %copy-done.7, s32[32,4]{1,0:T(8,128)S(1)} %copy.48.mask, s32[1]{0:T(128)} %bitcast.1.me, bf16[512,1024]{1,0:T(8,128)(2,1)S(1)} %get-tuple-element.264.own, bf16[8192,1024]{1,0:T(8,128)(2,1)} %bitcast.19, ...), custom_call_target="tpu_custom_call", output_to_operand_aliasing={{}: (21, {})} | custom-call | flops 4294967296 | bytes 16777216 | tf_op jit(solution)/shard_map/update/pallas_call | solution.py:404
  157.7 8.8 %collective-permute-done.42.refs_10_ = bf16[256,512]{1,0:T(8,128)(2,1)S(1)} collective-permute-done((bf16[256,512]{1,0:T(8,128)(2,1)S(1)}, bf16[256,512]{1,0:T(8,128)(2,1)S(1)}, u32[]{:S(2)}, u32[]{:S(2)}) %collective-permute-start.42) | collective-permute-done | bytes 262176 | tf_op jit(solution)/shard_map/ppermute | solution.py:558
  166.5 4.4 %collective-permute-done.43.refs_11_ = bf16[256,512]{1,0:T(8,128)(2,1)S(1)} collective-permute-done((bf16[256,512]{1,0:T(8,128)(2,1)S(1)}, bf16[256,512]{1,0:T(8,128)(2,1)S(1)}, u32[]{:S(2)}, u32[]{:S(2)}) %collective-permute-start.43) | collective-permute-done | bytes 262176 | tf_op jit(solution)/shard_map/ppermute | solution.py:558
  171.6 6.5 %update.5 = bf16[8192,1024]{1,0:T(8,128)(2,1)} custom-call(s32[8,46]{1,0:T(8,128)S(1)} %copy-done.7, s32[32,4]{1,0:T(8,128)S(1)} %copy.48.mask, s32[1]{0:T(128)} %bitcast.1.me, bf16[512,1024]{1,0:T(8,128)(2,1)S(1)} %get-tuple-element.264.own, bf16[8192,1024]{1,0:T(8,128)(2,1)} %bitcast.20, ...), custom_call_target="tpu_custom_call", output_to_operand_aliasing={{}: (17, {})} | custom-call | flops 3758096384 | bytes 14680064 | tf_op jit(solution)/shard_map/update/pallas_call | solution.py:404
  178.4 1.7 sum_parents.1
  (177 shorter events, 12.1 us)
Async XLA Ops:
  5.2 9.7 %copy-start.5 = (bf16[256,512]{1,0:T(8,128)(2,1)}, bf16[256,512]{1,0:T(8,128)(2,1)S(1)}, u32[]{:S(2)}) copy-start(bf16[256,512]{1,0:T(8,128)(2,1)S(1)} %get-tuple-element.151.refs_18_) | copy-start | bytes 786436
  5.2 12.2 %collective-permute-start = (bf16[256,512]{1,0:T(8,128)(2,1)S(1)}, bf16[256,512]{1,0:T(8,128)(2,1)S(1)}, u32[]{:S(2)}, u32[]{:S(2)}) collective-permute-start(bf16[256,512]{1,0:T(8,128)(2,1)S(1)} %get-tuple-element.151.refs_18_), channel_id=1, source_target_pairs={{0,2},{1,3},{2,4},{3,5},{4,6},{5,7},{6,0},{7,1},{8,10},{9,11},{10,... | collective-permute-start | bytes 786440 | tf_op jit(solution)/shard_map/ppermute | solution.py:558
  8.3 9.2 %collective-permute-start.1 = (bf16[256,512]{1,0:T(8,128)(2,1)S(1)}, bf16[256,512]{1,0:T(8,128)(2,1)S(1)}, u32[]{:S(2)}, u32[]{:S(2)}) collective-permute-start(bf16[256,512]{1,0:T(8,128)(2,1)S(1)} %get-tuple-element.152), channel_id=1, source_target_pairs={{0,1},{1,0},{2,3},{3,2},{4,5},{5,4},{6,7},{7,6},{8,9},{9,8},{10,11... | collective-permute-start | bytes 786440 | tf_op jit(solution)/shard_map/ppermute | solution.py:558
  9.8 13.3 %collective-permute-start.4 = (bf16[256,512]{1,0:T(8,128)(2,1)S(1)}, bf16[256,512]{1,0:T(8,128)(2,1)S(1)}, u32[]{:S(2)}, u32[]{:S(2)}) collective-permute-start(bf16[256,512]{1,0:T(8,128)(2,1)S(1)} %get-tuple-element.153), channel_id=1, source_target_pairs={{0,2},{1,3},{2,4},{3,5},{4,6},{5,7},{6,0},{7,1},{8,10},{9,11},{10,... | collective-permute-start | bytes 786440 | tf_op jit(solution)/shard_map/ppermute | solution.py:558
  11.4 11.8 %collective-permute-start.5 = (bf16[256,512]{1,0:T(8,128)(2,1)S(1)}, bf16[256,512]{1,0:T(8,128)(2,1)S(1)}, u32[]{:S(2)}, u32[]{:S(2)}) collective-permute-start(bf16[256,512]{1,0:T(8,128)(2,1)S(1)} %get-tuple-element.154), channel_id=1, source_target_pairs={{0,1},{1,0},{2,3},{3,2},{4,5},{5,4},{6,7},{7,6},{8,9},{9,8},{10,11... | collective-permute-start | bytes 786440 | tf_op jit(solution)/shard_map/ppermute | solution.py:558
  17.6 11.8 %collective-permute-start.2 = (bf16[256,512]{1,0:T(8,128)(2,1)S(1)}, bf16[256,512]{1,0:T(8,128)(2,1)S(1)}, u32[]{:S(2)}, u32[]{:S(2)}) collective-permute-start(bf16[256,512]{1,0:T(8,128)(2,1)S(1)} %get-tuple-element.161), channel_id=1, source_target_pairs={{0,2},{1,3},{2,4},{3,5},{4,6},{5,7},{6,0},{7,1},{8,10},{9,11},{10,... | collective-permute-start | bytes 786440 | tf_op jit(solution)/shard_map/ppermute | solution.py:558
  19.2 10.2 %collective-permute-start.3 = (bf16[256,512]{1,0:T(8,128)(2,1)S(1)}, bf16[256,512]{1,0:T(8,128)(2,1)S(1)}, u32[]{:S(2)}, u32[]{:S(2)}) collective-permute-start(bf16[256,512]{1,0:T(8,128)(2,1)S(1)} %get-tuple-element.162), channel_id=1, source_target_pairs={{0,1},{1,0},{2,3},{3,2},{4,5},{5,4},{6,7},{7,6},{8,9},{9,8},{10,11... | collective-permute-start | bytes 786440 | tf_op jit(solution)/shard_map/ppermute | solution.py:558
  23.0 6.3 %copy-start.29 = (bf16[256,512]{1,0:T(8,128)(2,1)}, bf16[256,512]{1,0:T(8,128)(2,1)S(1)}, u32[]{:S(2)}) copy-start(bf16[256,512]{1,0:T(8,128)(2,1)S(1)} %collective-permute-done.4.refs_2_) | copy-start | bytes 786436
  23.1 6.2 %copy-start.30 = (bf16[256,512]{1,0:T(8,128)(2,1)}, bf16[256,512]{1,0:T(8,128)(2,1)S(1)}, u32[]{:S(2)}) copy-start(bf16[256,512]{1,0:T(8,128)(2,1)S(1)} %collective-permute-done.5.refs_3_) | copy-start | bytes 786436
  23.2 11.1 %collective-permute-start.8 = (bf16[256,512]{1,0:T(8,128)(2,1)S(1)}, bf16[256,512]{1,0:T(8,128)(2,1)S(1)}, u32[]{:S(2)}, u32[]{:S(2)}) collective-permute-start(bf16[256,512]{1,0:T(8,128)(2,1)S(1)} %get-tuple-element.170), channel_id=1, source_target_pairs={{0,2},{1,3},{2,4},{3,5},{4,6},{5,7},{6,0},{7,1},{8,10},{9,11},{10,... | collective-permute-start | bytes 786440 | tf_op jit(solution)/shard_map/ppermute | solution.py:558
  24.8 9.5 %collective-permute-start.9 = (bf16[256,512]{1,0:T(8,128)(2,1)S(1)}, bf16[256,512]{1,0:T(8,128)(2,1)S(1)}, u32[]{:S(2)}, u32[]{:S(2)}) collective-permute-start(bf16[256,512]{1,0:T(8,128)(2,1)S(1)} %get-tuple-element.171), channel_id=1, source_target_pairs={{0,1},{1,0},{2,3},{3,2},{4,5},{5,4},{6,7},{7,6},{8,9},{9,8},{10,11... | collective-permute-start | bytes 786440 | tf_op jit(solution)/shard_map/ppermute | solution.py:558
  29.5 11.1 %collective-permute-start.6 = (bf16[256,512]{1,0:T(8,128)(2,1)S(1)}, bf16[256,512]{1,0:T(8,128)(2,1)S(1)}, u32[]{:S(2)}, u32[]{:S(2)}) collective-permute-start(bf16[256,512]{1,0:T(8,128)(2,1)S(1)} %get-tuple-element.175), channel_id=1, source_target_pairs={{0,2},{1,3},{2,4},{3,5},{4,6},{5,7},{6,0},{7,1},{8,10},{9,11},{10,... | collective-permute-start | bytes 786440 | tf_op jit(solution)/shard_map/ppermute | solution.py:558
  31.1 9.5 %collective-permute-start.7 = (bf16[256,512]{1,0:T(8,128)(2,1)S(1)}, bf16[256,512]{1,0:T(8,128)(2,1)S(1)}, u32[]{:S(2)}, u32[]{:S(2)}) collective-permute-start(bf16[256,512]{1,0:T(8,128)(2,1)S(1)} %get-tuple-element.176), channel_id=1, source_target_pairs={{0,1},{1,0},{2,3},{3,2},{4,5},{5,4},{6,7},{7,6},{8,9},{9,8},{10,11... | collective-permute-start | bytes 786440 | tf_op jit(solution)/shard_map/ppermute | solution.py:558
  34.3 6.3 %copy-start.31 = (bf16[256,512]{1,0:T(8,128)(2,1)}, bf16[256,512]{1,0:T(8,128)(2,1)S(1)}, u32[]{:S(2)}) copy-start(bf16[256,512]{1,0:T(8,128)(2,1)S(1)} %collective-permute-done.8.refs_6_) | copy-start | bytes 786436
  34.4 6.2 %copy-start.32 = (bf16[256,512]{1,0:T(8,128)(2,1)}, bf16[256,512]{1,0:T(8,128)(2,1)S(1)}, u32[]{:S(2)}) copy-start(bf16[256,512]{1,0:T(8,128)(2,1)S(1)} %collective-permute-done.9.refs_7_) | copy-start | bytes 786436
  34.4 11.7 %collective-permute-start.12 = (bf16[256,512]{1,0:T(8,128)(2,1)S(1)}, bf16[256,512]{1,0:T(8,128)(2,1)S(1)}, u32[]{:S(2)}, u32[]{:S(2)}) collective-permute-start(bf16[256,512]{1,0:T(8,128)(2,1)S(1)} %get-tuple-element.184), channel_id=1, source_target_pairs={{0,2},{1,3},{2,4},{3,5},{4,6},{5,7},{6,0},{7,1},{8,10},{9,11},{10,... | collective-permute-start | bytes 786440 | tf_op jit(solution)/shard_map/ppermute | solution.py:558
  36.1 10.1 %collective-permute-start.13 = (bf16[256,512]{1,0:T(8,128)(2,1)S(1)}, bf16[256,512]{1,0:T(8,128)(2,1)S(1)}, u32[]{:S(2)}, u32[]{:S(2)}) collective-permute-start(bf16[256,512]{1,0:T(8,128)(2,1)S(1)} %get-tuple-element.185), channel_id=1, source_target_pairs={{0,1},{1,0},{2,3},{3,2},{4,5},{5,4},{6,7},{7,6},{8,9},{9,8},{10,11... | collective-permute-start | bytes 786440 | tf_op jit(solution)/shard_map/ppermute | solution.py:558
  40.7 11.1 %collective-permute-start.10 = (bf16[256,512]{1,0:T(8,128)(2,1)S(1)}, bf16[256,512]{1,0:T(8,128)(2,1)S(1)}, u32[]{:S(2)}, u32[]{:S(2)}) collective-permute-start(bf16[256,512]{1,0:T(8,128)(2,1)S(1)} %get-tuple-element.189), channel_id=1, source_target_pairs={{0,2},{1,3},{2,4},{3,5},{4,6},{5,7},{6,0},{7,1},{8,10},{9,11},{10,... | collective-permute-start | bytes 786440 | tf_op jit(solution)/shard_map/ppermute | solution.py:558
  42.3 9.5 %collective-permute-start.11 = (bf16[256,512]{1,0:T(8,128)(2,1)S(1)}, bf16[256,512]{1,0:T(8,128)(2,1)S(1)}, u32[]{:S(2)}, u32[]{:S(2)}) collective-permute-start(bf16[256,512]{1,0:T(8,128)(2,1)S(1)} %get-tuple-element.190), channel_id=1, source_target_pairs={{0,1},{1,0},{2,3},{3,2},{4,5},{5,4},{6,7},{7,6},{8,9},{9,8},{10,11... | collective-permute-start | bytes 786440 | tf_op jit(solution)/shard_map/ppermute | solution.py:558
  46.3 11.1 %collective-permute-start.16 = (bf16[256,512]{1,0:T(8,128)(2,1)S(1)}, bf16[256,512]{1,0:T(8,128)(2,1)S(1)}, u32[]{:S(2)}, u32[]{:S(2)}) collective-permute-start(bf16[256,512]{1,0:T(8,128)(2,1)S(1)} %get-tuple-element.198), channel_id=1, source_target_pairs={{0,2},{1,3},{2,4},{3,5},{4,6},{5,7},{6,0},{7,1},{8,10},{9,11},{10,... | collective-permute-start | bytes 786440 | tf_op jit(solution)/shard_map/ppermute | solution.py:558
  47.3 10.1 %collective-permute-start.17 = (bf16[256,512]{1,0:T(8,128)(2,1)S(1)}, bf16[256,512]{1,0:T(8,128)(2,1)S(1)}, u32[]{:S(2)}, u32[]{:S(2)}) collective-permute-start(bf16[256,512]{1,0:T(8,128)(2,1)S(1)} %get-tuple-element.199), channel_id=1, source_target_pairs={{0,1},{1,0},{2,3},{3,2},{4,5},{5,4},{6,7},{7,6},{8,9},{9,8},{10,11... | collective-permute-start | bytes 786440 | tf_op jit(solution)/shard_map/ppermute | solution.py:558
  51.9 11.1 %collective-permute-start.14 = (bf16[256,512]{1,0:T(8,128)(2,1)S(1)}, bf16[256,512]{1,0:T(8,128)(2,1)S(1)}, u32[]{:S(2)}, u32[]{:S(2)}) collective-permute-start(bf16[256,512]{1,0:T(8,128)(2,1)S(1)} %get-tuple-element.203), channel_id=1, source_target_pairs={{0,2},{1,3},{2,4},{3,5},{4,6},{5,7},{6,0},{7,1},{8,10},{9,11},{10,... | collective-permute-start | bytes 786440 | tf_op jit(solution)/shard_map/ppermute | solution.py:558
  53.6 9.5 %collective-permute-start.15 = (bf16[256,512]{1,0:T(8,128)(2,1)S(1)}, bf16[256,512]{1,0:T(8,128)(2,1)S(1)}, u32[]{:S(2)}, u32[]{:S(2)}) collective-permute-start(bf16[256,512]{1,0:T(8,128)(2,1)S(1)} %get-tuple-element.204), channel_id=1, source_target_pairs={{0,1},{1,0},{2,3},{3,2},{4,5},{5,4},{6,7},{7,6},{8,9},{9,8},{10,11... | collective-permute-start | bytes 786440 | tf_op jit(solution)/shard_map/ppermute | solution.py:558
  57.5 11.1 %collective-permute-start.20 = (bf16[256,512]{1,0:T(8,128)(2,1)S(1)}, bf16[256,512]{1,0:T(8,128)(2,1)S(1)}, u32[]{:S(2)}, u32[]{:S(2)}) collective-permute-start(bf16[256,512]{1,0:T(8,128)(2,1)S(1)} %get-tuple-element.212), channel_id=1, source_target_pairs={{0,2},{1,3},{2,4},{3,5},{4,6},{5,7},{6,0},{7,1},{8,10},{9,11},{10,... | collective-permute-start | bytes 786440 | tf_op jit(solution)/shard_map/ppermute | solution.py:558
  58.5 10.1 %collective-permute-start.21 = (bf16[256,512]{1,0:T(8,128)(2,1)S(1)}, bf16[256,512]{1,0:T(8,128)(2,1)S(1)}, u32[]{:S(2)}, u32[]{:S(2)}) collective-permute-start(bf16[256,512]{1,0:T(8,128)(2,1)S(1)} %get-tuple-element.213), channel_id=1, source_target_pairs={{0,1},{1,0},{2,3},{3,2},{4,5},{5,4},{6,7},{7,6},{8,9},{9,8},{10,11... | collective-permute-start | bytes 786440 | tf_op jit(solution)/shard_map/ppermute | solution.py:558
  63.2 11.3 %collective-permute-start.18 = (bf16[256,512]{1,0:T(8,128)(2,1)S(1)}, bf16[256,512]{1,0:T(8,128)(2,1)S(1)}, u32[]{:S(2)}, u32[]{:S(2)}) collective-permute-start(bf16[256,512]{1,0:T(8,128)(2,1)S(1)} %get-tuple-element.217), channel_id=1, source_target_pairs={{0,2},{1,3},{2,4},{3,5},{4,6},{5,7},{6,0},{7,1},{8,10},{9,11},{10,... | collective-permute-start | bytes 786440 | tf_op jit(solution)/shard_map/ppermute | solution.py:558
  64.8 9.7 %collective-permute-start.19 = (bf16[256,512]{1,0:T(8,128)(2,1)S(1)}, bf16[256,512]{1,0:T(8,128)(2,1)S(1)}, u32[]{:S(2)}, u32[]{:S(2)}) collective-permute-start(bf16[256,512]{1,0:T(8,128)(2,1)S(1)} %get-tuple-element.218), channel_id=1, source_target_pairs={{0,1},{1,0},{2,3},{3,2},{4,5},{5,4},{6,7},{7,6},{8,9},{9,8},{10,11... | collective-permute-start | bytes 786440 | tf_op jit(solution)/shard_map/ppermute | solution.py:558
  68.6 5.8 %copy-start.13 = (bf16[256,512]{1,0:T(8,128)(2,1)}, bf16[256,512]{1,0:T(8,128)(2,1)S(1)}, u32[]{:S(2)}) copy-start(bf16[256,512]{1,0:T(8,128)(2,1)S(1)} %collective-permute-done.20.refs_8_.refs_2_) | copy-start | bytes 786436
  68.7 11.3 %collective-permute-start.24 = (bf16[256,512]{1,0:T(8,128)(2,1)S(1)}, bf16[256,512]{1,0:T(8,128)(2,1)S(1)}, u32[]{:S(2)}, u32[]{:S(2)}) collective-permute-start(bf16[256,512]{1,0:T(8,128)(2,1)S(1)} %get-tuple-element.226), channel_id=1, source_target_pairs={{0,2},{1,3},{2,4},{3,5},{4,6},{5,7},{6,0},{7,1},{8,10},{9,11},{10,... | collective-permute-start | bytes 786440 | tf_op jit(solution)/shard_map/ppermute | solution.py:558
  70.0 10.1 %collective-permute-start.25 = (bf16[256,512]{1,0:T(8,128)(2,1)S(1)}, bf16[256,512]{1,0:T(8,128)(2,1)S(1)}, u32[]{:S(2)}, u32[]{:S(2)}) collective-permute-start(bf16[256,512]{1,0:T(8,128)(2,1)S(1)} %get-tuple-element.227), channel_id=1, source_target_pairs={{0,1},{1,0},{2,3},{3,2},{4,5},{5,4},{6,7},{7,6},{8,9},{9,8},{10,11... | collective-permute-start | bytes 786440 | tf_op jit(solution)/shard_map/ppermute | solution.py:558
  74.6 11.0 %collective-permute-start.22 = (bf16[256,512]{1,0:T(8,128)(2,1)S(1)}, bf16[256,512]{1,0:T(8,128)(2,1)S(1)}, u32[]{:S(2)}, u32[]{:S(2)}) collective-permute-start(bf16[256,512]{1,0:T(8,128)(2,1)S(1)} %get-tuple-element.231), channel_id=1, source_target_pairs={{0,2},{1,3},{2,4},{3,5},{4,6},{5,7},{6,0},{7,1},{8,10},{9,11},{10,... | collective-permute-start | bytes 786440 | tf_op jit(solution)/shard_map/ppermute | solution.py:558
  76.2 9.4 %collective-permute-start.23 = (bf16[256,512]{1,0:T(8,128)(2,1)S(1)}, bf16[256,512]{1,0:T(8,128)(2,1)S(1)}, u32[]{:S(2)}, u32[]{:S(2)}) collective-permute-start(bf16[256,512]{1,0:T(8,128)(2,1)S(1)} %get-tuple-element.232), channel_id=1, source_target_pairs={{0,1},{1,0},{2,3},{3,2},{4,5},{5,4},{6,7},{7,6},{8,9},{9,8},{10,11... | collective-permute-start | bytes 786440 | tf_op jit(solution)/shard_map/ppermute | solution.py:558
  80.1 11.1 %collective-permute-start.28 = (bf16[256,512]{1,0:T(8,128)(2,1)S(1)}, bf16[256,512]{1,0:T(8,128)(2,1)S(1)}, u32[]{:S(2)}, u32[]{:S(2)}) collective-permute-start(bf16[256,512]{1,0:T(8,128)(2,1)S(1)} %get-tuple-element.240), channel_id=1, source_target_pairs={{0,2},{1,3},{2,4},{3,5},{4,6},{5,7},{6,0},{7,1},{8,10},{9,11},{10,... | collective-permute-start | bytes 786440 | tf_op jit(solution)/shard_map/ppermute | solution.py:558
  81.0 10.3 %collective-permute-start.29 = (bf16[256,512]{1,0:T(8,128)(2,1)S(1)}, bf16[256,512]{1,0:T(8,128)(2,1)S(1)}, u32[]{:S(2)}, u32[]{:S(2)}) collective-permute-start(bf16[256,512]{1,0:T(8,128)(2,1)S(1)} %get-tuple-element.241), channel_id=1, source_target_pairs={{0,1},{1,0},{2,3},{3,2},{4,5},{5,4},{6,7},{7,6},{8,9},{9,8},{10,11... | collective-permute-start | bytes 786440 | tf_op jit(solution)/shard_map/ppermute | solution.py:558
  85.5 5.8 %copy-start = (bf16[256,512]{1,0:T(8,128)(2,1)}, bf16[256,512]{1,0:T(8,128)(2,1)S(1)}, u32[]{:S(2)}) copy-start(bf16[256,512]{1,0:T(8,128)(2,1)S(1)} %get-tuple-element.247.refs_14_) | copy-start | bytes 786436
  85.5 5.8 %copy-start.2 = (bf16[256,512]{1,0:T(8,128)(2,1)}, bf16[256,512]{1,0:T(8,128)(2,1)S(1)}, u32[]{:S(2)}) copy-start(bf16[256,512]{1,0:T(8,128)(2,1)S(1)} %get-tuple-element.235.refs_5_) | copy-start | bytes 786436
  85.6 5.8 %copy-start.4 = (bf16[256,512]{1,0:T(8,128)(2,1)}, bf16[256,512]{1,0:T(8,128)(2,1)S(1)}, u32[]{:S(2)}) copy-start(bf16[256,512]{1,0:T(8,128)(2,1)S(1)} %get-tuple-element.244.refs_11_) | copy-start | bytes 786436
  85.7 8.1 %copy-start.8 = (s32[1,1,4]{2,1,0:T(1,128)S(1)}, s32[1,1,4]{2,1,0:T(1,128)}, u32[]{:S(2)}) copy-start(s32[1,1,4]{2,1,0:T(1,128)} %param.8) | copy-start | bytes 52
  85.7 12.1 %collective-permute-start.26 = (bf16[256,512]{1,0:T(8,128)(2,1)S(1)}, bf16[256,512]{1,0:T(8,128)(2,1)S(1)}, u32[]{:S(2)}, u32[]{:S(2)}) collective-permute-start(bf16[256,512]{1,0:T(8,128)(2,1)S(1)} %get-tuple-element.245), channel_id=1, source_target_pairs={{0,2},{1,3},{2,4},{3,5},{4,6},{5,7},{6,0},{7,1},{8,10},{9,11},{10,... | collective-permute-start | bytes 786440 | tf_op jit(solution)/shard_map/ppermute | solution.py:558
  87.4 10.5 %collective-permute-start.27 = (bf16[256,512]{1,0:T(8,128)(2,1)S(1)}, bf16[256,512]{1,0:T(8,128)(2,1)S(1)}, u32[]{:S(2)}, u32[]{:S(2)}) collective-permute-start(bf16[256,512]{1,0:T(8,128)(2,1)S(1)} %get-tuple-element.246), channel_id=1, source_target_pairs={{0,1},{1,0},{2,3},{3,2},{4,5},{5,4},{6,7},{7,6},{8,9},{9,8},{10,11... | collective-permute-start | bytes 786440 | tf_op jit(solution)/shard_map/ppermute | solution.py:558
  91.4 11.1 %collective-permute-start.32 = (bf16[256,512]{1,0:T(8,128)(2,1)S(1)}, bf16[256,512]{1,0:T(8,128)(2,1)S(1)}, u32[]{:S(2)}, u32[]{:S(2)}) collective-permute-start(bf16[256,512]{1,0:T(8,128)(2,1)S(1)} %get-tuple-element.250), channel_id=1, source_target_pairs={{0,2},{1,3},{2,4},{3,5},{4,6},{5,7},{6,0},{7,1},{8,10},{9,11},{10,... | collective-permute-start | bytes 786440 | tf_op jit(solution)/shard_map/ppermute | solution.py:558
  92.3 10.2 %collective-permute-start.33 = (bf16[256,512]{1,0:T(8,128)(2,1)S(1)}, bf16[256,512]{1,0:T(8,128)(2,1)S(1)}, u32[]{:S(2)}, u32[]{:S(2)}) collective-permute-start(bf16[256,512]{1,0:T(8,128)(2,1)S(1)} %get-tuple-element.251), channel_id=1, source_target_pairs={{0,1},{1,0},{2,3},{3,2},{4,5},{5,4},{6,7},{7,6},{8,9},{9,8},{10,11... | collective-permute-start | bytes 786440 | tf_op jit(solution)/shard_map/ppermute | solution.py:558
  97.8 8.0 %copy-start.7 = (s32[8,46]{1,0:T(8,128)S(1)}, s32[8,46]{1,0:T(8,128)}, u32[]{:S(2)}) copy-start(s32[8,46]{1,0:T(8,128)} %constant.14.clone.table) | copy-start | bytes 4420
  98.0 15.6 %collective-permute-start.30 = (bf16[256,512]{1,0:T(8,128)(2,1)S(1)}, bf16[256,512]{1,0:T(8,128)(2,1)S(1)}, u32[]{:S(2)}, u32[]{:S(2)}) collective-permute-start(bf16[256,512]{1,0:T(8,128)(2,1)S(1)} %get-tuple-element.254), channel_id=1, source_target_pairs={{0,2},{1,3},{2,4},{3,5},{4,6},{5,7},{6,0},{7,1},{8,10},{9,11},{10,... | collective-permute-start | bytes 786440 | tf_op jit(solution)/shard_map/ppermute | solution.py:558
  99.6 14.0 %collective-permute-start.31 = (bf16[256,512]{1,0:T(8,128)(2,1)S(1)}, bf16[256,512]{1,0:T(8,128)(2,1)S(1)}, u32[]{:S(2)}, u32[]{:S(2)}) collective-permute-start(bf16[256,512]{1,0:T(8,128)(2,1)S(1)} %get-tuple-element.255), channel_id=1, source_target_pairs={{0,1},{1,0},{2,3},{3,2},{4,5},{5,4},{6,7},{7,6},{8,9},{9,8},{10,11... | collective-permute-start | bytes 786440 | tf_op jit(solution)/shard_map/ppermute | solution.py:558
  102.5 11.1 %copy-start.44 = (bf16[256,512]{1,0:T(8,128)(2,1)}, bf16[256,512]{1,0:T(8,128)(2,1)S(1)}, u32[]{:S(2)}) copy-start(bf16[256,512]{1,0:T(8,128)(2,1)S(1)} %collective-permute-done.33.refs_15_) | copy-start | bytes 786436
  103.4 18.5 %collective-permute-start.36 = (bf16[256,512]{1,0:T(8,128)(2,1)}, bf16[256,512]{1,0:T(8,128)(2,1)S(1)}, u32[]{:S(2)}, u32[]{:S(2)}) collective-permute-start(bf16[256,512]{1,0:T(8,128)(2,1)} %get-tuple-element.258), channel_id=1, source_target_pairs={{0,2},{1,3},{2,4},{3,5},{4,6},{5,7},{6,0},{7,1},{8,10},{9,11},{10,... | collective-permute-start | bytes 786440 | tf_op jit(solution)/shard_map/ppermute | solution.py:558
  104.3 17.6 %collective-permute-start.37 = (bf16[256,512]{1,0:T(8,128)(2,1)}, bf16[256,512]{1,0:T(8,128)(2,1)S(1)}, u32[]{:S(2)}, u32[]{:S(2)}) collective-permute-start(bf16[256,512]{1,0:T(8,128)(2,1)} %get-tuple-element.259), channel_id=1, source_target_pairs={{0,1},{1,0},{2,3},{3,2},{4,5},{5,4},{6,7},{7,6},{8,9},{9,8},{10,11... | collective-permute-start | bytes 786440 | tf_op jit(solution)/shard_map/ppermute | solution.py:558
  105.8 7.8 %copy-start.1 = (bf16[256,512]{1,0:T(8,128)(2,1)S(1)}, bf16[256,512]{1,0:T(8,128)(2,1)}, u32[]{:S(2)}) copy-start(bf16[256,512]{1,0:T(8,128)(2,1)} %copy-done) | copy-start | bytes 786436
  114.6 9.0 %collective-permute-start.34 = (bf16[256,512]{1,0:T(8,128)(2,1)}, bf16[256,512]{1,0:T(8,128)(2,1)S(1)}, u32[]{:S(2)}, u32[]{:S(2)}) collective-permute-start(bf16[256,512]{1,0:T(8,128)(2,1)} %get-tuple-element.265), channel_id=1, source_target_pairs={{0,2},{1,3},{2,4},{3,5},{4,6},{5,7},{6,0},{7,1},{8,10},{9,11},{10,... | collective-permute-start | bytes 786440 | tf_op jit(solution)/shard_map/ppermute | solution.py:558
  117.9 6.6 %collective-permute-start.35 = (bf16[256,512]{1,0:T(8,128)(2,1)}, bf16[256,512]{1,0:T(8,128)(2,1)S(1)}, u32[]{:S(2)}, u32[]{:S(2)}) collective-permute-start(bf16[256,512]{1,0:T(8,128)(2,1)} %get-tuple-element.266), channel_id=1, source_target_pairs={{0,1},{1,0},{2,3},{3,2},{4,5},{5,4},{6,7},{7,6},{8,9},{9,8},{10,11... | collective-permute-start | bytes 786440 | tf_op jit(solution)/shard_map/ppermute | solution.py:558
  118.4 21.2 %all-to-all-start = ((bf16[4,528,256]{2,1,0:T(8,128)(2,1)}), bf16[4,528,256]{2,1,0:T(8,128)(2,1)S(1)}, u32[]{:S(2)}, u32[]{:S(2)}) async-start(bf16[4,528,256]{2,1,0:T(8,128)(2,1)} %get-tuple-element.285), calls=%async_computation | async-start | bytes 2162688 | tf_op jit(solution)/shard_map/all_to_all | solution.py:528
  121.9 11.9 %copy-start.37 = (bf16[256,512]{1,0:T(8,128)(2,1)}, bf16[256,512]{1,0:T(8,128)(2,1)S(1)}, u32[]{:S(2)}) copy-start(bf16[256,512]{1,0:T(8,128)(2,1)S(1)} %collective-permute-done.36.refs_2_) | copy-start | bytes 786436
  122.0 11.9 %copy-start.38 = (bf16[256,512]{1,0:T(8,128)(2,1)}, bf16[256,512]{1,0:T(8,128)(2,1)S(1)}, u32[]{:S(2)}) copy-start(bf16[256,512]{1,0:T(8,128)(2,1)S(1)} %collective-permute-done.37.refs_3_) | copy-start | bytes 786436
  122.0 11.0 %collective-permute-start.40 = (bf16[256,512]{1,0:T(8,128)(2,1)S(1)}, bf16[256,512]{1,0:T(8,128)(2,1)S(1)}, u32[]{:S(2)}, u32[]{:S(2)}) collective-permute-start(bf16[256,512]{1,0:T(8,128)(2,1)S(1)} %get-tuple-element.269), channel_id=1, source_target_pairs={{0,2},{1,3},{2,4},{3,5},{4,6},{5,7},{6,0},{7,1},{8,10},{9,11},{10,... | collective-permute-start | bytes 786440 | tf_op jit(solution)/shard_map/ppermute | solution.py:558
  122.1 10.9 %collective-permute-start.41 = (bf16[256,512]{1,0:T(8,128)(2,1)S(1)}, bf16[256,512]{1,0:T(8,128)(2,1)S(1)}, u32[]{:S(2)}, u32[]{:S(2)}) collective-permute-start(bf16[256,512]{1,0:T(8,128)(2,1)S(1)} %get-tuple-element.270), channel_id=1, source_target_pairs={{0,1},{1,0},{2,3},{3,2},{4,5},{5,4},{6,7},{7,6},{8,9},{9,8},{10,11... | collective-permute-start | bytes 786440 | tf_op jit(solution)/shard_map/ppermute | solution.py:558
  123.6 15.9 %copy-start.39 = (bf16[256,512]{1,0:T(8,128)(2,1)}, bf16[256,512]{1,0:T(8,128)(2,1)S(1)}, u32[]{:S(2)}) copy-start(bf16[256,512]{1,0:T(8,128)(2,1)S(1)} %collective-permute-done.34.refs_4_) | copy-start | bytes 786436
  124.4 15.1 %copy-start.40 = (bf16[256,512]{1,0:T(8,128)(2,1)}, bf16[256,512]{1,0:T(8,128)(2,1)S(1)}, u32[]{:S(2)}) copy-start(bf16[256,512]{1,0:T(8,128)(2,1)S(1)} %collective-permute-done.35.refs_5_) | copy-start | bytes 786436
  124.5 13.6 %collective-permute-start.38 = (bf16[256,512]{1,0:T(8,128)(2,1)S(1)}, bf16[256,512]{1,0:T(8,128)(2,1)S(1)}, u32[]{:S(2)}, u32[]{:S(2)}) collective-permute-start(bf16[256,512]{1,0:T(8,128)(2,1)S(1)} %get-tuple-element.273), channel_id=1, source_target_pairs={{0,2},{1,3},{2,4},{3,5},{4,6},{5,7},{6,0},{7,1},{8,10},{9,11},{10,... | collective-permute-start | bytes 786440 | tf_op jit(solution)/shard_map/ppermute | solution.py:558
  124.6 13.6 %collective-permute-start.39 = (bf16[256,512]{1,0:T(8,128)(2,1)S(1)}, bf16[256,512]{1,0:T(8,128)(2,1)S(1)}, u32[]{:S(2)}, u32[]{:S(2)}) collective-permute-start(bf16[256,512]{1,0:T(8,128)(2,1)S(1)} %get-tuple-element.274), channel_id=1, source_target_pairs={{0,1},{1,0},{2,3},{3,2},{4,5},{5,4},{6,7},{7,6},{8,9},{9,8},{10,11... | collective-permute-start | bytes 786440 | tf_op jit(solution)/shard_map/ppermute | solution.py:558
  133.0 8.7 %copy-start.47 = (bf16[256,512]{1,0:T(8,128)(2,1)}, bf16[256,512]{1,0:T(8,128)(2,1)S(1)}, u32[]{:S(2)}) copy-start(bf16[256,512]{1,0:T(8,128)(2,1)S(1)} %collective-permute-done.40.refs_6_) | copy-start | bytes 786436
  141.6 36.5 %all-to-all-start.1 = ((bf16[8,272,256]{2,1,0:T(8,128)(2,1)}), bf16[8,272,256]{2,1,0:T(8,128)(2,1)S(1)}, u32[]{:S(2)}, u32[]{:S(2)}) async-start(bf16[8,272,256]{2,1,0:T(8,128)(2,1)} %relay.1), calls=%async_computation.1 | async-start | bytes 2228224 | tf_op jit(solution)/shard_map/all_to_all | solution.py:528
  145.3 21.1 %collective-permute-start.42 = (bf16[256,512]{1,0:T(8,128)(2,1)S(1)}, bf16[256,512]{1,0:T(8,128)(2,1)S(1)}, u32[]{:S(2)}, u32[]{:S(2)}) collective-permute-start(bf16[256,512]{1,0:T(8,128)(2,1)S(1)} %copy-done.53), channel_id=1, source_target_pairs={{0,1},{1,0},{2,3},{3,2},{4,5},{5,4},{6,7},{7,6},{8,9},{9,8},{10,11... | collective-permute-start | bytes 786440 | tf_op jit(solution)/shard_map/ppermute | solution.py:558
  147.3 23.6 %collective-permute-start.43 = (bf16[256,512]{1,0:T(8,128)(2,1)S(1)}, bf16[256,512]{1,0:T(8,128)(2,1)S(1)}, u32[]{:S(2)}, u32[]{:S(2)}) collective-permute-start(bf16[256,512]{1,0:T(8,128)(2,1)S(1)} %broadcast_select_fusion), channel_id=1, source_target_pairs={{0,1},{1,0},{2,3},{3,2},{4,5},{5,4},{6,7},{7,6},{8,9},{9,8},{10,11... | collective-permute-start | bytes 786440 | tf_op jit(solution)/shard_map/ppermute | solution.py:558
  (36 other events, 165.5 us)

commit v6 on v5

--- a/solution.py
+++ b/solution.py
@@ -9,7 +9,6 @@
 
 TILE = 256
 CHAINS = 2
-RELAY_AFTER = 7
 LABEL_ROWS = 16
 VMEM_LIMIT = 16 * 1024 * 1024
 UPDATE_LIMIT = 32 * 1024 * 1024
@@ -455,7 +454,7 @@
     perms, rules = routes(n_grp)
     lists = stream_plan(perms, rules, n_grp, tiles, cols_dev, rows_out)
     if n_grp == 8:
-        lists[1] += lists[0][-2 * CHAINS :]
+        lists = [lists[0] + lists[1][-1:], lists[1] + lists[0][-2 * CHAINS :]]
     got = travel(perms, rules, lists, n_grp, tiles)
     events = len(got)
     longest = max(len(lists[0]), len(lists[1]))
@@ -529,7 +528,7 @@
 
     def relayed(arrived):
         digits = arrived[:, 2 * TILE, :4].astype(jnp.int32).reshape(n_front, 2, 2)
-        return exchange(relay(digits[..., 0] * 32 + digits[..., 1], arrived, slots_dev, n_grp), "grp")
+        return relay(digits[..., 0] * 32 + digits[..., 1], arrived, slots_dev, n_grp)
 
     held, turn, result, done = [], (), None, 0
 
@@ -541,7 +540,6 @@
         blocks = [held[n // 2][n % 2] for n in numbers]
         result = update(rows, mask, here, own, front, numbers, blocks, 2 * count, base=result)
 
-    relay_after = min(RELAY_AFTER, events - 1 - ready - CHAINS)
     for e in range(events):
         values = []
         for s in (0, 1):
@@ -564,13 +562,13 @@
             own, sends = own_part()
         if late == 1:
             arrived = exchange(after((sends,), *turn)[0], "front")
-        if late == relay_after:
-            arrived = relayed(after((arrived,), *turn)[0])
-        elif late == 2 or late > RELAY_AFTER and e % 4 == 0:
-            step(min(8, e - CHAINS + 1 - done), *turn)
+        if late >= 2 and late % 2 == 0 and e < events - 1:
+            step(min(4, e - CHAINS + 1 - done), *turn)
             turn = (*turn, result)
+    passed = relayed(after((arrived,), *held[-1], *held[-2])[0])
+    arrived = exchange(passed, "grp")
     while done < events:
-        step(min(8, events - done), *turn)
+        step(min(8, events - done), passed)
     slots_here = after((arrived,), result)[0]
     parent_tiles = sum_parents(slots_here[:, TILE, 0].astype(jnp.int32), slots_here, slots_dev)
     return (result[None], parent_tiles)

time: 181 us -> 179 us (0.989)
  Pallas kernels: 56.7 us -> 59.1 us
    ppermute x44 -> x43, waiting for transfers between devices: 51.3 us -> 40.3 us  [shards(): lax.ppermute(turn[s], 'grp', perms[s])]
    all_to_all x2, waiting for transfers between devices: 0.01 us -> 9.42 us  [exchange(): return lax.all_to_all(blocks, axis, split_axis=0, concat_axis=0, tiled=True)]
    pallas_call x3 -> x4, Pallas kernels: 24.5 us -> 26.9 us  [update(): pl.pallas_call(functools.partial(update_kernel, tuple(numbers), room, wid...]
    ppermute x44 -> x43, starting transfers between devices: 56.1 us -> 55.4 us  [shards(): lax.ppermute(turn[s], 'grp', perms[s])]
  transfers between devices with their start and end apart: 46 -> 45, of which waited for: 18 -> 20; matrix products, arithmetic and copies ran while one was open for 2% -> 2% of each run, Pallas kernels for 27% -> 29%
where the time goes in v6:
time: 179 us; the launch traced here: 178 us
  starting transfers between devices  62.5 us (35%)
  Pallas kernels  59.1 us (33%)
  waiting for transfers between devices  49.7 us (28%)
  other arithmetic  2.93 us (2%)
  local copies, waits for them, and re-layouts  2.56 us (1%)
    ppermute x43, starting transfers between devices, shards(): lax.ppermute(turn[s], 'grp', perms[s])  55.4 us
    ppermute x43, waiting for transfers between devices, shards(): lax.ppermute(turn[s], 'grp', perms[s])  40.3 us
    pallas_call x4, Pallas kernels, update(): pl.pallas_call(functools.partial(update_kernel, tuple(numbers), room, wid...  26.9 us
    pallas_call x8, Pallas kernels, factor(): pl.pallas_call(functools.partial(factor_kernel, tuple(tiles), head), out_...  24.7 us
    all_to_all x2, waiting for transfers between devices, exchange(): return lax.all_to_all(blocks, axis, split_axis=0, concat_axis=0, tiled=True)  9.42 us
    all_to_all x2, starting transfers between devices, exchange(): return lax.all_to_all(blocks, axis, split_axis=0, concat_axis=0, tiled=True)  7.14 us
    pallas_call x1, Pallas kernels, own_panels(): pl.pallas_call(functools.partial(own_kernel, choices, len(blocks), width...  4.08 us
  transfers between devices with their start and end apart: 45, of which 20 were waited for; matrix products, arithmetic and copies ran while one was open for 2% of the time, Pallas kernels for 29%

profile of v6, /device:TPU:0, one launch (start us, length us, event | category | flops | bytes accessed | tf_op | source)
XLA Modules:
  0.0 178.4 jit_solution(431144717221782015)
XLA Ops:
  1.4 3.8 %factor.8 = (bf16[256,512]{1,0:T(8,128)(2,1)S(1)}, bf16[256,512]{1,0:T(8,128)(2,1)S(1)}, bf16[256,512]{1,0:T(8,128)(2,1)S(1)}, bf16[256,512]{1,0:T(8,128)(2,1)S(...) custom-call(s32[32,4]{1,0:T(8,128)S(1)} %copy.54.mask, bf16[8192,1024]{1,0:T(8,128)(2,1)} %bitcast.9, ...), custom_call_target="tpu_custom_call" | custom-call | flops 805306368 | bytes 2097152 | tf_op jit(solution)/shard_map/factor/pallas_call | solution.py:178
  5.2 3.1 %collective-permute-start = (bf16[256,512]{1,0:T(8,128)(2,1)S(1)}, bf16[256,512]{1,0:T(8,128)(2,1)S(1)}, u32[]{:S(2)}, u32[]{:S(2)}) collective-permute-start(bf16[256,512]{1,0:T(8,128)(2,1)S(1)} %get-tuple-element.147.refs_18_), channel_id=1, source_target_pairs={{0,2},{1,3},{2,4},{3,5},{4,6},{5,7},{6,0},{7,1},{8,10},{9,11},{10,... | collective-permute-start | bytes 786440 | tf_op jit(solution)/shard_map/ppermute | solution.py:556
  8.3 1.5 collective-permute-start.1
  9.8 1.6 collective-permute-start.4
  11.9 3.0 %factor.9 = (bf16[256,512]{1,0:T(8,128)(2,1)S(1)}, bf16[256,512]{1,0:T(8,128)(2,1)S(1)}, bf16[256,512]{1,0:T(8,128)(2,1)S(1)}, bf16[256,512]{1,0:T(8,128)(2,1)S(1)}) custom-call(s32[32,4]{1,0:T(8,128)S(1)} %copy.54.mask, bf16[8192,1024]{1,0:T(8,128)(2,1)} %bitcast.10, bf16[4,256,256]{2,1,0:T(8,128)(2,1)S(1)} %get-tuple-element.229.refs_0_, ...), custom_call_target="tpu_custom_call" | custom-call | flops 805306368 | bytes 2097152 | tf_op jit(solution)/shard_map/factor/pallas_call | solution.py:178
  14.9 2.6 %collective-permute-done.refs_19_.refs_0_ = bf16[256,512]{1,0:T(8,128)(2,1)S(1)} collective-permute-done((bf16[256,512]{1,0:T(8,128)(2,1)S(1)}, bf16[256,512]{1,0:T(8,128)(2,1)S(1)}, u32[]{:S(2)}, u32[]{:S(2)}) %collective-permute-start) | collective-permute-done | bytes 262176 | tf_op jit(solution)/shard_map/ppermute | solution.py:556
  17.6 1.6 collective-permute-start.2
  19.2 1.5 collective-permute-start.3
  20.7 2.3 %collective-permute-done.4.refs_2_ = bf16[256,512]{1,0:T(8,128)(2,1)S(1)} collective-permute-done((bf16[256,512]{1,0:T(8,128)(2,1)S(1)}, bf16[256,512]{1,0:T(8,128)(2,1)S(1)}, u32[]{:S(2)}, u32[]{:S(2)}) %collective-permute-start.4) | collective-permute-done | bytes 262176 | tf_op jit(solution)/shard_map/ppermute | solution.py:556
  23.2 1.6 collective-permute-start.8
  24.8 1.5 collective-permute-start.9
  26.3 3.0 %factor.10 = (bf16[256,512]{1,0:T(8,128)(2,1)S(1)}, bf16[256,512]{1,0:T(8,128)(2,1)S(1)}, bf16[256,512]{1,0:T(8,128)(2,1)S(1)}, bf16[256,512]{1,0:T(8,128)(2,1)S(1)}) custom-call(s32[32,4]{1,0:T(8,128)S(1)} %copy.54.mask, bf16[8192,1024]{1,0:T(8,128)(2,1)} %bitcast.11, bf16[4,256,256]{2,1,0:T(8,128)(2,1)S(1)} %get-tuple-element.229.refs_0_, ...), custom_call_target="tpu_custom_call" | custom-call | flops 805306368 | bytes 2097152 | tf_op jit(solution)/shard_map/factor/pallas_call | solution.py:178
  29.5 1.6 collective-permute-start.6
  31.9 2.3 %collective-permute-done.8.refs_6_ = bf16[256,512]{1,0:T(8,128)(2,1)S(1)} collective-permute-done((bf16[256,512]{1,0:T(8,128)(2,1)S(1)}, bf16[256,512]{1,0:T(8,128)(2,1)S(1)}, u32[]{:S(2)}, u32[]{:S(2)}) %collective-permute-start.8) | collective-permute-done | bytes 262176 | tf_op jit(solution)/shard_map/ppermute | solution.py:556
  34.4 1.6 collective-permute-start.12
  36.1 1.5 collective-permute-start.13
  37.6 3.0 %factor.11 = (bf16[256,512]{1,0:T(8,128)(2,1)S(1)}, bf16[256,512]{1,0:T(8,128)(2,1)S(1)}, bf16[256,512]{1,0:T(8,128)(2,1)S(1)}, bf16[256,512]{1,0:T(8,128)(2,1)S(1)}) custom-call(s32[32,4]{1,0:T(8,128)S(1)} %copy.54.mask, bf16[8192,1024]{1,0:T(8,128)(2,1)} %bitcast.12, bf16[4,256,256]{2,1,0:T(8,128)(2,1)S(1)} %get-tuple-element.229.refs_0_, ...), custom_call_target="tpu_custom_call" | custom-call | flops 805306368 | bytes 2097152 | tf_op jit(solution)/shard_map/factor/pallas_call | solution.py:178
  40.7 1.6 collective-permute-start.10
  43.2 3.0 %collective-permute-done.12.refs_2_ = bf16[256,512]{1,0:T(8,128)(2,1)S(1)} collective-permute-done((bf16[256,512]{1,0:T(8,128)(2,1)S(1)}, bf16[256,512]{1,0:T(8,128)(2,1)S(1)}, u32[]{:S(2)}, u32[]{:S(2)}) %collective-permute-start.12) | collective-permute-done | bytes 262176 | tf_op jit(solution)/shard_map/ppermute | solution.py:556
  46.3 1.0 collective-permute-start.16
  47.3 1.5 collective-permute-start.17
  48.8 3.0 %factor.12 = (bf16[256,512]{1,0:T(8,128)(2,1)S(1)}, bf16[256,512]{1,0:T(8,128)(2,1)S(1)}, bf16[256,512]{1,0:T(8,128)(2,1)S(1)}, bf16[256,512]{1,0:T(8,128)(2,1)S(1)}) custom-call(s32[32,4]{1,0:T(8,128)S(1)} %copy.54.mask, bf16[8192,1024]{1,0:T(8,128)(2,1)} %bitcast.13, bf16[4,256,256]{2,1,0:T(8,128)(2,1)S(1)} %get-tuple-element.229.refs_0_, ...), custom_call_target="tpu_custom_call" | custom-call | flops 805306368 | bytes 2097152 | tf_op jit(solution)/shard_map/factor/pallas_call | solution.py:178
  51.9 1.6 collective-permute-start.14
  54.4 3.0 %collective-permute-done.16.refs_9_.refs_6_ = bf16[256,512]{1,0:T(8,128)(2,1)S(1)} collective-permute-done((bf16[256,512]{1,0:T(8,128)(2,1)S(1)}, bf16[256,512]{1,0:T(8,128)(2,1)S(1)}, u32[]{:S(2)}, u32[]{:S(2)}) %collective-permute-start.16) | collective-permute-done | bytes 262176 | tf_op jit(solution)/shard_map/ppermute | solution.py:556
  57.5 1.0 collective-permute-start.20
  58.5 1.5 collective-permute-start.21
  60.0 3.0 %factor.13 = (bf16[256,512]{1,0:T(8,128)(2,1)S(1)}, bf16[256,512]{1,0:T(8,128)(2,1)S(1)}, bf16[256,512]{1,0:T(8,128)(2,1)S(1)}, bf16[256,512]{1,0:T(8,128)(2,1)S(1)}) custom-call(s32[32,4]{1,0:T(8,128)S(1)} %copy.54.mask, bf16[8192,1024]{1,0:T(8,128)(2,1)} %bitcast.14, bf16[4,256,256]{2,1,0:T(8,128)(2,1)S(1)} %get-tuple-element.229.refs_0_, ...), custom_call_target="tpu_custom_call" | custom-call | flops 805306368 | bytes 2097152 | tf_op jit(solution)/shard_map/factor/pallas_call | solution.py:178
  63.2 1.6 collective-permute-start.18
  65.6 3.0 %collective-permute-done.20.refs_8_.refs_2_ = bf16[256,512]{1,0:T(8,128)(2,1)S(1)} collective-permute-done((bf16[256,512]{1,0:T(8,128)(2,1)S(1)}, bf16[256,512]{1,0:T(8,128)(2,1)S(1)}, u32[]{:S(2)}, u32[]{:S(2)}) %collective-permute-start.20) | collective-permute-done | bytes 262176 | tf_op jit(solution)/shard_map/ppermute | solution.py:556
  68.7 1.2 collective-permute-start.22
  70.0 1.5 collective-permute-start.23
  71.5 3.0 %factor.14 = (bf16[256,512]{1,0:T(8,128)(2,1)S(1)}, bf16[256,512]{1,0:T(8,128)(2,1)S(1)}, bf16[256,512]{1,0:T(8,128)(2,1)S(1)}, bf16[256,512]{1,0:T(8,128)(2,1)S(1)}) custom-call(s32[32,4]{1,0:T(8,128)S(1)} %copy.54.mask, bf16[8192,1024]{1,0:T(8,128)(2,1)} %bitcast.15, bf16[4,256,256]{2,1,0:T(8,128)(2,1)S(1)} %get-tuple-element.229.refs_0_, ...), custom_call_target="tpu_custom_call" | custom-call | flops 805306368 | bytes 2097152 | tf_op jit(solution)/shard_map/factor/pallas_call | solution.py:178
  74.6 1.6 collective-permute-start.24
  76.9 3.1 %collective-permute-done.22.refs_7_.refs_6_ = bf16[256,512]{1,0:T(8,128)(2,1)S(1)} collective-permute-done((bf16[256,512]{1,0:T(8,128)(2,1)S(1)}, bf16[256,512]{1,0:T(8,128)(2,1)S(1)}, u32[]{:S(2)}, u32[]{:S(2)}) %collective-permute-start.22) | collective-permute-done | bytes 262176 | tf_op jit(solution)/shard_map/ppermute | solution.py:556
  80.1 0.9 collective-permute-start.26
  81.0 1.5 collective-permute-start.27
  82.5 3.0 %factor.15 = (bf16[256,512]{1,0:T(8,128)(2,1)S(1)}, bf16[256,512]{1,0:T(8,128)(2,1)S(1)}, bf16[256,512]{1,0:T(8,128)(2,1)S(1)}, bf16[256,512]{1,0:T(8,128)(2,1)S(1)}) custom-call(s32[32,4]{1,0:T(8,128)S(1)} %copy.54.mask, bf16[8192,1024]{1,0:T(8,128)(2,1)} %bitcast.16, bf16[4,256,256]{2,1,0:T(8,128)(2,1)S(1)} %get-tuple-element.229.refs_0_, ...), custom_call_target="tpu_custom_call" | custom-call | flops 805306368 | bytes 2097152 | tf_op jit(solution)/shard_map/factor/pallas_call | solution.py:178
  85.7 1.6 collective-permute-start.28
  88.1 3.1 %collective-permute-done.26.refs_16_.refs_10_ = bf16[256,512]{1,0:T(8,128)(2,1)S(1)} collective-permute-done((bf16[256,512]{1,0:T(8,128)(2,1)S(1)}, bf16[256,512]{1,0:T(8,128)(2,1)S(1)}, u32[]{:S(2)}, u32[]{:S(2)}) %collective-permute-start.26) | collective-permute-done | bytes 262176 | tf_op jit(solution)/shard_map/ppermute | solution.py:556
  91.4 0.9 collective-permute-start.30
  92.3 1.5 collective-permute-start.31
  93.8 4.1 %own_panels.1 = (bf16[512,1024]{1,0:T(8,128)(2,1)S(1)}, bf16[4,528,256]{2,1,0:T(8,128)(2,1)}) custom-call(s32[32,4]{1,0:T(8,128)S(1)} %copy.54.mask, s32[4]{0:T(128)S(1)} %bitcast.8, s32[1]{0:T(128)} %bitcast.1.me, bf16[8192,1024]{1,0:T(8,128)(2,1)} %bitcast.17, bf16[256,512]{1,0:T(8,128)(2,1)} %copy-done.7, bf16[256,512]{1,0:T(8,128)(2,1)} %copy-done.22, ...), custom_call_target="tpu_custom_call" | custom-call | flops 268435456 | bytes 2621440 | tf_op jit(solution)/shard_map/own_panels/pallas_call | solution.py:238
  98.8 1.6 collective-permute-start.34
  102.3 0.9 select_select_fusion.1
  103.2 1.1 collective-permute-start.32
  104.3 1.5 collective-permute-start.33
  105.8 3.5 %all-to-all-start = ((bf16[4,528,256]{2,1,0:T(8,128)(2,1)}), bf16[4,528,256]{2,1,0:T(8,128)(2,1)S(1)}, u32[]{:S(2)}, u32[]{:S(2)}) async-start(bf16[4,528,256]{2,1,0:T(8,128)(2,1)} %get-tuple-element.254), calls=%async_computation | async-start | bytes 2162688 | tf_op jit(solution)/shard_map/all_to_all | solution.py:527
  109.4 4.4 %update.4.refs_8_ = bf16[8192,1024]{1,0:T(8,128)(2,1)} custom-call(s32[8,44]{1,0:T(8,128)S(1)} %copy-done.8, s32[32,4]{1,0:T(8,128)S(1)} %copy.54.mask, s32[1]{0:T(128)} %bitcast.1.me, bf16[512,1024]{1,0:T(8,128)(2,1)S(1)} %get-tuple-element.262.own, bf16[8192,1024]{1,0:T(8,128)(2,1)} %bitcast.18, bf16[256,512]{1,0:T(8,128)(2,1)} %copy-done.10, ...), custom_call_target="tpu_custom_call" | custom-call | flops 2147483648 | bytes 8388608 | tf_op jit(solution)/shard_map/update/pallas_call | solution.py:403
  114.6 2.7 %collective-permute-start.38 = (bf16[256,512]{1,0:T(8,128)(2,1)S(1)}, bf16[256,512]{1,0:T(8,128)(2,1)S(1)}, u32[]{:S(2)}, u32[]{:S(2)}) collective-permute-start(bf16[256,512]{1,0:T(8,128)(2,1)S(1)} %get-tuple-element.263), channel_id=1, source_target_pairs={{0,2},{1,3},{2,4},{3,5},{4,6},{5,7},{6,0},{7,1},{8,10},{9,11},{10,... | collective-permute-start | bytes 786440 | tf_op jit(solution)/shard_map/ppermute | solution.py:556
  117.7 1.9 %collective-permute-start.37 = (bf16[256,512]{1,0:T(8,128)(2,1)S(1)}, bf16[256,512]{1,0:T(8,128)(2,1)S(1)}, u32[]{:S(2)}, u32[]{:S(2)}) collective-permute-start(bf16[256,512]{1,0:T(8,128)(2,1)S(1)} %get-tuple-element.268), channel_id=1, source_target_pairs={{0,1},{1,0},{2,3},{3,2},{4,5},{5,4},{6,7},{7,6},{8,9},{9,8},{10,11... | collective-permute-start | bytes 786440 | tf_op jit(solution)/shard_map/ppermute | solution.py:556
  119.6 5.8 %update.5.refs_16_ = bf16[8192,1024]{1,0:T(8,128)(2,1)} custom-call(s32[8,44]{1,0:T(8,128)S(1)} %copy-done.8, s32[32,4]{1,0:T(8,128)S(1)} %copy.54.mask, s32[1]{0:T(128)} %bitcast.1.me, bf16[512,1024]{1,0:T(8,128)(2,1)S(1)} %get-tuple-element.262.own, bf16[8192,1024]{1,0:T(8,128)(2,1)} %bitcast.19, ...), custom_call_target="tpu_custom_call", output_to_operand_aliasing={{}: (13, {})} | custom-call | flops 2147483648 | bytes 8388608 | tf_op jit(solution)/shard_map/update/pallas_call | solution.py:403
  125.5 1.0 collective-permute-done.39.refs_5_
  126.5 4.1 %collective-permute-done.36.refs_6_ = bf16[256,512]{1,0:T(8,128)(2,1)S(1)} collective-permute-done((bf16[256,512]{1,0:T(8,128)(2,1)S(1)}, bf16[256,512]{1,0:T(8,128)(2,1)S(1)}, u32[]{:S(2)}, u32[]{:S(2)}) %collective-permute-start.36) | collective-permute-done | bytes 262176 | tf_op jit(solution)/shard_map/ppermute | solution.py:556
  131.3 1.1 collective-permute-start.40
  132.5 1.3 collective-permute-start.42
  133.7 6.9 %collective-permute-done.40.refs_10_ = bf16[256,512]{1,0:T(8,128)(2,1)S(1)} collective-permute-done((bf16[256,512]{1,0:T(8,128)(2,1)S(1)}, bf16[256,512]{1,0:T(8,128)(2,1)S(1)}, u32[]{:S(2)}, u32[]{:S(2)}) %collective-permute-start.40) | collective-permute-done | bytes 262176 | tf_op jit(solution)/shard_map/ppermute | solution.py:556
  140.7 1.2 collective-permute-done.41.refs_8_
  141.8 2.8 %collective-permute-done.42.refs_9_ = bf16[256,512]{1,0:T(8,128)(2,1)} collective-permute-done((bf16[256,512]{1,0:T(8,128)(2,1)S(1)}, bf16[256,512]{1,0:T(8,128)(2,1)}, u32[]{:S(2)}, u32[]{:S(2)}) %collective-permute-start.42) | collective-permute-done | bytes 262176 | tf_op jit(solution)/shard_map/ppermute | solution.py:556
  144.9 1.8 %relay.1 = bf16[8,272,256]{2,1,0:T(8,128)(2,1)} custom-call(s32[4,2]{1,0:T(4,128)S(1)} %copy.52.labels, bf16[4,528,256]{2,1,0:T(8,128)(2,1)S(1)} %all-to-all-done.arrived), custom_call_target="tpu_custom_call" | custom-call | bytes 2097152 | tf_op jit(solution)/shard_map/relay/pallas_call | solution.py:278
  146.7 3.6 %all-to-all-start.1 = ((bf16[8,272,256]{2,1,0:T(8,128)(2,1)}), bf16[8,272,256]{2,1,0:T(8,128)(2,1)S(1)}, u32[]{:S(2)}, u32[]{:S(2)}) async-start(bf16[8,272,256]{2,1,0:T(8,128)(2,1)} %relay.1), calls=%async_computation.1 | async-start | bytes 2228224 | tf_op jit(solution)/shard_map/all_to_all | solution.py:527
  150.3 10.2 %update.6.refs_11_ = bf16[8192,1024]{1,0:T(8,128)(2,1)} custom-call(s32[8,44]{1,0:T(8,128)S(1)} %copy-done.8, s32[32,4]{1,0:T(8,128)S(1)} %copy.54.mask, s32[1]{0:T(128)} %bitcast.1.me, bf16[512,1024]{1,0:T(8,128)(2,1)S(1)} %get-tuple-element.262.own, bf16[8192,1024]{1,0:T(8,128)(2,1)} %bitcast.20, ...), custom_call_target="tpu_custom_call", output_to_operand_aliasing={{}: (21, {})} | custom-call | flops 4294967296 | bytes 16777216 | tf_op jit(solution)/shard_map/update/pallas_call | solution.py:403
  160.6 6.5 %update.7 = bf16[8192,1024]{1,0:T(8,128)(2,1)} custom-call(s32[8,44]{1,0:T(8,128)S(1)} %copy-done.8, s32[32,4]{1,0:T(8,128)S(1)} %copy.54.mask, s32[1]{0:T(128)} %bitcast.1.me, bf16[512,1024]{1,0:T(8,128)(2,1)S(1)} %get-tuple-element.262.own, bf16[8192,1024]{1,0:T(8,128)(2,1)} %bitcast.21, ...), custom_call_target="tpu_custom_call", output_to_operand_aliasing={{}: (16, {})} | custom-call | flops 3221225472 | bytes 12582912 | tf_op jit(solution)/shard_map/update/pallas_call | solution.py:403
  167.0 9.4 %all-to-all-done.1.arrived = bf16[8,272,256]{2,1,0:T(8,128)(2,1)S(1)} async-done(((bf16[8,272,256]{2,1,0:T(8,128)(2,1)}), bf16[8,272,256]{2,1,0:T(8,128)(2,1)S(1)}, u32[]{:S(2)}, u32[]{:S(2)}) %all-to-all-start.1) | async-done | bytes 1114144 | tf_op jit(solution)/shard_map/all_to_all | solution.py:527
  176.7 1.7 sum_parents.1
  (171 shorter events, 12.5 us)
Async XLA Ops:
  5.2 9.7 %copy-start.6 = (bf16[256,512]{1,0:T(8,128)(2,1)}, bf16[256,512]{1,0:T(8,128)(2,1)S(1)}, u32[]{:S(2)}) copy-start(bf16[256,512]{1,0:T(8,128)(2,1)S(1)} %get-tuple-element.147.refs_18_) | copy-start | bytes 786436
  5.2 12.2 %collective-permute-start = (bf16[256,512]{1,0:T(8,128)(2,1)S(1)}, bf16[256,512]{1,0:T(8,128)(2,1)S(1)}, u32[]{:S(2)}, u32[]{:S(2)}) collective-permute-start(bf16[256,512]{1,0:T(8,128)(2,1)S(1)} %get-tuple-element.147.refs_18_), channel_id=1, source_target_pairs={{0,2},{1,3},{2,4},{3,5},{4,6},{5,7},{6,0},{7,1},{8,10},{9,11},{10,... | collective-permute-start | bytes 786440 | tf_op jit(solution)/shard_map/ppermute | solution.py:556
  8.3 9.2 %collective-permute-start.1 = (bf16[256,512]{1,0:T(8,128)(2,1)S(1)}, bf16[256,512]{1,0:T(8,128)(2,1)S(1)}, u32[]{:S(2)}, u32[]{:S(2)}) collective-permute-start(bf16[256,512]{1,0:T(8,128)(2,1)S(1)} %get-tuple-element.148), channel_id=1, source_target_pairs={{0,1},{1,0},{2,3},{3,2},{4,5},{5,4},{6,7},{7,6},{8,9},{9,8},{10,11... | collective-permute-start | bytes 786440 | tf_op jit(solution)/shard_map/ppermute | solution.py:556
  9.8 13.3 %collective-permute-start.4 = (bf16[256,512]{1,0:T(8,128)(2,1)S(1)}, bf16[256,512]{1,0:T(8,128)(2,1)S(1)}, u32[]{:S(2)}, u32[]{:S(2)}) collective-permute-start(bf16[256,512]{1,0:T(8,128)(2,1)S(1)} %get-tuple-element.149), channel_id=1, source_target_pairs={{0,2},{1,3},{2,4},{3,5},{4,6},{5,7},{6,0},{7,1},{8,10},{9,11},{10,... | collective-permute-start | bytes 786440 | tf_op jit(solution)/shard_map/ppermute | solution.py:556
  11.4 11.8 %collective-permute-start.5 = (bf16[256,512]{1,0:T(8,128)(2,1)S(1)}, bf16[256,512]{1,0:T(8,128)(2,1)S(1)}, u32[]{:S(2)}, u32[]{:S(2)}) collective-permute-start(bf16[256,512]{1,0:T(8,128)(2,1)S(1)} %get-tuple-element.150), channel_id=1, source_target_pairs={{0,1},{1,0},{2,3},{3,2},{4,5},{5,4},{6,7},{7,6},{8,9},{9,8},{10,11... | collective-permute-start | bytes 786440 | tf_op jit(solution)/shard_map/ppermute | solution.py:556
  17.6 11.8 %collective-permute-start.2 = (bf16[256,512]{1,0:T(8,128)(2,1)S(1)}, bf16[256,512]{1,0:T(8,128)(2,1)S(1)}, u32[]{:S(2)}, u32[]{:S(2)}) collective-permute-start(bf16[256,512]{1,0:T(8,128)(2,1)S(1)} %get-tuple-element.157), channel_id=1, source_target_pairs={{0,2},{1,3},{2,4},{3,5},{4,6},{5,7},{6,0},{7,1},{8,10},{9,11},{10,... | collective-permute-start | bytes 786440 | tf_op jit(solution)/shard_map/ppermute | solution.py:556
  19.2 10.2 %collective-permute-start.3 = (bf16[256,512]{1,0:T(8,128)(2,1)S(1)}, bf16[256,512]{1,0:T(8,128)(2,1)S(1)}, u32[]{:S(2)}, u32[]{:S(2)}) collective-permute-start(bf16[256,512]{1,0:T(8,128)(2,1)S(1)} %get-tuple-element.158), channel_id=1, source_target_pairs={{0,1},{1,0},{2,3},{3,2},{4,5},{5,4},{6,7},{7,6},{8,9},{9,8},{10,11... | collective-permute-start | bytes 786440 | tf_op jit(solution)/shard_map/ppermute | solution.py:556
  23.0 6.3 %copy-start.30 = (bf16[256,512]{1,0:T(8,128)(2,1)}, bf16[256,512]{1,0:T(8,128)(2,1)S(1)}, u32[]{:S(2)}) copy-start(bf16[256,512]{1,0:T(8,128)(2,1)S(1)} %collective-permute-done.4.refs_2_) | copy-start | bytes 786436
  23.1 6.2 %copy-start.31 = (bf16[256,512]{1,0:T(8,128)(2,1)}, bf16[256,512]{1,0:T(8,128)(2,1)S(1)}, u32[]{:S(2)}) copy-start(bf16[256,512]{1,0:T(8,128)(2,1)S(1)} %collective-permute-done.5.refs_3_) | copy-start | bytes 786436
  23.2 11.1 %collective-permute-start.8 = (bf16[256,512]{1,0:T(8,128)(2,1)S(1)}, bf16[256,512]{1,0:T(8,128)(2,1)S(1)}, u32[]{:S(2)}, u32[]{:S(2)}) collective-permute-start(bf16[256,512]{1,0:T(8,128)(2,1)S(1)} %get-tuple-element.166), channel_id=1, source_target_pairs={{0,2},{1,3},{2,4},{3,5},{4,6},{5,7},{6,0},{7,1},{8,10},{9,11},{10,... | collective-permute-start | bytes 786440 | tf_op jit(solution)/shard_map/ppermute | solution.py:556
  24.8 9.5 %collective-permute-start.9 = (bf16[256,512]{1,0:T(8,128)(2,1)S(1)}, bf16[256,512]{1,0:T(8,128)(2,1)S(1)}, u32[]{:S(2)}, u32[]{:S(2)}) collective-permute-start(bf16[256,512]{1,0:T(8,128)(2,1)S(1)} %get-tuple-element.167), channel_id=1, source_target_pairs={{0,1},{1,0},{2,3},{3,2},{4,5},{5,4},{6,7},{7,6},{8,9},{9,8},{10,11... | collective-permute-start | bytes 786440 | tf_op jit(solution)/shard_map/ppermute | solution.py:556
  29.5 11.1 %collective-permute-start.6 = (bf16[256,512]{1,0:T(8,128)(2,1)S(1)}, bf16[256,512]{1,0:T(8,128)(2,1)S(1)}, u32[]{:S(2)}, u32[]{:S(2)}) collective-permute-start(bf16[256,512]{1,0:T(8,128)(2,1)S(1)} %get-tuple-element.171), channel_id=1, source_target_pairs={{0,2},{1,3},{2,4},{3,5},{4,6},{5,7},{6,0},{7,1},{8,10},{9,11},{10,... | collective-permute-start | bytes 786440 | tf_op jit(solution)/shard_map/ppermute | solution.py:556
  31.1 9.5 %collective-permute-start.7 = (bf16[256,512]{1,0:T(8,128)(2,1)S(1)}, bf16[256,512]{1,0:T(8,128)(2,1)S(1)}, u32[]{:S(2)}, u32[]{:S(2)}) collective-permute-start(bf16[256,512]{1,0:T(8,128)(2,1)S(1)} %get-tuple-element.172), channel_id=1, source_target_pairs={{0,1},{1,0},{2,3},{3,2},{4,5},{5,4},{6,7},{7,6},{8,9},{9,8},{10,11... | collective-permute-start | bytes 786440 | tf_op jit(solution)/shard_map/ppermute | solution.py:556
  34.3 6.3 %copy-start.32 = (bf16[256,512]{1,0:T(8,128)(2,1)}, bf16[256,512]{1,0:T(8,128)(2,1)S(1)}, u32[]{:S(2)}) copy-start(bf16[256,512]{1,0:T(8,128)(2,1)S(1)} %collective-permute-done.8.refs_6_) | copy-start | bytes 786436
  34.4 6.2 %copy-start.33 = (bf16[256,512]{1,0:T(8,128)(2,1)}, bf16[256,512]{1,0:T(8,128)(2,1)S(1)}, u32[]{:S(2)}) copy-start(bf16[256,512]{1,0:T(8,128)(2,1)S(1)} %collective-permute-done.9.refs_7_) | copy-start | bytes 786436
  34.4 11.7 %collective-permute-start.12 = (bf16[256,512]{1,0:T(8,128)(2,1)S(1)}, bf16[256,512]{1,0:T(8,128)(2,1)S(1)}, u32[]{:S(2)}, u32[]{:S(2)}) collective-permute-start(bf16[256,512]{1,0:T(8,128)(2,1)S(1)} %get-tuple-element.180), channel_id=1, source_target_pairs={{0,2},{1,3},{2,4},{3,5},{4,6},{5,7},{6,0},{7,1},{8,10},{9,11},{10,... | collective-permute-start | bytes 786440 | tf_op jit(solution)/shard_map/ppermute | solution.py:556
  36.1 10.1 %collective-permute-start.13 = (bf16[256,512]{1,0:T(8,128)(2,1)S(1)}, bf16[256,512]{1,0:T(8,128)(2,1)S(1)}, u32[]{:S(2)}, u32[]{:S(2)}) collective-permute-start(bf16[256,512]{1,0:T(8,128)(2,1)S(1)} %get-tuple-element.181), channel_id=1, source_target_pairs={{0,1},{1,0},{2,3},{3,2},{4,5},{5,4},{6,7},{7,6},{8,9},{9,8},{10,11... | collective-permute-start | bytes 786440 | tf_op jit(solution)/shard_map/ppermute | solution.py:556
  40.7 11.1 %collective-permute-start.10 = (bf16[256,512]{1,0:T(8,128)(2,1)S(1)}, bf16[256,512]{1,0:T(8,128)(2,1)S(1)}, u32[]{:S(2)}, u32[]{:S(2)}) collective-permute-start(bf16[256,512]{1,0:T(8,128)(2,1)S(1)} %get-tuple-element.185), channel_id=1, source_target_pairs={{0,2},{1,3},{2,4},{3,5},{4,6},{5,7},{6,0},{7,1},{8,10},{9,11},{10,... | collective-permute-start | bytes 786440 | tf_op jit(solution)/shard_map/ppermute | solution.py:556
  42.3 9.5 %collective-permute-start.11 = (bf16[256,512]{1,0:T(8,128)(2,1)S(1)}, bf16[256,512]{1,0:T(8,128)(2,1)S(1)}, u32[]{:S(2)}, u32[]{:S(2)}) collective-permute-start(bf16[256,512]{1,0:T(8,128)(2,1)S(1)} %get-tuple-element.186), channel_id=1, source_target_pairs={{0,1},{1,0},{2,3},{3,2},{4,5},{5,4},{6,7},{7,6},{8,9},{9,8},{10,11... | collective-permute-start | bytes 786440 | tf_op jit(solution)/shard_map/ppermute | solution.py:556
  46.3 11.1 %collective-permute-start.16 = (bf16[256,512]{1,0:T(8,128)(2,1)S(1)}, bf16[256,512]{1,0:T(8,128)(2,1)S(1)}, u32[]{:S(2)}, u32[]{:S(2)}) collective-permute-start(bf16[256,512]{1,0:T(8,128)(2,1)S(1)} %get-tuple-element.194), channel_id=1, source_target_pairs={{0,2},{1,3},{2,4},{3,5},{4,6},{5,7},{6,0},{7,1},{8,10},{9,11},{10,... | collective-permute-start | bytes 786440 | tf_op jit(solution)/shard_map/ppermute | solution.py:556
  47.3 10.1 %collective-permute-start.17 = (bf16[256,512]{1,0:T(8,128)(2,1)S(1)}, bf16[256,512]{1,0:T(8,128)(2,1)S(1)}, u32[]{:S(2)}, u32[]{:S(2)}) collective-permute-start(bf16[256,512]{1,0:T(8,128)(2,1)S(1)} %get-tuple-element.195), channel_id=1, source_target_pairs={{0,1},{1,0},{2,3},{3,2},{4,5},{5,4},{6,7},{7,6},{8,9},{9,8},{10,11... | collective-permute-start | bytes 786440 | tf_op jit(solution)/shard_map/ppermute | solution.py:556
  51.9 11.1 %collective-permute-start.14 = (bf16[256,512]{1,0:T(8,128)(2,1)S(1)}, bf16[256,512]{1,0:T(8,128)(2,1)S(1)}, u32[]{:S(2)}, u32[]{:S(2)}) collective-permute-start(bf16[256,512]{1,0:T(8,128)(2,1)S(1)} %get-tuple-element.199), channel_id=1, source_target_pairs={{0,2},{1,3},{2,4},{3,5},{4,6},{5,7},{6,0},{7,1},{8,10},{9,11},{10,... | collective-permute-start | bytes 786440 | tf_op jit(solution)/shard_map/ppermute | solution.py:556
  53.6 9.5 %collective-permute-start.15 = (bf16[256,512]{1,0:T(8,128)(2,1)S(1)}, bf16[256,512]{1,0:T(8,128)(2,1)S(1)}, u32[]{:S(2)}, u32[]{:S(2)}) collective-permute-start(bf16[256,512]{1,0:T(8,128)(2,1)S(1)} %get-tuple-element.200), channel_id=1, source_target_pairs={{0,1},{1,0},{2,3},{3,2},{4,5},{5,4},{6,7},{7,6},{8,9},{9,8},{10,11... | collective-permute-start | bytes 786440 | tf_op jit(solution)/shard_map/ppermute | solution.py:556
  57.5 11.1 %collective-permute-start.20 = (bf16[256,512]{1,0:T(8,128)(2,1)S(1)}, bf16[256,512]{1,0:T(8,128)(2,1)S(1)}, u32[]{:S(2)}, u32[]{:S(2)}) collective-permute-start(bf16[256,512]{1,0:T(8,128)(2,1)S(1)} %get-tuple-element.208), channel_id=1, source_target_pairs={{0,2},{1,3},{2,4},{3,5},{4,6},{5,7},{6,0},{7,1},{8,10},{9,11},{10,... | collective-permute-start | bytes 786440 | tf_op jit(solution)/shard_map/ppermute | solution.py:556
  58.5 10.1 %collective-permute-start.21 = (bf16[256,512]{1,0:T(8,128)(2,1)S(1)}, bf16[256,512]{1,0:T(8,128)(2,1)S(1)}, u32[]{:S(2)}, u32[]{:S(2)}) collective-permute-start(bf16[256,512]{1,0:T(8,128)(2,1)S(1)} %get-tuple-element.209), channel_id=1, source_target_pairs={{0,1},{1,0},{2,3},{3,2},{4,5},{5,4},{6,7},{7,6},{8,9},{9,8},{10,11... | collective-permute-start | bytes 786440 | tf_op jit(solution)/shard_map/ppermute | solution.py:556
  63.2 11.3 %collective-permute-start.18 = (bf16[256,512]{1,0:T(8,128)(2,1)S(1)}, bf16[256,512]{1,0:T(8,128)(2,1)S(1)}, u32[]{:S(2)}, u32[]{:S(2)}) collective-permute-start(bf16[256,512]{1,0:T(8,128)(2,1)S(1)} %get-tuple-element.213), channel_id=1, source_target_pairs={{0,2},{1,3},{2,4},{3,5},{4,6},{5,7},{6,0},{7,1},{8,10},{9,11},{10,... | collective-permute-start | bytes 786440 | tf_op jit(solution)/shard_map/ppermute | solution.py:556
  64.8 9.7 %collective-permute-start.19 = (bf16[256,512]{1,0:T(8,128)(2,1)S(1)}, bf16[256,512]{1,0:T(8,128)(2,1)S(1)}, u32[]{:S(2)}, u32[]{:S(2)}) collective-permute-start(bf16[256,512]{1,0:T(8,128)(2,1)S(1)} %get-tuple-element.214), channel_id=1, source_target_pairs={{0,1},{1,0},{2,3},{3,2},{4,5},{5,4},{6,7},{7,6},{8,9},{9,8},{10,11... | collective-permute-start | bytes 786440 | tf_op jit(solution)/shard_map/ppermute | solution.py:556
  68.6 5.8 %copy-start.16 = (bf16[256,512]{1,0:T(8,128)(2,1)}, bf16[256,512]{1,0:T(8,128)(2,1)S(1)}, u32[]{:S(2)}) copy-start(bf16[256,512]{1,0:T(8,128)(2,1)S(1)} %collective-permute-done.20.refs_8_.refs_2_) | copy-start | bytes 786436
  68.7 5.8 %copy-start.37 = (bf16[256,512]{1,0:T(8,128)(2,1)}, bf16[256,512]{1,0:T(8,128)(2,1)S(1)}, u32[]{:S(2)}) copy-start(bf16[256,512]{1,0:T(8,128)(2,1)S(1)} %collective-permute-done.21.refs_3_) | copy-start | bytes 786436
  68.7 11.3 %collective-permute-start.22 = (bf16[256,512]{1,0:T(8,128)(2,1)S(1)}, bf16[256,512]{1,0:T(8,128)(2,1)S(1)}, u32[]{:S(2)}, u32[]{:S(2)}) collective-permute-start(bf16[256,512]{1,0:T(8,128)(2,1)S(1)} %get-tuple-element.222), channel_id=1, source_target_pairs={{0,2},{1,3},{2,4},{3,5},{4,6},{5,7},{6,0},{7,1},{8,10},{9,11},{10,... | collective-permute-start | bytes 786440 | tf_op jit(solution)/shard_map/ppermute | solution.py:556
  70.0 10.1 %collective-permute-start.23 = (bf16[256,512]{1,0:T(8,128)(2,1)S(1)}, bf16[256,512]{1,0:T(8,128)(2,1)S(1)}, u32[]{:S(2)}, u32[]{:S(2)}) collective-permute-start(bf16[256,512]{1,0:T(8,128)(2,1)S(1)} %get-tuple-element.223), channel_id=1, source_target_pairs={{0,1},{1,0},{2,3},{3,2},{4,5},{5,4},{6,7},{7,6},{8,9},{9,8},{10,11... | collective-permute-start | bytes 786440 | tf_op jit(solution)/shard_map/ppermute | solution.py:556
  74.6 11.0 %collective-permute-start.24 = (bf16[256,512]{1,0:T(8,128)(2,1)S(1)}, bf16[256,512]{1,0:T(8,128)(2,1)S(1)}, u32[]{:S(2)}, u32[]{:S(2)}) collective-permute-start(bf16[256,512]{1,0:T(8,128)(2,1)S(1)} %get-tuple-element.227), channel_id=1, source_target_pairs={{0,2},{1,3},{2,4},{3,5},{4,6},{5,7},{6,0},{7,1},{8,10},{9,11},{10,... | collective-permute-start | bytes 786440 | tf_op jit(solution)/shard_map/ppermute | solution.py:556
  76.2 9.4 %collective-permute-start.25 = (bf16[256,512]{1,0:T(8,128)(2,1)S(1)}, bf16[256,512]{1,0:T(8,128)(2,1)S(1)}, u32[]{:S(2)}, u32[]{:S(2)}) collective-permute-start(bf16[256,512]{1,0:T(8,128)(2,1)S(1)} %get-tuple-element.228), channel_id=1, source_target_pairs={{0,1},{1,0},{2,3},{3,2},{4,5},{5,4},{6,7},{7,6},{8,9},{9,8},{10,11... | collective-permute-start | bytes 786440 | tf_op jit(solution)/shard_map/ppermute | solution.py:556
  80.1 11.1 %collective-permute-start.26 = (bf16[256,512]{1,0:T(8,128)(2,1)S(1)}, bf16[256,512]{1,0:T(8,128)(2,1)S(1)}, u32[]{:S(2)}, u32[]{:S(2)}) collective-permute-start(bf16[256,512]{1,0:T(8,128)(2,1)S(1)} %get-tuple-element.238), channel_id=1, source_target_pairs={{0,2},{1,3},{2,4},{3,5},{4,6},{5,7},{6,0},{7,1},{8,10},{9,11},{10,... | collective-permute-start | bytes 786440 | tf_op jit(solution)/shard_map/ppermute | solution.py:556
  81.0 10.2 %collective-permute-start.27 = (bf16[256,512]{1,0:T(8,128)(2,1)S(1)}, bf16[256,512]{1,0:T(8,128)(2,1)S(1)}, u32[]{:S(2)}, u32[]{:S(2)}) collective-permute-start(bf16[256,512]{1,0:T(8,128)(2,1)S(1)} %get-tuple-element.239), channel_id=1, source_target_pairs={{0,1},{1,0},{2,3},{3,2},{4,5},{5,4},{6,7},{7,6},{8,9},{9,8},{10,11... | collective-permute-start | bytes 786440 | tf_op jit(solution)/shard_map/ppermute | solution.py:556
  85.5 5.8 %copy-start = (bf16[256,512]{1,0:T(8,128)(2,1)}, bf16[256,512]{1,0:T(8,128)(2,1)S(1)}, u32[]{:S(2)}) copy-start(bf16[256,512]{1,0:T(8,128)(2,1)S(1)} %get-tuple-element.235.refs_11_) | copy-start | bytes 786436
  85.5 5.8 %copy-start.2 = (bf16[256,512]{1,0:T(8,128)(2,1)}, bf16[256,512]{1,0:T(8,128)(2,1)S(1)}, u32[]{:S(2)}) copy-start(bf16[256,512]{1,0:T(8,128)(2,1)S(1)} %get-tuple-element.242.refs_14_) | copy-start | bytes 786436
  85.6 5.8 %copy-start.4 = (bf16[256,512]{1,0:T(8,128)(2,1)}, bf16[256,512]{1,0:T(8,128)(2,1)S(1)}, u32[]{:S(2)}) copy-start(bf16[256,512]{1,0:T(8,128)(2,1)S(1)} %get-tuple-element.232.refs_5_) | copy-start | bytes 786436
  85.7 8.1 %copy-start.9 = (s32[1,1,4]{2,1,0:T(1,128)S(1)}, s32[1,1,4]{2,1,0:T(1,128)}, u32[]{:S(2)}) copy-start(s32[1,1,4]{2,1,0:T(1,128)} %param.8) | copy-start | bytes 52
  85.7 12.2 %collective-permute-start.28 = (bf16[256,512]{1,0:T(8,128)(2,1)S(1)}, bf16[256,512]{1,0:T(8,128)(2,1)S(1)}, u32[]{:S(2)}, u32[]{:S(2)}) collective-permute-start(bf16[256,512]{1,0:T(8,128)(2,1)S(1)} %get-tuple-element.243), channel_id=1, source_target_pairs={{0,2},{1,3},{2,4},{3,5},{4,6},{5,7},{6,0},{7,1},{8,10},{9,11},{10,... | collective-permute-start | bytes 786440 | tf_op jit(solution)/shard_map/ppermute | solution.py:556
  87.3 10.6 %collective-permute-start.29 = (bf16[256,512]{1,0:T(8,128)(2,1)S(1)}, bf16[256,512]{1,0:T(8,128)(2,1)S(1)}, u32[]{:S(2)}, u32[]{:S(2)}) collective-permute-start(bf16[256,512]{1,0:T(8,128)(2,1)S(1)} %get-tuple-element.244), channel_id=1, source_target_pairs={{0,1},{1,0},{2,3},{3,2},{4,5},{5,4},{6,7},{7,6},{8,9},{9,8},{10,11... | collective-permute-start | bytes 786440 | tf_op jit(solution)/shard_map/ppermute | solution.py:556
  91.4 10.2 %collective-permute-start.30 = (bf16[256,512]{1,0:T(8,128)(2,1)S(1)}, bf16[256,512]{1,0:T(8,128)(2,1)S(1)}, u32[]{:S(2)}, u32[]{:S(2)}) collective-permute-start(bf16[256,512]{1,0:T(8,128)(2,1)S(1)} %get-tuple-element.248), channel_id=1, source_target_pairs={{0,2},{1,3},{2,4},{3,5},{4,6},{5,7},{6,0},{7,1},{8,10},{9,11},{10,... | collective-permute-start | bytes 786440 | tf_op jit(solution)/shard_map/ppermute | solution.py:556
  92.3 9.3 %collective-permute-start.31 = (bf16[256,512]{1,0:T(8,128)(2,1)S(1)}, bf16[256,512]{1,0:T(8,128)(2,1)S(1)}, u32[]{:S(2)}, u32[]{:S(2)}) collective-permute-start(bf16[256,512]{1,0:T(8,128)(2,1)S(1)} %get-tuple-element.249), channel_id=1, source_target_pairs={{0,1},{1,0},{2,3},{3,2},{4,5},{5,4},{6,7},{7,6},{8,9},{9,8},{10,11... | collective-permute-start | bytes 786440 | tf_op jit(solution)/shard_map/ppermute | solution.py:556
  98.8 15.0 %collective-permute-start.34 = (bf16[256,512]{1,0:T(8,128)(2,1)}, bf16[256,512]{1,0:T(8,128)(2,1)S(1)}, u32[]{:S(2)}, u32[]{:S(2)}) collective-permute-start(bf16[256,512]{1,0:T(8,128)(2,1)} %get-tuple-element.252), channel_id=1, source_target_pairs={{0,2},{1,3},{2,4},{3,5},{4,6},{5,7},{6,0},{7,1},{8,10},{9,11},{10,... | collective-permute-start | bytes 786440 | tf_op jit(solution)/shard_map/ppermute | solution.py:556
  100.4 13.4 %collective-permute-start.35 = (bf16[256,512]{1,0:T(8,128)(2,1)}, bf16[256,512]{1,0:T(8,128)(2,1)S(1)}, u32[]{:S(2)}, u32[]{:S(2)}) collective-permute-start(bf16[256,512]{1,0:T(8,128)(2,1)} %get-tuple-element.253), channel_id=1, source_target_pairs={{0,1},{1,0},{2,3},{3,2},{4,5},{5,4},{6,7},{7,6},{8,9},{9,8},{10,11... | collective-permute-start | bytes 786440 | tf_op jit(solution)/shard_map/ppermute | solution.py:556
  103.2 6.1 %copy-start.8 = (s32[8,44]{1,0:T(8,128)S(1)}, s32[8,44]{1,0:T(8,128)}, u32[]{:S(2)}) copy-start(s32[8,44]{1,0:T(8,128)} %constant.14.clone.table) | copy-start | bytes 4228
  103.2 14.3 %collective-permute-start.32 = (bf16[256,512]{1,0:T(8,128)(2,1)}, bf16[256,512]{1,0:T(8,128)(2,1)S(1)}, u32[]{:S(2)}, u32[]{:S(2)}) collective-permute-start(bf16[256,512]{1,0:T(8,128)(2,1)} %get-tuple-element.257), channel_id=1, source_target_pairs={{0,2},{1,3},{2,4},{3,5},{4,6},{5,7},{6,0},{7,1},{8,10},{9,11},{10,... | collective-permute-start | bytes 786440 | tf_op jit(solution)/shard_map/ppermute | solution.py:556
  104.3 13.3 %collective-permute-start.33 = (bf16[256,512]{1,0:T(8,128)(2,1)}, bf16[256,512]{1,0:T(8,128)(2,1)S(1)}, u32[]{:S(2)}, u32[]{:S(2)}) collective-permute-start(bf16[256,512]{1,0:T(8,128)(2,1)} %get-tuple-element.258), channel_id=1, source_target_pairs={{0,1},{1,0},{2,3},{3,2},{4,5},{5,4},{6,7},{7,6},{8,9},{9,8},{10,11... | collective-permute-start | bytes 786440 | tf_op jit(solution)/shard_map/ppermute | solution.py:556
  105.8 38.8 %all-to-all-start = ((bf16[4,528,256]{2,1,0:T(8,128)(2,1)}), bf16[4,528,256]{2,1,0:T(8,128)(2,1)S(1)}, u32[]{:S(2)}, u32[]{:S(2)}) async-start(bf16[4,528,256]{2,1,0:T(8,128)(2,1)} %get-tuple-element.254), calls=%async_computation | async-start | bytes 2162688 | tf_op jit(solution)/shard_map/all_to_all | solution.py:527
  114.6 10.9 %collective-permute-start.38 = (bf16[256,512]{1,0:T(8,128)(2,1)S(1)}, bf16[256,512]{1,0:T(8,128)(2,1)S(1)}, u32[]{:S(2)}, u32[]{:S(2)}) collective-permute-start(bf16[256,512]{1,0:T(8,128)(2,1)S(1)} %get-tuple-element.263), channel_id=1, source_target_pairs={{0,2},{1,3},{2,4},{3,5},{4,6},{5,7},{6,0},{7,1},{8,10},{9,11},{10,... | collective-permute-start | bytes 786440 | tf_op jit(solution)/shard_map/ppermute | solution.py:556
  117.3 9.2 %collective-permute-start.39 = (bf16[256,512]{1,0:T(8,128)(2,1)S(1)}, bf16[256,512]{1,0:T(8,128)(2,1)S(1)}, u32[]{:S(2)}, u32[]{:S(2)}) collective-permute-start(bf16[256,512]{1,0:T(8,128)(2,1)S(1)} %get-tuple-element.264), channel_id=1, source_target_pairs={{0,1},{1,0},{2,3},{3,2},{4,5},{5,4},{6,7},{7,6},{8,9},{9,8},{10,11... | collective-permute-start | bytes 786440 | tf_op jit(solution)/shard_map/ppermute | solution.py:556
  117.6 7.8 %copy-start.40 = (bf16[256,512]{1,0:T(8,128)(2,1)}, bf16[256,512]{1,0:T(8,128)(2,1)S(1)}, u32[]{:S(2)}) copy-start(bf16[256,512]{1,0:T(8,128)(2,1)S(1)} %collective-permute-done.32.refs_2_) | copy-start | bytes 786436
  117.6 7.8 %copy-start.41 = (bf16[256,512]{1,0:T(8,128)(2,1)}, bf16[256,512]{1,0:T(8,128)(2,1)S(1)}, u32[]{:S(2)}) copy-start(bf16[256,512]{1,0:T(8,128)(2,1)S(1)} %collective-permute-done.33.refs_3_) | copy-start | bytes 786436
  117.6 13.0 %collective-permute-start.36 = (bf16[256,512]{1,0:T(8,128)(2,1)S(1)}, bf16[256,512]{1,0:T(8,128)(2,1)S(1)}, u32[]{:S(2)}, u32[]{:S(2)}) collective-permute-start(bf16[256,512]{1,0:T(8,128)(2,1)S(1)} %get-tuple-element.267), channel_id=1, source_target_pairs={{0,2},{1,3},{2,4},{3,5},{4,6},{5,7},{6,0},{7,1},{8,10},{9,11},{10,... | collective-permute-start | bytes 786440 | tf_op jit(solution)/shard_map/ppermute | solution.py:556
  117.7 13.6 %collective-permute-start.37 = (bf16[256,512]{1,0:T(8,128)(2,1)S(1)}, bf16[256,512]{1,0:T(8,128)(2,1)S(1)}, u32[]{:S(2)}, u32[]{:S(2)}) collective-permute-start(bf16[256,512]{1,0:T(8,128)(2,1)S(1)} %get-tuple-element.268), channel_id=1, source_target_pairs={{0,1},{1,0},{2,3},{3,2},{4,5},{5,4},{6,7},{7,6},{8,9},{9,8},{10,11... | collective-permute-start | bytes 786440 | tf_op jit(solution)/shard_map/ppermute | solution.py:556
  125.5 21.2 %copy-start.42 = (bf16[256,512]{1,0:T(8,128)(2,1)}, bf16[256,512]{1,0:T(8,128)(2,1)S(1)}, u32[]{:S(2)}) copy-start(bf16[256,512]{1,0:T(8,128)(2,1)S(1)} %collective-permute-done.38.refs_4_) | copy-start | bytes 786436
  126.5 20.2 %copy-start.43 = (bf16[256,512]{1,0:T(8,128)(2,1)}, bf16[256,512]{1,0:T(8,128)(2,1)S(1)}, u32[]{:S(2)}) copy-start(bf16[256,512]{1,0:T(8,128)(2,1)S(1)} %collective-permute-done.39.refs_5_) | copy-start | bytes 786436
  130.7 16.0 %copy-start.48 = (bf16[256,512]{1,0:T(8,128)(2,1)}, bf16[256,512]{1,0:T(8,128)(2,1)S(1)}, u32[]{:S(2)}) copy-start(bf16[256,512]{1,0:T(8,128)(2,1)S(1)} %collective-permute-done.36.refs_6_) | copy-start | bytes 786436
  131.3 10.5 %copy-start.49 = (bf16[256,512]{1,0:T(8,128)(2,1)}, bf16[256,512]{1,0:T(8,128)(2,1)S(1)}, u32[]{:S(2)}) copy-start(bf16[256,512]{1,0:T(8,128)(2,1)S(1)} %collective-permute-done.37.refs_7_) | copy-start | bytes 786436
  131.3 9.3 %collective-permute-start.40 = (bf16[256,512]{1,0:T(8,128)(2,1)S(1)}, bf16[256,512]{1,0:T(8,128)(2,1)S(1)}, u32[]{:S(2)}, u32[]{:S(2)}) collective-permute-start(bf16[256,512]{1,0:T(8,128)(2,1)S(1)} %broadcast_select_fusion), channel_id=1, source_target_pairs={{0,1},{1,0},{2,3},{3,2},{4,5},{5,4},{6,7},{7,6},{8,9},{9,8},{10,11... | collective-permute-start | bytes 786440 | tf_op jit(solution)/shard_map/ppermute | solution.py:556
  132.5 9.4 %collective-permute-start.41 = (bf16[256,512]{1,0:T(8,128)(2,1)S(1)}, bf16[256,512]{1,0:T(8,128)(2,1)S(1)}, u32[]{:S(2)}, u32[]{:S(2)}) collective-permute-start(bf16[256,512]{1,0:T(8,128)(2,1)S(1)} %get-tuple-element.272), channel_id=1, source_target_pairs={{0,2},{1,3},{2,4},{3,5},{4,6},{5,7},{6,0},{7,1},{8,10},{9,11},{10,... | collective-permute-start | bytes 786440 | tf_op jit(solution)/shard_map/ppermute | solution.py:556
  132.5 12.2 %collective-permute-start.42 = (bf16[256,512]{1,0:T(8,128)(2,1)S(1)}, bf16[256,512]{1,0:T(8,128)(2,1)}, u32[]{:S(2)}, u32[]{:S(2)}) collective-permute-start(bf16[256,512]{1,0:T(8,128)(2,1)S(1)} %get-tuple-element.273), channel_id=1, source_target_pairs={{0,1},{1,0},{2,3},{3,2},{4,5},{5,4},{6,7},{7,6},{8,9},{9,8},{10,11... | collective-permute-start | bytes 786440 | tf_op jit(solution)/shard_map/ppermute | solution.py:556
  140.6 6.0 %copy-start.50 = (bf16[256,512]{1,0:T(8,128)(2,1)}, bf16[256,512]{1,0:T(8,128)(2,1)S(1)}, u32[]{:S(2)}) copy-start(bf16[256,512]{1,0:T(8,128)(2,1)S(1)} %collective-permute-done.40.refs_10_) | copy-start | bytes 786436
  146.7 29.8 %all-to-all-start.1 = ((bf16[8,272,256]{2,1,0:T(8,128)(2,1)}), bf16[8,272,256]{2,1,0:T(8,128)(2,1)S(1)}, u32[]{:S(2)}, u32[]{:S(2)}) async-start(bf16[8,272,256]{2,1,0:T(8,128)(2,1)} %relay.1), calls=%async_computation.1 | async-start | bytes 2228224 | tf_op jit(solution)/shard_map/all_to_all | solution.py:527
  (33 other events, 157.1 us)

commit v7 on v6

--- a/solution.py
+++ b/solution.py
@@ -562,8 +562,8 @@
             own, sends = own_part()
         if late == 1:
             arrived = exchange(after((sends,), *turn)[0], "front")
-        if late >= 2 and late % 2 == 0 and e < events - 1:
-            step(min(4, e - CHAINS + 1 - done), *turn)
+        if late >= 3 and e < events - 1:
+            step(2, *turn)
             turn = (*turn, result)
     passed = relayed(after((arrived,), *held[-1], *held[-2])[0])
     arrived = exchange(passed, "grp")

time: 179 us -> 183 us (1.022)
  starting transfers between devices: 62.5 us -> 59.4 us
  waiting for transfers between devices: 49.7 us -> 52.6 us
  Pallas kernels: 59.1 us -> 61.8 us
  other arithmetic: 2.93 us -> 5.38 us
    ppermute x43, waiting for transfers between devices: 40.3 us -> 45.1 us  [shards(): lax.ppermute(turn[s], 'grp', perms[s])]
    ppermute x43, starting transfers between devices: 55.4 us -> 52.3 us  [shards(): lax.ppermute(turn[s], 'grp', perms[s])]
    pallas_call x4 -> x5, Pallas kernels: 26.9 us -> 29.6 us  [update(): pl.pallas_call(functools.partial(update_kernel, tuple(numbers), room, wid...]
    all_to_all x2, waiting for transfers between devices: 9.42 us -> 7.45 us  [exchange(): return lax.all_to_all(blocks, axis, split_axis=0, concat_axis=0, tiled=True)]
  transfers between devices with their start and end apart: 45 -> 45, of which waited for: 20 -> 21; matrix products, arithmetic and copies ran while one was open for 2% -> 3% of each run, Pallas kernels for 29% -> 30%
where the time goes in v7:
time: 183 us; the launch traced here: 182 us
  Pallas kernels  61.8 us (34%)
  starting transfers between devices  59.4 us (32%)
  waiting for transfers between devices  52.6 us (29%)
  other arithmetic  5.38 us (3%)
    ppermute x43, starting transfers between devices, shards(): lax.ppermute(turn[s], 'grp', perms[s])  52.3 us
    ppermute x43, waiting for transfers between devices, shards(): lax.ppermute(turn[s], 'grp', perms[s])  45.1 us
    pallas_call x5, Pallas kernels, update(): pl.pallas_call(functools.partial(update_kernel, tuple(numbers), room, wid...  29.6 us
    pallas_call x8, Pallas kernels, factor(): pl.pallas_call(functools.partial(factor_kernel, tuple(tiles), head), out_...  24.7 us
    all_to_all x2, waiting for transfers between devices, exchange(): return lax.all_to_all(blocks, axis, split_axis=0, concat_axis=0, tiled=True)  7.45 us
    all_to_all x2, starting transfers between devices, exchange(): return lax.all_to_all(blocks, axis, split_axis=0, concat_axis=0, tiled=True)  7.09 us
    pallas_call x1, Pallas kernels, own_panels(): pl.pallas_call(functools.partial(own_kernel, choices, len(blocks), width...  4.01 us
    select_n x17, other arithmetic, shards(): jnp.where(root, made[which][n], value)  3.98 us
  transfers between devices with their start and end apart: 45, of which 21 were waited for; matrix products, arithmetic and copies ran while one was open for 3% of the time, Pallas kernels for 30%

profile of v7, /device:TPU:0, one launch (start us, length us, event | category | flops | bytes accessed | tf_op | source)
XLA Modules:
  0.0 182.3 jit_solution(8138874393680504929)
XLA Ops:
  1.4 3.8 %factor.8 = (bf16[256,512]{1,0:T(8,128)(2,1)S(1)}, bf16[256,512]{1,0:T(8,128)(2,1)S(1)}, bf16[256,512]{1,0:T(8,128)(2,1)S(1)}, bf16[256,512]{1,0:T(8,128)(2,1)S(...) custom-call(s32[32,4]{1,0:T(8,128)S(1)} %copy.58.mask, bf16[8192,1024]{1,0:T(8,128)(2,1)} %bitcast.9, ...), custom_call_target="tpu_custom_call" | custom-call | flops 805306368 | bytes 2097152 | tf_op jit(solution)/shard_map/factor/pallas_call | solution.py:178
  5.2 3.1 %collective-permute-start = (bf16[256,512]{1,0:T(8,128)(2,1)S(1)}, bf16[256,512]{1,0:T(8,128)(2,1)S(1)}, u32[]{:S(2)}, u32[]{:S(2)}) collective-permute-start(bf16[256,512]{1,0:T(8,128)(2,1)S(1)} %get-tuple-element.148.refs_18_), channel_id=1, source_target_pairs={{0,2},{1,3},{2,4},{3,5},{4,6},{5,7},{6,0},{7,1},{8,10},{9,11},{10,... | collective-permute-start | bytes 786440 | tf_op jit(solution)/shard_map/ppermute | solution.py:556
  8.3 1.5 collective-permute-start.1
  9.8 1.6 collective-permute-start.4
  11.9 3.0 %factor.9 = (bf16[256,512]{1,0:T(8,128)(2,1)S(1)}, bf16[256,512]{1,0:T(8,128)(2,1)S(1)}, bf16[256,512]{1,0:T(8,128)(2,1)S(1)}, bf16[256,512]{1,0:T(8,128)(2,1)S(1)}) custom-call(s32[32,4]{1,0:T(8,128)S(1)} %copy.58.mask, bf16[8192,1024]{1,0:T(8,128)(2,1)} %bitcast.10, bf16[4,256,256]{2,1,0:T(8,128)(2,1)S(1)} %get-tuple-element.230.refs_0_, ...), custom_call_target="tpu_custom_call" | custom-call | flops 805306368 | bytes 2097152 | tf_op jit(solution)/shard_map/factor/pallas_call | solution.py:178
  14.9 2.6 %collective-permute-done.refs_19_.refs_0_ = bf16[256,512]{1,0:T(8,128)(2,1)S(1)} collective-permute-done((bf16[256,512]{1,0:T(8,128)(2,1)S(1)}, bf16[256,512]{1,0:T(8,128)(2,1)S(1)}, u32[]{:S(2)}, u32[]{:S(2)}) %collective-permute-start) | collective-permute-done | bytes 262176 | tf_op jit(solution)/shard_map/ppermute | solution.py:556
  17.6 1.6 collective-permute-start.2
  19.2 1.5 collective-permute-start.3
  20.7 2.3 %collective-permute-done.4.refs_2_ = bf16[256,512]{1,0:T(8,128)(2,1)S(1)} collective-permute-done((bf16[256,512]{1,0:T(8,128)(2,1)S(1)}, bf16[256,512]{1,0:T(8,128)(2,1)S(1)}, u32[]{:S(2)}, u32[]{:S(2)}) %collective-permute-start.4) | collective-permute-done | bytes 262176 | tf_op jit(solution)/shard_map/ppermute | solution.py:556
  23.2 1.6 collective-permute-start.8
  24.8 1.5 collective-permute-start.9
  26.3 3.0 %factor.10 = (bf16[256,512]{1,0:T(8,128)(2,1)S(1)}, bf16[256,512]{1,0:T(8,128)(2,1)S(1)}, bf16[256,512]{1,0:T(8,128)(2,1)S(1)}, bf16[256,512]{1,0:T(8,128)(2,1)S(1)}) custom-call(s32[32,4]{1,0:T(8,128)S(1)} %copy.58.mask, bf16[8192,1024]{1,0:T(8,128)(2,1)} %bitcast.11, bf16[4,256,256]{2,1,0:T(8,128)(2,1)S(1)} %get-tuple-element.230.refs_0_, ...), custom_call_target="tpu_custom_call" | custom-call | flops 805306368 | bytes 2097152 | tf_op jit(solution)/shard_map/factor/pallas_call | solution.py:178
  29.4 1.6 collective-permute-start.6
  31.1 0.9 collective-permute-start.7
  31.9 2.3 %collective-permute-done.8.refs_2_ = bf16[256,512]{1,0:T(8,128)(2,1)S(1)} collective-permute-done((bf16[256,512]{1,0:T(8,128)(2,1)S(1)}, bf16[256,512]{1,0:T(8,128)(2,1)S(1)}, u32[]{:S(2)}, u32[]{:S(2)}) %collective-permute-start.8) | collective-permute-done | bytes 262176 | tf_op jit(solution)/shard_map/ppermute | solution.py:556
  34.4 1.6 collective-permute-start.12
  36.0 1.5 collective-permute-start.13
  37.6 3.0 %factor.11 = (bf16[256,512]{1,0:T(8,128)(2,1)S(1)}, bf16[256,512]{1,0:T(8,128)(2,1)S(1)}, bf16[256,512]{1,0:T(8,128)(2,1)S(1)}, bf16[256,512]{1,0:T(8,128)(2,1)S(1)}) custom-call(s32[32,4]{1,0:T(8,128)S(1)} %copy.58.mask, bf16[8192,1024]{1,0:T(8,128)(2,1)} %bitcast.12, bf16[4,256,256]{2,1,0:T(8,128)(2,1)S(1)} %get-tuple-element.230.refs_0_, ...), custom_call_target="tpu_custom_call" | custom-call | flops 805306368 | bytes 2097152 | tf_op jit(solution)/shard_map/factor/pallas_call | solution.py:178
  40.7 1.6 collective-permute-start.10
  43.2 3.0 %collective-permute-done.12.refs_2_ = bf16[256,512]{1,0:T(8,128)(2,1)S(1)} collective-permute-done((bf16[256,512]{1,0:T(8,128)(2,1)S(1)}, bf16[256,512]{1,0:T(8,128)(2,1)S(1)}, u32[]{:S(2)}, u32[]{:S(2)}) %collective-permute-start.12) | collective-permute-done | bytes 262176 | tf_op jit(solution)/shard_map/ppermute | solution.py:556
  47.3 1.5 collective-permute-start.17
  48.8 3.0 %factor.12 = (bf16[256,512]{1,0:T(8,128)(2,1)S(1)}, bf16[256,512]{1,0:T(8,128)(2,1)S(1)}, bf16[256,512]{1,0:T(8,128)(2,1)S(1)}, bf16[256,512]{1,0:T(8,128)(2,1)S(1)}) custom-call(s32[32,4]{1,0:T(8,128)S(1)} %copy.58.mask, bf16[8192,1024]{1,0:T(8,128)(2,1)} %bitcast.13, bf16[4,256,256]{2,1,0:T(8,128)(2,1)S(1)} %get-tuple-element.230.refs_0_, ...), custom_call_target="tpu_custom_call" | custom-call | flops 805306368 | bytes 2097152 | tf_op jit(solution)/shard_map/factor/pallas_call | solution.py:178
  51.9 1.6 collective-permute-start.14
  54.4 3.5 %collective-permute-done.16.refs_9_.refs_2_ = bf16[256,512]{1,0:T(8,128)(2,1)S(1)} collective-permute-done((bf16[256,512]{1,0:T(8,128)(2,1)S(1)}, bf16[256,512]{1,0:T(8,128)(2,1)S(1)}, u32[]{:S(2)}, u32[]{:S(2)}) %collective-permute-start.16) | collective-permute-done | bytes 262176 | tf_op jit(solution)/shard_map/ppermute | solution.py:556
  58.5 1.5 collective-permute-start.21
  60.0 3.0 %factor.13 = (bf16[256,512]{1,0:T(8,128)(2,1)S(1)}, bf16[256,512]{1,0:T(8,128)(2,1)S(1)}, bf16[256,512]{1,0:T(8,128)(2,1)S(1)}, bf16[256,512]{1,0:T(8,128)(2,1)S(1)}) custom-call(s32[32,4]{1,0:T(8,128)S(1)} %copy.58.mask, bf16[8192,1024]{1,0:T(8,128)(2,1)} %bitcast.14, bf16[4,256,256]{2,1,0:T(8,128)(2,1)S(1)} %get-tuple-element.230.refs_0_, ...), custom_call_target="tpu_custom_call" | custom-call | flops 805306368 | bytes 2097152 | tf_op jit(solution)/shard_map/factor/pallas_call | solution.py:178
  63.6 1.2 collective-permute-start.18
  65.7 3.5 %collective-permute-done.20.refs_8_.refs_6_ = bf16[256,512]{1,0:T(8,128)(2,1)S(1)} collective-permute-done((bf16[256,512]{1,0:T(8,128)(2,1)S(1)}, bf16[256,512]{1,0:T(8,128)(2,1)S(1)}, u32[]{:S(2)}, u32[]{:S(2)}) %collective-permute-start.20) | collective-permute-done | bytes 262176 | tf_op jit(solution)/shard_map/ppermute | solution.py:556
  69.9 1.5 collective-permute-start.23
  71.5 3.0 %factor.14 = (bf16[256,512]{1,0:T(8,128)(2,1)S(1)}, bf16[256,512]{1,0:T(8,128)(2,1)S(1)}, bf16[256,512]{1,0:T(8,128)(2,1)S(1)}, bf16[256,512]{1,0:T(8,128)(2,1)S(1)}) custom-call(s32[32,4]{1,0:T(8,128)S(1)} %copy.58.mask, bf16[8192,1024]{1,0:T(8,128)(2,1)} %bitcast.15, bf16[4,256,256]{2,1,0:T(8,128)(2,1)S(1)} %get-tuple-element.230.refs_0_, ...), custom_call_target="tpu_custom_call" | custom-call | flops 805306368 | bytes 2097152 | tf_op jit(solution)/shard_map/factor/pallas_call | solution.py:178
  74.9 1.4 collective-permute-start.24
  76.9 3.6 %collective-permute-done.22.refs_7_.refs_10_ = bf16[256,512]{1,0:T(8,128)(2,1)S(1)} collective-permute-done((bf16[256,512]{1,0:T(8,128)(2,1)S(1)}, bf16[256,512]{1,0:T(8,128)(2,1)S(1)}, u32[]{:S(2)}, u32[]{:S(2)}) %collective-permute-start.22) | collective-permute-done | bytes 262176 | tf_op jit(solution)/shard_map/ppermute | solution.py:556
  81.0 1.5 collective-permute-start.27
  82.5 3.0 %factor.15 = (bf16[256,512]{1,0:T(8,128)(2,1)S(1)}, bf16[256,512]{1,0:T(8,128)(2,1)S(1)}, bf16[256,512]{1,0:T(8,128)(2,1)S(1)}, bf16[256,512]{1,0:T(8,128)(2,1)S(1)}) custom-call(s32[32,4]{1,0:T(8,128)S(1)} %copy.58.mask, bf16[8192,1024]{1,0:T(8,128)(2,1)} %bitcast.16, bf16[4,256,256]{2,1,0:T(8,128)(2,1)S(1)} %get-tuple-element.230.refs_0_, ...), custom_call_target="tpu_custom_call" | custom-call | flops 805306368 | bytes 2097152 | tf_op jit(solution)/shard_map/factor/pallas_call | solution.py:178
  86.2 1.1 collective-permute-start.28
  88.1 3.6 %collective-permute-done.26.refs_16_.refs_14_ = bf16[256,512]{1,0:T(8,128)(2,1)S(1)} collective-permute-done((bf16[256,512]{1,0:T(8,128)(2,1)S(1)}, bf16[256,512]{1,0:T(8,128)(2,1)S(1)}, u32[]{:S(2)}, u32[]{:S(2)}) %collective-permute-start.26) | collective-permute-done | bytes 262176 | tf_op jit(solution)/shard_map/ppermute | solution.py:556
  92.2 1.5 collective-permute-start.31
  93.7 3.6 %collective-permute-done.28.refs_0_ = bf16[256,512]{1,0:T(8,128)(2,1)S(1)} collective-permute-done((bf16[256,512]{1,0:T(8,128)(2,1)S(1)}, bf16[256,512]{1,0:T(8,128)(2,1)S(1)}, u32[]{:S(2)}, u32[]{:S(2)}) %collective-permute-start.28) | collective-permute-done | bytes 262176 | tf_op jit(solution)/shard_map/ppermute | solution.py:556
  97.3 1.0 select_select_fusion.2
  98.6 1.5 collective-permute-start.35
  100.2 2.6 %collective-permute-done.30.refs_2_ = bf16[256,512]{1,0:T(8,128)(2,1)S(1)} collective-permute-done((bf16[256,512]{1,0:T(8,128)(2,1)S(1)}, bf16[256,512]{1,0:T(8,128)(2,1)S(1)}, u32[]{:S(2)}, u32[]{:S(2)}) %collective-permute-start.30) | collective-permute-done | bytes 262176 | tf_op jit(solution)/shard_map/ppermute | solution.py:556
  102.8 0.9 select_select_fusion.1
  104.2 1.5 collective-permute-start.33
  105.8 4.0 %own_panels.1 = (bf16[512,1024]{1,0:T(8,128)(2,1)S(1)}, bf16[4,528,256]{2,1,0:T(8,128)(2,1)}) custom-call(s32[32,4]{1,0:T(8,128)S(1)} %copy.58.mask, s32[4]{0:T(128)S(1)} %bitcast.8, s32[1]{0:T(128)} %bitcast.1.me, bf16[8192,1024]{1,0:T(8,128)(2,1)} %bitcast.17, bf16[256,512]{1,0:T(8,128)(2,1)} %copy-done.4, bf16[256,512]{1,0:T(8,128)(2,1)} %copy-done.19, ...), custom_call_target="tpu_custom_call" | custom-call | flops 268435456 | bytes 2621440 | tf_op jit(solution)/shard_map/own_panels/pallas_call | solution.py:238
  109.9 3.5 %all-to-all-start = ((bf16[4,528,256]{2,1,0:T(8,128)(2,1)}), bf16[4,528,256]{2,1,0:T(8,128)(2,1)S(1)}, u32[]{:S(2)}, u32[]{:S(2)}) async-start(bf16[4,528,256]{2,1,0:T(8,128)(2,1)} %get-tuple-element.255), calls=%async_computation | async-start | bytes 2162688 | tf_op jit(solution)/shard_map/all_to_all | solution.py:527
  113.4 1.2 select_select_fusion
  114.6 1.6 collective-permute-start.38
  116.7 1.1 broadcast_select_fusion.2
  117.8 2.9 %update.5.refs_4_ = bf16[8192,1024]{1,0:T(8,128)(2,1)} custom-call(s32[8,44]{1,0:T(8,128)S(1)} %copy-done.5, s32[32,4]{1,0:T(8,128)S(1)} %copy.58.mask, s32[1]{0:T(128)} %bitcast.1.me, bf16[512,1024]{1,0:T(8,128)(2,1)S(1)} %get-tuple-element.267.own, bf16[8192,1024]{1,0:T(8,128)(2,1)} %bitcast.18, bf16[256,512]{1,0:T(8,128)(2,1)} %copy-done.7, ...), custom_call_target="tpu_custom_call" | custom-call | flops 1073741824 | bytes 4194304 | tf_op jit(solution)/shard_map/update/pallas_call | solution.py:403
  120.6 2.1 %collective-permute-start.36 = (bf16[256,512]{1,0:T(8,128)(2,1)S(1)}, bf16[256,512]{1,0:T(8,128)(2,1)S(1)}, u32[]{:S(2)}, u32[]{:S(2)}) collective-permute-start(bf16[256,512]{1,0:T(8,128)(2,1)S(1)} %get-tuple-element.268), channel_id=1, source_target_pairs={{0,2},{1,3},{2,4},{3,5},{4,6},{5,7},{6,0},{7,1},{8,10},{9,11},{10,... | collective-permute-start | bytes 786440 | tf_op jit(solution)/shard_map/ppermute | solution.py:556
  122.8 0.9 collective-permute-start.37
  123.7 4.1 %update.6.refs_4_ = bf16[8192,1024]{1,0:T(8,128)(2,1)} custom-call(s32[8,44]{1,0:T(8,128)S(1)} %copy-done.5, s32[32,4]{1,0:T(8,128)S(1)} %copy.58.mask, s32[1]{0:T(128)} %bitcast.1.me, bf16[512,1024]{1,0:T(8,128)(2,1)S(1)} %get-tuple-element.267.own, bf16[8192,1024]{1,0:T(8,128)(2,1)} %bitcast.19, ...), custom_call_target="tpu_custom_call", output_to_operand_aliasing={{}: (9, {})} | custom-call | flops 1073741824 | bytes 4194304 | tf_op jit(solution)/shard_map/update/pallas_call | solution.py:403
  127.9 2.9 %collective-permute-done.36.refs_10_ = bf16[256,512]{1,0:T(8,128)(2,1)S(1)} collective-permute-done((bf16[256,512]{1,0:T(8,128)(2,1)S(1)}, bf16[256,512]{1,0:T(8,128)(2,1)S(1)}, u32[]{:S(2)}, u32[]{:S(2)}) %collective-permute-start.36) | collective-permute-done | bytes 262176 | tf_op jit(solution)/shard_map/ppermute | solution.py:556
  130.7 4.1 %update.7.refs_16_ = bf16[8192,1024]{1,0:T(8,128)(2,1)} custom-call(s32[8,44]{1,0:T(8,128)S(1)} %copy-done.5, s32[32,4]{1,0:T(8,128)S(1)} %copy.58.mask, s32[1]{0:T(128)} %bitcast.1.me, bf16[512,1024]{1,0:T(8,128)(2,1)S(1)} %get-tuple-element.267.own, bf16[8192,1024]{1,0:T(8,128)(2,1)} %bitcast.20, ...), custom_call_target="tpu_custom_call", output_to_operand_aliasing={{}: (9, {})} | custom-call | flops 1073741824 | bytes 4194304 | tf_op jit(solution)/shard_map/update/pallas_call | solution.py:403
  134.9 2.7 %collective-permute-start.40 = (bf16[256,512]{1,0:T(8,128)(2,1)S(1)}, bf16[256,512]{1,0:T(8,128)(2,1)S(1)}, u32[]{:S(2)}, u32[]{:S(2)}) collective-permute-start(bf16[256,512]{1,0:T(8,128)(2,1)S(1)} %broadcast_select_fusion), channel_id=1, source_target_pairs={{0,1},{1,0},{2,3},{3,2},{4,5},{5,4},{6,7},{7,6},{8,9},{9,8},{10,11... | collective-permute-start | bytes 786440 | tf_op jit(solution)/shard_map/ppermute | solution.py:556
  138.5 6.4 %collective-permute-done.40.refs_14_ = bf16[256,512]{1,0:T(8,128)(2,1)S(1)} collective-permute-done((bf16[256,512]{1,0:T(8,128)(2,1)S(1)}, bf16[256,512]{1,0:T(8,128)(2,1)S(1)}, u32[]{:S(2)}, u32[]{:S(2)}) %collective-permute-start.40) | collective-permute-done | bytes 262176 | tf_op jit(solution)/shard_map/ppermute | solution.py:556
  144.9 1.5 collective-permute-done.41.refs_12_
  146.4 2.4 %collective-permute-done.42.refs_13_ = bf16[256,512]{1,0:T(8,128)(2,1)S(1)} collective-permute-done((bf16[256,512]{1,0:T(8,128)(2,1)S(1)}, bf16[256,512]{1,0:T(8,128)(2,1)S(1)}, u32[]{:S(2)}, u32[]{:S(2)}) %collective-permute-start.42) | collective-permute-done | bytes 262176 | tf_op jit(solution)/shard_map/ppermute | solution.py:556
  149.0 1.8 relay.1
  150.8 3.6 %all-to-all-start.1 = ((bf16[8,272,256]{2,1,0:T(8,128)(2,1)}), bf16[8,272,256]{2,1,0:T(8,128)(2,1)S(1)}, u32[]{:S(2)}, u32[]{:S(2)}) async-start(bf16[8,272,256]{2,1,0:T(8,128)(2,1)} %relay.1), calls=%async_computation.1 | async-start | bytes 2228224 | tf_op jit(solution)/shard_map/all_to_all | solution.py:527
  154.3 10.3 %update.8.refs_15_ = bf16[8192,1024]{1,0:T(8,128)(2,1)} custom-call(s32[8,44]{1,0:T(8,128)S(1)} %copy-done.5, s32[32,4]{1,0:T(8,128)S(1)} %copy.58.mask, s32[1]{0:T(128)} %bitcast.1.me, bf16[512,1024]{1,0:T(8,128)(2,1)S(1)} %get-tuple-element.267.own, bf16[8192,1024]{1,0:T(8,128)(2,1)} %bitcast.21, ...), custom_call_target="tpu_custom_call", output_to_operand_aliasing={{}: (21, {})} | custom-call | flops 4294967296 | bytes 16777216 | tf_op jit(solution)/shard_map/update/pallas_call | solution.py:403
  164.6 8.3 %update.9 = bf16[8192,1024]{1,0:T(8,128)(2,1)} custom-call(s32[8,44]{1,0:T(8,128)S(1)} %copy-done.5, s32[32,4]{1,0:T(8,128)S(1)} %copy.58.mask, s32[1]{0:T(128)} %bitcast.1.me, bf16[512,1024]{1,0:T(8,128)(2,1)S(1)} %get-tuple-element.267.own, bf16[8192,1024]{1,0:T(8,128)(2,1)} %bitcast.22, ...), custom_call_target="tpu_custom_call", output_to_operand_aliasing={{}: (20, {})} | custom-call | flops 4294967296 | bytes 16777216 | tf_op jit(solution)/shard_map/update/pallas_call | solution.py:403
  172.9 7.4 %all-to-all-done.1.arrived = bf16[8,272,256]{2,1,0:T(8,128)(2,1)S(1)} async-done(((bf16[8,272,256]{2,1,0:T(8,128)(2,1)}), bf16[8,272,256]{2,1,0:T(8,128)(2,1)S(1)}, u32[]{:S(2)}, u32[]{:S(2)}) %all-to-all-start.1) | async-done | bytes 1114144 | tf_op jit(solution)/shard_map/all_to_all | solution.py:527
  180.6 1.7 sum_parents.1
  (160 shorter events, 13.8 us)
Async XLA Ops:
  5.2 24.1 %copy-start.3 = (bf16[256,512]{1,0:T(8,128)(2,1)}, bf16[256,512]{1,0:T(8,128)(2,1)S(1)}, u32[]{:S(2)}) copy-start(bf16[256,512]{1,0:T(8,128)(2,1)S(1)} %get-tuple-element.148.refs_18_) | copy-start | bytes 786436
  5.2 12.2 %collective-permute-start = (bf16[256,512]{1,0:T(8,128)(2,1)S(1)}, bf16[256,512]{1,0:T(8,128)(2,1)S(1)}, u32[]{:S(2)}, u32[]{:S(2)}) collective-permute-start(bf16[256,512]{1,0:T(8,128)(2,1)S(1)} %get-tuple-element.148.refs_18_), channel_id=1, source_target_pairs={{0,2},{1,3},{2,4},{3,5},{4,6},{5,7},{6,0},{7,1},{8,10},{9,11},{10,... | collective-permute-start | bytes 786440 | tf_op jit(solution)/shard_map/ppermute | solution.py:556
  8.3 9.2 %collective-permute-start.1 = (bf16[256,512]{1,0:T(8,128)(2,1)S(1)}, bf16[256,512]{1,0:T(8,128)(2,1)S(1)}, u32[]{:S(2)}, u32[]{:S(2)}) collective-permute-start(bf16[256,512]{1,0:T(8,128)(2,1)S(1)} %get-tuple-element.149), channel_id=1, source_target_pairs={{0,1},{1,0},{2,3},{3,2},{4,5},{5,4},{6,7},{7,6},{8,9},{9,8},{10,11... | collective-permute-start | bytes 786440 | tf_op jit(solution)/shard_map/ppermute | solution.py:556
  9.8 13.3 %collective-permute-start.4 = (bf16[256,512]{1,0:T(8,128)(2,1)S(1)}, bf16[256,512]{1,0:T(8,128)(2,1)S(1)}, u32[]{:S(2)}, u32[]{:S(2)}) collective-permute-start(bf16[256,512]{1,0:T(8,128)(2,1)S(1)} %get-tuple-element.150), channel_id=1, source_target_pairs={{0,2},{1,3},{2,4},{3,5},{4,6},{5,7},{6,0},{7,1},{8,10},{9,11},{10,... | collective-permute-start | bytes 786440 | tf_op jit(solution)/shard_map/ppermute | solution.py:556
  11.4 11.8 %collective-permute-start.5 = (bf16[256,512]{1,0:T(8,128)(2,1)S(1)}, bf16[256,512]{1,0:T(8,128)(2,1)S(1)}, u32[]{:S(2)}, u32[]{:S(2)}) collective-permute-start(bf16[256,512]{1,0:T(8,128)(2,1)S(1)} %get-tuple-element.151), channel_id=1, source_target_pairs={{0,1},{1,0},{2,3},{3,2},{4,5},{5,4},{6,7},{7,6},{8,9},{9,8},{10,11... | collective-permute-start | bytes 786440 | tf_op jit(solution)/shard_map/ppermute | solution.py:556
  17.4 23.1 %copy-start.7 = (bf16[256,512]{1,0:T(8,128)(2,1)}, bf16[256,512]{1,0:T(8,128)(2,1)S(1)}, u32[]{:S(2)}) copy-start(bf16[256,512]{1,0:T(8,128)(2,1)S(1)} %collective-permute-done.refs_19_.refs_0_) | copy-start | bytes 786436
  17.5 23.1 %copy-start.26 = (bf16[256,512]{1,0:T(8,128)(2,1)}, bf16[256,512]{1,0:T(8,128)(2,1)S(1)}, u32[]{:S(2)}) copy-start(bf16[256,512]{1,0:T(8,128)(2,1)S(1)} %collective-permute-done.1.refs_1_) | copy-start | bytes 786436
  17.6 11.8 %collective-permute-start.2 = (bf16[256,512]{1,0:T(8,128)(2,1)S(1)}, bf16[256,512]{1,0:T(8,128)(2,1)S(1)}, u32[]{:S(2)}, u32[]{:S(2)}) collective-permute-start(bf16[256,512]{1,0:T(8,128)(2,1)S(1)} %get-tuple-element.158), channel_id=1, source_target_pairs={{0,2},{1,3},{2,4},{3,5},{4,6},{5,7},{6,0},{7,1},{8,10},{9,11},{10,... | collective-permute-start | bytes 786440 | tf_op jit(solution)/shard_map/ppermute | solution.py:556
  19.2 10.1 %collective-permute-start.3 = (bf16[256,512]{1,0:T(8,128)(2,1)S(1)}, bf16[256,512]{1,0:T(8,128)(2,1)S(1)}, u32[]{:S(2)}, u32[]{:S(2)}) collective-permute-start(bf16[256,512]{1,0:T(8,128)(2,1)S(1)} %get-tuple-element.159), channel_id=1, source_target_pairs={{0,1},{1,0},{2,3},{3,2},{4,5},{5,4},{6,7},{7,6},{8,9},{9,8},{10,11... | collective-permute-start | bytes 786440 | tf_op jit(solution)/shard_map/ppermute | solution.py:556
  23.2 11.1 %collective-permute-start.8 = (bf16[256,512]{1,0:T(8,128)(2,1)S(1)}, bf16[256,512]{1,0:T(8,128)(2,1)S(1)}, u32[]{:S(2)}, u32[]{:S(2)}) collective-permute-start(bf16[256,512]{1,0:T(8,128)(2,1)S(1)} %get-tuple-element.167), channel_id=1, source_target_pairs={{0,2},{1,3},{2,4},{3,5},{4,6},{5,7},{6,0},{7,1},{8,10},{9,11},{10,... | collective-permute-start | bytes 786440 | tf_op jit(solution)/shard_map/ppermute | solution.py:556
  24.8 9.5 %collective-permute-start.9 = (bf16[256,512]{1,0:T(8,128)(2,1)S(1)}, bf16[256,512]{1,0:T(8,128)(2,1)S(1)}, u32[]{:S(2)}, u32[]{:S(2)}) collective-permute-start(bf16[256,512]{1,0:T(8,128)(2,1)S(1)} %get-tuple-element.168), channel_id=1, source_target_pairs={{0,1},{1,0},{2,3},{3,2},{4,5},{5,4},{6,7},{7,6},{8,9},{9,8},{10,11... | collective-permute-start | bytes 786440 | tf_op jit(solution)/shard_map/ppermute | solution.py:556
  29.3 22.5 %copy-start.8 = (bf16[256,512]{1,0:T(8,128)(2,1)}, bf16[256,512]{1,0:T(8,128)(2,1)S(1)}, u32[]{:S(2)}) copy-start(bf16[256,512]{1,0:T(8,128)(2,1)S(1)} %collective-permute-done.2.refs_21_.refs_0_) | copy-start | bytes 786436
  29.4 22.5 %copy-start.9 = (bf16[256,512]{1,0:T(8,128)(2,1)}, bf16[256,512]{1,0:T(8,128)(2,1)S(1)}, u32[]{:S(2)}) copy-start(bf16[256,512]{1,0:T(8,128)(2,1)S(1)} %collective-permute-done.3.refs_20_.refs_1_) | copy-start | bytes 786436
  29.4 11.2 %collective-permute-start.6 = (bf16[256,512]{1,0:T(8,128)(2,1)S(1)}, bf16[256,512]{1,0:T(8,128)(2,1)S(1)}, u32[]{:S(2)}, u32[]{:S(2)}) collective-permute-start(bf16[256,512]{1,0:T(8,128)(2,1)S(1)} %get-tuple-element.172), channel_id=1, source_target_pairs={{0,2},{1,3},{2,4},{3,5},{4,6},{5,7},{6,0},{7,1},{8,10},{9,11},{10,... | collective-permute-start | bytes 786440 | tf_op jit(solution)/shard_map/ppermute | solution.py:556
  31.1 9.6 %collective-permute-start.7 = (bf16[256,512]{1,0:T(8,128)(2,1)S(1)}, bf16[256,512]{1,0:T(8,128)(2,1)S(1)}, u32[]{:S(2)}, u32[]{:S(2)}) collective-permute-start(bf16[256,512]{1,0:T(8,128)(2,1)S(1)} %get-tuple-element.173), channel_id=1, source_target_pairs={{0,1},{1,0},{2,3},{3,2},{4,5},{5,4},{6,7},{7,6},{8,9},{9,8},{10,11... | collective-permute-start | bytes 786440 | tf_op jit(solution)/shard_map/ppermute | solution.py:556
  34.4 11.7 %collective-permute-start.12 = (bf16[256,512]{1,0:T(8,128)(2,1)S(1)}, bf16[256,512]{1,0:T(8,128)(2,1)S(1)}, u32[]{:S(2)}, u32[]{:S(2)}) collective-permute-start(bf16[256,512]{1,0:T(8,128)(2,1)S(1)} %get-tuple-element.181), channel_id=1, source_target_pairs={{0,2},{1,3},{2,4},{3,5},{4,6},{5,7},{6,0},{7,1},{8,10},{9,11},{10,... | collective-permute-start | bytes 786440 | tf_op jit(solution)/shard_map/ppermute | solution.py:556
  36.0 10.1 %collective-permute-start.13 = (bf16[256,512]{1,0:T(8,128)(2,1)S(1)}, bf16[256,512]{1,0:T(8,128)(2,1)S(1)}, u32[]{:S(2)}, u32[]{:S(2)}) collective-permute-start(bf16[256,512]{1,0:T(8,128)(2,1)S(1)} %get-tuple-element.182), channel_id=1, source_target_pairs={{0,1},{1,0},{2,3},{3,2},{4,5},{5,4},{6,7},{7,6},{8,9},{9,8},{10,11... | collective-permute-start | bytes 786440 | tf_op jit(solution)/shard_map/ppermute | solution.py:556
  40.6 22.4 %copy-start.11 = (bf16[256,512]{1,0:T(8,128)(2,1)}, bf16[256,512]{1,0:T(8,128)(2,1)S(1)}, u32[]{:S(2)}) copy-start(bf16[256,512]{1,0:T(8,128)(2,1)S(1)} %collective-permute-done.6.refs_23_.refs_0_) | copy-start | bytes 786436
  40.6 22.4 %copy-start.13 = (bf16[256,512]{1,0:T(8,128)(2,1)}, bf16[256,512]{1,0:T(8,128)(2,1)S(1)}, u32[]{:S(2)}) copy-start(bf16[256,512]{1,0:T(8,128)(2,1)S(1)} %collective-permute-done.7.refs_22_.refs_1_) | copy-start | bytes 786436
  40.7 11.1 %collective-permute-start.10 = (bf16[256,512]{1,0:T(8,128)(2,1)S(1)}, bf16[256,512]{1,0:T(8,128)(2,1)S(1)}, u32[]{:S(2)}, u32[]{:S(2)}) collective-permute-start(bf16[256,512]{1,0:T(8,128)(2,1)S(1)} %get-tuple-element.186), channel_id=1, source_target_pairs={{0,2},{1,3},{2,4},{3,5},{4,6},{5,7},{6,0},{7,1},{8,10},{9,11},{10,... | collective-permute-start | bytes 786440 | tf_op jit(solution)/shard_map/ppermute | solution.py:556
  42.3 9.5 %collective-permute-start.11 = (bf16[256,512]{1,0:T(8,128)(2,1)S(1)}, bf16[256,512]{1,0:T(8,128)(2,1)S(1)}, u32[]{:S(2)}, u32[]{:S(2)}) collective-permute-start(bf16[256,512]{1,0:T(8,128)(2,1)S(1)} %get-tuple-element.187), channel_id=1, source_target_pairs={{0,1},{1,0},{2,3},{3,2},{4,5},{5,4},{6,7},{7,6},{8,9},{9,8},{10,11... | collective-permute-start | bytes 786440 | tf_op jit(solution)/shard_map/ppermute | solution.py:556
  46.9 11.0 %collective-permute-start.16 = (bf16[256,512]{1,0:T(8,128)(2,1)S(1)}, bf16[256,512]{1,0:T(8,128)(2,1)S(1)}, u32[]{:S(2)}, u32[]{:S(2)}) collective-permute-start(bf16[256,512]{1,0:T(8,128)(2,1)S(1)} %get-tuple-element.195), channel_id=1, source_target_pairs={{0,2},{1,3},{2,4},{3,5},{4,6},{5,7},{6,0},{7,1},{8,10},{9,11},{10,... | collective-permute-start | bytes 786440 | tf_op jit(solution)/shard_map/ppermute | solution.py:556
  47.3 10.6 %collective-permute-start.17 = (bf16[256,512]{1,0:T(8,128)(2,1)S(1)}, bf16[256,512]{1,0:T(8,128)(2,1)S(1)}, u32[]{:S(2)}, u32[]{:S(2)}) collective-permute-start(bf16[256,512]{1,0:T(8,128)(2,1)S(1)} %get-tuple-element.196), channel_id=1, source_target_pairs={{0,1},{1,0},{2,3},{3,2},{4,5},{5,4},{6,7},{7,6},{8,9},{9,8},{10,11... | collective-permute-start | bytes 786440 | tf_op jit(solution)/shard_map/ppermute | solution.py:556
  51.8 22.6 %copy-start.10 = (bf16[256,512]{1,0:T(8,128)(2,1)}, bf16[256,512]{1,0:T(8,128)(2,1)S(1)}, u32[]{:S(2)}) copy-start(bf16[256,512]{1,0:T(8,128)(2,1)S(1)} %collective-permute-done.10.refs_4_.refs_0_) | copy-start | bytes 786436
  51.9 22.6 %copy-start.12 = (bf16[256,512]{1,0:T(8,128)(2,1)}, bf16[256,512]{1,0:T(8,128)(2,1)S(1)}, u32[]{:S(2)}) copy-start(bf16[256,512]{1,0:T(8,128)(2,1)S(1)} %collective-permute-done.11.refs_17_.refs_1_) | copy-start | bytes 786436
  51.9 11.6 %collective-permute-start.14 = (bf16[256,512]{1,0:T(8,128)(2,1)S(1)}, bf16[256,512]{1,0:T(8,128)(2,1)S(1)}, u32[]{:S(2)}, u32[]{:S(2)}) collective-permute-start(bf16[256,512]{1,0:T(8,128)(2,1)S(1)} %get-tuple-element.200), channel_id=1, source_target_pairs={{0,2},{1,3},{2,4},{3,5},{4,6},{5,7},{6,0},{7,1},{8,10},{9,11},{10,... | collective-permute-start | bytes 786440 | tf_op jit(solution)/shard_map/ppermute | solution.py:556
  53.6 9.9 %collective-permute-start.15 = (bf16[256,512]{1,0:T(8,128)(2,1)S(1)}, bf16[256,512]{1,0:T(8,128)(2,1)S(1)}, u32[]{:S(2)}, u32[]{:S(2)}) collective-permute-start(bf16[256,512]{1,0:T(8,128)(2,1)S(1)} %get-tuple-element.201), channel_id=1, source_target_pairs={{0,1},{1,0},{2,3},{3,2},{4,5},{5,4},{6,7},{7,6},{8,9},{9,8},{10,11... | collective-permute-start | bytes 786440 | tf_op jit(solution)/shard_map/ppermute | solution.py:556
  58.0 11.2 %collective-permute-start.20 = (bf16[256,512]{1,0:T(8,128)(2,1)S(1)}, bf16[256,512]{1,0:T(8,128)(2,1)S(1)}, u32[]{:S(2)}, u32[]{:S(2)}) collective-permute-start(bf16[256,512]{1,0:T(8,128)(2,1)S(1)} %get-tuple-element.209), channel_id=1, source_target_pairs={{0,2},{1,3},{2,4},{3,5},{4,6},{5,7},{6,0},{7,1},{8,10},{9,11},{10,... | collective-permute-start | bytes 786440 | tf_op jit(solution)/shard_map/ppermute | solution.py:556
  58.5 10.6 %collective-permute-start.21 = (bf16[256,512]{1,0:T(8,128)(2,1)S(1)}, bf16[256,512]{1,0:T(8,128)(2,1)S(1)}, u32[]{:S(2)}, u32[]{:S(2)}) collective-permute-start(bf16[256,512]{1,0:T(8,128)(2,1)S(1)} %get-tuple-element.210), channel_id=1, source_target_pairs={{0,1},{1,0},{2,3},{3,2},{4,5},{5,4},{6,7},{7,6},{8,9},{9,8},{10,11... | collective-permute-start | bytes 786440 | tf_op jit(solution)/shard_map/ppermute | solution.py:556
  63.5 22.0 %copy-start.16 = (bf16[256,512]{1,0:T(8,128)(2,1)}, bf16[256,512]{1,0:T(8,128)(2,1)S(1)}, u32[]{:S(2)}) copy-start(bf16[256,512]{1,0:T(8,128)(2,1)S(1)} %collective-permute-done.14.refs_3_.refs_4_) | copy-start | bytes 786436
  63.6 11.2 %collective-permute-start.18 = (bf16[256,512]{1,0:T(8,128)(2,1)S(1)}, bf16[256,512]{1,0:T(8,128)(2,1)S(1)}, u32[]{:S(2)}, u32[]{:S(2)}) collective-permute-start(bf16[256,512]{1,0:T(8,128)(2,1)S(1)} %get-tuple-element.214), channel_id=1, source_target_pairs={{0,2},{1,3},{2,4},{3,5},{4,6},{5,7},{6,0},{7,1},{8,10},{9,11},{10,... | collective-permute-start | bytes 786440 | tf_op jit(solution)/shard_map/ppermute | solution.py:556
  64.8 10.0 %collective-permute-start.19 = (bf16[256,512]{1,0:T(8,128)(2,1)S(1)}, bf16[256,512]{1,0:T(8,128)(2,1)S(1)}, u32[]{:S(2)}, u32[]{:S(2)}) collective-permute-start(bf16[256,512]{1,0:T(8,128)(2,1)S(1)} %get-tuple-element.215), channel_id=1, source_target_pairs={{0,1},{1,0},{2,3},{3,2},{4,5},{5,4},{6,7},{7,6},{8,9},{9,8},{10,11... | collective-permute-start | bytes 786440 | tf_op jit(solution)/shard_map/ppermute | solution.py:556
  69.2 11.3 %collective-permute-start.22 = (bf16[256,512]{1,0:T(8,128)(2,1)S(1)}, bf16[256,512]{1,0:T(8,128)(2,1)S(1)}, u32[]{:S(2)}, u32[]{:S(2)}) collective-permute-start(bf16[256,512]{1,0:T(8,128)(2,1)S(1)} %get-tuple-element.223), channel_id=1, source_target_pairs={{0,2},{1,3},{2,4},{3,5},{4,6},{5,7},{6,0},{7,1},{8,10},{9,11},{10,... | collective-permute-start | bytes 786440 | tf_op jit(solution)/shard_map/ppermute | solution.py:556
  69.9 10.5 %collective-permute-start.23 = (bf16[256,512]{1,0:T(8,128)(2,1)S(1)}, bf16[256,512]{1,0:T(8,128)(2,1)S(1)}, u32[]{:S(2)}, u32[]{:S(2)}) collective-permute-start(bf16[256,512]{1,0:T(8,128)(2,1)S(1)} %get-tuple-element.224), channel_id=1, source_target_pairs={{0,1},{1,0},{2,3},{3,2},{4,5},{5,4},{6,7},{7,6},{8,9},{9,8},{10,11... | collective-permute-start | bytes 786440 | tf_op jit(solution)/shard_map/ppermute | solution.py:556
  74.5 31.3 %copy-start.6 = (s32[1,1,4]{2,1,0:T(1,128)S(1)}, s32[1,1,4]{2,1,0:T(1,128)}, u32[]{:S(2)}) copy-start(s32[1,1,4]{2,1,0:T(1,128)} %param.8) | copy-start | bytes 52
  74.7 31.0 %copy-start.18 = (bf16[256,512]{1,0:T(8,128)(2,1)}, bf16[256,512]{1,0:T(8,128)(2,1)S(1)}, u32[]{:S(2)}) copy-start(bf16[256,512]{1,0:T(8,128)(2,1)S(1)} %collective-permute-done.18.refs_2_.refs_8_) | copy-start | bytes 786436
  74.8 31.0 %copy-start.19 = (bf16[256,512]{1,0:T(8,128)(2,1)}, bf16[256,512]{1,0:T(8,128)(2,1)S(1)}, u32[]{:S(2)}) copy-start(bf16[256,512]{1,0:T(8,128)(2,1)S(1)} %collective-permute-done.19.refs_1_.refs_9_) | copy-start | bytes 786436
  74.9 11.2 %collective-permute-start.24 = (bf16[256,512]{1,0:T(8,128)(2,1)S(1)}, bf16[256,512]{1,0:T(8,128)(2,1)S(1)}, u32[]{:S(2)}, u32[]{:S(2)}) collective-permute-start(bf16[256,512]{1,0:T(8,128)(2,1)S(1)} %get-tuple-element.228), channel_id=1, source_target_pairs={{0,2},{1,3},{2,4},{3,5},{4,6},{5,7},{6,0},{7,1},{8,10},{9,11},{10,... | collective-permute-start | bytes 786440 | tf_op jit(solution)/shard_map/ppermute | solution.py:556
  76.3 9.8 %collective-permute-start.25 = (bf16[256,512]{1,0:T(8,128)(2,1)S(1)}, bf16[256,512]{1,0:T(8,128)(2,1)S(1)}, u32[]{:S(2)}, u32[]{:S(2)}) collective-permute-start(bf16[256,512]{1,0:T(8,128)(2,1)S(1)} %get-tuple-element.229), channel_id=1, source_target_pairs={{0,1},{1,0},{2,3},{3,2},{4,5},{5,4},{6,7},{7,6},{8,9},{9,8},{10,11... | collective-permute-start | bytes 786440 | tf_op jit(solution)/shard_map/ppermute | solution.py:556
  80.5 25.3 %copy-start.20 = (bf16[256,512]{1,0:T(8,128)(2,1)}, bf16[256,512]{1,0:T(8,128)(2,1)S(1)}, u32[]{:S(2)}) copy-start(bf16[256,512]{1,0:T(8,128)(2,1)S(1)} %collective-permute-done.22.refs_7_.refs_10_) | copy-start | bytes 786436
  80.5 25.3 %copy-start.21 = (bf16[256,512]{1,0:T(8,128)(2,1)}, bf16[256,512]{1,0:T(8,128)(2,1)S(1)}, u32[]{:S(2)}) copy-start(bf16[256,512]{1,0:T(8,128)(2,1)S(1)} %collective-permute-done.23.refs_6_.refs_11_) | copy-start | bytes 786436
  80.6 11.2 %collective-permute-start.26 = (bf16[256,512]{1,0:T(8,128)(2,1)S(1)}, bf16[256,512]{1,0:T(8,128)(2,1)S(1)}, u32[]{:S(2)}, u32[]{:S(2)}) collective-permute-start(bf16[256,512]{1,0:T(8,128)(2,1)S(1)} %get-tuple-element.239), channel_id=1, source_target_pairs={{0,2},{1,3},{2,4},{3,5},{4,6},{5,7},{6,0},{7,1},{8,10},{9,11},{10,... | collective-permute-start | bytes 786440 | tf_op jit(solution)/shard_map/ppermute | solution.py:556
  81.0 10.7 %collective-permute-start.27 = (bf16[256,512]{1,0:T(8,128)(2,1)S(1)}, bf16[256,512]{1,0:T(8,128)(2,1)S(1)}, u32[]{:S(2)}, u32[]{:S(2)}) collective-permute-start(bf16[256,512]{1,0:T(8,128)(2,1)S(1)} %get-tuple-element.240), channel_id=1, source_target_pairs={{0,1},{1,0},{2,3},{3,2},{4,5},{5,4},{6,7},{7,6},{8,9},{9,8},{10,11... | collective-permute-start | bytes 786440 | tf_op jit(solution)/shard_map/ppermute | solution.py:556
  85.5 20.2 %copy-start = (bf16[256,512]{1,0:T(8,128)(2,1)}, bf16[256,512]{1,0:T(8,128)(2,1)S(1)}, u32[]{:S(2)}) copy-start(bf16[256,512]{1,0:T(8,128)(2,1)S(1)} %get-tuple-element.236.refs_11_) | copy-start | bytes 786436
  86.1 31.6 %copy-start.5 = (s32[8,44]{1,0:T(8,128)S(1)}, s32[8,44]{1,0:T(8,128)}, u32[]{:S(2)}) copy-start(s32[8,44]{1,0:T(8,128)} %constant.14.clone.table) | copy-start | bytes 4228
  86.2 11.1 %collective-permute-start.28 = (bf16[256,512]{1,0:T(8,128)(2,1)S(1)}, bf16[256,512]{1,0:T(8,128)(2,1)S(1)}, u32[]{:S(2)}, u32[]{:S(2)}) collective-permute-start(bf16[256,512]{1,0:T(8,128)(2,1)S(1)} %get-tuple-element.244), channel_id=1, source_target_pairs={{0,2},{1,3},{2,4},{3,5},{4,6},{5,7},{6,0},{7,1},{8,10},{9,11},{10,... | collective-permute-start | bytes 786440 | tf_op jit(solution)/shard_map/ppermute | solution.py:556
  87.3 10.0 %collective-permute-start.29 = (bf16[256,512]{1,0:T(8,128)(2,1)S(1)}, bf16[256,512]{1,0:T(8,128)(2,1)S(1)}, u32[]{:S(2)}, u32[]{:S(2)}) collective-permute-start(bf16[256,512]{1,0:T(8,128)(2,1)S(1)} %get-tuple-element.245), channel_id=1, source_target_pairs={{0,1},{1,0},{2,3},{3,2},{4,5},{5,4},{6,7},{7,6},{8,9},{9,8},{10,11... | collective-permute-start | bytes 786440 | tf_op jit(solution)/shard_map/ppermute | solution.py:556
  91.8 11.0 %collective-permute-start.30 = (bf16[256,512]{1,0:T(8,128)(2,1)S(1)}, bf16[256,512]{1,0:T(8,128)(2,1)S(1)}, u32[]{:S(2)}, u32[]{:S(2)}) collective-permute-start(bf16[256,512]{1,0:T(8,128)(2,1)S(1)} %get-tuple-element.249), channel_id=1, source_target_pairs={{0,2},{1,3},{2,4},{3,5},{4,6},{5,7},{6,0},{7,1},{8,10},{9,11},{10,... | collective-permute-start | bytes 786440 | tf_op jit(solution)/shard_map/ppermute | solution.py:556
  92.2 10.6 %collective-permute-start.31 = (bf16[256,512]{1,0:T(8,128)(2,1)S(1)}, bf16[256,512]{1,0:T(8,128)(2,1)S(1)}, u32[]{:S(2)}, u32[]{:S(2)}) collective-permute-start(bf16[256,512]{1,0:T(8,128)(2,1)S(1)} %get-tuple-element.250), channel_id=1, source_target_pairs={{0,1},{1,0},{2,3},{3,2},{4,5},{5,4},{6,7},{7,6},{8,9},{9,8},{10,11... | collective-permute-start | bytes 786440 | tf_op jit(solution)/shard_map/ppermute | solution.py:556
  97.3 23.3 %copy-start.35 = (bf16[256,512]{1,0:T(8,128)(2,1)}, bf16[256,512]{1,0:T(8,128)(2,1)S(1)}, u32[]{:S(2)}) copy-start(bf16[256,512]{1,0:T(8,128)(2,1)S(1)} %collective-permute-done.28.refs_0_) | copy-start | bytes 786436
  97.3 23.3 %copy-start.36 = (bf16[256,512]{1,0:T(8,128)(2,1)}, bf16[256,512]{1,0:T(8,128)(2,1)S(1)}, u32[]{:S(2)}) copy-start(bf16[256,512]{1,0:T(8,128)(2,1)S(1)} %collective-permute-done.29.refs_1_) | copy-start | bytes 786436
  98.3 15.1 %collective-permute-start.34 = (bf16[256,512]{1,0:T(8,128)(2,1)}, bf16[256,512]{1,0:T(8,128)(2,1)}, u32[]{:S(2)}, u32[]{:S(2)}) collective-permute-start(bf16[256,512]{1,0:T(8,128)(2,1)} %get-tuple-element.253), channel_id=1, source_target_pairs={{0,2},{1,3},{2,4},{3,5},{4,6},{5,7},{6,0},{7,1},{8,10},{9,11},{10,... | collective-permute-start | bytes 786440 | tf_op jit(solution)/shard_map/ppermute | solution.py:556
  98.6 14.8 %collective-permute-start.35 = (bf16[256,512]{1,0:T(8,128)(2,1)}, bf16[256,512]{1,0:T(8,128)(2,1)}, u32[]{:S(2)}, u32[]{:S(2)}) collective-permute-start(bf16[256,512]{1,0:T(8,128)(2,1)} %get-tuple-element.254), channel_id=1, source_target_pairs={{0,1},{1,0},{2,3},{3,2},{4,5},{5,4},{6,7},{7,6},{8,9},{9,8},{10,11... | collective-permute-start | bytes 786440 | tf_op jit(solution)/shard_map/ppermute | solution.py:556
  103.7 12.9 %collective-permute-start.32 = (bf16[256,512]{1,0:T(8,128)(2,1)}, bf16[256,512]{1,0:T(8,128)(2,1)}, u32[]{:S(2)}, u32[]{:S(2)}) collective-permute-start(bf16[256,512]{1,0:T(8,128)(2,1)} %get-tuple-element.258), channel_id=1, source_target_pairs={{0,2},{1,3},{2,4},{3,5},{4,6},{5,7},{6,0},{7,1},{8,10},{9,11},{10,... | collective-permute-start | bytes 786440 | tf_op jit(solution)/shard_map/ppermute | solution.py:556
  104.2 12.5 %collective-permute-start.33 = (bf16[256,512]{1,0:T(8,128)(2,1)}, bf16[256,512]{1,0:T(8,128)(2,1)}, u32[]{:S(2)}, u32[]{:S(2)}) collective-permute-start(bf16[256,512]{1,0:T(8,128)(2,1)} %get-tuple-element.259), channel_id=1, source_target_pairs={{0,1},{1,0},{2,3},{3,2},{4,5},{5,4},{6,7},{7,6},{8,9},{9,8},{10,11... | collective-permute-start | bytes 786440 | tf_op jit(solution)/shard_map/ppermute | solution.py:556
  109.9 38.9 %all-to-all-start = ((bf16[4,528,256]{2,1,0:T(8,128)(2,1)}), bf16[4,528,256]{2,1,0:T(8,128)(2,1)S(1)}, u32[]{:S(2)}, u32[]{:S(2)}) async-start(bf16[4,528,256]{2,1,0:T(8,128)(2,1)} %get-tuple-element.255), calls=%async_computation | async-start | bytes 2162688 | tf_op jit(solution)/shard_map/all_to_all | solution.py:527
  114.6 13.2 %collective-permute-start.38 = (bf16[256,512]{1,0:T(8,128)(2,1)S(1)}, bf16[256,512]{1,0:T(8,128)(2,1)S(1)}, u32[]{:S(2)}, u32[]{:S(2)}) collective-permute-start(bf16[256,512]{1,0:T(8,128)(2,1)S(1)} %get-tuple-element.262), channel_id=1, source_target_pairs={{0,2},{1,3},{2,4},{3,5},{4,6},{5,7},{6,0},{7,1},{8,10},{9,11},{10,... | collective-permute-start | bytes 786440 | tf_op jit(solution)/shard_map/ppermute | solution.py:556
  116.2 11.6 %collective-permute-start.39 = (bf16[256,512]{1,0:T(8,128)(2,1)S(1)}, bf16[256,512]{1,0:T(8,128)(2,1)S(1)}, u32[]{:S(2)}, u32[]{:S(2)}) collective-permute-start(bf16[256,512]{1,0:T(8,128)(2,1)S(1)} %get-tuple-element.263), channel_id=1, source_target_pairs={{0,1},{1,0},{2,3},{3,2},{4,5},{5,4},{6,7},{7,6},{8,9},{9,8},{10,11... | collective-permute-start | bytes 786440 | tf_op jit(solution)/shard_map/ppermute | solution.py:556
  120.6 10.1 %collective-permute-start.36 = (bf16[256,512]{1,0:T(8,128)(2,1)S(1)}, bf16[256,512]{1,0:T(8,128)(2,1)S(1)}, u32[]{:S(2)}, u32[]{:S(2)}) collective-permute-start(bf16[256,512]{1,0:T(8,128)(2,1)S(1)} %get-tuple-element.268), channel_id=1, source_target_pairs={{0,2},{1,3},{2,4},{3,5},{4,6},{5,7},{6,0},{7,1},{8,10},{9,11},{10,... | collective-permute-start | bytes 786440 | tf_op jit(solution)/shard_map/ppermute | solution.py:556
  122.8 8.0 %collective-permute-start.37 = (bf16[256,512]{1,0:T(8,128)(2,1)S(1)}, bf16[256,512]{1,0:T(8,128)(2,1)S(1)}, u32[]{:S(2)}, u32[]{:S(2)}) collective-permute-start(bf16[256,512]{1,0:T(8,128)(2,1)S(1)} %get-tuple-element.269), channel_id=1, source_target_pairs={{0,1},{1,0},{2,3},{3,2},{4,5},{5,4},{6,7},{7,6},{8,9},{9,8},{10,11... | collective-permute-start | bytes 786440 | tf_op jit(solution)/shard_map/ppermute | solution.py:556
  134.9 10.0 %collective-permute-start.40 = (bf16[256,512]{1,0:T(8,128)(2,1)S(1)}, bf16[256,512]{1,0:T(8,128)(2,1)S(1)}, u32[]{:S(2)}, u32[]{:S(2)}) collective-permute-start(bf16[256,512]{1,0:T(8,128)(2,1)S(1)} %broadcast_select_fusion), channel_id=1, source_target_pairs={{0,1},{1,0},{2,3},{3,2},{4,5},{5,4},{6,7},{7,6},{8,9},{9,8},{10,11... | collective-permute-start | bytes 786440 | tf_op jit(solution)/shard_map/ppermute | solution.py:556
  137.7 8.7 %collective-permute-start.41 = (bf16[256,512]{1,0:T(8,128)(2,1)S(1)}, bf16[256,512]{1,0:T(8,128)(2,1)S(1)}, u32[]{:S(2)}, u32[]{:S(2)}) collective-permute-start(bf16[256,512]{1,0:T(8,128)(2,1)S(1)} %get-tuple-element.273), channel_id=1, source_target_pairs={{0,2},{1,3},{2,4},{3,5},{4,6},{5,7},{6,0},{7,1},{8,10},{9,11},{10,... | collective-permute-start | bytes 786440 | tf_op jit(solution)/shard_map/ppermute | solution.py:556
  137.7 11.1 %collective-permute-start.42 = (bf16[256,512]{1,0:T(8,128)(2,1)S(1)}, bf16[256,512]{1,0:T(8,128)(2,1)S(1)}, u32[]{:S(2)}, u32[]{:S(2)}) collective-permute-start(bf16[256,512]{1,0:T(8,128)(2,1)S(1)} %get-tuple-element.274), channel_id=1, source_target_pairs={{0,1},{1,0},{2,3},{3,2},{4,5},{5,4},{6,7},{7,6},{8,9},{9,8},{10,11... | collective-permute-start | bytes 786440 | tf_op jit(solution)/shard_map/ppermute | solution.py:556
  150.8 29.6 %all-to-all-start.1 = ((bf16[8,272,256]{2,1,0:T(8,128)(2,1)}), bf16[8,272,256]{2,1,0:T(8,128)(2,1)S(1)}, u32[]{:S(2)}, u32[]{:S(2)}) async-start(bf16[8,272,256]{2,1,0:T(8,128)(2,1)} %relay.1), calls=%async_computation.1 | async-start | bytes 2228224 | tf_op jit(solution)/shard_map/all_to_all | solution.py:527
  (27 other events, 353.3 us)

commit v8 on v7

--- a/solution.py
+++ b/solution.py
@@ -562,8 +562,8 @@
             own, sends = own_part()
         if late == 1:
             arrived = exchange(after((sends,), *turn)[0], "front")
-        if late >= 3 and e < events - 1:
-            step(2, *turn)
+        if late == 4:
+            step(4, *turn)
             turn = (*turn, result)
     passed = relayed(after((arrived,), *held[-1], *held[-2])[0])
     arrived = exchange(passed, "grp")

time: 183 us -> 179 us (0.978)
  Pallas kernels: 61.8 us -> 59 us
    all_to_all x2, waiting for transfers between devices: 7.45 us -> 4.02 us  [exchange(): return lax.all_to_all(blocks, axis, split_axis=0, concat_axis=0, tiled=True)]
    pallas_call x5 -> x4, Pallas kernels: 29.6 us -> 26.9 us  [update(): pl.pallas_call(functools.partial(update_kernel, tuple(numbers), room, wid...]
    ppermute x43, waiting for transfers between devices: 45.1 us -> 47 us  [shards(): lax.ppermute(turn[s], 'grp', perms[s])]
  transfers between devices with their start and end apart: 45 -> 45, of which waited for: 21 -> 20; matrix products, arithmetic and copies ran while one was open for 3% -> 2% of each run, Pallas kernels for 30% -> 29%
where the time goes in v8:
time: 179 us; the launch traced here: 178 us
  starting transfers between devices  61 us (34%)
  Pallas kernels  59 us (33%)
  waiting for transfers between devices  51 us (28%)
  other arithmetic  4.38 us (2%)
    ppermute x43, starting transfers between devices, shards(): lax.ppermute(turn[s], 'grp', perms[s])  53.7 us
    ppermute x43, waiting for transfers between devices, shards(): lax.ppermute(turn[s], 'grp', perms[s])  47 us
    pallas_call x4, Pallas kernels, update(): pl.pallas_call(functools.partial(update_kernel, tuple(numbers), room, wid...  26.9 us
    pallas_call x8, Pallas kernels, factor(): pl.pallas_call(functools.partial(factor_kernel, tuple(tiles), head), out_...  24.7 us
    all_to_all x2, starting transfers between devices, exchange(): return lax.all_to_all(blocks, axis, split_axis=0, concat_axis=0, tiled=True)  7.23 us
    select_n x17, other arithmetic, shards(): jnp.where(root, made[which][n], value)  4.02 us
    all_to_all x2, waiting for transfers between devices, exchange(): return lax.all_to_all(blocks, axis, split_axis=0, concat_axis=0, tiled=True)  4.02 us
    pallas_call x1, Pallas kernels, own_panels(): pl.pallas_call(functools.partial(own_kernel, choices, len(blocks), width...  3.97 us
  transfers between devices with their start and end apart: 45, of which 20 were waited for; matrix products, arithmetic and copies ran while one was open for 2% of the time, Pallas kernels for 29%

profile of v8, /device:TPU:0, one launch (start us, length us, event | category | flops | bytes accessed | tf_op | source)
XLA Modules:
  0.0 178.5 jit_solution(5275995193959909609)
XLA Ops:
  1.4 3.8 %factor.8 = (bf16[256,512]{1,0:T(8,128)(2,1)S(1)}, bf16[256,512]{1,0:T(8,128)(2,1)S(1)}, bf16[256,512]{1,0:T(8,128)(2,1)S(1)}, bf16[256,512]{1,0:T(8,128)(2,1)S(...) custom-call(s32[32,4]{1,0:T(8,128)S(1)} %copy.54.mask, bf16[8192,1024]{1,0:T(8,128)(2,1)} %bitcast.9, ...), custom_call_target="tpu_custom_call" | custom-call | flops 805306368 | bytes 2097152 | tf_op jit(solution)/shard_map/factor/pallas_call | solution.py:178
  5.2 3.1 %collective-permute-start = (bf16[256,512]{1,0:T(8,128)(2,1)S(1)}, bf16[256,512]{1,0:T(8,128)(2,1)S(1)}, u32[]{:S(2)}, u32[]{:S(2)}) collective-permute-start(bf16[256,512]{1,0:T(8,128)(2,1)S(1)} %get-tuple-element.146.refs_18_), channel_id=1, source_target_pairs={{0,2},{1,3},{2,4},{3,5},{4,6},{5,7},{6,0},{7,1},{8,10},{9,11},{10,... | collective-permute-start | bytes 786440 | tf_op jit(solution)/shard_map/ppermute | solution.py:556
  8.3 1.5 collective-permute-start.1
  9.8 1.6 collective-permute-start.4
  11.9 3.0 %factor.9 = (bf16[256,512]{1,0:T(8,128)(2,1)S(1)}, bf16[256,512]{1,0:T(8,128)(2,1)S(1)}, bf16[256,512]{1,0:T(8,128)(2,1)S(1)}, bf16[256,512]{1,0:T(8,128)(2,1)S(1)}) custom-call(s32[32,4]{1,0:T(8,128)S(1)} %copy.54.mask, bf16[8192,1024]{1,0:T(8,128)(2,1)} %bitcast.10, bf16[4,256,256]{2,1,0:T(8,128)(2,1)S(1)} %get-tuple-element.228.refs_0_, ...), custom_call_target="tpu_custom_call" | custom-call | flops 805306368 | bytes 2097152 | tf_op jit(solution)/shard_map/factor/pallas_call | solution.py:178
  14.9 2.6 %collective-permute-done.refs_19_.refs_0_ = bf16[256,512]{1,0:T(8,128)(2,1)S(1)} collective-permute-done((bf16[256,512]{1,0:T(8,128)(2,1)S(1)}, bf16[256,512]{1,0:T(8,128)(2,1)S(1)}, u32[]{:S(2)}, u32[]{:S(2)}) %collective-permute-start) | collective-permute-done | bytes 262176 | tf_op jit(solution)/shard_map/ppermute | solution.py:556
  17.6 1.6 collective-permute-start.2
  19.2 1.5 collective-permute-start.3
  20.7 2.3 %collective-permute-done.4.refs_2_ = bf16[256,512]{1,0:T(8,128)(2,1)S(1)} collective-permute-done((bf16[256,512]{1,0:T(8,128)(2,1)S(1)}, bf16[256,512]{1,0:T(8,128)(2,1)S(1)}, u32[]{:S(2)}, u32[]{:S(2)}) %collective-permute-start.4) | collective-permute-done | bytes 262176 | tf_op jit(solution)/shard_map/ppermute | solution.py:556
  23.2 1.6 collective-permute-start.8
  24.8 1.5 collective-permute-start.9
  26.4 3.0 %factor.10 = (bf16[256,512]{1,0:T(8,128)(2,1)S(1)}, bf16[256,512]{1,0:T(8,128)(2,1)S(1)}, bf16[256,512]{1,0:T(8,128)(2,1)S(1)}, bf16[256,512]{1,0:T(8,128)(2,1)S(1)}) custom-call(s32[32,4]{1,0:T(8,128)S(1)} %copy.54.mask, bf16[8192,1024]{1,0:T(8,128)(2,1)} %bitcast.11, bf16[4,256,256]{2,1,0:T(8,128)(2,1)S(1)} %get-tuple-element.228.refs_0_, ...), custom_call_target="tpu_custom_call" | custom-call | flops 805306368 | bytes 2097152 | tf_op jit(solution)/shard_map/factor/pallas_call | solution.py:178
  29.5 1.6 collective-permute-start.6
  31.9 2.3 %collective-permute-done.8.refs_6_ = bf16[256,512]{1,0:T(8,128)(2,1)S(1)} collective-permute-done((bf16[256,512]{1,0:T(8,128)(2,1)S(1)}, bf16[256,512]{1,0:T(8,128)(2,1)S(1)}, u32[]{:S(2)}, u32[]{:S(2)}) %collective-permute-start.8) | collective-permute-done | bytes 262176 | tf_op jit(solution)/shard_map/ppermute | solution.py:556
  35.0 1.1 collective-permute-start.12
  36.1 1.5 collective-permute-start.13
  37.6 3.0 %factor.11 = (bf16[256,512]{1,0:T(8,128)(2,1)S(1)}, bf16[256,512]{1,0:T(8,128)(2,1)S(1)}, bf16[256,512]{1,0:T(8,128)(2,1)S(1)}, bf16[256,512]{1,0:T(8,128)(2,1)S(1)}) custom-call(s32[32,4]{1,0:T(8,128)S(1)} %copy.54.mask, bf16[8192,1024]{1,0:T(8,128)(2,1)} %bitcast.12, bf16[4,256,256]{2,1,0:T(8,128)(2,1)S(1)} %get-tuple-element.228.refs_0_, ...), custom_call_target="tpu_custom_call" | custom-call | flops 805306368 | bytes 2097152 | tf_op jit(solution)/shard_map/factor/pallas_call | solution.py:178
  40.7 1.6 collective-permute-start.10
  43.2 2.9 %collective-permute-done.12.refs_2_ = bf16[256,512]{1,0:T(8,128)(2,1)S(1)} collective-permute-done((bf16[256,512]{1,0:T(8,128)(2,1)S(1)}, bf16[256,512]{1,0:T(8,128)(2,1)S(1)}, u32[]{:S(2)}, u32[]{:S(2)}) %collective-permute-start.12) | collective-permute-done | bytes 262176 | tf_op jit(solution)/shard_map/ppermute | solution.py:556
  46.1 1.2 collective-permute-start.16
  47.3 1.5 collective-permute-start.17
  48.8 3.0 %factor.12 = (bf16[256,512]{1,0:T(8,128)(2,1)S(1)}, bf16[256,512]{1,0:T(8,128)(2,1)S(1)}, bf16[256,512]{1,0:T(8,128)(2,1)S(1)}, bf16[256,512]{1,0:T(8,128)(2,1)S(1)}) custom-call(s32[32,4]{1,0:T(8,128)S(1)} %copy.54.mask, bf16[8192,1024]{1,0:T(8,128)(2,1)} %bitcast.13, bf16[4,256,256]{2,1,0:T(8,128)(2,1)S(1)} %get-tuple-element.228.refs_0_, ...), custom_call_target="tpu_custom_call" | custom-call | flops 805306368 | bytes 2097152 | tf_op jit(solution)/shard_map/factor/pallas_call | solution.py:178
  51.9 1.6 collective-permute-start.14
  54.4 3.0 %collective-permute-done.16.refs_9_.refs_6_ = bf16[256,512]{1,0:T(8,128)(2,1)S(1)} collective-permute-done((bf16[256,512]{1,0:T(8,128)(2,1)S(1)}, bf16[256,512]{1,0:T(8,128)(2,1)S(1)}, u32[]{:S(2)}, u32[]{:S(2)}) %collective-permute-start.16) | collective-permute-done | bytes 262176 | tf_op jit(solution)/shard_map/ppermute | solution.py:556
  57.5 1.0 collective-permute-start.20
  58.5 1.5 collective-permute-start.21
  60.0 3.0 %factor.13 = (bf16[256,512]{1,0:T(8,128)(2,1)S(1)}, bf16[256,512]{1,0:T(8,128)(2,1)S(1)}, bf16[256,512]{1,0:T(8,128)(2,1)S(1)}, bf16[256,512]{1,0:T(8,128)(2,1)S(1)}) custom-call(s32[32,4]{1,0:T(8,128)S(1)} %copy.54.mask, bf16[8192,1024]{1,0:T(8,128)(2,1)} %bitcast.14, bf16[4,256,256]{2,1,0:T(8,128)(2,1)S(1)} %get-tuple-element.228.refs_0_, ...), custom_call_target="tpu_custom_call" | custom-call | flops 805306368 | bytes 2097152 | tf_op jit(solution)/shard_map/factor/pallas_call | solution.py:178
  63.2 1.6 collective-permute-start.18
  65.6 3.0 %collective-permute-done.20.refs_8_.refs_10_ = bf16[256,512]{1,0:T(8,128)(2,1)S(1)} collective-permute-done((bf16[256,512]{1,0:T(8,128)(2,1)S(1)}, bf16[256,512]{1,0:T(8,128)(2,1)S(1)}, u32[]{:S(2)}, u32[]{:S(2)}) %collective-permute-start.20) | collective-permute-done | bytes 262176 | tf_op jit(solution)/shard_map/ppermute | solution.py:556
  68.7 1.2 collective-permute-start.22
  70.0 1.5 collective-permute-start.23
  71.5 3.0 %factor.14 = (bf16[256,512]{1,0:T(8,128)(2,1)S(1)}, bf16[256,512]{1,0:T(8,128)(2,1)S(1)}, bf16[256,512]{1,0:T(8,128)(2,1)S(1)}, bf16[256,512]{1,0:T(8,128)(2,1)S(1)}) custom-call(s32[32,4]{1,0:T(8,128)S(1)} %copy.54.mask, bf16[8192,1024]{1,0:T(8,128)(2,1)} %bitcast.15, bf16[4,256,256]{2,1,0:T(8,128)(2,1)S(1)} %get-tuple-element.228.refs_0_, ...), custom_call_target="tpu_custom_call" | custom-call | flops 805306368 | bytes 2097152 | tf_op jit(solution)/shard_map/factor/pallas_call | solution.py:178
  74.6 1.6 collective-permute-start.24
  76.9 3.1 %collective-permute-done.22.refs_7_.refs_14_ = bf16[256,512]{1,0:T(8,128)(2,1)S(1)} collective-permute-done((bf16[256,512]{1,0:T(8,128)(2,1)S(1)}, bf16[256,512]{1,0:T(8,128)(2,1)S(1)}, u32[]{:S(2)}, u32[]{:S(2)}) %collective-permute-start.22) | collective-permute-done | bytes 262176 | tf_op jit(solution)/shard_map/ppermute | solution.py:556
  80.1 0.9 collective-permute-start.26
  81.0 1.5 collective-permute-start.27
  82.5 3.0 %factor.15 = (bf16[256,512]{1,0:T(8,128)(2,1)S(1)}, bf16[256,512]{1,0:T(8,128)(2,1)S(1)}, bf16[256,512]{1,0:T(8,128)(2,1)S(1)}, bf16[256,512]{1,0:T(8,128)(2,1)S(1)}) custom-call(s32[32,4]{1,0:T(8,128)S(1)} %copy.54.mask, bf16[8192,1024]{1,0:T(8,128)(2,1)} %bitcast.16, bf16[4,256,256]{2,1,0:T(8,128)(2,1)S(1)} %get-tuple-element.228.refs_0_, ...), custom_call_target="tpu_custom_call" | custom-call | flops 805306368 | bytes 2097152 | tf_op jit(solution)/shard_map/factor/pallas_call | solution.py:178
  85.8 1.5 collective-permute-start.28
  88.1 3.2 %collective-permute-done.26.refs_16_.refs_2_ = bf16[256,512]{1,0:T(8,128)(2,1)S(1)} collective-permute-done((bf16[256,512]{1,0:T(8,128)(2,1)S(1)}, bf16[256,512]{1,0:T(8,128)(2,1)S(1)}, u32[]{:S(2)}, u32[]{:S(2)}) %collective-permute-start.26) | collective-permute-done | bytes 262176 | tf_op jit(solution)/shard_map/ppermute | solution.py:556
  92.3 1.5 collective-permute-start.31
  93.8 3.1 %collective-permute-done.28.refs_4_ = bf16[256,512]{1,0:T(8,128)(2,1)S(1)} collective-permute-done((bf16[256,512]{1,0:T(8,128)(2,1)S(1)}, bf16[256,512]{1,0:T(8,128)(2,1)S(1)}, u32[]{:S(2)}, u32[]{:S(2)}) %collective-permute-start.28) | collective-permute-done | bytes 262176 | tf_op jit(solution)/shard_map/ppermute | solution.py:556
  97.0 1.0 select_select_fusion.2
  98.6 1.5 collective-permute-start.35
  100.1 2.3 %collective-permute-done.30.refs_6_ = bf16[256,512]{1,0:T(8,128)(2,1)S(1)} collective-permute-done((bf16[256,512]{1,0:T(8,128)(2,1)S(1)}, bf16[256,512]{1,0:T(8,128)(2,1)S(1)}, u32[]{:S(2)}, u32[]{:S(2)}) %collective-permute-start.30) | collective-permute-done | bytes 262176 | tf_op jit(solution)/shard_map/ppermute | solution.py:556
  102.4 1.1 select_select_fusion.1
  104.3 1.5 collective-permute-start.33
  105.8 4.0 %own_panels.1 = (bf16[512,1024]{1,0:T(8,128)(2,1)S(1)}, bf16[4,528,256]{2,1,0:T(8,128)(2,1)}) custom-call(s32[32,4]{1,0:T(8,128)S(1)} %copy.54.mask, s32[4]{0:T(128)S(1)} %bitcast.8, s32[1]{0:T(128)} %bitcast.1.me, bf16[8192,1024]{1,0:T(8,128)(2,1)} %bitcast.17, bf16[256,512]{1,0:T(8,128)(2,1)} %copy-done.5, bf16[256,512]{1,0:T(8,128)(2,1)} %copy-done.20, ...), custom_call_target="tpu_custom_call" | custom-call | flops 268435456 | bytes 2621440 | tf_op jit(solution)/shard_map/own_panels/pallas_call | solution.py:238
  109.8 3.7 %all-to-all-start = ((bf16[4,528,256]{2,1,0:T(8,128)(2,1)}), bf16[4,528,256]{2,1,0:T(8,128)(2,1)S(1)}, u32[]{:S(2)}, u32[]{:S(2)}) async-start(bf16[4,528,256]{2,1,0:T(8,128)(2,1)} %get-tuple-element.253), calls=%async_computation | async-start | bytes 2162688 | tf_op jit(solution)/shard_map/all_to_all | solution.py:527
  113.5 1.1 select_select_fusion
  114.6 1.6 collective-permute-start.38
  117.4 1.5 collective-permute-start.37
  118.9 4.4 %update.4.refs_16_ = bf16[8192,1024]{1,0:T(8,128)(2,1)} custom-call(s32[8,44]{1,0:T(8,128)S(1)} %copy-done.6, s32[32,4]{1,0:T(8,128)S(1)} %copy.54.mask, s32[1]{0:T(128)} %bitcast.1.me, bf16[512,1024]{1,0:T(8,128)(2,1)S(1)} %get-tuple-element.269.own, bf16[8192,1024]{1,0:T(8,128)(2,1)} %bitcast.18, bf16[256,512]{1,0:T(8,128)(2,1)} %copy-done.8, ...), custom_call_target="tpu_custom_call" | custom-call | flops 2147483648 | bytes 8388608 | tf_op jit(solution)/shard_map/update/pallas_call | solution.py:403
  123.4 2.2 %collective-permute-done.38.refs_12_ = bf16[256,512]{1,0:T(8,128)(2,1)S(1)} collective-permute-done((bf16[256,512]{1,0:T(8,128)(2,1)S(1)}, bf16[256,512]{1,0:T(8,128)(2,1)S(1)}, u32[]{:S(2)}, u32[]{:S(2)}) %collective-permute-start.38) | collective-permute-done | bytes 262176 | tf_op jit(solution)/shard_map/ppermute | solution.py:556
  125.6 5.1 %collective-permute-done.36.refs_14_ = bf16[256,512]{1,0:T(8,128)(2,1)S(1)} collective-permute-done((bf16[256,512]{1,0:T(8,128)(2,1)S(1)}, bf16[256,512]{1,0:T(8,128)(2,1)S(1)}, u32[]{:S(2)}, u32[]{:S(2)}) %collective-permute-start.36) | collective-permute-done | bytes 262176 | tf_op jit(solution)/shard_map/ppermute | solution.py:556
  131.4 1.5 collective-permute-start.42
  132.9 7.2 %collective-permute-done.40.refs_2_ = bf16[256,512]{1,0:T(8,128)(2,1)S(1)} collective-permute-done((bf16[256,512]{1,0:T(8,128)(2,1)S(1)}, bf16[256,512]{1,0:T(8,128)(2,1)S(1)}, u32[]{:S(2)}, u32[]{:S(2)}) %collective-permute-start.40) | collective-permute-done | bytes 262176 | tf_op jit(solution)/shard_map/ppermute | solution.py:556
  140.8 3.7 %collective-permute-done.42.refs_1_ = bf16[256,512]{1,0:T(8,128)(2,1)} collective-permute-done((bf16[256,512]{1,0:T(8,128)(2,1)S(1)}, bf16[256,512]{1,0:T(8,128)(2,1)}, u32[]{:S(2)}, u32[]{:S(2)}) %collective-permute-start.42) | collective-permute-done | bytes 262176 | tf_op jit(solution)/shard_map/ppermute | solution.py:556
  144.7 1.8 relay.1
  146.4 3.6 %all-to-all-start.1 = ((bf16[8,272,256]{2,1,0:T(8,128)(2,1)}), bf16[8,272,256]{2,1,0:T(8,128)(2,1)S(1)}, u32[]{:S(2)}, u32[]{:S(2)}) async-start(bf16[8,272,256]{2,1,0:T(8,128)(2,1)} %relay.1), calls=%async_computation.1 | async-start | bytes 2228224 | tf_op jit(solution)/shard_map/all_to_all | solution.py:527
  150.0 9.4 %update.5.refs_16_ = bf16[8192,1024]{1,0:T(8,128)(2,1)} custom-call(s32[8,44]{1,0:T(8,128)S(1)} %copy-done.6, s32[32,4]{1,0:T(8,128)S(1)} %copy.54.mask, s32[1]{0:T(128)} %bitcast.1.me, bf16[512,1024]{1,0:T(8,128)(2,1)S(1)} %get-tuple-element.269.own, bf16[8192,1024]{1,0:T(8,128)(2,1)} %bitcast.19, ...), custom_call_target="tpu_custom_call", output_to_operand_aliasing={{}: (21, {})} | custom-call | flops 4294967296 | bytes 16777216 | tf_op jit(solution)/shard_map/update/pallas_call | solution.py:403
  159.4 9.4 %update.6.refs_3_ = bf16[8192,1024]{1,0:T(8,128)(2,1)} custom-call(s32[8,44]{1,0:T(8,128)S(1)} %copy-done.6, s32[32,4]{1,0:T(8,128)S(1)} %copy.54.mask, s32[1]{0:T(128)} %bitcast.1.me, bf16[512,1024]{1,0:T(8,128)(2,1)S(1)} %get-tuple-element.269.own, bf16[8192,1024]{1,0:T(8,128)(2,1)} %bitcast.20, ...), custom_call_target="tpu_custom_call", output_to_operand_aliasing={{}: (21, {})} | custom-call | flops 4294967296 | bytes 16777216 | tf_op jit(solution)/shard_map/update/pallas_call | solution.py:403
  168.8 3.7 %update.7 = bf16[8192,1024]{1,0:T(8,128)(2,1)} custom-call(s32[8,44]{1,0:T(8,128)S(1)} %copy-done.6, s32[32,4]{1,0:T(8,128)S(1)} %copy.54.mask, s32[1]{0:T(128)} %bitcast.1.me, bf16[512,1024]{1,0:T(8,128)(2,1)S(1)} %get-tuple-element.269.own, bf16[8192,1024]{1,0:T(8,128)(2,1)} %bitcast.21, ...), custom_call_target="tpu_custom_call", output_to_operand_aliasing={{}: (8, {})} | custom-call | flops 1073741824 | bytes 4194304 | tf_op jit(solution)/shard_map/update/pallas_call | solution.py:403
  172.5 4.0 %all-to-all-done.1.arrived = bf16[8,272,256]{2,1,0:T(8,128)(2,1)S(1)} async-done(((bf16[8,272,256]{2,1,0:T(8,128)(2,1)}), bf16[8,272,256]{2,1,0:T(8,128)(2,1)S(1)}, u32[]{:S(2)}, u32[]{:S(2)}) %all-to-all-start.1) | async-done | bytes 1114144 | tf_op jit(solution)/shard_map/all_to_all | solution.py:527
  176.8 1.7 sum_parents.1
  (163 shorter events, 13.4 us)
Async XLA Ops:
  5.2 9.7 %copy-start.4 = (bf16[256,512]{1,0:T(8,128)(2,1)}, bf16[256,512]{1,0:T(8,128)(2,1)S(1)}, u32[]{:S(2)}) copy-start(bf16[256,512]{1,0:T(8,128)(2,1)S(1)} %get-tuple-element.146.refs_18_) | copy-start | bytes 786436
  5.2 12.2 %collective-permute-start = (bf16[256,512]{1,0:T(8,128)(2,1)S(1)}, bf16[256,512]{1,0:T(8,128)(2,1)S(1)}, u32[]{:S(2)}, u32[]{:S(2)}) collective-permute-start(bf16[256,512]{1,0:T(8,128)(2,1)S(1)} %get-tuple-element.146.refs_18_), channel_id=1, source_target_pairs={{0,2},{1,3},{2,4},{3,5},{4,6},{5,7},{6,0},{7,1},{8,10},{9,11},{10,... | collective-permute-start | bytes 786440 | tf_op jit(solution)/shard_map/ppermute | solution.py:556
  8.3 9.2 %collective-permute-start.1 = (bf16[256,512]{1,0:T(8,128)(2,1)S(1)}, bf16[256,512]{1,0:T(8,128)(2,1)S(1)}, u32[]{:S(2)}, u32[]{:S(2)}) collective-permute-start(bf16[256,512]{1,0:T(8,128)(2,1)S(1)} %get-tuple-element.147), channel_id=1, source_target_pairs={{0,1},{1,0},{2,3},{3,2},{4,5},{5,4},{6,7},{7,6},{8,9},{9,8},{10,11... | collective-permute-start | bytes 786440 | tf_op jit(solution)/shard_map/ppermute | solution.py:556
  9.8 13.3 %collective-permute-start.4 = (bf16[256,512]{1,0:T(8,128)(2,1)S(1)}, bf16[256,512]{1,0:T(8,128)(2,1)S(1)}, u32[]{:S(2)}, u32[]{:S(2)}) collective-permute-start(bf16[256,512]{1,0:T(8,128)(2,1)S(1)} %get-tuple-element.148), channel_id=1, source_target_pairs={{0,2},{1,3},{2,4},{3,5},{4,6},{5,7},{6,0},{7,1},{8,10},{9,11},{10,... | collective-permute-start | bytes 786440 | tf_op jit(solution)/shard_map/ppermute | solution.py:556
  11.4 11.8 %collective-permute-start.5 = (bf16[256,512]{1,0:T(8,128)(2,1)S(1)}, bf16[256,512]{1,0:T(8,128)(2,1)S(1)}, u32[]{:S(2)}, u32[]{:S(2)}) collective-permute-start(bf16[256,512]{1,0:T(8,128)(2,1)S(1)} %get-tuple-element.149), channel_id=1, source_target_pairs={{0,1},{1,0},{2,3},{3,2},{4,5},{5,4},{6,7},{7,6},{8,9},{9,8},{10,11... | collective-permute-start | bytes 786440 | tf_op jit(solution)/shard_map/ppermute | solution.py:556
  17.6 11.8 %collective-permute-start.2 = (bf16[256,512]{1,0:T(8,128)(2,1)S(1)}, bf16[256,512]{1,0:T(8,128)(2,1)S(1)}, u32[]{:S(2)}, u32[]{:S(2)}) collective-permute-start(bf16[256,512]{1,0:T(8,128)(2,1)S(1)} %get-tuple-element.156), channel_id=1, source_target_pairs={{0,2},{1,3},{2,4},{3,5},{4,6},{5,7},{6,0},{7,1},{8,10},{9,11},{10,... | collective-permute-start | bytes 786440 | tf_op jit(solution)/shard_map/ppermute | solution.py:556
  19.2 10.2 %collective-permute-start.3 = (bf16[256,512]{1,0:T(8,128)(2,1)S(1)}, bf16[256,512]{1,0:T(8,128)(2,1)S(1)}, u32[]{:S(2)}, u32[]{:S(2)}) collective-permute-start(bf16[256,512]{1,0:T(8,128)(2,1)S(1)} %get-tuple-element.157), channel_id=1, source_target_pairs={{0,1},{1,0},{2,3},{3,2},{4,5},{5,4},{6,7},{7,6},{8,9},{9,8},{10,11... | collective-permute-start | bytes 786440 | tf_op jit(solution)/shard_map/ppermute | solution.py:556
  23.0 6.3 %copy-start.28 = (bf16[256,512]{1,0:T(8,128)(2,1)}, bf16[256,512]{1,0:T(8,128)(2,1)S(1)}, u32[]{:S(2)}) copy-start(bf16[256,512]{1,0:T(8,128)(2,1)S(1)} %collective-permute-done.4.refs_2_) | copy-start | bytes 786436
  23.1 6.2 %copy-start.29 = (bf16[256,512]{1,0:T(8,128)(2,1)}, bf16[256,512]{1,0:T(8,128)(2,1)S(1)}, u32[]{:S(2)}) copy-start(bf16[256,512]{1,0:T(8,128)(2,1)S(1)} %collective-permute-done.5.refs_3_) | copy-start | bytes 786436
  23.2 11.1 %collective-permute-start.8 = (bf16[256,512]{1,0:T(8,128)(2,1)S(1)}, bf16[256,512]{1,0:T(8,128)(2,1)S(1)}, u32[]{:S(2)}, u32[]{:S(2)}) collective-permute-start(bf16[256,512]{1,0:T(8,128)(2,1)S(1)} %get-tuple-element.165), channel_id=1, source_target_pairs={{0,2},{1,3},{2,4},{3,5},{4,6},{5,7},{6,0},{7,1},{8,10},{9,11},{10,... | collective-permute-start | bytes 786440 | tf_op jit(solution)/shard_map/ppermute | solution.py:556
  24.8 9.5 %collective-permute-start.9 = (bf16[256,512]{1,0:T(8,128)(2,1)S(1)}, bf16[256,512]{1,0:T(8,128)(2,1)S(1)}, u32[]{:S(2)}, u32[]{:S(2)}) collective-permute-start(bf16[256,512]{1,0:T(8,128)(2,1)S(1)} %get-tuple-element.166), channel_id=1, source_target_pairs={{0,1},{1,0},{2,3},{3,2},{4,5},{5,4},{6,7},{7,6},{8,9},{9,8},{10,11... | collective-permute-start | bytes 786440 | tf_op jit(solution)/shard_map/ppermute | solution.py:556
  29.5 11.1 %collective-permute-start.6 = (bf16[256,512]{1,0:T(8,128)(2,1)S(1)}, bf16[256,512]{1,0:T(8,128)(2,1)S(1)}, u32[]{:S(2)}, u32[]{:S(2)}) collective-permute-start(bf16[256,512]{1,0:T(8,128)(2,1)S(1)} %get-tuple-element.170), channel_id=1, source_target_pairs={{0,2},{1,3},{2,4},{3,5},{4,6},{5,7},{6,0},{7,1},{8,10},{9,11},{10,... | collective-permute-start | bytes 786440 | tf_op jit(solution)/shard_map/ppermute | solution.py:556
  31.1 9.5 %collective-permute-start.7 = (bf16[256,512]{1,0:T(8,128)(2,1)S(1)}, bf16[256,512]{1,0:T(8,128)(2,1)S(1)}, u32[]{:S(2)}, u32[]{:S(2)}) collective-permute-start(bf16[256,512]{1,0:T(8,128)(2,1)S(1)} %get-tuple-element.171), channel_id=1, source_target_pairs={{0,1},{1,0},{2,3},{3,2},{4,5},{5,4},{6,7},{7,6},{8,9},{9,8},{10,11... | collective-permute-start | bytes 786440 | tf_op jit(solution)/shard_map/ppermute | solution.py:556
  34.4 6.2 %copy-start.33 = (bf16[256,512]{1,0:T(8,128)(2,1)}, bf16[256,512]{1,0:T(8,128)(2,1)S(1)}, u32[]{:S(2)}) copy-start(bf16[256,512]{1,0:T(8,128)(2,1)S(1)} %collective-permute-done.9.refs_7_) | copy-start | bytes 786436
  35.0 11.0 %collective-permute-start.12 = (bf16[256,512]{1,0:T(8,128)(2,1)S(1)}, bf16[256,512]{1,0:T(8,128)(2,1)S(1)}, u32[]{:S(2)}, u32[]{:S(2)}) collective-permute-start(bf16[256,512]{1,0:T(8,128)(2,1)S(1)} %get-tuple-element.179), channel_id=1, source_target_pairs={{0,2},{1,3},{2,4},{3,5},{4,6},{5,7},{6,0},{7,1},{8,10},{9,11},{10,... | collective-permute-start | bytes 786440 | tf_op jit(solution)/shard_map/ppermute | solution.py:556
  36.1 10.0 %collective-permute-start.13 = (bf16[256,512]{1,0:T(8,128)(2,1)S(1)}, bf16[256,512]{1,0:T(8,128)(2,1)S(1)}, u32[]{:S(2)}, u32[]{:S(2)}) collective-permute-start(bf16[256,512]{1,0:T(8,128)(2,1)S(1)} %get-tuple-element.180), channel_id=1, source_target_pairs={{0,1},{1,0},{2,3},{3,2},{4,5},{5,4},{6,7},{7,6},{8,9},{9,8},{10,11... | collective-permute-start | bytes 786440 | tf_op jit(solution)/shard_map/ppermute | solution.py:556
  40.7 11.1 %collective-permute-start.10 = (bf16[256,512]{1,0:T(8,128)(2,1)S(1)}, bf16[256,512]{1,0:T(8,128)(2,1)S(1)}, u32[]{:S(2)}, u32[]{:S(2)}) collective-permute-start(bf16[256,512]{1,0:T(8,128)(2,1)S(1)} %get-tuple-element.184), channel_id=1, source_target_pairs={{0,2},{1,3},{2,4},{3,5},{4,6},{5,7},{6,0},{7,1},{8,10},{9,11},{10,... | collective-permute-start | bytes 786440 | tf_op jit(solution)/shard_map/ppermute | solution.py:556
  42.3 9.5 %collective-permute-start.11 = (bf16[256,512]{1,0:T(8,128)(2,1)S(1)}, bf16[256,512]{1,0:T(8,128)(2,1)S(1)}, u32[]{:S(2)}, u32[]{:S(2)}) collective-permute-start(bf16[256,512]{1,0:T(8,128)(2,1)S(1)} %get-tuple-element.185), channel_id=1, source_target_pairs={{0,1},{1,0},{2,3},{3,2},{4,5},{5,4},{6,7},{7,6},{8,9},{9,8},{10,11... | collective-permute-start | bytes 786440 | tf_op jit(solution)/shard_map/ppermute | solution.py:556
  46.1 11.3 %collective-permute-start.16 = (bf16[256,512]{1,0:T(8,128)(2,1)S(1)}, bf16[256,512]{1,0:T(8,128)(2,1)S(1)}, u32[]{:S(2)}, u32[]{:S(2)}) collective-permute-start(bf16[256,512]{1,0:T(8,128)(2,1)S(1)} %get-tuple-element.193), channel_id=1, source_target_pairs={{0,2},{1,3},{2,4},{3,5},{4,6},{5,7},{6,0},{7,1},{8,10},{9,11},{10,... | collective-permute-start | bytes 786440 | tf_op jit(solution)/shard_map/ppermute | solution.py:556
  47.3 10.1 %collective-permute-start.17 = (bf16[256,512]{1,0:T(8,128)(2,1)S(1)}, bf16[256,512]{1,0:T(8,128)(2,1)S(1)}, u32[]{:S(2)}, u32[]{:S(2)}) collective-permute-start(bf16[256,512]{1,0:T(8,128)(2,1)S(1)} %get-tuple-element.194), channel_id=1, source_target_pairs={{0,1},{1,0},{2,3},{3,2},{4,5},{5,4},{6,7},{7,6},{8,9},{9,8},{10,11... | collective-permute-start | bytes 786440 | tf_op jit(solution)/shard_map/ppermute | solution.py:556
  51.9 11.1 %collective-permute-start.14 = (bf16[256,512]{1,0:T(8,128)(2,1)S(1)}, bf16[256,512]{1,0:T(8,128)(2,1)S(1)}, u32[]{:S(2)}, u32[]{:S(2)}) collective-permute-start(bf16[256,512]{1,0:T(8,128)(2,1)S(1)} %get-tuple-element.198), channel_id=1, source_target_pairs={{0,2},{1,3},{2,4},{3,5},{4,6},{5,7},{6,0},{7,1},{8,10},{9,11},{10,... | collective-permute-start | bytes 786440 | tf_op jit(solution)/shard_map/ppermute | solution.py:556
  53.6 9.5 %collective-permute-start.15 = (bf16[256,512]{1,0:T(8,128)(2,1)S(1)}, bf16[256,512]{1,0:T(8,128)(2,1)S(1)}, u32[]{:S(2)}, u32[]{:S(2)}) collective-permute-start(bf16[256,512]{1,0:T(8,128)(2,1)S(1)} %get-tuple-element.199), channel_id=1, source_target_pairs={{0,1},{1,0},{2,3},{3,2},{4,5},{5,4},{6,7},{7,6},{8,9},{9,8},{10,11... | collective-permute-start | bytes 786440 | tf_op jit(solution)/shard_map/ppermute | solution.py:556
  57.5 11.1 %collective-permute-start.20 = (bf16[256,512]{1,0:T(8,128)(2,1)S(1)}, bf16[256,512]{1,0:T(8,128)(2,1)S(1)}, u32[]{:S(2)}, u32[]{:S(2)}) collective-permute-start(bf16[256,512]{1,0:T(8,128)(2,1)S(1)} %get-tuple-element.207), channel_id=1, source_target_pairs={{0,2},{1,3},{2,4},{3,5},{4,6},{5,7},{6,0},{7,1},{8,10},{9,11},{10,... | collective-permute-start | bytes 786440 | tf_op jit(solution)/shard_map/ppermute | solution.py:556
  58.5 10.1 %collective-permute-start.21 = (bf16[256,512]{1,0:T(8,128)(2,1)S(1)}, bf16[256,512]{1,0:T(8,128)(2,1)S(1)}, u32[]{:S(2)}, u32[]{:S(2)}) collective-permute-start(bf16[256,512]{1,0:T(8,128)(2,1)S(1)} %get-tuple-element.208), channel_id=1, source_target_pairs={{0,1},{1,0},{2,3},{3,2},{4,5},{5,4},{6,7},{7,6},{8,9},{9,8},{10,11... | collective-permute-start | bytes 786440 | tf_op jit(solution)/shard_map/ppermute | solution.py:556
  63.2 11.3 %collective-permute-start.18 = (bf16[256,512]{1,0:T(8,128)(2,1)S(1)}, bf16[256,512]{1,0:T(8,128)(2,1)S(1)}, u32[]{:S(2)}, u32[]{:S(2)}) collective-permute-start(bf16[256,512]{1,0:T(8,128)(2,1)S(1)} %get-tuple-element.212), channel_id=1, source_target_pairs={{0,2},{1,3},{2,4},{3,5},{4,6},{5,7},{6,0},{7,1},{8,10},{9,11},{10,... | collective-permute-start | bytes 786440 | tf_op jit(solution)/shard_map/ppermute | solution.py:556
  64.8 9.7 %collective-permute-start.19 = (bf16[256,512]{1,0:T(8,128)(2,1)S(1)}, bf16[256,512]{1,0:T(8,128)(2,1)S(1)}, u32[]{:S(2)}, u32[]{:S(2)}) collective-permute-start(bf16[256,512]{1,0:T(8,128)(2,1)S(1)} %get-tuple-element.213), channel_id=1, source_target_pairs={{0,1},{1,0},{2,3},{3,2},{4,5},{5,4},{6,7},{7,6},{8,9},{9,8},{10,11... | collective-permute-start | bytes 786440 | tf_op jit(solution)/shard_map/ppermute | solution.py:556
  68.7 11.3 %collective-permute-start.22 = (bf16[256,512]{1,0:T(8,128)(2,1)S(1)}, bf16[256,512]{1,0:T(8,128)(2,1)S(1)}, u32[]{:S(2)}, u32[]{:S(2)}) collective-permute-start(bf16[256,512]{1,0:T(8,128)(2,1)S(1)} %get-tuple-element.221), channel_id=1, source_target_pairs={{0,2},{1,3},{2,4},{3,5},{4,6},{5,7},{6,0},{7,1},{8,10},{9,11},{10,... | collective-permute-start | bytes 786440 | tf_op jit(solution)/shard_map/ppermute | solution.py:556
  70.0 10.1 %collective-permute-start.23 = (bf16[256,512]{1,0:T(8,128)(2,1)S(1)}, bf16[256,512]{1,0:T(8,128)(2,1)S(1)}, u32[]{:S(2)}, u32[]{:S(2)}) collective-permute-start(bf16[256,512]{1,0:T(8,128)(2,1)S(1)} %get-tuple-element.222), channel_id=1, source_target_pairs={{0,1},{1,0},{2,3},{3,2},{4,5},{5,4},{6,7},{7,6},{8,9},{9,8},{10,11... | collective-permute-start | bytes 786440 | tf_op jit(solution)/shard_map/ppermute | solution.py:556
  74.6 11.1 %collective-permute-start.24 = (bf16[256,512]{1,0:T(8,128)(2,1)S(1)}, bf16[256,512]{1,0:T(8,128)(2,1)S(1)}, u32[]{:S(2)}, u32[]{:S(2)}) collective-permute-start(bf16[256,512]{1,0:T(8,128)(2,1)S(1)} %get-tuple-element.226), channel_id=1, source_target_pairs={{0,2},{1,3},{2,4},{3,5},{4,6},{5,7},{6,0},{7,1},{8,10},{9,11},{10,... | collective-permute-start | bytes 786440 | tf_op jit(solution)/shard_map/ppermute | solution.py:556
  76.3 9.5 %collective-permute-start.25 = (bf16[256,512]{1,0:T(8,128)(2,1)S(1)}, bf16[256,512]{1,0:T(8,128)(2,1)S(1)}, u32[]{:S(2)}, u32[]{:S(2)}) collective-permute-start(bf16[256,512]{1,0:T(8,128)(2,1)S(1)} %get-tuple-element.227), channel_id=1, source_target_pairs={{0,1},{1,0},{2,3},{3,2},{4,5},{5,4},{6,7},{7,6},{8,9},{9,8},{10,11... | collective-permute-start | bytes 786440 | tf_op jit(solution)/shard_map/ppermute | solution.py:556
  80.1 11.2 %collective-permute-start.26 = (bf16[256,512]{1,0:T(8,128)(2,1)S(1)}, bf16[256,512]{1,0:T(8,128)(2,1)S(1)}, u32[]{:S(2)}, u32[]{:S(2)}) collective-permute-start(bf16[256,512]{1,0:T(8,128)(2,1)S(1)} %get-tuple-element.237), channel_id=1, source_target_pairs={{0,2},{1,3},{2,4},{3,5},{4,6},{5,7},{6,0},{7,1},{8,10},{9,11},{10,... | collective-permute-start | bytes 786440 | tf_op jit(solution)/shard_map/ppermute | solution.py:556
  81.0 10.3 %collective-permute-start.27 = (bf16[256,512]{1,0:T(8,128)(2,1)S(1)}, bf16[256,512]{1,0:T(8,128)(2,1)S(1)}, u32[]{:S(2)}, u32[]{:S(2)}) collective-permute-start(bf16[256,512]{1,0:T(8,128)(2,1)S(1)} %get-tuple-element.238), channel_id=1, source_target_pairs={{0,1},{1,0},{2,3},{3,2},{4,5},{5,4},{6,7},{7,6},{8,9},{9,8},{10,11... | collective-permute-start | bytes 786440 | tf_op jit(solution)/shard_map/ppermute | solution.py:556
  85.6 11.4 %copy-start = (bf16[256,512]{1,0:T(8,128)(2,1)}, bf16[256,512]{1,0:T(8,128)(2,1)S(1)}, u32[]{:S(2)}) copy-start(bf16[256,512]{1,0:T(8,128)(2,1)S(1)} %get-tuple-element.234.refs_11_) | copy-start | bytes 786436
  85.6 16.9 %copy-start.3 = (bf16[256,512]{1,0:T(8,128)(2,1)}, bf16[256,512]{1,0:T(8,128)(2,1)S(1)}, u32[]{:S(2)}) copy-start(bf16[256,512]{1,0:T(8,128)(2,1)S(1)} %get-tuple-element.231.refs_5_) | copy-start | bytes 786436
  85.8 11.1 %collective-permute-start.28 = (bf16[256,512]{1,0:T(8,128)(2,1)S(1)}, bf16[256,512]{1,0:T(8,128)(2,1)S(1)}, u32[]{:S(2)}, u32[]{:S(2)}) collective-permute-start(bf16[256,512]{1,0:T(8,128)(2,1)S(1)} %get-tuple-element.242), channel_id=1, source_target_pairs={{0,2},{1,3},{2,4},{3,5},{4,6},{5,7},{6,0},{7,1},{8,10},{9,11},{10,... | collective-permute-start | bytes 786440 | tf_op jit(solution)/shard_map/ppermute | solution.py:556
  87.4 9.6 %collective-permute-start.29 = (bf16[256,512]{1,0:T(8,128)(2,1)S(1)}, bf16[256,512]{1,0:T(8,128)(2,1)S(1)}, u32[]{:S(2)}, u32[]{:S(2)}) collective-permute-start(bf16[256,512]{1,0:T(8,128)(2,1)S(1)} %get-tuple-element.243), channel_id=1, source_target_pairs={{0,1},{1,0},{2,3},{3,2},{4,5},{5,4},{6,7},{7,6},{8,9},{9,8},{10,11... | collective-permute-start | bytes 786440 | tf_op jit(solution)/shard_map/ppermute | solution.py:556
  91.3 6.6 %copy-start.25 = (bf16[256,512]{1,0:T(8,128)(2,1)}, bf16[256,512]{1,0:T(8,128)(2,1)S(1)}, u32[]{:S(2)}) copy-start(bf16[256,512]{1,0:T(8,128)(2,1)S(1)} %collective-permute-done.26.refs_16_.refs_2_) | copy-start | bytes 786436
  91.3 6.6 %copy-start.26 = (bf16[256,512]{1,0:T(8,128)(2,1)}, bf16[256,512]{1,0:T(8,128)(2,1)S(1)}, u32[]{:S(2)}) copy-start(bf16[256,512]{1,0:T(8,128)(2,1)S(1)} %collective-permute-done.27.refs_15_.refs_3_) | copy-start | bytes 786436
  91.5 14.4 %copy-start.7 = (s32[1,1,4]{2,1,0:T(1,128)S(1)}, s32[1,1,4]{2,1,0:T(1,128)}, u32[]{:S(2)}) copy-start(s32[1,1,4]{2,1,0:T(1,128)} %param.8) | copy-start | bytes 52
  91.5 10.9 %collective-permute-start.30 = (bf16[256,512]{1,0:T(8,128)(2,1)S(1)}, bf16[256,512]{1,0:T(8,128)(2,1)S(1)}, u32[]{:S(2)}, u32[]{:S(2)}) collective-permute-start(bf16[256,512]{1,0:T(8,128)(2,1)S(1)} %get-tuple-element.247), channel_id=1, source_target_pairs={{0,2},{1,3},{2,4},{3,5},{4,6},{5,7},{6,0},{7,1},{8,10},{9,11},{10,... | collective-permute-start | bytes 786440 | tf_op jit(solution)/shard_map/ppermute | solution.py:556
  92.3 10.1 %collective-permute-start.31 = (bf16[256,512]{1,0:T(8,128)(2,1)S(1)}, bf16[256,512]{1,0:T(8,128)(2,1)S(1)}, u32[]{:S(2)}, u32[]{:S(2)}) collective-permute-start(bf16[256,512]{1,0:T(8,128)(2,1)S(1)} %get-tuple-element.248), channel_id=1, source_target_pairs={{0,1},{1,0},{2,3},{3,2},{4,5},{5,4},{6,7},{7,6},{8,9},{9,8},{10,11... | collective-permute-start | bytes 786440 | tf_op jit(solution)/shard_map/ppermute | solution.py:556
  97.0 6.5 %copy-start.36 = (bf16[256,512]{1,0:T(8,128)(2,1)}, bf16[256,512]{1,0:T(8,128)(2,1)S(1)}, u32[]{:S(2)}) copy-start(bf16[256,512]{1,0:T(8,128)(2,1)S(1)} %collective-permute-done.28.refs_4_) | copy-start | bytes 786436
  97.0 6.5 %copy-start.37 = (bf16[256,512]{1,0:T(8,128)(2,1)}, bf16[256,512]{1,0:T(8,128)(2,1)S(1)}, u32[]{:S(2)}) copy-start(bf16[256,512]{1,0:T(8,128)(2,1)S(1)} %collective-permute-done.29.refs_5_) | copy-start | bytes 786436
  97.9 15.6 %collective-permute-start.34 = (bf16[256,512]{1,0:T(8,128)(2,1)}, bf16[256,512]{1,0:T(8,128)(2,1)}, u32[]{:S(2)}, u32[]{:S(2)}) collective-permute-start(bf16[256,512]{1,0:T(8,128)(2,1)} %get-tuple-element.251), channel_id=1, source_target_pairs={{0,2},{1,3},{2,4},{3,5},{4,6},{5,7},{6,0},{7,1},{8,10},{9,11},{10,... | collective-permute-start | bytes 786440 | tf_op jit(solution)/shard_map/ppermute | solution.py:556
  98.6 14.9 %collective-permute-start.35 = (bf16[256,512]{1,0:T(8,128)(2,1)}, bf16[256,512]{1,0:T(8,128)(2,1)}, u32[]{:S(2)}, u32[]{:S(2)}) collective-permute-start(bf16[256,512]{1,0:T(8,128)(2,1)} %get-tuple-element.252), channel_id=1, source_target_pairs={{0,1},{1,0},{2,3},{3,2},{4,5},{5,4},{6,7},{7,6},{8,9},{9,8},{10,11... | collective-permute-start | bytes 786440 | tf_op jit(solution)/shard_map/ppermute | solution.py:556
  102.4 7.4 %copy-start.42 = (bf16[256,512]{1,0:T(8,128)(2,1)}, bf16[256,512]{1,0:T(8,128)(2,1)S(1)}, u32[]{:S(2)}) copy-start(bf16[256,512]{1,0:T(8,128)(2,1)S(1)} %collective-permute-done.30.refs_6_) | copy-start | bytes 786436
  103.5 13.3 %collective-permute-start.32 = (bf16[256,512]{1,0:T(8,128)(2,1)}, bf16[256,512]{1,0:T(8,128)(2,1)S(1)}, u32[]{:S(2)}, u32[]{:S(2)}) collective-permute-start(bf16[256,512]{1,0:T(8,128)(2,1)} %get-tuple-element.256), channel_id=1, source_target_pairs={{0,2},{1,3},{2,4},{3,5},{4,6},{5,7},{6,0},{7,1},{8,10},{9,11},{10,... | collective-permute-start | bytes 786440 | tf_op jit(solution)/shard_map/ppermute | solution.py:556
  104.3 12.5 %collective-permute-start.33 = (bf16[256,512]{1,0:T(8,128)(2,1)}, bf16[256,512]{1,0:T(8,128)(2,1)S(1)}, u32[]{:S(2)}, u32[]{:S(2)}) collective-permute-start(bf16[256,512]{1,0:T(8,128)(2,1)} %get-tuple-element.257), channel_id=1, source_target_pairs={{0,1},{1,0},{2,3},{3,2},{4,5},{5,4},{6,7},{7,6},{8,9},{9,8},{10,11... | collective-permute-start | bytes 786440 | tf_op jit(solution)/shard_map/ppermute | solution.py:556
  109.8 34.6 %all-to-all-start = ((bf16[4,528,256]{2,1,0:T(8,128)(2,1)}), bf16[4,528,256]{2,1,0:T(8,128)(2,1)S(1)}, u32[]{:S(2)}, u32[]{:S(2)}) async-start(bf16[4,528,256]{2,1,0:T(8,128)(2,1)} %get-tuple-element.253), calls=%async_computation | async-start | bytes 2162688 | tf_op jit(solution)/shard_map/all_to_all | solution.py:527
  114.6 11.0 %collective-permute-start.38 = (bf16[256,512]{1,0:T(8,128)(2,1)S(1)}, bf16[256,512]{1,0:T(8,128)(2,1)S(1)}, u32[]{:S(2)}, u32[]{:S(2)}) collective-permute-start(bf16[256,512]{1,0:T(8,128)(2,1)S(1)} %get-tuple-element.260), channel_id=1, source_target_pairs={{0,2},{1,3},{2,4},{3,5},{4,6},{5,7},{6,0},{7,1},{8,10},{9,11},{10,... | collective-permute-start | bytes 786440 | tf_op jit(solution)/shard_map/ppermute | solution.py:556
  116.3 9.3 %collective-permute-start.39 = (bf16[256,512]{1,0:T(8,128)(2,1)S(1)}, bf16[256,512]{1,0:T(8,128)(2,1)S(1)}, u32[]{:S(2)}, u32[]{:S(2)}) collective-permute-start(bf16[256,512]{1,0:T(8,128)(2,1)S(1)} %get-tuple-element.261), channel_id=1, source_target_pairs={{0,1},{1,0},{2,3},{3,2},{4,5},{5,4},{6,7},{7,6},{8,9},{9,8},{10,11... | collective-permute-start | bytes 786440 | tf_op jit(solution)/shard_map/ppermute | solution.py:556
  116.8 6.6 %copy-start.38 = (bf16[256,512]{1,0:T(8,128)(2,1)}, bf16[256,512]{1,0:T(8,128)(2,1)S(1)}, u32[]{:S(2)}) copy-start(bf16[256,512]{1,0:T(8,128)(2,1)S(1)} %collective-permute-done.32.refs_10_) | copy-start | bytes 786436
  116.8 6.6 %copy-start.39 = (bf16[256,512]{1,0:T(8,128)(2,1)}, bf16[256,512]{1,0:T(8,128)(2,1)S(1)}, u32[]{:S(2)}) copy-start(bf16[256,512]{1,0:T(8,128)(2,1)S(1)} %collective-permute-done.33.refs_11_) | copy-start | bytes 786436
  116.8 13.9 %collective-permute-start.36 = (bf16[256,512]{1,0:T(8,128)(2,1)S(1)}, bf16[256,512]{1,0:T(8,128)(2,1)S(1)}, u32[]{:S(2)}, u32[]{:S(2)}) collective-permute-start(bf16[256,512]{1,0:T(8,128)(2,1)S(1)} %get-tuple-element.264), channel_id=1, source_target_pairs={{0,2},{1,3},{2,4},{3,5},{4,6},{5,7},{6,0},{7,1},{8,10},{9,11},{10,... | collective-permute-start | bytes 786440 | tf_op jit(solution)/shard_map/ppermute | solution.py:556
  117.4 13.3 %collective-permute-start.37 = (bf16[256,512]{1,0:T(8,128)(2,1)S(1)}, bf16[256,512]{1,0:T(8,128)(2,1)S(1)}, u32[]{:S(2)}, u32[]{:S(2)}) collective-permute-start(bf16[256,512]{1,0:T(8,128)(2,1)S(1)} %get-tuple-element.265), channel_id=1, source_target_pairs={{0,1},{1,0},{2,3},{3,2},{4,5},{5,4},{6,7},{7,6},{8,9},{9,8},{10,11... | collective-permute-start | bytes 786440 | tf_op jit(solution)/shard_map/ppermute | solution.py:556
  125.6 20.8 %copy-start.40 = (bf16[256,512]{1,0:T(8,128)(2,1)}, bf16[256,512]{1,0:T(8,128)(2,1)S(1)}, u32[]{:S(2)}) copy-start(bf16[256,512]{1,0:T(8,128)(2,1)S(1)} %collective-permute-done.38.refs_12_) | copy-start | bytes 786436
  125.6 20.8 %copy-start.41 = (bf16[256,512]{1,0:T(8,128)(2,1)}, bf16[256,512]{1,0:T(8,128)(2,1)S(1)}, u32[]{:S(2)}) copy-start(bf16[256,512]{1,0:T(8,128)(2,1)S(1)} %collective-permute-done.39.refs_13_) | copy-start | bytes 786436
  130.7 15.7 %copy-start.44 = (bf16[256,512]{1,0:T(8,128)(2,1)}, bf16[256,512]{1,0:T(8,128)(2,1)S(1)}, u32[]{:S(2)}) copy-start(bf16[256,512]{1,0:T(8,128)(2,1)S(1)} %collective-permute-done.36.refs_14_) | copy-start | bytes 786436
  130.7 10.0 %copy-start.45 = (bf16[256,512]{1,0:T(8,128)(2,1)}, bf16[256,512]{1,0:T(8,128)(2,1)S(1)}, u32[]{:S(2)}) copy-start(bf16[256,512]{1,0:T(8,128)(2,1)S(1)} %collective-permute-done.37.refs_15_) | copy-start | bytes 786436
  130.8 9.3 %collective-permute-start.40 = (bf16[256,512]{1,0:T(8,128)(2,1)S(1)}, bf16[256,512]{1,0:T(8,128)(2,1)S(1)}, u32[]{:S(2)}, u32[]{:S(2)}) collective-permute-start(bf16[256,512]{1,0:T(8,128)(2,1)S(1)} %broadcast_select_fusion), channel_id=1, source_target_pairs={{0,1},{1,0},{2,3},{3,2},{4,5},{5,4},{6,7},{7,6},{8,9},{9,8},{10,11... | collective-permute-start | bytes 786440 | tf_op jit(solution)/shard_map/ppermute | solution.py:556
  131.4 9.4 %collective-permute-start.41 = (bf16[256,512]{1,0:T(8,128)(2,1)S(1)}, bf16[256,512]{1,0:T(8,128)(2,1)S(1)}, u32[]{:S(2)}, u32[]{:S(2)}) collective-permute-start(bf16[256,512]{1,0:T(8,128)(2,1)S(1)} %get-tuple-element.270), channel_id=1, source_target_pairs={{0,2},{1,3},{2,4},{3,5},{4,6},{5,7},{6,0},{7,1},{8,10},{9,11},{10,... | collective-permute-start | bytes 786440 | tf_op jit(solution)/shard_map/ppermute | solution.py:556
  131.4 13.1 %collective-permute-start.42 = (bf16[256,512]{1,0:T(8,128)(2,1)S(1)}, bf16[256,512]{1,0:T(8,128)(2,1)}, u32[]{:S(2)}, u32[]{:S(2)}) collective-permute-start(bf16[256,512]{1,0:T(8,128)(2,1)S(1)} %get-tuple-element.271), channel_id=1, source_target_pairs={{0,1},{1,0},{2,3},{3,2},{4,5},{5,4},{6,7},{7,6},{8,9},{9,8},{10,11... | collective-permute-start | bytes 786440 | tf_op jit(solution)/shard_map/ppermute | solution.py:556
  140.1 6.4 %copy-start.46 = (bf16[256,512]{1,0:T(8,128)(2,1)}, bf16[256,512]{1,0:T(8,128)(2,1)S(1)}, u32[]{:S(2)}) copy-start(bf16[256,512]{1,0:T(8,128)(2,1)S(1)} %collective-permute-done.40.refs_2_) | copy-start | bytes 786436
  146.4 30.1 %all-to-all-start.1 = ((bf16[8,272,256]{2,1,0:T(8,128)(2,1)}), bf16[8,272,256]{2,1,0:T(8,128)(2,1)S(1)}, u32[]{:S(2)}, u32[]{:S(2)}) async-start(bf16[8,272,256]{2,1,0:T(8,128)(2,1)} %relay.1), calls=%async_computation.1 | async-start | bytes 2228224 | tf_op jit(solution)/shard_map/all_to_all | solution.py:527
  (29 other events, 149.4 us)

commit v9 on v8

--- a/solution.py
+++ b/solution.py
@@ -560,6 +560,7 @@
         late = e - ready - CHAINS
         if late == 0:
             own, sends = own_part()
+            turn = (*turn, own)
         if late == 1:
             arrived = exchange(after((sends,), *turn)[0], "front")
         if late == 4:

time: 179 us -> 176 us (0.983)
  waiting for transfers between devices: 51 us -> 46.2 us
    ppermute x43, waiting for transfers between devices: 47 us -> 42.2 us  [shards(): lax.ppermute(turn[s], 'grp', perms[s])]
  transfers between devices with their start and end apart: 45 -> 45, of which waited for: 20 -> 18; matrix products, arithmetic and copies ran while one was open for 2% -> 2% of each run, Pallas kernels for 29% -> 30%
where the time goes in v9:
time: 176 us; the launch traced here: 175 us
  starting transfers between devices  61.9 us (35%)
  Pallas kernels  58.9 us (33%)
  waiting for transfers between devices  46.2 us (26%)
  other arithmetic  4.02 us (2%)
  local copies, waits for them, and re-layouts  2.44 us (1%)
    ppermute x43, starting transfers between devices, shards(): lax.ppermute(turn[s], 'grp', perms[s])  54.8 us
    ppermute x43, waiting for transfers between devices, shards(): lax.ppermute(turn[s], 'grp', perms[s])  42.2 us
    pallas_call x4, Pallas kernels, update(): pl.pallas_call(functools.partial(update_kernel, tuple(numbers), room, wid...  26.9 us
    pallas_call x8, Pallas kernels, factor(): pl.pallas_call(functools.partial(factor_kernel, tuple(tiles), head), out_...  24.7 us
    all_to_all x2, starting transfers between devices, exchange(): return lax.all_to_all(blocks, axis, split_axis=0, concat_axis=0, tiled=True)  7.09 us
    all_to_all x2, waiting for transfers between devices, exchange(): return lax.all_to_all(blocks, axis, split_axis=0, concat_axis=0, tiled=True)  4.01 us
    pallas_call x1, Pallas kernels, own_panels(): pl.pallas_call(functools.partial(own_kernel, choices, len(blocks), width...  3.98 us
    select_n x17, other arithmetic, shards(): jnp.where(root, made[which][n], value)  3.66 us
  transfers between devices with their start and end apart: 45, of which 18 were waited for; matrix products, arithmetic and copies ran while one was open for 2% of the time, Pallas kernels for 30%

profile of v9, /device:TPU:0, one launch (start us, length us, event | category | flops | bytes accessed | tf_op | source)
XLA Modules:
  0.0 175.0 jit_solution(7025811000174813666)
XLA Ops:
  1.4 3.8 %factor.8 = (bf16[256,512]{1,0:T(8,128)(2,1)S(1)}, bf16[256,512]{1,0:T(8,128)(2,1)S(1)}, bf16[256,512]{1,0:T(8,128)(2,1)S(1)}, bf16[256,512]{1,0:T(8,128)(2,1)S(...) custom-call(s32[32,4]{1,0:T(8,128)S(1)} %copy.54.mask, bf16[8192,1024]{1,0:T(8,128)(2,1)} %bitcast.9, ...), custom_call_target="tpu_custom_call" | custom-call | flops 805306368 | bytes 2097152 | tf_op jit(solution)/shard_map/factor/pallas_call | solution.py:178
  5.2 3.1 %collective-permute-start = (bf16[256,512]{1,0:T(8,128)(2,1)S(1)}, bf16[256,512]{1,0:T(8,128)(2,1)S(1)}, u32[]{:S(2)}, u32[]{:S(2)}) collective-permute-start(bf16[256,512]{1,0:T(8,128)(2,1)S(1)} %get-tuple-element.146.refs_18_), channel_id=1, source_target_pairs={{0,2},{1,3},{2,4},{3,5},{4,6},{5,7},{6,0},{7,1},{8,10},{9,11},{10,... | collective-permute-start | bytes 786440 | tf_op jit(solution)/shard_map/ppermute | solution.py:556
  8.3 1.5 collective-permute-start.1
  9.8 1.6 collective-permute-start.4
  11.9 3.0 %factor.9 = (bf16[256,512]{1,0:T(8,128)(2,1)S(1)}, bf16[256,512]{1,0:T(8,128)(2,1)S(1)}, bf16[256,512]{1,0:T(8,128)(2,1)S(1)}, bf16[256,512]{1,0:T(8,128)(2,1)S(1)}) custom-call(s32[32,4]{1,0:T(8,128)S(1)} %copy.54.mask, bf16[8192,1024]{1,0:T(8,128)(2,1)} %bitcast.10, bf16[4,256,256]{2,1,0:T(8,128)(2,1)S(1)} %get-tuple-element.228.refs_0_, ...), custom_call_target="tpu_custom_call" | custom-call | flops 805306368 | bytes 2097152 | tf_op jit(solution)/shard_map/factor/pallas_call | solution.py:178
  14.9 2.6 %collective-permute-done.refs_19_.refs_0_ = bf16[256,512]{1,0:T(8,128)(2,1)S(1)} collective-permute-done((bf16[256,512]{1,0:T(8,128)(2,1)S(1)}, bf16[256,512]{1,0:T(8,128)(2,1)S(1)}, u32[]{:S(2)}, u32[]{:S(2)}) %collective-permute-start) | collective-permute-done | bytes 262176 | tf_op jit(solution)/shard_map/ppermute | solution.py:556
  17.6 1.6 collective-permute-start.2
  19.2 1.5 collective-permute-start.3
  20.7 2.3 %collective-permute-done.4.refs_2_ = bf16[256,512]{1,0:T(8,128)(2,1)S(1)} collective-permute-done((bf16[256,512]{1,0:T(8,128)(2,1)S(1)}, bf16[256,512]{1,0:T(8,128)(2,1)S(1)}, u32[]{:S(2)}, u32[]{:S(2)}) %collective-permute-start.4) | collective-permute-done | bytes 262176 | tf_op jit(solution)/shard_map/ppermute | solution.py:556
  23.2 1.6 collective-permute-start.8
  24.8 1.5 collective-permute-start.9
  26.4 3.0 %factor.10 = (bf16[256,512]{1,0:T(8,128)(2,1)S(1)}, bf16[256,512]{1,0:T(8,128)(2,1)S(1)}, bf16[256,512]{1,0:T(8,128)(2,1)S(1)}, bf16[256,512]{1,0:T(8,128)(2,1)S(1)}) custom-call(s32[32,4]{1,0:T(8,128)S(1)} %copy.54.mask, bf16[8192,1024]{1,0:T(8,128)(2,1)} %bitcast.11, bf16[4,256,256]{2,1,0:T(8,128)(2,1)S(1)} %get-tuple-element.228.refs_0_, ...), custom_call_target="tpu_custom_call" | custom-call | flops 805306368 | bytes 2097152 | tf_op jit(solution)/shard_map/factor/pallas_call | solution.py:178
  29.5 1.6 collective-permute-start.6
  31.9 2.3 %collective-permute-done.8.refs_6_ = bf16[256,512]{1,0:T(8,128)(2,1)S(1)} collective-permute-done((bf16[256,512]{1,0:T(8,128)(2,1)S(1)}, bf16[256,512]{1,0:T(8,128)(2,1)S(1)}, u32[]{:S(2)}, u32[]{:S(2)}) %collective-permute-start.8) | collective-permute-done | bytes 262176 | tf_op jit(solution)/shard_map/ppermute | solution.py:556
  35.0 1.1 collective-permute-start.12
  36.1 1.5 collective-permute-start.13
  37.6 3.0 %factor.11 = (bf16[256,512]{1,0:T(8,128)(2,1)S(1)}, bf16[256,512]{1,0:T(8,128)(2,1)S(1)}, bf16[256,512]{1,0:T(8,128)(2,1)S(1)}, bf16[256,512]{1,0:T(8,128)(2,1)S(1)}) custom-call(s32[32,4]{1,0:T(8,128)S(1)} %copy.54.mask, bf16[8192,1024]{1,0:T(8,128)(2,1)} %bitcast.12, bf16[4,256,256]{2,1,0:T(8,128)(2,1)S(1)} %get-tuple-element.228.refs_0_, ...), custom_call_target="tpu_custom_call" | custom-call | flops 805306368 | bytes 2097152 | tf_op jit(solution)/shard_map/factor/pallas_call | solution.py:178
  40.7 1.6 collective-permute-start.10
  43.2 2.8 %collective-permute-done.12.refs_2_ = bf16[256,512]{1,0:T(8,128)(2,1)S(1)} collective-permute-done((bf16[256,512]{1,0:T(8,128)(2,1)S(1)}, bf16[256,512]{1,0:T(8,128)(2,1)S(1)}, u32[]{:S(2)}, u32[]{:S(2)}) %collective-permute-start.12) | collective-permute-done | bytes 262176 | tf_op jit(solution)/shard_map/ppermute | solution.py:556
  46.1 1.2 collective-permute-start.16
  47.3 1.5 collective-permute-start.17
  48.8 3.0 %factor.12 = (bf16[256,512]{1,0:T(8,128)(2,1)S(1)}, bf16[256,512]{1,0:T(8,128)(2,1)S(1)}, bf16[256,512]{1,0:T(8,128)(2,1)S(1)}, bf16[256,512]{1,0:T(8,128)(2,1)S(1)}) custom-call(s32[32,4]{1,0:T(8,128)S(1)} %copy.54.mask, bf16[8192,1024]{1,0:T(8,128)(2,1)} %bitcast.13, bf16[4,256,256]{2,1,0:T(8,128)(2,1)S(1)} %get-tuple-element.228.refs_0_, ...), custom_call_target="tpu_custom_call" | custom-call | flops 805306368 | bytes 2097152 | tf_op jit(solution)/shard_map/factor/pallas_call | solution.py:178
  51.9 1.6 collective-permute-start.14
  54.4 3.0 %collective-permute-done.16.refs_9_.refs_6_ = bf16[256,512]{1,0:T(8,128)(2,1)S(1)} collective-permute-done((bf16[256,512]{1,0:T(8,128)(2,1)S(1)}, bf16[256,512]{1,0:T(8,128)(2,1)S(1)}, u32[]{:S(2)}, u32[]{:S(2)}) %collective-permute-start.16) | collective-permute-done | bytes 262176 | tf_op jit(solution)/shard_map/ppermute | solution.py:556
  57.5 1.0 collective-permute-start.20
  58.5 1.5 collective-permute-start.21
  60.0 3.0 %factor.13 = (bf16[256,512]{1,0:T(8,128)(2,1)S(1)}, bf16[256,512]{1,0:T(8,128)(2,1)S(1)}, bf16[256,512]{1,0:T(8,128)(2,1)S(1)}, bf16[256,512]{1,0:T(8,128)(2,1)S(1)}) custom-call(s32[32,4]{1,0:T(8,128)S(1)} %copy.54.mask, bf16[8192,1024]{1,0:T(8,128)(2,1)} %bitcast.14, bf16[4,256,256]{2,1,0:T(8,128)(2,1)S(1)} %get-tuple-element.228.refs_0_, ...), custom_call_target="tpu_custom_call" | custom-call | flops 805306368 | bytes 2097152 | tf_op jit(solution)/shard_map/factor/pallas_call | solution.py:178
  63.2 1.6 collective-permute-start.18
  64.8 0.8 collective-permute-start.19
  65.6 3.0 %collective-permute-done.20.refs_8_.refs_10_ = bf16[256,512]{1,0:T(8,128)(2,1)S(1)} collective-permute-done((bf16[256,512]{1,0:T(8,128)(2,1)S(1)}, bf16[256,512]{1,0:T(8,128)(2,1)S(1)}, u32[]{:S(2)}, u32[]{:S(2)}) %collective-permute-start.20) | collective-permute-done | bytes 262176 | tf_op jit(solution)/shard_map/ppermute | solution.py:556
  68.7 1.2 collective-permute-start.22
  70.0 1.5 collective-permute-start.23
  71.5 3.0 %factor.14 = (bf16[256,512]{1,0:T(8,128)(2,1)S(1)}, bf16[256,512]{1,0:T(8,128)(2,1)S(1)}, bf16[256,512]{1,0:T(8,128)(2,1)S(1)}, bf16[256,512]{1,0:T(8,128)(2,1)S(1)}) custom-call(s32[32,4]{1,0:T(8,128)S(1)} %copy.54.mask, bf16[8192,1024]{1,0:T(8,128)(2,1)} %bitcast.15, bf16[4,256,256]{2,1,0:T(8,128)(2,1)S(1)} %get-tuple-element.228.refs_0_, ...), custom_call_target="tpu_custom_call" | custom-call | flops 805306368 | bytes 2097152 | tf_op jit(solution)/shard_map/factor/pallas_call | solution.py:178
  74.6 1.6 collective-permute-start.24
  76.9 3.1 %collective-permute-done.22.refs_7_.refs_14_ = bf16[256,512]{1,0:T(8,128)(2,1)S(1)} collective-permute-done((bf16[256,512]{1,0:T(8,128)(2,1)S(1)}, bf16[256,512]{1,0:T(8,128)(2,1)S(1)}, u32[]{:S(2)}, u32[]{:S(2)}) %collective-permute-start.22) | collective-permute-done | bytes 262176 | tf_op jit(solution)/shard_map/ppermute | solution.py:556
  80.1 0.9 collective-permute-start.26
  81.0 1.5 collective-permute-start.27
  82.5 3.0 %factor.15 = (bf16[256,512]{1,0:T(8,128)(2,1)S(1)}, bf16[256,512]{1,0:T(8,128)(2,1)S(1)}, bf16[256,512]{1,0:T(8,128)(2,1)S(1)}, bf16[256,512]{1,0:T(8,128)(2,1)S(1)}) custom-call(s32[32,4]{1,0:T(8,128)S(1)} %copy.54.mask, bf16[8192,1024]{1,0:T(8,128)(2,1)} %bitcast.16, bf16[4,256,256]{2,1,0:T(8,128)(2,1)S(1)} %get-tuple-element.228.refs_0_, ...), custom_call_target="tpu_custom_call" | custom-call | flops 805306368 | bytes 2097152 | tf_op jit(solution)/shard_map/factor/pallas_call | solution.py:178
  85.7 1.6 collective-permute-start.28
  88.2 3.1 %collective-permute-done.26.refs_16_.refs_2_ = bf16[256,512]{1,0:T(8,128)(2,1)S(1)} collective-permute-done((bf16[256,512]{1,0:T(8,128)(2,1)S(1)}, bf16[256,512]{1,0:T(8,128)(2,1)S(1)}, u32[]{:S(2)}, u32[]{:S(2)}) %collective-permute-start.26) | collective-permute-done | bytes 262176 | tf_op jit(solution)/shard_map/ppermute | solution.py:556
  91.4 0.9 collective-permute-start.30
  92.3 1.5 collective-permute-start.31
  93.8 4.0 %own_panels.1 = (bf16[512,1024]{1,0:T(8,128)(2,1)S(1)}, bf16[4,528,256]{2,1,0:T(8,128)(2,1)}) custom-call(s32[32,4]{1,0:T(8,128)S(1)} %copy.54.mask, s32[4]{0:T(128)S(1)} %bitcast.8, s32[1]{0:T(128)} %bitcast.1.me, bf16[8192,1024]{1,0:T(8,128)(2,1)} %bitcast.17, bf16[256,512]{1,0:T(8,128)(2,1)} %copy-done.7, bf16[256,512]{1,0:T(8,128)(2,1)} %copy-done.22, ...), custom_call_target="tpu_custom_call" | custom-call | flops 268435456 | bytes 2621440 | tf_op jit(solution)/shard_map/own_panels/pallas_call | solution.py:238
  97.9 0.9 select_select_fusion.2
  98.7 1.6 collective-permute-start.34
  103.3 1.7 collective-permute-start.32
  105.0 1.5 collective-permute-start.33
  106.5 3.5 %all-to-all-start = ((bf16[4,528,256]{2,1,0:T(8,128)(2,1)}), bf16[4,528,256]{2,1,0:T(8,128)(2,1)S(1)}, u32[]{:S(2)}, u32[]{:S(2)}) async-start(bf16[4,528,256]{2,1,0:T(8,128)(2,1)} %get-tuple-element.254), calls=%async_computation | async-start | bytes 2162688 | tf_op jit(solution)/shard_map/all_to_all | solution.py:527
  110.0 1.1 select_select_fusion
  111.1 1.6 collective-permute-start.38
  114.1 1.4 collective-permute-start.37
  115.6 4.4 %update.4.refs_16_ = bf16[8192,1024]{1,0:T(8,128)(2,1)} custom-call(s32[8,44]{1,0:T(8,128)S(1)} %copy-done.8, s32[32,4]{1,0:T(8,128)S(1)} %copy.54.mask, s32[1]{0:T(128)} %bitcast.1.me, bf16[512,1024]{1,0:T(8,128)(2,1)S(1)} %get-tuple-element.251.own, bf16[8192,1024]{1,0:T(8,128)(2,1)} %bitcast.18, bf16[256,512]{1,0:T(8,128)(2,1)} %copy-done.10, ...), custom_call_target="tpu_custom_call" | custom-call | flops 2147483648 | bytes 8388608 | tf_op jit(solution)/shard_map/update/pallas_call | solution.py:403
  120.0 2.1 %collective-permute-done.38.refs_12_ = bf16[256,512]{1,0:T(8,128)(2,1)S(1)} collective-permute-done((bf16[256,512]{1,0:T(8,128)(2,1)S(1)}, bf16[256,512]{1,0:T(8,128)(2,1)S(1)}, u32[]{:S(2)}, u32[]{:S(2)}) %collective-permute-start.38) | collective-permute-done | bytes 262176 | tf_op jit(solution)/shard_map/ppermute | solution.py:556
  122.1 5.1 %collective-permute-done.36.refs_14_ = bf16[256,512]{1,0:T(8,128)(2,1)S(1)} collective-permute-done((bf16[256,512]{1,0:T(8,128)(2,1)S(1)}, bf16[256,512]{1,0:T(8,128)(2,1)S(1)}, u32[]{:S(2)}, u32[]{:S(2)}) %collective-permute-start.36) | collective-permute-done | bytes 262176 | tf_op jit(solution)/shard_map/ppermute | solution.py:556
  127.9 1.5 collective-permute-start.42
  129.4 7.2 %collective-permute-done.40.refs_2_ = bf16[256,512]{1,0:T(8,128)(2,1)S(1)} collective-permute-done((bf16[256,512]{1,0:T(8,128)(2,1)S(1)}, bf16[256,512]{1,0:T(8,128)(2,1)S(1)}, u32[]{:S(2)}, u32[]{:S(2)}) %collective-permute-start.40) | collective-permute-done | bytes 262176 | tf_op jit(solution)/shard_map/ppermute | solution.py:556
  137.3 3.7 %collective-permute-done.42.refs_1_ = bf16[256,512]{1,0:T(8,128)(2,1)} collective-permute-done((bf16[256,512]{1,0:T(8,128)(2,1)S(1)}, bf16[256,512]{1,0:T(8,128)(2,1)}, u32[]{:S(2)}, u32[]{:S(2)}) %collective-permute-start.42) | collective-permute-done | bytes 262176 | tf_op jit(solution)/shard_map/ppermute | solution.py:556
  141.2 1.7 relay.1
  142.9 3.6 %all-to-all-start.1 = ((bf16[8,272,256]{2,1,0:T(8,128)(2,1)}), bf16[8,272,256]{2,1,0:T(8,128)(2,1)S(1)}, u32[]{:S(2)}, u32[]{:S(2)}) async-start(bf16[8,272,256]{2,1,0:T(8,128)(2,1)} %relay.1), calls=%async_computation.1 | async-start | bytes 2228224 | tf_op jit(solution)/shard_map/all_to_all | solution.py:527
  146.5 9.4 %update.5.refs_16_ = bf16[8192,1024]{1,0:T(8,128)(2,1)} custom-call(s32[8,44]{1,0:T(8,128)S(1)} %copy-done.8, s32[32,4]{1,0:T(8,128)S(1)} %copy.54.mask, s32[1]{0:T(128)} %bitcast.1.me, bf16[512,1024]{1,0:T(8,128)(2,1)S(1)} %get-tuple-element.251.own, bf16[8192,1024]{1,0:T(8,128)(2,1)} %bitcast.19, ...), custom_call_target="tpu_custom_call", output_to_operand_aliasing={{}: (21, {})} | custom-call | flops 4294967296 | bytes 16777216 | tf_op jit(solution)/shard_map/update/pallas_call | solution.py:403
  155.9 9.4 %update.6.refs_3_ = bf16[8192,1024]{1,0:T(8,128)(2,1)} custom-call(s32[8,44]{1,0:T(8,128)S(1)} %copy-done.8, s32[32,4]{1,0:T(8,128)S(1)} %copy.54.mask, s32[1]{0:T(128)} %bitcast.1.me, bf16[512,1024]{1,0:T(8,128)(2,1)S(1)} %get-tuple-element.251.own, bf16[8192,1024]{1,0:T(8,128)(2,1)} %bitcast.20, ...), custom_call_target="tpu_custom_call", output_to_operand_aliasing={{}: (21, {})} | custom-call | flops 4294967296 | bytes 16777216 | tf_op jit(solution)/shard_map/update/pallas_call | solution.py:403
  165.3 3.7 %update.7 = bf16[8192,1024]{1,0:T(8,128)(2,1)} custom-call(s32[8,44]{1,0:T(8,128)S(1)} %copy-done.8, s32[32,4]{1,0:T(8,128)S(1)} %copy.54.mask, s32[1]{0:T(128)} %bitcast.1.me, bf16[512,1024]{1,0:T(8,128)(2,1)S(1)} %get-tuple-element.251.own, bf16[8192,1024]{1,0:T(8,128)(2,1)} %bitcast.21, ...), custom_call_target="tpu_custom_call", output_to_operand_aliasing={{}: (8, {})} | custom-call | flops 1073741824 | bytes 4194304 | tf_op jit(solution)/shard_map/update/pallas_call | solution.py:403
  169.0 4.0 %all-to-all-done.1.arrived = bf16[8,272,256]{2,1,0:T(8,128)(2,1)S(1)} async-done(((bf16[8,272,256]{2,1,0:T(8,128)(2,1)}), bf16[8,272,256]{2,1,0:T(8,128)(2,1)S(1)}, u32[]{:S(2)}, u32[]{:S(2)}) %all-to-all-start.1) | async-done | bytes 1114144 | tf_op jit(solution)/shard_map/all_to_all | solution.py:527
  173.2 1.7 sum_parents.1
  (167 shorter events, 13.2 us)
Async XLA Ops:
  5.2 9.7 %copy-start.6 = (bf16[256,512]{1,0:T(8,128)(2,1)}, bf16[256,512]{1,0:T(8,128)(2,1)S(1)}, u32[]{:S(2)}) copy-start(bf16[256,512]{1,0:T(8,128)(2,1)S(1)} %get-tuple-element.146.refs_18_) | copy-start | bytes 786436
  5.2 12.2 %collective-permute-start = (bf16[256,512]{1,0:T(8,128)(2,1)S(1)}, bf16[256,512]{1,0:T(8,128)(2,1)S(1)}, u32[]{:S(2)}, u32[]{:S(2)}) collective-permute-start(bf16[256,512]{1,0:T(8,128)(2,1)S(1)} %get-tuple-element.146.refs_18_), channel_id=1, source_target_pairs={{0,2},{1,3},{2,4},{3,5},{4,6},{5,7},{6,0},{7,1},{8,10},{9,11},{10,... | collective-permute-start | bytes 786440 | tf_op jit(solution)/shard_map/ppermute | solution.py:556
  8.3 9.2 %collective-permute-start.1 = (bf16[256,512]{1,0:T(8,128)(2,1)S(1)}, bf16[256,512]{1,0:T(8,128)(2,1)S(1)}, u32[]{:S(2)}, u32[]{:S(2)}) collective-permute-start(bf16[256,512]{1,0:T(8,128)(2,1)S(1)} %get-tuple-element.147), channel_id=1, source_target_pairs={{0,1},{1,0},{2,3},{3,2},{4,5},{5,4},{6,7},{7,6},{8,9},{9,8},{10,11... | collective-permute-start | bytes 786440 | tf_op jit(solution)/shard_map/ppermute | solution.py:556
  9.8 13.3 %collective-permute-start.4 = (bf16[256,512]{1,0:T(8,128)(2,1)S(1)}, bf16[256,512]{1,0:T(8,128)(2,1)S(1)}, u32[]{:S(2)}, u32[]{:S(2)}) collective-permute-start(bf16[256,512]{1,0:T(8,128)(2,1)S(1)} %get-tuple-element.148), channel_id=1, source_target_pairs={{0,2},{1,3},{2,4},{3,5},{4,6},{5,7},{6,0},{7,1},{8,10},{9,11},{10,... | collective-permute-start | bytes 786440 | tf_op jit(solution)/shard_map/ppermute | solution.py:556
  11.4 11.8 %collective-permute-start.5 = (bf16[256,512]{1,0:T(8,128)(2,1)S(1)}, bf16[256,512]{1,0:T(8,128)(2,1)S(1)}, u32[]{:S(2)}, u32[]{:S(2)}) collective-permute-start(bf16[256,512]{1,0:T(8,128)(2,1)S(1)} %get-tuple-element.149), channel_id=1, source_target_pairs={{0,1},{1,0},{2,3},{3,2},{4,5},{5,4},{6,7},{7,6},{8,9},{9,8},{10,11... | collective-permute-start | bytes 786440 | tf_op jit(solution)/shard_map/ppermute | solution.py:556
  17.6 11.8 %collective-permute-start.2 = (bf16[256,512]{1,0:T(8,128)(2,1)S(1)}, bf16[256,512]{1,0:T(8,128)(2,1)S(1)}, u32[]{:S(2)}, u32[]{:S(2)}) collective-permute-start(bf16[256,512]{1,0:T(8,128)(2,1)S(1)} %get-tuple-element.156), channel_id=1, source_target_pairs={{0,2},{1,3},{2,4},{3,5},{4,6},{5,7},{6,0},{7,1},{8,10},{9,11},{10,... | collective-permute-start | bytes 786440 | tf_op jit(solution)/shard_map/ppermute | solution.py:556
  19.2 10.2 %collective-permute-start.3 = (bf16[256,512]{1,0:T(8,128)(2,1)S(1)}, bf16[256,512]{1,0:T(8,128)(2,1)S(1)}, u32[]{:S(2)}, u32[]{:S(2)}) collective-permute-start(bf16[256,512]{1,0:T(8,128)(2,1)S(1)} %get-tuple-element.157), channel_id=1, source_target_pairs={{0,1},{1,0},{2,3},{3,2},{4,5},{5,4},{6,7},{7,6},{8,9},{9,8},{10,11... | collective-permute-start | bytes 786440 | tf_op jit(solution)/shard_map/ppermute | solution.py:556
  23.0 6.3 %copy-start.30 = (bf16[256,512]{1,0:T(8,128)(2,1)}, bf16[256,512]{1,0:T(8,128)(2,1)S(1)}, u32[]{:S(2)}) copy-start(bf16[256,512]{1,0:T(8,128)(2,1)S(1)} %collective-permute-done.4.refs_2_) | copy-start | bytes 786436
  23.1 6.2 %copy-start.31 = (bf16[256,512]{1,0:T(8,128)(2,1)}, bf16[256,512]{1,0:T(8,128)(2,1)S(1)}, u32[]{:S(2)}) copy-start(bf16[256,512]{1,0:T(8,128)(2,1)S(1)} %collective-permute-done.5.refs_3_) | copy-start | bytes 786436
  23.2 11.1 %collective-permute-start.8 = (bf16[256,512]{1,0:T(8,128)(2,1)S(1)}, bf16[256,512]{1,0:T(8,128)(2,1)S(1)}, u32[]{:S(2)}, u32[]{:S(2)}) collective-permute-start(bf16[256,512]{1,0:T(8,128)(2,1)S(1)} %get-tuple-element.165), channel_id=1, source_target_pairs={{0,2},{1,3},{2,4},{3,5},{4,6},{5,7},{6,0},{7,1},{8,10},{9,11},{10,... | collective-permute-start | bytes 786440 | tf_op jit(solution)/shard_map/ppermute | solution.py:556
  24.8 9.5 %collective-permute-start.9 = (bf16[256,512]{1,0:T(8,128)(2,1)S(1)}, bf16[256,512]{1,0:T(8,128)(2,1)S(1)}, u32[]{:S(2)}, u32[]{:S(2)}) collective-permute-start(bf16[256,512]{1,0:T(8,128)(2,1)S(1)} %get-tuple-element.166), channel_id=1, source_target_pairs={{0,1},{1,0},{2,3},{3,2},{4,5},{5,4},{6,7},{7,6},{8,9},{9,8},{10,11... | collective-permute-start | bytes 786440 | tf_op jit(solution)/shard_map/ppermute | solution.py:556
  29.5 11.1 %collective-permute-start.6 = (bf16[256,512]{1,0:T(8,128)(2,1)S(1)}, bf16[256,512]{1,0:T(8,128)(2,1)S(1)}, u32[]{:S(2)}, u32[]{:S(2)}) collective-permute-start(bf16[256,512]{1,0:T(8,128)(2,1)S(1)} %get-tuple-element.170), channel_id=1, source_target_pairs={{0,2},{1,3},{2,4},{3,5},{4,6},{5,7},{6,0},{7,1},{8,10},{9,11},{10,... | collective-permute-start | bytes 786440 | tf_op jit(solution)/shard_map/ppermute | solution.py:556
  31.1 9.5 %collective-permute-start.7 = (bf16[256,512]{1,0:T(8,128)(2,1)S(1)}, bf16[256,512]{1,0:T(8,128)(2,1)S(1)}, u32[]{:S(2)}, u32[]{:S(2)}) collective-permute-start(bf16[256,512]{1,0:T(8,128)(2,1)S(1)} %get-tuple-element.171), channel_id=1, source_target_pairs={{0,1},{1,0},{2,3},{3,2},{4,5},{5,4},{6,7},{7,6},{8,9},{9,8},{10,11... | collective-permute-start | bytes 786440 | tf_op jit(solution)/shard_map/ppermute | solution.py:556
  34.4 6.2 %copy-start.35 = (bf16[256,512]{1,0:T(8,128)(2,1)}, bf16[256,512]{1,0:T(8,128)(2,1)S(1)}, u32[]{:S(2)}) copy-start(bf16[256,512]{1,0:T(8,128)(2,1)S(1)} %collective-permute-done.9.refs_7_) | copy-start | bytes 786436
  35.0 11.0 %collective-permute-start.12 = (bf16[256,512]{1,0:T(8,128)(2,1)S(1)}, bf16[256,512]{1,0:T(8,128)(2,1)S(1)}, u32[]{:S(2)}, u32[]{:S(2)}) collective-permute-start(bf16[256,512]{1,0:T(8,128)(2,1)S(1)} %get-tuple-element.179), channel_id=1, source_target_pairs={{0,2},{1,3},{2,4},{3,5},{4,6},{5,7},{6,0},{7,1},{8,10},{9,11},{10,... | collective-permute-start | bytes 786440 | tf_op jit(solution)/shard_map/ppermute | solution.py:556
  36.1 10.0 %collective-permute-start.13 = (bf16[256,512]{1,0:T(8,128)(2,1)S(1)}, bf16[256,512]{1,0:T(8,128)(2,1)S(1)}, u32[]{:S(2)}, u32[]{:S(2)}) collective-permute-start(bf16[256,512]{1,0:T(8,128)(2,1)S(1)} %get-tuple-element.180), channel_id=1, source_target_pairs={{0,1},{1,0},{2,3},{3,2},{4,5},{5,4},{6,7},{7,6},{8,9},{9,8},{10,11... | collective-permute-start | bytes 786440 | tf_op jit(solution)/shard_map/ppermute | solution.py:556
  40.7 11.1 %collective-permute-start.10 = (bf16[256,512]{1,0:T(8,128)(2,1)S(1)}, bf16[256,512]{1,0:T(8,128)(2,1)S(1)}, u32[]{:S(2)}, u32[]{:S(2)}) collective-permute-start(bf16[256,512]{1,0:T(8,128)(2,1)S(1)} %get-tuple-element.184), channel_id=1, source_target_pairs={{0,2},{1,3},{2,4},{3,5},{4,6},{5,7},{6,0},{7,1},{8,10},{9,11},{10,... | collective-permute-start | bytes 786440 | tf_op jit(solution)/shard_map/ppermute | solution.py:556
  42.3 9.5 %collective-permute-start.11 = (bf16[256,512]{1,0:T(8,128)(2,1)S(1)}, bf16[256,512]{1,0:T(8,128)(2,1)S(1)}, u32[]{:S(2)}, u32[]{:S(2)}) collective-permute-start(bf16[256,512]{1,0:T(8,128)(2,1)S(1)} %get-tuple-element.185), channel_id=1, source_target_pairs={{0,1},{1,0},{2,3},{3,2},{4,5},{5,4},{6,7},{7,6},{8,9},{9,8},{10,11... | collective-permute-start | bytes 786440 | tf_op jit(solution)/shard_map/ppermute | solution.py:556
  46.0 5.8 %copy-start.32 = (bf16[256,512]{1,0:T(8,128)(2,1)}, bf16[256,512]{1,0:T(8,128)(2,1)S(1)}, u32[]{:S(2)}) copy-start(bf16[256,512]{1,0:T(8,128)(2,1)S(1)} %collective-permute-done.12.refs_2_) | copy-start | bytes 786436
  46.0 5.8 %copy-start.33 = (bf16[256,512]{1,0:T(8,128)(2,1)}, bf16[256,512]{1,0:T(8,128)(2,1)S(1)}, u32[]{:S(2)}) copy-start(bf16[256,512]{1,0:T(8,128)(2,1)S(1)} %collective-permute-done.13.refs_3_) | copy-start | bytes 786436
  46.1 11.3 %collective-permute-start.16 = (bf16[256,512]{1,0:T(8,128)(2,1)S(1)}, bf16[256,512]{1,0:T(8,128)(2,1)S(1)}, u32[]{:S(2)}, u32[]{:S(2)}) collective-permute-start(bf16[256,512]{1,0:T(8,128)(2,1)S(1)} %get-tuple-element.193), channel_id=1, source_target_pairs={{0,2},{1,3},{2,4},{3,5},{4,6},{5,7},{6,0},{7,1},{8,10},{9,11},{10,... | collective-permute-start | bytes 786440 | tf_op jit(solution)/shard_map/ppermute | solution.py:556
  47.3 10.1 %collective-permute-start.17 = (bf16[256,512]{1,0:T(8,128)(2,1)S(1)}, bf16[256,512]{1,0:T(8,128)(2,1)S(1)}, u32[]{:S(2)}, u32[]{:S(2)}) collective-permute-start(bf16[256,512]{1,0:T(8,128)(2,1)S(1)} %get-tuple-element.194), channel_id=1, source_target_pairs={{0,1},{1,0},{2,3},{3,2},{4,5},{5,4},{6,7},{7,6},{8,9},{9,8},{10,11... | collective-permute-start | bytes 786440 | tf_op jit(solution)/shard_map/ppermute | solution.py:556
  51.9 11.1 %collective-permute-start.14 = (bf16[256,512]{1,0:T(8,128)(2,1)S(1)}, bf16[256,512]{1,0:T(8,128)(2,1)S(1)}, u32[]{:S(2)}, u32[]{:S(2)}) collective-permute-start(bf16[256,512]{1,0:T(8,128)(2,1)S(1)} %get-tuple-element.198), channel_id=1, source_target_pairs={{0,2},{1,3},{2,4},{3,5},{4,6},{5,7},{6,0},{7,1},{8,10},{9,11},{10,... | collective-permute-start | bytes 786440 | tf_op jit(solution)/shard_map/ppermute | solution.py:556
  53.6 9.5 %collective-permute-start.15 = (bf16[256,512]{1,0:T(8,128)(2,1)S(1)}, bf16[256,512]{1,0:T(8,128)(2,1)S(1)}, u32[]{:S(2)}, u32[]{:S(2)}) collective-permute-start(bf16[256,512]{1,0:T(8,128)(2,1)S(1)} %get-tuple-element.199), channel_id=1, source_target_pairs={{0,1},{1,0},{2,3},{3,2},{4,5},{5,4},{6,7},{7,6},{8,9},{9,8},{10,11... | collective-permute-start | bytes 786440 | tf_op jit(solution)/shard_map/ppermute | solution.py:556
  57.5 11.1 %collective-permute-start.20 = (bf16[256,512]{1,0:T(8,128)(2,1)S(1)}, bf16[256,512]{1,0:T(8,128)(2,1)S(1)}, u32[]{:S(2)}, u32[]{:S(2)}) collective-permute-start(bf16[256,512]{1,0:T(8,128)(2,1)S(1)} %get-tuple-element.207), channel_id=1, source_target_pairs={{0,2},{1,3},{2,4},{3,5},{4,6},{5,7},{6,0},{7,1},{8,10},{9,11},{10,... | collective-permute-start | bytes 786440 | tf_op jit(solution)/shard_map/ppermute | solution.py:556
  58.5 10.1 %collective-permute-start.21 = (bf16[256,512]{1,0:T(8,128)(2,1)S(1)}, bf16[256,512]{1,0:T(8,128)(2,1)S(1)}, u32[]{:S(2)}, u32[]{:S(2)}) collective-permute-start(bf16[256,512]{1,0:T(8,128)(2,1)S(1)} %get-tuple-element.208), channel_id=1, source_target_pairs={{0,1},{1,0},{2,3},{3,2},{4,5},{5,4},{6,7},{7,6},{8,9},{9,8},{10,11... | collective-permute-start | bytes 786440 | tf_op jit(solution)/shard_map/ppermute | solution.py:556
  63.2 11.3 %collective-permute-start.18 = (bf16[256,512]{1,0:T(8,128)(2,1)S(1)}, bf16[256,512]{1,0:T(8,128)(2,1)S(1)}, u32[]{:S(2)}, u32[]{:S(2)}) collective-permute-start(bf16[256,512]{1,0:T(8,128)(2,1)S(1)} %get-tuple-element.212), channel_id=1, source_target_pairs={{0,2},{1,3},{2,4},{3,5},{4,6},{5,7},{6,0},{7,1},{8,10},{9,11},{10,... | collective-permute-start | bytes 786440 | tf_op jit(solution)/shard_map/ppermute | solution.py:556
  64.8 9.7 %collective-permute-start.19 = (bf16[256,512]{1,0:T(8,128)(2,1)S(1)}, bf16[256,512]{1,0:T(8,128)(2,1)S(1)}, u32[]{:S(2)}, u32[]{:S(2)}) collective-permute-start(bf16[256,512]{1,0:T(8,128)(2,1)S(1)} %get-tuple-element.213), channel_id=1, source_target_pairs={{0,1},{1,0},{2,3},{3,2},{4,5},{5,4},{6,7},{7,6},{8,9},{9,8},{10,11... | collective-permute-start | bytes 786440 | tf_op jit(solution)/shard_map/ppermute | solution.py:556
  68.6 5.8 %copy-start.20 = (bf16[256,512]{1,0:T(8,128)(2,1)}, bf16[256,512]{1,0:T(8,128)(2,1)S(1)}, u32[]{:S(2)}) copy-start(bf16[256,512]{1,0:T(8,128)(2,1)S(1)} %collective-permute-done.20.refs_8_.refs_10_) | copy-start | bytes 786436
  68.7 5.8 %copy-start.37 = (bf16[256,512]{1,0:T(8,128)(2,1)}, bf16[256,512]{1,0:T(8,128)(2,1)S(1)}, u32[]{:S(2)}) copy-start(bf16[256,512]{1,0:T(8,128)(2,1)S(1)} %collective-permute-done.21.refs_11_) | copy-start | bytes 786436
  68.7 11.3 %collective-permute-start.22 = (bf16[256,512]{1,0:T(8,128)(2,1)S(1)}, bf16[256,512]{1,0:T(8,128)(2,1)S(1)}, u32[]{:S(2)}, u32[]{:S(2)}) collective-permute-start(bf16[256,512]{1,0:T(8,128)(2,1)S(1)} %get-tuple-element.221), channel_id=1, source_target_pairs={{0,2},{1,3},{2,4},{3,5},{4,6},{5,7},{6,0},{7,1},{8,10},{9,11},{10,... | collective-permute-start | bytes 786440 | tf_op jit(solution)/shard_map/ppermute | solution.py:556
  70.0 10.1 %collective-permute-start.23 = (bf16[256,512]{1,0:T(8,128)(2,1)S(1)}, bf16[256,512]{1,0:T(8,128)(2,1)S(1)}, u32[]{:S(2)}, u32[]{:S(2)}) collective-permute-start(bf16[256,512]{1,0:T(8,128)(2,1)S(1)} %get-tuple-element.222), channel_id=1, source_target_pairs={{0,1},{1,0},{2,3},{3,2},{4,5},{5,4},{6,7},{7,6},{8,9},{9,8},{10,11... | collective-permute-start | bytes 786440 | tf_op jit(solution)/shard_map/ppermute | solution.py:556
  74.6 11.0 %collective-permute-start.24 = (bf16[256,512]{1,0:T(8,128)(2,1)S(1)}, bf16[256,512]{1,0:T(8,128)(2,1)S(1)}, u32[]{:S(2)}, u32[]{:S(2)}) collective-permute-start(bf16[256,512]{1,0:T(8,128)(2,1)S(1)} %get-tuple-element.226), channel_id=1, source_target_pairs={{0,2},{1,3},{2,4},{3,5},{4,6},{5,7},{6,0},{7,1},{8,10},{9,11},{10,... | collective-permute-start | bytes 786440 | tf_op jit(solution)/shard_map/ppermute | solution.py:556
  76.2 9.4 %collective-permute-start.25 = (bf16[256,512]{1,0:T(8,128)(2,1)S(1)}, bf16[256,512]{1,0:T(8,128)(2,1)S(1)}, u32[]{:S(2)}, u32[]{:S(2)}) collective-permute-start(bf16[256,512]{1,0:T(8,128)(2,1)S(1)} %get-tuple-element.227), channel_id=1, source_target_pairs={{0,1},{1,0},{2,3},{3,2},{4,5},{5,4},{6,7},{7,6},{8,9},{9,8},{10,11... | collective-permute-start | bytes 786440 | tf_op jit(solution)/shard_map/ppermute | solution.py:556
  80.1 11.1 %collective-permute-start.26 = (bf16[256,512]{1,0:T(8,128)(2,1)S(1)}, bf16[256,512]{1,0:T(8,128)(2,1)S(1)}, u32[]{:S(2)}, u32[]{:S(2)}) collective-permute-start(bf16[256,512]{1,0:T(8,128)(2,1)S(1)} %get-tuple-element.237), channel_id=1, source_target_pairs={{0,2},{1,3},{2,4},{3,5},{4,6},{5,7},{6,0},{7,1},{8,10},{9,11},{10,... | collective-permute-start | bytes 786440 | tf_op jit(solution)/shard_map/ppermute | solution.py:556
  81.0 10.2 %collective-permute-start.27 = (bf16[256,512]{1,0:T(8,128)(2,1)S(1)}, bf16[256,512]{1,0:T(8,128)(2,1)S(1)}, u32[]{:S(2)}, u32[]{:S(2)}) collective-permute-start(bf16[256,512]{1,0:T(8,128)(2,1)S(1)} %get-tuple-element.238), channel_id=1, source_target_pairs={{0,1},{1,0},{2,3},{3,2},{4,5},{5,4},{6,7},{7,6},{8,9},{9,8},{10,11... | collective-permute-start | bytes 786440 | tf_op jit(solution)/shard_map/ppermute | solution.py:556
  85.5 5.8 %copy-start = (bf16[256,512]{1,0:T(8,128)(2,1)}, bf16[256,512]{1,0:T(8,128)(2,1)S(1)}, u32[]{:S(2)}) copy-start(bf16[256,512]{1,0:T(8,128)(2,1)S(1)} %get-tuple-element.234.refs_11_) | copy-start | bytes 786436
  85.6 5.8 %copy-start.2 = (bf16[256,512]{1,0:T(8,128)(2,1)}, bf16[256,512]{1,0:T(8,128)(2,1)S(1)}, u32[]{:S(2)}) copy-start(bf16[256,512]{1,0:T(8,128)(2,1)S(1)} %get-tuple-element.241.refs_14_) | copy-start | bytes 786436
  85.7 8.1 %copy-start.9 = (s32[1,1,4]{2,1,0:T(1,128)S(1)}, s32[1,1,4]{2,1,0:T(1,128)}, u32[]{:S(2)}) copy-start(s32[1,1,4]{2,1,0:T(1,128)} %param.8) | copy-start | bytes 52
  85.7 12.1 %collective-permute-start.28 = (bf16[256,512]{1,0:T(8,128)(2,1)S(1)}, bf16[256,512]{1,0:T(8,128)(2,1)S(1)}, u32[]{:S(2)}, u32[]{:S(2)}) collective-permute-start(bf16[256,512]{1,0:T(8,128)(2,1)S(1)} %get-tuple-element.242), channel_id=1, source_target_pairs={{0,2},{1,3},{2,4},{3,5},{4,6},{5,7},{6,0},{7,1},{8,10},{9,11},{10,... | collective-permute-start | bytes 786440 | tf_op jit(solution)/shard_map/ppermute | solution.py:556
  87.4 10.5 %collective-permute-start.29 = (bf16[256,512]{1,0:T(8,128)(2,1)S(1)}, bf16[256,512]{1,0:T(8,128)(2,1)S(1)}, u32[]{:S(2)}, u32[]{:S(2)}) collective-permute-start(bf16[256,512]{1,0:T(8,128)(2,1)S(1)} %get-tuple-element.243), channel_id=1, source_target_pairs={{0,1},{1,0},{2,3},{3,2},{4,5},{5,4},{6,7},{7,6},{8,9},{9,8},{10,11... | collective-permute-start | bytes 786440 | tf_op jit(solution)/shard_map/ppermute | solution.py:556
  91.4 10.3 %collective-permute-start.30 = (bf16[256,512]{1,0:T(8,128)(2,1)S(1)}, bf16[256,512]{1,0:T(8,128)(2,1)S(1)}, u32[]{:S(2)}, u32[]{:S(2)}) collective-permute-start(bf16[256,512]{1,0:T(8,128)(2,1)S(1)} %get-tuple-element.247), channel_id=1, source_target_pairs={{0,2},{1,3},{2,4},{3,5},{4,6},{5,7},{6,0},{7,1},{8,10},{9,11},{10,... | collective-permute-start | bytes 786440 | tf_op jit(solution)/shard_map/ppermute | solution.py:556
  92.3 9.4 %collective-permute-start.31 = (bf16[256,512]{1,0:T(8,128)(2,1)S(1)}, bf16[256,512]{1,0:T(8,128)(2,1)S(1)}, u32[]{:S(2)}, u32[]{:S(2)}) collective-permute-start(bf16[256,512]{1,0:T(8,128)(2,1)S(1)} %get-tuple-element.248), channel_id=1, source_target_pairs={{0,1},{1,0},{2,3},{3,2},{4,5},{5,4},{6,7},{7,6},{8,9},{9,8},{10,11... | collective-permute-start | bytes 786440 | tf_op jit(solution)/shard_map/ppermute | solution.py:556
  98.7 11.3 %collective-permute-start.34 = (bf16[256,512]{1,0:T(8,128)(2,1)}, bf16[256,512]{1,0:T(8,128)(2,1)}, u32[]{:S(2)}, u32[]{:S(2)}) collective-permute-start(bf16[256,512]{1,0:T(8,128)(2,1)} %get-tuple-element.252), channel_id=1, source_target_pairs={{0,2},{1,3},{2,4},{3,5},{4,6},{5,7},{6,0},{7,1},{8,10},{9,11},{10,... | collective-permute-start | bytes 786440 | tf_op jit(solution)/shard_map/ppermute | solution.py:556
  100.3 9.7 %collective-permute-start.35 = (bf16[256,512]{1,0:T(8,128)(2,1)}, bf16[256,512]{1,0:T(8,128)(2,1)}, u32[]{:S(2)}, u32[]{:S(2)}) collective-permute-start(bf16[256,512]{1,0:T(8,128)(2,1)} %get-tuple-element.253), channel_id=1, source_target_pairs={{0,1},{1,0},{2,3},{3,2},{4,5},{5,4},{6,7},{7,6},{8,9},{9,8},{10,11... | collective-permute-start | bytes 786440 | tf_op jit(solution)/shard_map/ppermute | solution.py:556
  103.3 6.8 %copy-start.3 = (bf16[256,512]{1,0:T(8,128)(2,1)S(1)}, bf16[256,512]{1,0:T(8,128)(2,1)}, u32[]{:S(2)}) copy-start(bf16[256,512]{1,0:T(8,128)(2,1)} %copy-done.2) | copy-start | bytes 786436
  103.3 10.0 %collective-permute-start.32 = (bf16[256,512]{1,0:T(8,128)(2,1)}, bf16[256,512]{1,0:T(8,128)(2,1)S(1)}, u32[]{:S(2)}, u32[]{:S(2)}) collective-permute-start(bf16[256,512]{1,0:T(8,128)(2,1)} %get-tuple-element.257), channel_id=1, source_target_pairs={{0,2},{1,3},{2,4},{3,5},{4,6},{5,7},{6,0},{7,1},{8,10},{9,11},{10,... | collective-permute-start | bytes 786440 | tf_op jit(solution)/shard_map/ppermute | solution.py:556
  105.0 8.3 %collective-permute-start.33 = (bf16[256,512]{1,0:T(8,128)(2,1)}, bf16[256,512]{1,0:T(8,128)(2,1)S(1)}, u32[]{:S(2)}, u32[]{:S(2)}) collective-permute-start(bf16[256,512]{1,0:T(8,128)(2,1)} %get-tuple-element.258), channel_id=1, source_target_pairs={{0,1},{1,0},{2,3},{3,2},{4,5},{5,4},{6,7},{7,6},{8,9},{9,8},{10,11... | collective-permute-start | bytes 786440 | tf_op jit(solution)/shard_map/ppermute | solution.py:556
  106.5 34.5 %all-to-all-start = ((bf16[4,528,256]{2,1,0:T(8,128)(2,1)}), bf16[4,528,256]{2,1,0:T(8,128)(2,1)S(1)}, u32[]{:S(2)}, u32[]{:S(2)}) async-start(bf16[4,528,256]{2,1,0:T(8,128)(2,1)} %get-tuple-element.254), calls=%async_computation | async-start | bytes 2162688 | tf_op jit(solution)/shard_map/all_to_all | solution.py:527
  111.1 11.0 %collective-permute-start.38 = (bf16[256,512]{1,0:T(8,128)(2,1)S(1)}, bf16[256,512]{1,0:T(8,128)(2,1)S(1)}, u32[]{:S(2)}, u32[]{:S(2)}) collective-permute-start(bf16[256,512]{1,0:T(8,128)(2,1)S(1)} %get-tuple-element.261), channel_id=1, source_target_pairs={{0,2},{1,3},{2,4},{3,5},{4,6},{5,7},{6,0},{7,1},{8,10},{9,11},{10,... | collective-permute-start | bytes 786440 | tf_op jit(solution)/shard_map/ppermute | solution.py:556
  112.8 9.3 %collective-permute-start.39 = (bf16[256,512]{1,0:T(8,128)(2,1)S(1)}, bf16[256,512]{1,0:T(8,128)(2,1)S(1)}, u32[]{:S(2)}, u32[]{:S(2)}) collective-permute-start(bf16[256,512]{1,0:T(8,128)(2,1)S(1)} %get-tuple-element.262), channel_id=1, source_target_pairs={{0,1},{1,0},{2,3},{3,2},{4,5},{5,4},{6,7},{7,6},{8,9},{9,8},{10,11... | collective-permute-start | bytes 786440 | tf_op jit(solution)/shard_map/ppermute | solution.py:556
  113.3 6.7 %copy-start.40 = (bf16[256,512]{1,0:T(8,128)(2,1)}, bf16[256,512]{1,0:T(8,128)(2,1)S(1)}, u32[]{:S(2)}) copy-start(bf16[256,512]{1,0:T(8,128)(2,1)S(1)} %collective-permute-done.32.refs_10_) | copy-start | bytes 786436
  113.3 6.7 %copy-start.41 = (bf16[256,512]{1,0:T(8,128)(2,1)}, bf16[256,512]{1,0:T(8,128)(2,1)S(1)}, u32[]{:S(2)}) copy-start(bf16[256,512]{1,0:T(8,128)(2,1)S(1)} %collective-permute-done.33.refs_11_) | copy-start | bytes 786436
  113.3 13.9 %collective-permute-start.36 = (bf16[256,512]{1,0:T(8,128)(2,1)S(1)}, bf16[256,512]{1,0:T(8,128)(2,1)S(1)}, u32[]{:S(2)}, u32[]{:S(2)}) collective-permute-start(bf16[256,512]{1,0:T(8,128)(2,1)S(1)} %get-tuple-element.265), channel_id=1, source_target_pairs={{0,2},{1,3},{2,4},{3,5},{4,6},{5,7},{6,0},{7,1},{8,10},{9,11},{10,... | collective-permute-start | bytes 786440 | tf_op jit(solution)/shard_map/ppermute | solution.py:556
  114.1 13.1 %collective-permute-start.37 = (bf16[256,512]{1,0:T(8,128)(2,1)S(1)}, bf16[256,512]{1,0:T(8,128)(2,1)S(1)}, u32[]{:S(2)}, u32[]{:S(2)}) collective-permute-start(bf16[256,512]{1,0:T(8,128)(2,1)S(1)} %get-tuple-element.266), channel_id=1, source_target_pairs={{0,1},{1,0},{2,3},{3,2},{4,5},{5,4},{6,7},{7,6},{8,9},{9,8},{10,11... | collective-permute-start | bytes 786440 | tf_op jit(solution)/shard_map/ppermute | solution.py:556
  122.1 20.8 %copy-start.42 = (bf16[256,512]{1,0:T(8,128)(2,1)}, bf16[256,512]{1,0:T(8,128)(2,1)S(1)}, u32[]{:S(2)}) copy-start(bf16[256,512]{1,0:T(8,128)(2,1)S(1)} %collective-permute-done.38.refs_12_) | copy-start | bytes 786436
  122.1 20.8 %copy-start.43 = (bf16[256,512]{1,0:T(8,128)(2,1)}, bf16[256,512]{1,0:T(8,128)(2,1)S(1)}, u32[]{:S(2)}) copy-start(bf16[256,512]{1,0:T(8,128)(2,1)S(1)} %collective-permute-done.39.refs_13_) | copy-start | bytes 786436
  127.3 15.7 %copy-start.46 = (bf16[256,512]{1,0:T(8,128)(2,1)}, bf16[256,512]{1,0:T(8,128)(2,1)S(1)}, u32[]{:S(2)}) copy-start(bf16[256,512]{1,0:T(8,128)(2,1)S(1)} %collective-permute-done.36.refs_14_) | copy-start | bytes 786436
  127.3 10.0 %copy-start.47 = (bf16[256,512]{1,0:T(8,128)(2,1)}, bf16[256,512]{1,0:T(8,128)(2,1)S(1)}, u32[]{:S(2)}) copy-start(bf16[256,512]{1,0:T(8,128)(2,1)S(1)} %collective-permute-done.37.refs_15_) | copy-start | bytes 786436
  127.3 9.3 %collective-permute-start.40 = (bf16[256,512]{1,0:T(8,128)(2,1)S(1)}, bf16[256,512]{1,0:T(8,128)(2,1)S(1)}, u32[]{:S(2)}, u32[]{:S(2)}) collective-permute-start(bf16[256,512]{1,0:T(8,128)(2,1)S(1)} %broadcast_select_fusion), channel_id=1, source_target_pairs={{0,1},{1,0},{2,3},{3,2},{4,5},{5,4},{6,7},{7,6},{8,9},{9,8},{10,11... | collective-permute-start | bytes 786440 | tf_op jit(solution)/shard_map/ppermute | solution.py:556
  127.9 9.4 %collective-permute-start.41 = (bf16[256,512]{1,0:T(8,128)(2,1)S(1)}, bf16[256,512]{1,0:T(8,128)(2,1)S(1)}, u32[]{:S(2)}, u32[]{:S(2)}) collective-permute-start(bf16[256,512]{1,0:T(8,128)(2,1)S(1)} %get-tuple-element.270), channel_id=1, source_target_pairs={{0,2},{1,3},{2,4},{3,5},{4,6},{5,7},{6,0},{7,1},{8,10},{9,11},{10,... | collective-permute-start | bytes 786440 | tf_op jit(solution)/shard_map/ppermute | solution.py:556
  127.9 13.1 %collective-permute-start.42 = (bf16[256,512]{1,0:T(8,128)(2,1)S(1)}, bf16[256,512]{1,0:T(8,128)(2,1)}, u32[]{:S(2)}, u32[]{:S(2)}) collective-permute-start(bf16[256,512]{1,0:T(8,128)(2,1)S(1)} %get-tuple-element.271), channel_id=1, source_target_pairs={{0,1},{1,0},{2,3},{3,2},{4,5},{5,4},{6,7},{7,6},{8,9},{9,8},{10,11... | collective-permute-start | bytes 786440 | tf_op jit(solution)/shard_map/ppermute | solution.py:556
  136.6 6.3 %copy-start.48 = (bf16[256,512]{1,0:T(8,128)(2,1)}, bf16[256,512]{1,0:T(8,128)(2,1)S(1)}, u32[]{:S(2)}) copy-start(bf16[256,512]{1,0:T(8,128)(2,1)S(1)} %collective-permute-done.40.refs_2_) | copy-start | bytes 786436
  142.9 30.1 %all-to-all-start.1 = ((bf16[8,272,256]{2,1,0:T(8,128)(2,1)}), bf16[8,272,256]{2,1,0:T(8,128)(2,1)S(1)}, u32[]{:S(2)}, u32[]{:S(2)}) async-start(bf16[8,272,256]{2,1,0:T(8,128)(2,1)} %relay.1), calls=%async_computation.1 | async-start | bytes 2228224 | tf_op jit(solution)/shard_map/all_to_all | solution.py:527
  (31 other events, 153.6 us)

commit v10 on v9

--- a/solution.py
+++ b/solution.py
@@ -530,15 +530,14 @@
         digits = arrived[:, 2 * TILE, :4].astype(jnp.int32).reshape(n_front, 2, 2)
         return relay(digits[..., 0] * 32 + digits[..., 1], arrived, slots_dev, n_grp)
 
-    held, turn, result, done = [], (), None, 0
-
-    def step(count, *waits):
-        nonlocal result, done
-        numbers = [n for n in range(2 * done, 2 * (done + count)) if any(line[n] for line in table)]
-        done += count
-        here = after((me,), *waits)[0] if waits else me
+    held, turn, result = [], (), None
+
+    def step(begin, end, *waits):
+        nonlocal result
+        numbers = [n for n in range(2 * begin, 2 * end) if any(line[n] for line in table)]
+        here = after((me,), *waits)[0]
         blocks = [held[n // 2][n % 2] for n in numbers]
-        result = update(rows, mask, here, own, front, numbers, blocks, 2 * count, base=result)
+        result = update(rows, mask, here, own, front, numbers, blocks, 2 * (end - begin), base=result)
 
     for e in range(events):
         values = []
@@ -564,12 +563,14 @@
         if late == 1:
             arrived = exchange(after((sends,), *turn)[0], "front")
         if late == 4:
-            step(4, *turn)
+            step(0, 4, *turn)
             turn = (*turn, result)
-    passed = relayed(after((arrived,), *held[-1], *held[-2])[0])
+    passed = relayed(after((arrived,), *turn, *held[-3])[0])
     arrived = exchange(passed, "grp")
-    while done < events:
-        step(min(8, events - done), passed)
+    last = events - 6
+    step(last, events, passed)
+    for begin in range(4, last, 8):
+        step(begin, min(begin + 8, last), passed)
     slots_here = after((arrived,), result)[0]
     parent_tiles = sum_parents(slots_here[:, TILE, 0].astype(jnp.int32), slots_here, slots_dev)
     return (result[None], parent_tiles)

time: 176 us -> 191 us (1.085)
  waiting for transfers between devices: 46.2 us -> 54.4 us
  local copies, waits for them, and re-layouts: 2.44 us -> 4.61 us
    ppermute x43, waiting for transfers between devices: 42.2 us -> 54.4 us  [shards(): lax.ppermute(turn[s], 'grp', perms[s])]
    all_to_all x2, waiting for transfers between devices: 4.01 us -> 0.01 us  [exchange(): return lax.all_to_all(blocks, axis, split_axis=0, concat_axis=0, tiled=True)]
    unnamed x100 -> x102, local copies, waits for them, and re-layouts: 1.48 us -> 3.66 us
  transfers between devices with their start and end apart: 45 -> 45, of which waited for: 18 -> 16; matrix products, arithmetic and copies ran while one was open for 2% -> 2% of each run, Pallas kernels for 30% -> 28%
where the time goes in v10:
time: 191 us; the launch traced here: 188 us
  starting transfers between devices  63.7 us (33%)
  Pallas kernels  59.1 us (31%)
  waiting for transfers between devices  54.4 us (28%)
  other arithmetic  4.76 us (2%)
  local copies, waits for them, and re-layouts  4.61 us (2%)
    ppermute x43, starting transfers between devices, shards(): lax.ppermute(turn[s], 'grp', perms[s])  56.6 us
    ppermute x43, waiting for transfers between devices, shards(): lax.ppermute(turn[s], 'grp', perms[s])  54.4 us
    pallas_call x4, Pallas kernels, update(): pl.pallas_call(functools.partial(update_kernel, tuple(numbers), room, wid...  26.9 us
    pallas_call x8, Pallas kernels, factor(): pl.pallas_call(functools.partial(factor_kernel, tuple(tiles), head), out_...  24.7 us
    all_to_all x2, starting transfers between devices, exchange(): return lax.all_to_all(blocks, axis, split_axis=0, concat_axis=0, tiled=True)  7.09 us
    pallas_call x1, Pallas kernels, own_panels(): pl.pallas_call(functools.partial(own_kernel, choices, len(blocks), width...  3.97 us
  transfers between devices with their start and end apart: 45, of which 16 were waited for; matrix products, arithmetic and copies ran while one was open for 2% of the time, Pallas kernels for 28%

profile of v10, /device:TPU:0, one launch (start us, length us, event | category | flops | bytes accessed | tf_op | source)
XLA Modules:
  0.0 188.1 jit_solution(272791722995595344)
XLA Ops:
  1.4 3.8 %factor.8 = (bf16[256,512]{1,0:T(8,128)(2,1)S(1)}, bf16[256,512]{1,0:T(8,128)(2,1)S(1)}, bf16[256,512]{1,0:T(8,128)(2,1)S(1)}, bf16[256,512]{1,0:T(8,128)(2,1)S(...) custom-call(s32[32,4]{1,0:T(8,128)S(1)} %copy.54.mask, bf16[8192,1024]{1,0:T(8,128)(2,1)} %bitcast.9, ...), custom_call_target="tpu_custom_call" | custom-call | flops 805306368 | bytes 2097152 | tf_op jit(solution)/shard_map/factor/pallas_call | solution.py:178
  5.2 3.1 %collective-permute-start = (bf16[256,512]{1,0:T(8,128)(2,1)S(1)}, bf16[256,512]{1,0:T(8,128)(2,1)S(1)}, u32[]{:S(2)}, u32[]{:S(2)}) collective-permute-start(bf16[256,512]{1,0:T(8,128)(2,1)S(1)} %get-tuple-element.146.refs_18_), channel_id=1, source_target_pairs={{0,2},{1,3},{2,4},{3,5},{4,6},{5,7},{6,0},{7,1},{8,10},{9,11},{10,... | collective-permute-start | bytes 786440 | tf_op jit(solution)/shard_map/ppermute | solution.py:555
  8.3 1.5 collective-permute-start.1
  9.8 1.6 collective-permute-start.4
  11.9 3.0 %factor.9 = (bf16[256,512]{1,0:T(8,128)(2,1)S(1)}, bf16[256,512]{1,0:T(8,128)(2,1)S(1)}, bf16[256,512]{1,0:T(8,128)(2,1)S(1)}, bf16[256,512]{1,0:T(8,128)(2,1)S(1)}) custom-call(s32[32,4]{1,0:T(8,128)S(1)} %copy.54.mask, bf16[8192,1024]{1,0:T(8,128)(2,1)} %bitcast.10, bf16[4,256,256]{2,1,0:T(8,128)(2,1)S(1)} %get-tuple-element.228.refs_0_, ...), custom_call_target="tpu_custom_call" | custom-call | flops 805306368 | bytes 2097152 | tf_op jit(solution)/shard_map/factor/pallas_call | solution.py:178
  14.9 2.6 %collective-permute-done.refs_19_.refs_0_ = bf16[256,512]{1,0:T(8,128)(2,1)S(1)} collective-permute-done((bf16[256,512]{1,0:T(8,128)(2,1)S(1)}, bf16[256,512]{1,0:T(8,128)(2,1)S(1)}, u32[]{:S(2)}, u32[]{:S(2)}) %collective-permute-start) | collective-permute-done | bytes 262176 | tf_op jit(solution)/shard_map/ppermute | solution.py:555
  17.6 1.6 collective-permute-start.2
  19.2 1.5 collective-permute-start.3
  20.7 2.3 %collective-permute-done.4.refs_2_ = bf16[256,512]{1,0:T(8,128)(2,1)S(1)} collective-permute-done((bf16[256,512]{1,0:T(8,128)(2,1)S(1)}, bf16[256,512]{1,0:T(8,128)(2,1)S(1)}, u32[]{:S(2)}, u32[]{:S(2)}) %collective-permute-start.4) | collective-permute-done | bytes 262176 | tf_op jit(solution)/shard_map/ppermute | solution.py:555
  23.2 1.6 collective-permute-start.8
  24.8 1.5 collective-permute-start.9
  26.3 3.0 %factor.10 = (bf16[256,512]{1,0:T(8,128)(2,1)S(1)}, bf16[256,512]{1,0:T(8,128)(2,1)S(1)}, bf16[256,512]{1,0:T(8,128)(2,1)S(1)}, bf16[256,512]{1,0:T(8,128)(2,1)S(1)}) custom-call(s32[32,4]{1,0:T(8,128)S(1)} %copy.54.mask, bf16[8192,1024]{1,0:T(8,128)(2,1)} %bitcast.11, bf16[4,256,256]{2,1,0:T(8,128)(2,1)S(1)} %get-tuple-element.228.refs_0_, ...), custom_call_target="tpu_custom_call" | custom-call | flops 805306368 | bytes 2097152 | tf_op jit(solution)/shard_map/factor/pallas_call | solution.py:178
  29.5 1.6 collective-permute-start.6
  32.0 2.3 %collective-permute-done.8.refs_6_ = bf16[256,512]{1,0:T(8,128)(2,1)S(1)} collective-permute-done((bf16[256,512]{1,0:T(8,128)(2,1)S(1)}, bf16[256,512]{1,0:T(8,128)(2,1)S(1)}, u32[]{:S(2)}, u32[]{:S(2)}) %collective-permute-start.8) | collective-permute-done | bytes 262176 | tf_op jit(solution)/shard_map/ppermute | solution.py:555
  35.0 1.1 collective-permute-start.12
  36.1 1.5 collective-permute-start.13
  37.6 3.0 %factor.11 = (bf16[256,512]{1,0:T(8,128)(2,1)S(1)}, bf16[256,512]{1,0:T(8,128)(2,1)S(1)}, bf16[256,512]{1,0:T(8,128)(2,1)S(1)}, bf16[256,512]{1,0:T(8,128)(2,1)S(1)}) custom-call(s32[32,4]{1,0:T(8,128)S(1)} %copy.54.mask, bf16[8192,1024]{1,0:T(8,128)(2,1)} %bitcast.12, bf16[4,256,256]{2,1,0:T(8,128)(2,1)S(1)} %get-tuple-element.228.refs_0_, ...), custom_call_target="tpu_custom_call" | custom-call | flops 805306368 | bytes 2097152 | tf_op jit(solution)/shard_map/factor/pallas_call | solution.py:178
  40.7 1.6 collective-permute-start.10
  43.2 2.9 %collective-permute-done.12.refs_2_ = bf16[256,512]{1,0:T(8,128)(2,1)S(1)} collective-permute-done((bf16[256,512]{1,0:T(8,128)(2,1)S(1)}, bf16[256,512]{1,0:T(8,128)(2,1)S(1)}, u32[]{:S(2)}, u32[]{:S(2)}) %collective-permute-start.12) | collective-permute-done | bytes 262176 | tf_op jit(solution)/shard_map/ppermute | solution.py:555
  46.1 1.2 collective-permute-start.16
  47.3 1.5 collective-permute-start.17
  48.8 3.0 %factor.12 = (bf16[256,512]{1,0:T(8,128)(2,1)S(1)}, bf16[256,512]{1,0:T(8,128)(2,1)S(1)}, bf16[256,512]{1,0:T(8,128)(2,1)S(1)}, bf16[256,512]{1,0:T(8,128)(2,1)S(1)}) custom-call(s32[32,4]{1,0:T(8,128)S(1)} %copy.54.mask, bf16[8192,1024]{1,0:T(8,128)(2,1)} %bitcast.13, bf16[4,256,256]{2,1,0:T(8,128)(2,1)S(1)} %get-tuple-element.228.refs_0_, ...), custom_call_target="tpu_custom_call" | custom-call | flops 805306368 | bytes 2097152 | tf_op jit(solution)/shard_map/factor/pallas_call | solution.py:178
  51.9 1.6 collective-permute-start.14
  54.4 3.0 %collective-permute-done.16.refs_9_.refs_6_ = bf16[256,512]{1,0:T(8,128)(2,1)S(1)} collective-permute-done((bf16[256,512]{1,0:T(8,128)(2,1)S(1)}, bf16[256,512]{1,0:T(8,128)(2,1)S(1)}, u32[]{:S(2)}, u32[]{:S(2)}) %collective-permute-start.16) | collective-permute-done | bytes 262176 | tf_op jit(solution)/shard_map/ppermute | solution.py:555
  57.5 1.0 collective-permute-start.20
  58.5 1.5 collective-permute-start.21
  60.0 3.0 %factor.13 = (bf16[256,512]{1,0:T(8,128)(2,1)S(1)}, bf16[256,512]{1,0:T(8,128)(2,1)S(1)}, bf16[256,512]{1,0:T(8,128)(2,1)S(1)}, bf16[256,512]{1,0:T(8,128)(2,1)S(1)}) custom-call(s32[32,4]{1,0:T(8,128)S(1)} %copy.54.mask, bf16[8192,1024]{1,0:T(8,128)(2,1)} %bitcast.14, bf16[4,256,256]{2,1,0:T(8,128)(2,1)S(1)} %get-tuple-element.228.refs_0_, ...), custom_call_target="tpu_custom_call" | custom-call | flops 805306368 | bytes 2097152 | tf_op jit(solution)/shard_map/factor/pallas_call | solution.py:178
  63.2 1.6 collective-permute-start.18
  65.6 3.0 %collective-permute-done.20.refs_8_.refs_10_ = bf16[256,512]{1,0:T(8,128)(2,1)S(1)} collective-permute-done((bf16[256,512]{1,0:T(8,128)(2,1)S(1)}, bf16[256,512]{1,0:T(8,128)(2,1)S(1)}, u32[]{:S(2)}, u32[]{:S(2)}) %collective-permute-start.20) | collective-permute-done | bytes 262176 | tf_op jit(solution)/shard_map/ppermute | solution.py:555
  68.7 1.2 collective-permute-start.22
  70.0 1.5 collective-permute-start.23
  71.5 3.0 %factor.14 = (bf16[256,512]{1,0:T(8,128)(2,1)S(1)}, bf16[256,512]{1,0:T(8,128)(2,1)S(1)}, bf16[256,512]{1,0:T(8,128)(2,1)S(1)}, bf16[256,512]{1,0:T(8,128)(2,1)S(1)}) custom-call(s32[32,4]{1,0:T(8,128)S(1)} %copy.54.mask, bf16[8192,1024]{1,0:T(8,128)(2,1)} %bitcast.15, bf16[4,256,256]{2,1,0:T(8,128)(2,1)S(1)} %get-tuple-element.228.refs_0_, ...), custom_call_target="tpu_custom_call" | custom-call | flops 805306368 | bytes 2097152 | tf_op jit(solution)/shard_map/factor/pallas_call | solution.py:178
  74.6 1.6 collective-permute-start.24
  76.9 3.1 %collective-permute-done.22.refs_7_.refs_14_ = bf16[256,512]{1,0:T(8,128)(2,1)S(1)} collective-permute-done((bf16[256,512]{1,0:T(8,128)(2,1)S(1)}, bf16[256,512]{1,0:T(8,128)(2,1)S(1)}, u32[]{:S(2)}, u32[]{:S(2)}) %collective-permute-start.22) | collective-permute-done | bytes 262176 | tf_op jit(solution)/shard_map/ppermute | solution.py:555
  80.1 0.9 collective-permute-start.26
  81.0 1.5 collective-permute-start.27
  82.5 3.0 %factor.15 = (bf16[256,512]{1,0:T(8,128)(2,1)S(1)}, bf16[256,512]{1,0:T(8,128)(2,1)S(1)}, bf16[256,512]{1,0:T(8,128)(2,1)S(1)}, bf16[256,512]{1,0:T(8,128)(2,1)S(1)}) custom-call(s32[32,4]{1,0:T(8,128)S(1)} %copy.54.mask, bf16[8192,1024]{1,0:T(8,128)(2,1)} %bitcast.16, bf16[4,256,256]{2,1,0:T(8,128)(2,1)S(1)} %get-tuple-element.228.refs_0_, ...), custom_call_target="tpu_custom_call" | custom-call | flops 805306368 | bytes 2097152 | tf_op jit(solution)/shard_map/factor/pallas_call | solution.py:178
  85.7 1.6 collective-permute-start.28
  88.2 3.1 %collective-permute-done.26.refs_16_.refs_2_ = bf16[256,512]{1,0:T(8,128)(2,1)S(1)} collective-permute-done((bf16[256,512]{1,0:T(8,128)(2,1)S(1)}, bf16[256,512]{1,0:T(8,128)(2,1)S(1)}, u32[]{:S(2)}, u32[]{:S(2)}) %collective-permute-start.26) | collective-permute-done | bytes 262176 | tf_op jit(solution)/shard_map/ppermute | solution.py:555
  91.4 0.9 collective-permute-start.30
  92.3 1.5 collective-permute-start.31
  93.8 4.0 %own_panels.1 = (bf16[512,1024]{1,0:T(8,128)(2,1)S(1)}, bf16[4,528,256]{2,1,0:T(8,128)(2,1)}) custom-call(s32[32,4]{1,0:T(8,128)S(1)} %copy.54.mask, s32[4]{0:T(128)S(1)} %bitcast.8, s32[1]{0:T(128)} %bitcast.1.me, bf16[8192,1024]{1,0:T(8,128)(2,1)} %bitcast.17, bf16[256,512]{1,0:T(8,128)(2,1)} %copy-done.7, bf16[256,512]{1,0:T(8,128)(2,1)} %copy-done.22, ...), custom_call_target="tpu_custom_call" | custom-call | flops 268435456 | bytes 2621440 | tf_op jit(solution)/shard_map/own_panels/pallas_call | solution.py:238
  97.9 0.9 select_select_fusion.2
  98.7 1.6 collective-permute-start.34
  102.4 0.9 select_select_fusion.1
  103.3 1.7 collective-permute-start.32
  105.0 1.5 collective-permute-start.33
  106.5 3.5 %all-to-all-start = ((bf16[4,528,256]{2,1,0:T(8,128)(2,1)}), bf16[4,528,256]{2,1,0:T(8,128)(2,1)S(1)}, u32[]{:S(2)}, u32[]{:S(2)}) async-start(bf16[4,528,256]{2,1,0:T(8,128)(2,1)} %get-tuple-element.254), calls=%async_computation | async-start | bytes 2162688 | tf_op jit(solution)/shard_map/all_to_all | solution.py:527
  110.1 1.1 select_select_fusion
  111.1 1.6 collective-permute-start.38
  114.1 1.5 collective-permute-start.37
  115.6 4.4 %update.4.refs_11_ = bf16[8192,1024]{1,0:T(8,128)(2,1)} custom-call(s32[8,44]{1,0:T(8,128)S(1)} %copy-done.8, s32[32,4]{1,0:T(8,128)S(1)} %copy.54.mask, s32[1]{0:T(128)} %bitcast.1.me, bf16[512,1024]{1,0:T(8,128)(2,1)S(1)} %get-tuple-element.251.own, bf16[8192,1024]{1,0:T(8,128)(2,1)} %bitcast.18, bf16[256,512]{1,0:T(8,128)(2,1)} %copy-done.12, ...), custom_call_target="tpu_custom_call" | custom-call | flops 2147483648 | bytes 8388608 | tf_op jit(solution)/shard_map/update/pallas_call | solution.py:403
  120.0 2.1 %collective-permute-done.38.refs_4_ = bf16[256,512]{1,0:T(8,128)(2,1)S(1)} collective-permute-done((bf16[256,512]{1,0:T(8,128)(2,1)S(1)}, bf16[256,512]{1,0:T(8,128)(2,1)S(1)}, u32[]{:S(2)}, u32[]{:S(2)}) %collective-permute-start.38) | collective-permute-done | bytes 262176 | tf_op jit(solution)/shard_map/ppermute | solution.py:555
  122.1 5.1 %collective-permute-done.36.refs_6_ = bf16[256,512]{1,0:T(8,128)(2,1)S(1)} collective-permute-done((bf16[256,512]{1,0:T(8,128)(2,1)S(1)}, bf16[256,512]{1,0:T(8,128)(2,1)S(1)}, u32[]{:S(2)}, u32[]{:S(2)}) %collective-permute-start.36) | collective-permute-done | bytes 262176 | tf_op jit(solution)/shard_map/ppermute | solution.py:555
  129.0 1.9 relay.1
  130.9 3.6 %all-to-all-start.1 = ((bf16[8,272,256]{2,1,0:T(8,128)(2,1)}), bf16[8,272,256]{2,1,0:T(8,128)(2,1)S(1)}, u32[]{:S(2)}, u32[]{:S(2)}) async-start(bf16[8,272,256]{2,1,0:T(8,128)(2,1)} %relay.1), calls=%async_computation.1 | async-start | bytes 2228224 | tf_op jit(solution)/shard_map/all_to_all | solution.py:527
  134.4 1.9 %collective-permute-start.42 = (bf16[256,512]{1,0:T(8,128)(2,1)}, bf16[256,512]{1,0:T(8,128)(2,1)S(1)}, u32[]{:S(2)}, u32[]{:S(2)}) collective-permute-start(bf16[256,512]{1,0:T(8,128)(2,1)} %broadcast_select_fusion), channel_id=1, source_target_pairs={{0,1},{1,0},{2,3},{3,2},{4,5},{5,4},{6,7},{7,6},{8,9},{9,8},{10,11... | collective-permute-start | bytes 786440 | tf_op jit(solution)/shard_map/ppermute | solution.py:555
  136.4 1.5 collective-permute-start.40
  138.4 17.2 %collective-permute-done.42.refs_10_ = bf16[256,512]{1,0:T(8,128)(2,1)S(1)} collective-permute-done((bf16[256,512]{1,0:T(8,128)(2,1)}, bf16[256,512]{1,0:T(8,128)(2,1)S(1)}, u32[]{:S(2)}, u32[]{:S(2)}) %collective-permute-start.42) | collective-permute-done | bytes 262176 | tf_op jit(solution)/shard_map/ppermute | solution.py:555
  155.6 6.5 %collective-permute-done.40.refs_8_ = bf16[256,512]{1,0:T(8,128)(2,1)S(1)} collective-permute-done((bf16[256,512]{1,0:T(8,128)(2,1)S(1)}, bf16[256,512]{1,0:T(8,128)(2,1)S(1)}, u32[]{:S(2)}, u32[]{:S(2)}) %collective-permute-start.40) | collective-permute-done | bytes 262176 | tf_op jit(solution)/shard_map/ppermute | solution.py:555
  163.6 6.5 %update.5.refs_16_ = bf16[8192,1024]{1,0:T(8,128)(2,1)} custom-call(s32[8,44]{1,0:T(8,128)S(1)} %copy-done.8, s32[32,4]{1,0:T(8,128)S(1)} %copy.54.mask, s32[1]{0:T(128)} %bitcast.1.me, bf16[512,1024]{1,0:T(8,128)(2,1)S(1)} %get-tuple-element.251.own, bf16[8192,1024]{1,0:T(8,128)(2,1)} %bitcast.19, ...), custom_call_target="tpu_custom_call", output_to_operand_aliasing={{}: (16, {})} | custom-call | flops 3221225472 | bytes 12582912 | tf_op jit(solution)/shard_map/update/pallas_call | solution.py:403
  170.0 9.4 %update.6.refs_8_ = bf16[8192,1024]{1,0:T(8,128)(2,1)} custom-call(s32[8,44]{1,0:T(8,128)S(1)} %copy-done.8, s32[32,4]{1,0:T(8,128)S(1)} %copy.54.mask, s32[1]{0:T(128)} %bitcast.1.me, bf16[512,1024]{1,0:T(8,128)(2,1)S(1)} %get-tuple-element.251.own, bf16[8192,1024]{1,0:T(8,128)(2,1)} %bitcast.20, ...), custom_call_target="tpu_custom_call", output_to_operand_aliasing={{}: (21, {})} | custom-call | flops 4294967296 | bytes 16777216 | tf_op jit(solution)/shard_map/update/pallas_call | solution.py:403
  179.4 6.6 %update.7 = bf16[8192,1024]{1,0:T(8,128)(2,1)} custom-call(s32[8,44]{1,0:T(8,128)S(1)} %copy-done.8, s32[32,4]{1,0:T(8,128)S(1)} %copy.54.mask, s32[1]{0:T(128)} %bitcast.1.me, bf16[512,1024]{1,0:T(8,128)(2,1)S(1)} %get-tuple-element.251.own, bf16[8192,1024]{1,0:T(8,128)(2,1)} %bitcast.21, ...), custom_call_target="tpu_custom_call", output_to_operand_aliasing={{}: (13, {})} | custom-call | flops 2147483648 | bytes 8388608 | tf_op jit(solution)/shard_map/update/pallas_call | solution.py:403
  186.3 1.7 sum_parents.1
  (169 shorter events, 15.4 us)
Async XLA Ops:
  5.2 9.7 %copy-start.6 = (bf16[256,512]{1,0:T(8,128)(2,1)}, bf16[256,512]{1,0:T(8,128)(2,1)S(1)}, u32[]{:S(2)}) copy-start(bf16[256,512]{1,0:T(8,128)(2,1)S(1)} %get-tuple-element.146.refs_18_) | copy-start | bytes 786436
  5.2 12.2 %collective-permute-start = (bf16[256,512]{1,0:T(8,128)(2,1)S(1)}, bf16[256,512]{1,0:T(8,128)(2,1)S(1)}, u32[]{:S(2)}, u32[]{:S(2)}) collective-permute-start(bf16[256,512]{1,0:T(8,128)(2,1)S(1)} %get-tuple-element.146.refs_18_), channel_id=1, source_target_pairs={{0,2},{1,3},{2,4},{3,5},{4,6},{5,7},{6,0},{7,1},{8,10},{9,11},{10,... | collective-permute-start | bytes 786440 | tf_op jit(solution)/shard_map/ppermute | solution.py:555
  8.3 9.2 %collective-permute-start.1 = (bf16[256,512]{1,0:T(8,128)(2,1)S(1)}, bf16[256,512]{1,0:T(8,128)(2,1)S(1)}, u32[]{:S(2)}, u32[]{:S(2)}) collective-permute-start(bf16[256,512]{1,0:T(8,128)(2,1)S(1)} %get-tuple-element.147), channel_id=1, source_target_pairs={{0,1},{1,0},{2,3},{3,2},{4,5},{5,4},{6,7},{7,6},{8,9},{9,8},{10,11... | collective-permute-start | bytes 786440 | tf_op jit(solution)/shard_map/ppermute | solution.py:555
  9.8 13.3 %collective-permute-start.4 = (bf16[256,512]{1,0:T(8,128)(2,1)S(1)}, bf16[256,512]{1,0:T(8,128)(2,1)S(1)}, u32[]{:S(2)}, u32[]{:S(2)}) collective-permute-start(bf16[256,512]{1,0:T(8,128)(2,1)S(1)} %get-tuple-element.148), channel_id=1, source_target_pairs={{0,2},{1,3},{2,4},{3,5},{4,6},{5,7},{6,0},{7,1},{8,10},{9,11},{10,... | collective-permute-start | bytes 786440 | tf_op jit(solution)/shard_map/ppermute | solution.py:555
  11.4 11.8 %collective-permute-start.5 = (bf16[256,512]{1,0:T(8,128)(2,1)S(1)}, bf16[256,512]{1,0:T(8,128)(2,1)S(1)}, u32[]{:S(2)}, u32[]{:S(2)}) collective-permute-start(bf16[256,512]{1,0:T(8,128)(2,1)S(1)} %get-tuple-element.149), channel_id=1, source_target_pairs={{0,1},{1,0},{2,3},{3,2},{4,5},{5,4},{6,7},{7,6},{8,9},{9,8},{10,11... | collective-permute-start | bytes 786440 | tf_op jit(solution)/shard_map/ppermute | solution.py:555
  17.6 11.8 %collective-permute-start.2 = (bf16[256,512]{1,0:T(8,128)(2,1)S(1)}, bf16[256,512]{1,0:T(8,128)(2,1)S(1)}, u32[]{:S(2)}, u32[]{:S(2)}) collective-permute-start(bf16[256,512]{1,0:T(8,128)(2,1)S(1)} %get-tuple-element.156), channel_id=1, source_target_pairs={{0,2},{1,3},{2,4},{3,5},{4,6},{5,7},{6,0},{7,1},{8,10},{9,11},{10,... | collective-permute-start | bytes 786440 | tf_op jit(solution)/shard_map/ppermute | solution.py:555
  19.2 10.2 %collective-permute-start.3 = (bf16[256,512]{1,0:T(8,128)(2,1)S(1)}, bf16[256,512]{1,0:T(8,128)(2,1)S(1)}, u32[]{:S(2)}, u32[]{:S(2)}) collective-permute-start(bf16[256,512]{1,0:T(8,128)(2,1)S(1)} %get-tuple-element.157), channel_id=1, source_target_pairs={{0,1},{1,0},{2,3},{3,2},{4,5},{5,4},{6,7},{7,6},{8,9},{9,8},{10,11... | collective-permute-start | bytes 786440 | tf_op jit(solution)/shard_map/ppermute | solution.py:555
  23.0 6.3 %copy-start.30 = (bf16[256,512]{1,0:T(8,128)(2,1)}, bf16[256,512]{1,0:T(8,128)(2,1)S(1)}, u32[]{:S(2)}) copy-start(bf16[256,512]{1,0:T(8,128)(2,1)S(1)} %collective-permute-done.4.refs_2_) | copy-start | bytes 786436
  23.1 6.2 %copy-start.31 = (bf16[256,512]{1,0:T(8,128)(2,1)}, bf16[256,512]{1,0:T(8,128)(2,1)S(1)}, u32[]{:S(2)}) copy-start(bf16[256,512]{1,0:T(8,128)(2,1)S(1)} %collective-permute-done.5.refs_3_) | copy-start | bytes 786436
  23.2 11.1 %collective-permute-start.8 = (bf16[256,512]{1,0:T(8,128)(2,1)S(1)}, bf16[256,512]{1,0:T(8,128)(2,1)S(1)}, u32[]{:S(2)}, u32[]{:S(2)}) collective-permute-start(bf16[256,512]{1,0:T(8,128)(2,1)S(1)} %get-tuple-element.165), channel_id=1, source_target_pairs={{0,2},{1,3},{2,4},{3,5},{4,6},{5,7},{6,0},{7,1},{8,10},{9,11},{10,... | collective-permute-start | bytes 786440 | tf_op jit(solution)/shard_map/ppermute | solution.py:555
  24.8 9.5 %collective-permute-start.9 = (bf16[256,512]{1,0:T(8,128)(2,1)S(1)}, bf16[256,512]{1,0:T(8,128)(2,1)S(1)}, u32[]{:S(2)}, u32[]{:S(2)}) collective-permute-start(bf16[256,512]{1,0:T(8,128)(2,1)S(1)} %get-tuple-element.166), channel_id=1, source_target_pairs={{0,1},{1,0},{2,3},{3,2},{4,5},{5,4},{6,7},{7,6},{8,9},{9,8},{10,11... | collective-permute-start | bytes 786440 | tf_op jit(solution)/shard_map/ppermute | solution.py:555
  29.5 11.1 %collective-permute-start.6 = (bf16[256,512]{1,0:T(8,128)(2,1)S(1)}, bf16[256,512]{1,0:T(8,128)(2,1)S(1)}, u32[]{:S(2)}, u32[]{:S(2)}) collective-permute-start(bf16[256,512]{1,0:T(8,128)(2,1)S(1)} %get-tuple-element.170), channel_id=1, source_target_pairs={{0,2},{1,3},{2,4},{3,5},{4,6},{5,7},{6,0},{7,1},{8,10},{9,11},{10,... | collective-permute-start | bytes 786440 | tf_op jit(solution)/shard_map/ppermute | solution.py:555
  31.1 9.5 %collective-permute-start.7 = (bf16[256,512]{1,0:T(8,128)(2,1)S(1)}, bf16[256,512]{1,0:T(8,128)(2,1)S(1)}, u32[]{:S(2)}, u32[]{:S(2)}) collective-permute-start(bf16[256,512]{1,0:T(8,128)(2,1)S(1)} %get-tuple-element.171), channel_id=1, source_target_pairs={{0,1},{1,0},{2,3},{3,2},{4,5},{5,4},{6,7},{7,6},{8,9},{9,8},{10,11... | collective-permute-start | bytes 786440 | tf_op jit(solution)/shard_map/ppermute | solution.py:555
  34.4 6.2 %copy-start.35 = (bf16[256,512]{1,0:T(8,128)(2,1)}, bf16[256,512]{1,0:T(8,128)(2,1)S(1)}, u32[]{:S(2)}) copy-start(bf16[256,512]{1,0:T(8,128)(2,1)S(1)} %collective-permute-done.9.refs_7_) | copy-start | bytes 786436
  35.0 11.0 %collective-permute-start.12 = (bf16[256,512]{1,0:T(8,128)(2,1)S(1)}, bf16[256,512]{1,0:T(8,128)(2,1)S(1)}, u32[]{:S(2)}, u32[]{:S(2)}) collective-permute-start(bf16[256,512]{1,0:T(8,128)(2,1)S(1)} %get-tuple-element.179), channel_id=1, source_target_pairs={{0,2},{1,3},{2,4},{3,5},{4,6},{5,7},{6,0},{7,1},{8,10},{9,11},{10,... | collective-permute-start | bytes 786440 | tf_op jit(solution)/shard_map/ppermute | solution.py:555
  36.1 10.0 %collective-permute-start.13 = (bf16[256,512]{1,0:T(8,128)(2,1)S(1)}, bf16[256,512]{1,0:T(8,128)(2,1)S(1)}, u32[]{:S(2)}, u32[]{:S(2)}) collective-permute-start(bf16[256,512]{1,0:T(8,128)(2,1)S(1)} %get-tuple-element.180), channel_id=1, source_target_pairs={{0,1},{1,0},{2,3},{3,2},{4,5},{5,4},{6,7},{7,6},{8,9},{9,8},{10,11... | collective-permute-start | bytes 786440 | tf_op jit(solution)/shard_map/ppermute | solution.py:555
  40.7 11.1 %collective-permute-start.10 = (bf16[256,512]{1,0:T(8,128)(2,1)S(1)}, bf16[256,512]{1,0:T(8,128)(2,1)S(1)}, u32[]{:S(2)}, u32[]{:S(2)}) collective-permute-start(bf16[256,512]{1,0:T(8,128)(2,1)S(1)} %get-tuple-element.184), channel_id=1, source_target_pairs={{0,2},{1,3},{2,4},{3,5},{4,6},{5,7},{6,0},{7,1},{8,10},{9,11},{10,... | collective-permute-start | bytes 786440 | tf_op jit(solution)/shard_map/ppermute | solution.py:555
  42.3 9.5 %collective-permute-start.11 = (bf16[256,512]{1,0:T(8,128)(2,1)S(1)}, bf16[256,512]{1,0:T(8,128)(2,1)S(1)}, u32[]{:S(2)}, u32[]{:S(2)}) collective-permute-start(bf16[256,512]{1,0:T(8,128)(2,1)S(1)} %get-tuple-element.185), channel_id=1, source_target_pairs={{0,1},{1,0},{2,3},{3,2},{4,5},{5,4},{6,7},{7,6},{8,9},{9,8},{10,11... | collective-permute-start | bytes 786440 | tf_op jit(solution)/shard_map/ppermute | solution.py:555
  46.0 5.8 %copy-start.32 = (bf16[256,512]{1,0:T(8,128)(2,1)}, bf16[256,512]{1,0:T(8,128)(2,1)S(1)}, u32[]{:S(2)}) copy-start(bf16[256,512]{1,0:T(8,128)(2,1)S(1)} %collective-permute-done.12.refs_2_) | copy-start | bytes 786436
  46.0 5.8 %copy-start.33 = (bf16[256,512]{1,0:T(8,128)(2,1)}, bf16[256,512]{1,0:T(8,128)(2,1)S(1)}, u32[]{:S(2)}) copy-start(bf16[256,512]{1,0:T(8,128)(2,1)S(1)} %collective-permute-done.13.refs_3_) | copy-start | bytes 786436
  46.1 11.3 %collective-permute-start.16 = (bf16[256,512]{1,0:T(8,128)(2,1)S(1)}, bf16[256,512]{1,0:T(8,128)(2,1)S(1)}, u32[]{:S(2)}, u32[]{:S(2)}) collective-permute-start(bf16[256,512]{1,0:T(8,128)(2,1)S(1)} %get-tuple-element.193), channel_id=1, source_target_pairs={{0,2},{1,3},{2,4},{3,5},{4,6},{5,7},{6,0},{7,1},{8,10},{9,11},{10,... | collective-permute-start | bytes 786440 | tf_op jit(solution)/shard_map/ppermute | solution.py:555
  47.3 10.1 %collective-permute-start.17 = (bf16[256,512]{1,0:T(8,128)(2,1)S(1)}, bf16[256,512]{1,0:T(8,128)(2,1)S(1)}, u32[]{:S(2)}, u32[]{:S(2)}) collective-permute-start(bf16[256,512]{1,0:T(8,128)(2,1)S(1)} %get-tuple-element.194), channel_id=1, source_target_pairs={{0,1},{1,0},{2,3},{3,2},{4,5},{5,4},{6,7},{7,6},{8,9},{9,8},{10,11... | collective-permute-start | bytes 786440 | tf_op jit(solution)/shard_map/ppermute | solution.py:555
  51.9 11.1 %collective-permute-start.14 = (bf16[256,512]{1,0:T(8,128)(2,1)S(1)}, bf16[256,512]{1,0:T(8,128)(2,1)S(1)}, u32[]{:S(2)}, u32[]{:S(2)}) collective-permute-start(bf16[256,512]{1,0:T(8,128)(2,1)S(1)} %get-tuple-element.198), channel_id=1, source_target_pairs={{0,2},{1,3},{2,4},{3,5},{4,6},{5,7},{6,0},{7,1},{8,10},{9,11},{10,... | collective-permute-start | bytes 786440 | tf_op jit(solution)/shard_map/ppermute | solution.py:555
  53.6 9.5 %collective-permute-start.15 = (bf16[256,512]{1,0:T(8,128)(2,1)S(1)}, bf16[256,512]{1,0:T(8,128)(2,1)S(1)}, u32[]{:S(2)}, u32[]{:S(2)}) collective-permute-start(bf16[256,512]{1,0:T(8,128)(2,1)S(1)} %get-tuple-element.199), channel_id=1, source_target_pairs={{0,1},{1,0},{2,3},{3,2},{4,5},{5,4},{6,7},{7,6},{8,9},{9,8},{10,11... | collective-permute-start | bytes 786440 | tf_op jit(solution)/shard_map/ppermute | solution.py:555
  57.5 11.1 %collective-permute-start.20 = (bf16[256,512]{1,0:T(8,128)(2,1)S(1)}, bf16[256,512]{1,0:T(8,128)(2,1)S(1)}, u32[]{:S(2)}, u32[]{:S(2)}) collective-permute-start(bf16[256,512]{1,0:T(8,128)(2,1)S(1)} %get-tuple-element.207), channel_id=1, source_target_pairs={{0,2},{1,3},{2,4},{3,5},{4,6},{5,7},{6,0},{7,1},{8,10},{9,11},{10,... | collective-permute-start | bytes 786440 | tf_op jit(solution)/shard_map/ppermute | solution.py:555
  58.5 10.1 %collective-permute-start.21 = (bf16[256,512]{1,0:T(8,128)(2,1)S(1)}, bf16[256,512]{1,0:T(8,128)(2,1)S(1)}, u32[]{:S(2)}, u32[]{:S(2)}) collective-permute-start(bf16[256,512]{1,0:T(8,128)(2,1)S(1)} %get-tuple-element.208), channel_id=1, source_target_pairs={{0,1},{1,0},{2,3},{3,2},{4,5},{5,4},{6,7},{7,6},{8,9},{9,8},{10,11... | collective-permute-start | bytes 786440 | tf_op jit(solution)/shard_map/ppermute | solution.py:555
  63.2 11.3 %collective-permute-start.18 = (bf16[256,512]{1,0:T(8,128)(2,1)S(1)}, bf16[256,512]{1,0:T(8,128)(2,1)S(1)}, u32[]{:S(2)}, u32[]{:S(2)}) collective-permute-start(bf16[256,512]{1,0:T(8,128)(2,1)S(1)} %get-tuple-element.212), channel_id=1, source_target_pairs={{0,2},{1,3},{2,4},{3,5},{4,6},{5,7},{6,0},{7,1},{8,10},{9,11},{10,... | collective-permute-start | bytes 786440 | tf_op jit(solution)/shard_map/ppermute | solution.py:555
  64.8 9.7 %collective-permute-start.19 = (bf16[256,512]{1,0:T(8,128)(2,1)S(1)}, bf16[256,512]{1,0:T(8,128)(2,1)S(1)}, u32[]{:S(2)}, u32[]{:S(2)}) collective-permute-start(bf16[256,512]{1,0:T(8,128)(2,1)S(1)} %get-tuple-element.213), channel_id=1, source_target_pairs={{0,1},{1,0},{2,3},{3,2},{4,5},{5,4},{6,7},{7,6},{8,9},{9,8},{10,11... | collective-permute-start | bytes 786440 | tf_op jit(solution)/shard_map/ppermute | solution.py:555
  68.6 5.8 %copy-start.20 = (bf16[256,512]{1,0:T(8,128)(2,1)}, bf16[256,512]{1,0:T(8,128)(2,1)S(1)}, u32[]{:S(2)}) copy-start(bf16[256,512]{1,0:T(8,128)(2,1)S(1)} %collective-permute-done.20.refs_8_.refs_10_) | copy-start | bytes 786436
  68.7 5.8 %copy-start.37 = (bf16[256,512]{1,0:T(8,128)(2,1)}, bf16[256,512]{1,0:T(8,128)(2,1)S(1)}, u32[]{:S(2)}) copy-start(bf16[256,512]{1,0:T(8,128)(2,1)S(1)} %collective-permute-done.21.refs_11_) | copy-start | bytes 786436
  68.7 11.3 %collective-permute-start.22 = (bf16[256,512]{1,0:T(8,128)(2,1)S(1)}, bf16[256,512]{1,0:T(8,128)(2,1)S(1)}, u32[]{:S(2)}, u32[]{:S(2)}) collective-permute-start(bf16[256,512]{1,0:T(8,128)(2,1)S(1)} %get-tuple-element.221), channel_id=1, source_target_pairs={{0,2},{1,3},{2,4},{3,5},{4,6},{5,7},{6,0},{7,1},{8,10},{9,11},{10,... | collective-permute-start | bytes 786440 | tf_op jit(solution)/shard_map/ppermute | solution.py:555
  70.0 10.1 %collective-permute-start.23 = (bf16[256,512]{1,0:T(8,128)(2,1)S(1)}, bf16[256,512]{1,0:T(8,128)(2,1)S(1)}, u32[]{:S(2)}, u32[]{:S(2)}) collective-permute-start(bf16[256,512]{1,0:T(8,128)(2,1)S(1)} %get-tuple-element.222), channel_id=1, source_target_pairs={{0,1},{1,0},{2,3},{3,2},{4,5},{5,4},{6,7},{7,6},{8,9},{9,8},{10,11... | collective-permute-start | bytes 786440 | tf_op jit(solution)/shard_map/ppermute | solution.py:555
  74.6 11.0 %collective-permute-start.24 = (bf16[256,512]{1,0:T(8,128)(2,1)S(1)}, bf16[256,512]{1,0:T(8,128)(2,1)S(1)}, u32[]{:S(2)}, u32[]{:S(2)}) collective-permute-start(bf16[256,512]{1,0:T(8,128)(2,1)S(1)} %get-tuple-element.226), channel_id=1, source_target_pairs={{0,2},{1,3},{2,4},{3,5},{4,6},{5,7},{6,0},{7,1},{8,10},{9,11},{10,... | collective-permute-start | bytes 786440 | tf_op jit(solution)/shard_map/ppermute | solution.py:555
  76.2 9.4 %collective-permute-start.25 = (bf16[256,512]{1,0:T(8,128)(2,1)S(1)}, bf16[256,512]{1,0:T(8,128)(2,1)S(1)}, u32[]{:S(2)}, u32[]{:S(2)}) collective-permute-start(bf16[256,512]{1,0:T(8,128)(2,1)S(1)} %get-tuple-element.227), channel_id=1, source_target_pairs={{0,1},{1,0},{2,3},{3,2},{4,5},{5,4},{6,7},{7,6},{8,9},{9,8},{10,11... | collective-permute-start | bytes 786440 | tf_op jit(solution)/shard_map/ppermute | solution.py:555
  80.1 11.1 %collective-permute-start.26 = (bf16[256,512]{1,0:T(8,128)(2,1)S(1)}, bf16[256,512]{1,0:T(8,128)(2,1)S(1)}, u32[]{:S(2)}, u32[]{:S(2)}) collective-permute-start(bf16[256,512]{1,0:T(8,128)(2,1)S(1)} %get-tuple-element.237), channel_id=1, source_target_pairs={{0,2},{1,3},{2,4},{3,5},{4,6},{5,7},{6,0},{7,1},{8,10},{9,11},{10,... | collective-permute-start | bytes 786440 | tf_op jit(solution)/shard_map/ppermute | solution.py:555
  81.0 10.2 %collective-permute-start.27 = (bf16[256,512]{1,0:T(8,128)(2,1)S(1)}, bf16[256,512]{1,0:T(8,128)(2,1)S(1)}, u32[]{:S(2)}, u32[]{:S(2)}) collective-permute-start(bf16[256,512]{1,0:T(8,128)(2,1)S(1)} %get-tuple-element.238), channel_id=1, source_target_pairs={{0,1},{1,0},{2,3},{3,2},{4,5},{5,4},{6,7},{7,6},{8,9},{9,8},{10,11... | collective-permute-start | bytes 786440 | tf_op jit(solution)/shard_map/ppermute | solution.py:555
  85.5 5.8 %copy-start = (bf16[256,512]{1,0:T(8,128)(2,1)}, bf16[256,512]{1,0:T(8,128)(2,1)S(1)}, u32[]{:S(2)}) copy-start(bf16[256,512]{1,0:T(8,128)(2,1)S(1)} %get-tuple-element.234.refs_11_) | copy-start | bytes 786436
  85.6 5.8 %copy-start.2 = (bf16[256,512]{1,0:T(8,128)(2,1)}, bf16[256,512]{1,0:T(8,128)(2,1)S(1)}, u32[]{:S(2)}) copy-start(bf16[256,512]{1,0:T(8,128)(2,1)S(1)} %get-tuple-element.241.refs_14_) | copy-start | bytes 786436
  85.6 5.8 %copy-start.4 = (bf16[256,512]{1,0:T(8,128)(2,1)}, bf16[256,512]{1,0:T(8,128)(2,1)S(1)}, u32[]{:S(2)}) copy-start(bf16[256,512]{1,0:T(8,128)(2,1)S(1)} %get-tuple-element.231.refs_5_) | copy-start | bytes 786436
  85.6 5.8 %copy-start.7 = (bf16[256,512]{1,0:T(8,128)(2,1)}, bf16[256,512]{1,0:T(8,128)(2,1)S(1)}, u32[]{:S(2)}) copy-start(bf16[256,512]{1,0:T(8,128)(2,1)S(1)} %get-tuple-element.230.refs_0_) | copy-start | bytes 786436
  85.7 8.1 %copy-start.9 = (s32[1,1,4]{2,1,0:T(1,128)S(1)}, s32[1,1,4]{2,1,0:T(1,128)}, u32[]{:S(2)}) copy-start(s32[1,1,4]{2,1,0:T(1,128)} %param.8) | copy-start | bytes 52
  85.7 12.1 %collective-permute-start.28 = (bf16[256,512]{1,0:T(8,128)(2,1)S(1)}, bf16[256,512]{1,0:T(8,128)(2,1)S(1)}, u32[]{:S(2)}, u32[]{:S(2)}) collective-permute-start(bf16[256,512]{1,0:T(8,128)(2,1)S(1)} %get-tuple-element.242), channel_id=1, source_target_pairs={{0,2},{1,3},{2,4},{3,5},{4,6},{5,7},{6,0},{7,1},{8,10},{9,11},{10,... | collective-permute-start | bytes 786440 | tf_op jit(solution)/shard_map/ppermute | solution.py:555
  87.4 10.5 %collective-permute-start.29 = (bf16[256,512]{1,0:T(8,128)(2,1)S(1)}, bf16[256,512]{1,0:T(8,128)(2,1)S(1)}, u32[]{:S(2)}, u32[]{:S(2)}) collective-permute-start(bf16[256,512]{1,0:T(8,128)(2,1)S(1)} %get-tuple-element.243), channel_id=1, source_target_pairs={{0,1},{1,0},{2,3},{3,2},{4,5},{5,4},{6,7},{7,6},{8,9},{9,8},{10,11... | collective-permute-start | bytes 786440 | tf_op jit(solution)/shard_map/ppermute | solution.py:555
  91.4 10.3 %collective-permute-start.30 = (bf16[256,512]{1,0:T(8,128)(2,1)S(1)}, bf16[256,512]{1,0:T(8,128)(2,1)S(1)}, u32[]{:S(2)}, u32[]{:S(2)}) collective-permute-start(bf16[256,512]{1,0:T(8,128)(2,1)S(1)} %get-tuple-element.247), channel_id=1, source_target_pairs={{0,2},{1,3},{2,4},{3,5},{4,6},{5,7},{6,0},{7,1},{8,10},{9,11},{10,... | collective-permute-start | bytes 786440 | tf_op jit(solution)/shard_map/ppermute | solution.py:555
  92.3 9.4 %collective-permute-start.31 = (bf16[256,512]{1,0:T(8,128)(2,1)S(1)}, bf16[256,512]{1,0:T(8,128)(2,1)S(1)}, u32[]{:S(2)}, u32[]{:S(2)}) collective-permute-start(bf16[256,512]{1,0:T(8,128)(2,1)S(1)} %get-tuple-element.248), channel_id=1, source_target_pairs={{0,1},{1,0},{2,3},{3,2},{4,5},{5,4},{6,7},{7,6},{8,9},{9,8},{10,11... | collective-permute-start | bytes 786440 | tf_op jit(solution)/shard_map/ppermute | solution.py:555
  98.7 11.3 %collective-permute-start.34 = (bf16[256,512]{1,0:T(8,128)(2,1)}, bf16[256,512]{1,0:T(8,128)(2,1)}, u32[]{:S(2)}, u32[]{:S(2)}) collective-permute-start(bf16[256,512]{1,0:T(8,128)(2,1)} %get-tuple-element.252), channel_id=1, source_target_pairs={{0,2},{1,3},{2,4},{3,5},{4,6},{5,7},{6,0},{7,1},{8,10},{9,11},{10,... | collective-permute-start | bytes 786440 | tf_op jit(solution)/shard_map/ppermute | solution.py:555
  100.3 9.7 %collective-permute-start.35 = (bf16[256,512]{1,0:T(8,128)(2,1)}, bf16[256,512]{1,0:T(8,128)(2,1)}, u32[]{:S(2)}, u32[]{:S(2)}) collective-permute-start(bf16[256,512]{1,0:T(8,128)(2,1)} %get-tuple-element.253), channel_id=1, source_target_pairs={{0,1},{1,0},{2,3},{3,2},{4,5},{5,4},{6,7},{7,6},{8,9},{9,8},{10,11... | collective-permute-start | bytes 786440 | tf_op jit(solution)/shard_map/ppermute | solution.py:555
  103.3 6.7 %copy-start.3 = (bf16[256,512]{1,0:T(8,128)(2,1)S(1)}, bf16[256,512]{1,0:T(8,128)(2,1)}, u32[]{:S(2)}) copy-start(bf16[256,512]{1,0:T(8,128)(2,1)} %copy-done.2) | copy-start | bytes 786436
  103.3 10.0 %collective-permute-start.32 = (bf16[256,512]{1,0:T(8,128)(2,1)}, bf16[256,512]{1,0:T(8,128)(2,1)S(1)}, u32[]{:S(2)}, u32[]{:S(2)}) collective-permute-start(bf16[256,512]{1,0:T(8,128)(2,1)} %get-tuple-element.257), channel_id=1, source_target_pairs={{0,2},{1,3},{2,4},{3,5},{4,6},{5,7},{6,0},{7,1},{8,10},{9,11},{10,... | collective-permute-start | bytes 786440 | tf_op jit(solution)/shard_map/ppermute | solution.py:555
  105.0 8.3 %collective-permute-start.33 = (bf16[256,512]{1,0:T(8,128)(2,1)}, bf16[256,512]{1,0:T(8,128)(2,1)S(1)}, u32[]{:S(2)}, u32[]{:S(2)}) collective-permute-start(bf16[256,512]{1,0:T(8,128)(2,1)} %get-tuple-element.258), channel_id=1, source_target_pairs={{0,1},{1,0},{2,3},{3,2},{4,5},{5,4},{6,7},{7,6},{8,9},{9,8},{10,11... | collective-permute-start | bytes 786440 | tf_op jit(solution)/shard_map/ppermute | solution.py:555
  106.5 22.3 %all-to-all-start = ((bf16[4,528,256]{2,1,0:T(8,128)(2,1)}), bf16[4,528,256]{2,1,0:T(8,128)(2,1)S(1)}, u32[]{:S(2)}, u32[]{:S(2)}) async-start(bf16[4,528,256]{2,1,0:T(8,128)(2,1)} %get-tuple-element.254), calls=%async_computation | async-start | bytes 2162688 | tf_op jit(solution)/shard_map/all_to_all | solution.py:527
  111.1 11.0 %collective-permute-start.38 = (bf16[256,512]{1,0:T(8,128)(2,1)S(1)}, bf16[256,512]{1,0:T(8,128)(2,1)S(1)}, u32[]{:S(2)}, u32[]{:S(2)}) collective-permute-start(bf16[256,512]{1,0:T(8,128)(2,1)S(1)} %get-tuple-element.261), channel_id=1, source_target_pairs={{0,2},{1,3},{2,4},{3,5},{4,6},{5,7},{6,0},{7,1},{8,10},{9,11},{10,... | collective-permute-start | bytes 786440 | tf_op jit(solution)/shard_map/ppermute | solution.py:555
  112.8 9.3 %collective-permute-start.39 = (bf16[256,512]{1,0:T(8,128)(2,1)S(1)}, bf16[256,512]{1,0:T(8,128)(2,1)S(1)}, u32[]{:S(2)}, u32[]{:S(2)}) collective-permute-start(bf16[256,512]{1,0:T(8,128)(2,1)S(1)} %get-tuple-element.262), channel_id=1, source_target_pairs={{0,1},{1,0},{2,3},{3,2},{4,5},{5,4},{6,7},{7,6},{8,9},{9,8},{10,11... | collective-permute-start | bytes 786440 | tf_op jit(solution)/shard_map/ppermute | solution.py:555
  113.3 6.7 %copy-start.40 = (bf16[256,512]{1,0:T(8,128)(2,1)}, bf16[256,512]{1,0:T(8,128)(2,1)S(1)}, u32[]{:S(2)}) copy-start(bf16[256,512]{1,0:T(8,128)(2,1)S(1)} %collective-permute-done.32.refs_2_) | copy-start | bytes 786436
  113.3 6.7 %copy-start.41 = (bf16[256,512]{1,0:T(8,128)(2,1)}, bf16[256,512]{1,0:T(8,128)(2,1)S(1)}, u32[]{:S(2)}) copy-start(bf16[256,512]{1,0:T(8,128)(2,1)S(1)} %collective-permute-done.33.refs_3_) | copy-start | bytes 786436
  113.3 13.9 %collective-permute-start.36 = (bf16[256,512]{1,0:T(8,128)(2,1)S(1)}, bf16[256,512]{1,0:T(8,128)(2,1)S(1)}, u32[]{:S(2)}, u32[]{:S(2)}) collective-permute-start(bf16[256,512]{1,0:T(8,128)(2,1)S(1)} %get-tuple-element.265), channel_id=1, source_target_pairs={{0,2},{1,3},{2,4},{3,5},{4,6},{5,7},{6,0},{7,1},{8,10},{9,11},{10,... | collective-permute-start | bytes 786440 | tf_op jit(solution)/shard_map/ppermute | solution.py:555
  114.1 13.2 %collective-permute-start.37 = (bf16[256,512]{1,0:T(8,128)(2,1)S(1)}, bf16[256,512]{1,0:T(8,128)(2,1)S(1)}, u32[]{:S(2)}, u32[]{:S(2)}) collective-permute-start(bf16[256,512]{1,0:T(8,128)(2,1)S(1)} %get-tuple-element.266), channel_id=1, source_target_pairs={{0,1},{1,0},{2,3},{3,2},{4,5},{5,4},{6,7},{7,6},{8,9},{9,8},{10,11... | collective-permute-start | bytes 786440 | tf_op jit(solution)/shard_map/ppermute | solution.py:555
  122.1 8.8 %copy-start.42 = (bf16[256,512]{1,0:T(8,128)(2,1)}, bf16[256,512]{1,0:T(8,128)(2,1)S(1)}, u32[]{:S(2)}) copy-start(bf16[256,512]{1,0:T(8,128)(2,1)S(1)} %collective-permute-done.38.refs_4_) | copy-start | bytes 786436
  122.1 8.8 %copy-start.43 = (bf16[256,512]{1,0:T(8,128)(2,1)}, bf16[256,512]{1,0:T(8,128)(2,1)S(1)}, u32[]{:S(2)}) copy-start(bf16[256,512]{1,0:T(8,128)(2,1)S(1)} %collective-permute-done.39.refs_5_) | copy-start | bytes 786436
  130.9 55.2 %all-to-all-start.1 = ((bf16[8,272,256]{2,1,0:T(8,128)(2,1)}), bf16[8,272,256]{2,1,0:T(8,128)(2,1)S(1)}, u32[]{:S(2)}, u32[]{:S(2)}) async-start(bf16[8,272,256]{2,1,0:T(8,128)(2,1)} %relay.1), calls=%async_computation.1 | async-start | bytes 2228224 | tf_op jit(solution)/shard_map/all_to_all | solution.py:527
  134.4 21.1 %collective-permute-start.42 = (bf16[256,512]{1,0:T(8,128)(2,1)}, bf16[256,512]{1,0:T(8,128)(2,1)S(1)}, u32[]{:S(2)}, u32[]{:S(2)}) collective-permute-start(bf16[256,512]{1,0:T(8,128)(2,1)} %broadcast_select_fusion), channel_id=1, source_target_pairs={{0,1},{1,0},{2,3},{3,2},{4,5},{5,4},{6,7},{7,6},{8,9},{9,8},{10,11... | collective-permute-start | bytes 786440 | tf_op jit(solution)/shard_map/ppermute | solution.py:555
  136.4 25.8 %collective-permute-start.40 = (bf16[256,512]{1,0:T(8,128)(2,1)S(1)}, bf16[256,512]{1,0:T(8,128)(2,1)S(1)}, u32[]{:S(2)}, u32[]{:S(2)}) collective-permute-start(bf16[256,512]{1,0:T(8,128)(2,1)S(1)} %get-tuple-element.270), channel_id=1, source_target_pairs={{0,2},{1,3},{2,4},{3,5},{4,6},{5,7},{6,0},{7,1},{8,10},{9,11},{10,... | collective-permute-start | bytes 786440 | tf_op jit(solution)/shard_map/ppermute | solution.py:555
  137.8 24.3 %collective-permute-start.41 = (bf16[256,512]{1,0:T(8,128)(2,1)S(1)}, bf16[256,512]{1,0:T(8,128)(2,1)S(1)}, u32[]{:S(2)}, u32[]{:S(2)}) collective-permute-start(bf16[256,512]{1,0:T(8,128)(2,1)S(1)} %get-tuple-element.271), channel_id=1, source_target_pairs={{0,1},{1,0},{2,3},{3,2},{4,5},{5,4},{6,7},{7,6},{8,9},{9,8},{10,11... | collective-permute-start | bytes 786440 | tf_op jit(solution)/shard_map/ppermute | solution.py:555
  155.6 6.6 %copy-start.48 = (bf16[256,512]{1,0:T(8,128)(2,1)}, bf16[256,512]{1,0:T(8,128)(2,1)S(1)}, u32[]{:S(2)}) copy-start(bf16[256,512]{1,0:T(8,128)(2,1)S(1)} %collective-permute-done.42.refs_10_) | copy-start | bytes 786436
  (32 other events, 142.3 us)

commit v11 on v9

--- a/solution.py
+++ b/solution.py
@@ -566,7 +566,7 @@
         if late == 4:
             step(4, *turn)
             turn = (*turn, result)
-    passed = relayed(after((arrived,), *held[-1], *held[-2])[0])
+    passed = relayed(after((arrived,), *turn, *held[-2])[0])
     arrived = exchange(passed, "grp")
     while done < events:
         step(min(8, events - done), passed)

time: 176 us -> 168 us (0.955)
  waiting for transfers between devices: 46.2 us -> 36.5 us
    ppermute x43, waiting for transfers between devices: 42.2 us -> 34.3 us  [shards(): lax.ppermute(turn[s], 'grp', perms[s])]
    all_to_all x2, waiting for transfers between devices: 4.01 us -> 2.2 us  [exchange(): return lax.all_to_all(blocks, axis, split_axis=0, concat_axis=0, tiled=True)]
  transfers between devices with their start and end apart: 45 -> 45, of which waited for: 18 -> 16; matrix products, arithmetic and copies ran while one was open for 2% -> 3% of each run, Pallas kernels for 30% -> 31%
where the time goes in v11:
time: 168 us
  starting transfers between devices  62.8 us (37%)
  Pallas kernels  58.9 us (35%)
  waiting for transfers between devices  36.5 us (22%)
  other arithmetic  4.78 us (3%)
  local copies, waits for them, and re-layouts  3.16 us (2%)
    ppermute x43, starting transfers between devices, shards(): lax.ppermute(turn[s], 'grp', perms[s])  55.8 us
    ppermute x43, waiting for transfers between devices, shards(): lax.ppermute(turn[s], 'grp', perms[s])  34.3 us
    pallas_call x4, Pallas kernels, update(): pl.pallas_call(functools.partial(update_kernel, tuple(numbers), room, wid...  26.8 us
    pallas_call x8, Pallas kernels, factor(): pl.pallas_call(functools.partial(factor_kernel, tuple(tiles), head), out_...  24.7 us
    all_to_all x2, starting transfers between devices, exchange(): return lax.all_to_all(blocks, axis, split_axis=0, concat_axis=0, tiled=True)  7.09 us
    pallas_call x1, Pallas kernels, own_panels(): pl.pallas_call(functools.partial(own_kernel, choices, len(blocks), width...  4 us
    select_n x17, other arithmetic, shards(): jnp.where(root, made[which][n], value)  3.65 us
  transfers between devices with their start and end apart: 45, of which 16 were waited for; matrix products, arithmetic and copies ran while one was open for 3% of the time, Pallas kernels for 31%

profile of v11, /device:TPU:0, one launch (start us, length us, event | category | flops | bytes accessed | tf_op | source)
XLA Modules:
  0.0 167.7 jit_solution(3843671951128893002)
XLA Ops:
  1.4 3.8 %factor.8 = (bf16[256,512]{1,0:T(8,128)(2,1)S(1)}, bf16[256,512]{1,0:T(8,128)(2,1)S(1)}, bf16[256,512]{1,0:T(8,128)(2,1)S(1)}, bf16[256,512]{1,0:T(8,128)(2,1)S(...) custom-call(s32[32,4]{1,0:T(8,128)S(1)} %copy.54.mask, bf16[8192,1024]{1,0:T(8,128)(2,1)} %bitcast.9, ...), custom_call_target="tpu_custom_call" | custom-call | flops 805306368 | bytes 2097152 | tf_op jit(solution)/shard_map/factor/pallas_call | solution.py:178
  5.2 3.1 %collective-permute-start = (bf16[256,512]{1,0:T(8,128)(2,1)S(1)}, bf16[256,512]{1,0:T(8,128)(2,1)S(1)}, u32[]{:S(2)}, u32[]{:S(2)}) collective-permute-start(bf16[256,512]{1,0:T(8,128)(2,1)S(1)} %get-tuple-element.146.refs_18_), channel_id=1, source_target_pairs={{0,2},{1,3},{2,4},{3,5},{4,6},{5,7},{6,0},{7,1},{8,10},{9,11},{10,... | collective-permute-start | bytes 786440 | tf_op jit(solution)/shard_map/ppermute | solution.py:556
  8.3 1.5 collective-permute-start.1
  9.8 1.6 collective-permute-start.4
  11.9 3.0 %factor.9 = (bf16[256,512]{1,0:T(8,128)(2,1)S(1)}, bf16[256,512]{1,0:T(8,128)(2,1)S(1)}, bf16[256,512]{1,0:T(8,128)(2,1)S(1)}, bf16[256,512]{1,0:T(8,128)(2,1)S(1)}) custom-call(s32[32,4]{1,0:T(8,128)S(1)} %copy.54.mask, bf16[8192,1024]{1,0:T(8,128)(2,1)} %bitcast.10, bf16[4,256,256]{2,1,0:T(8,128)(2,1)S(1)} %get-tuple-element.228.refs_0_, ...), custom_call_target="tpu_custom_call" | custom-call | flops 805306368 | bytes 2097152 | tf_op jit(solution)/shard_map/factor/pallas_call | solution.py:178
  14.9 2.6 %collective-permute-done.refs_19_.refs_0_ = bf16[256,512]{1,0:T(8,128)(2,1)S(1)} collective-permute-done((bf16[256,512]{1,0:T(8,128)(2,1)S(1)}, bf16[256,512]{1,0:T(8,128)(2,1)S(1)}, u32[]{:S(2)}, u32[]{:S(2)}) %collective-permute-start) | collective-permute-done | bytes 262176 | tf_op jit(solution)/shard_map/ppermute | solution.py:556
  17.6 1.6 collective-permute-start.2
  19.2 1.5 collective-permute-start.3
  20.7 2.3 %collective-permute-done.4.refs_2_ = bf16[256,512]{1,0:T(8,128)(2,1)S(1)} collective-permute-done((bf16[256,512]{1,0:T(8,128)(2,1)S(1)}, bf16[256,512]{1,0:T(8,128)(2,1)S(1)}, u32[]{:S(2)}, u32[]{:S(2)}) %collective-permute-start.4) | collective-permute-done | bytes 262176 | tf_op jit(solution)/shard_map/ppermute | solution.py:556
  23.2 1.6 collective-permute-start.8
  24.8 1.5 collective-permute-start.9
  26.4 3.0 %factor.10 = (bf16[256,512]{1,0:T(8,128)(2,1)S(1)}, bf16[256,512]{1,0:T(8,128)(2,1)S(1)}, bf16[256,512]{1,0:T(8,128)(2,1)S(1)}, bf16[256,512]{1,0:T(8,128)(2,1)S(1)}) custom-call(s32[32,4]{1,0:T(8,128)S(1)} %copy.54.mask, bf16[8192,1024]{1,0:T(8,128)(2,1)} %bitcast.11, bf16[4,256,256]{2,1,0:T(8,128)(2,1)S(1)} %get-tuple-element.228.refs_0_, ...), custom_call_target="tpu_custom_call" | custom-call | flops 805306368 | bytes 2097152 | tf_op jit(solution)/shard_map/factor/pallas_call | solution.py:178
  29.5 1.6 collective-permute-start.6
  31.9 2.3 %collective-permute-done.8.refs_6_ = bf16[256,512]{1,0:T(8,128)(2,1)S(1)} collective-permute-done((bf16[256,512]{1,0:T(8,128)(2,1)S(1)}, bf16[256,512]{1,0:T(8,128)(2,1)S(1)}, u32[]{:S(2)}, u32[]{:S(2)}) %collective-permute-start.8) | collective-permute-done | bytes 262176 | tf_op jit(solution)/shard_map/ppermute | solution.py:556
  35.0 1.1 collective-permute-start.12
  36.1 1.5 collective-permute-start.13
  37.6 3.0 %factor.11 = (bf16[256,512]{1,0:T(8,128)(2,1)S(1)}, bf16[256,512]{1,0:T(8,128)(2,1)S(1)}, bf16[256,512]{1,0:T(8,128)(2,1)S(1)}, bf16[256,512]{1,0:T(8,128)(2,1)S(1)}) custom-call(s32[32,4]{1,0:T(8,128)S(1)} %copy.54.mask, bf16[8192,1024]{1,0:T(8,128)(2,1)} %bitcast.12, bf16[4,256,256]{2,1,0:T(8,128)(2,1)S(1)} %get-tuple-element.228.refs_0_, ...), custom_call_target="tpu_custom_call" | custom-call | flops 805306368 | bytes 2097152 | tf_op jit(solution)/shard_map/factor/pallas_call | solution.py:178
  40.7 1.6 collective-permute-start.10
  43.2 2.9 %collective-permute-done.12.refs_2_ = bf16[256,512]{1,0:T(8,128)(2,1)S(1)} collective-permute-done((bf16[256,512]{1,0:T(8,128)(2,1)S(1)}, bf16[256,512]{1,0:T(8,128)(2,1)S(1)}, u32[]{:S(2)}, u32[]{:S(2)}) %collective-permute-start.12) | collective-permute-done | bytes 262176 | tf_op jit(solution)/shard_map/ppermute | solution.py:556
  46.1 1.2 collective-permute-start.16
  47.3 1.5 collective-permute-start.17
  48.8 3.0 %factor.12 = (bf16[256,512]{1,0:T(8,128)(2,1)S(1)}, bf16[256,512]{1,0:T(8,128)(2,1)S(1)}, bf16[256,512]{1,0:T(8,128)(2,1)S(1)}, bf16[256,512]{1,0:T(8,128)(2,1)S(1)}) custom-call(s32[32,4]{1,0:T(8,128)S(1)} %copy.54.mask, bf16[8192,1024]{1,0:T(8,128)(2,1)} %bitcast.13, bf16[4,256,256]{2,1,0:T(8,128)(2,1)S(1)} %get-tuple-element.228.refs_0_, ...), custom_call_target="tpu_custom_call" | custom-call | flops 805306368 | bytes 2097152 | tf_op jit(solution)/shard_map/factor/pallas_call | solution.py:178
  51.9 1.6 collective-permute-start.14
  54.4 3.0 %collective-permute-done.16.refs_9_.refs_6_ = bf16[256,512]{1,0:T(8,128)(2,1)S(1)} collective-permute-done((bf16[256,512]{1,0:T(8,128)(2,1)S(1)}, bf16[256,512]{1,0:T(8,128)(2,1)S(1)}, u32[]{:S(2)}, u32[]{:S(2)}) %collective-permute-start.16) | collective-permute-done | bytes 262176 | tf_op jit(solution)/shard_map/ppermute | solution.py:556
  57.5 1.0 collective-permute-start.20
  58.5 1.5 collective-permute-start.21
  60.0 3.0 %factor.13 = (bf16[256,512]{1,0:T(8,128)(2,1)S(1)}, bf16[256,512]{1,0:T(8,128)(2,1)S(1)}, bf16[256,512]{1,0:T(8,128)(2,1)S(1)}, bf16[256,512]{1,0:T(8,128)(2,1)S(1)}) custom-call(s32[32,4]{1,0:T(8,128)S(1)} %copy.54.mask, bf16[8192,1024]{1,0:T(8,128)(2,1)} %bitcast.14, bf16[4,256,256]{2,1,0:T(8,128)(2,1)S(1)} %get-tuple-element.228.refs_0_, ...), custom_call_target="tpu_custom_call" | custom-call | flops 805306368 | bytes 2097152 | tf_op jit(solution)/shard_map/factor/pallas_call | solution.py:178
  63.2 1.6 collective-permute-start.18
  64.8 0.8 collective-permute-start.19
  65.6 3.0 %collective-permute-done.20.refs_8_.refs_10_ = bf16[256,512]{1,0:T(8,128)(2,1)S(1)} collective-permute-done((bf16[256,512]{1,0:T(8,128)(2,1)S(1)}, bf16[256,512]{1,0:T(8,128)(2,1)S(1)}, u32[]{:S(2)}, u32[]{:S(2)}) %collective-permute-start.20) | collective-permute-done | bytes 262176 | tf_op jit(solution)/shard_map/ppermute | solution.py:556
  68.7 1.2 collective-permute-start.22
  70.0 1.5 collective-permute-start.23
  71.5 3.0 %factor.14 = (bf16[256,512]{1,0:T(8,128)(2,1)S(1)}, bf16[256,512]{1,0:T(8,128)(2,1)S(1)}, bf16[256,512]{1,0:T(8,128)(2,1)S(1)}, bf16[256,512]{1,0:T(8,128)(2,1)S(1)}) custom-call(s32[32,4]{1,0:T(8,128)S(1)} %copy.54.mask, bf16[8192,1024]{1,0:T(8,128)(2,1)} %bitcast.15, bf16[4,256,256]{2,1,0:T(8,128)(2,1)S(1)} %get-tuple-element.228.refs_0_, ...), custom_call_target="tpu_custom_call" | custom-call | flops 805306368 | bytes 2097152 | tf_op jit(solution)/shard_map/factor/pallas_call | solution.py:178
  74.6 1.6 collective-permute-start.24
  76.9 3.1 %collective-permute-done.22.refs_7_.refs_14_ = bf16[256,512]{1,0:T(8,128)(2,1)S(1)} collective-permute-done((bf16[256,512]{1,0:T(8,128)(2,1)S(1)}, bf16[256,512]{1,0:T(8,128)(2,1)S(1)}, u32[]{:S(2)}, u32[]{:S(2)}) %collective-permute-start.22) | collective-permute-done | bytes 262176 | tf_op jit(solution)/shard_map/ppermute | solution.py:556
  80.1 0.9 collective-permute-start.26
  81.0 1.5 collective-permute-start.27
  82.5 3.0 %factor.15 = (bf16[256,512]{1,0:T(8,128)(2,1)S(1)}, bf16[256,512]{1,0:T(8,128)(2,1)S(1)}, bf16[256,512]{1,0:T(8,128)(2,1)S(1)}, bf16[256,512]{1,0:T(8,128)(2,1)S(1)}) custom-call(s32[32,4]{1,0:T(8,128)S(1)} %copy.54.mask, bf16[8192,1024]{1,0:T(8,128)(2,1)} %bitcast.16, bf16[4,256,256]{2,1,0:T(8,128)(2,1)S(1)} %get-tuple-element.228.refs_0_, ...), custom_call_target="tpu_custom_call" | custom-call | flops 805306368 | bytes 2097152 | tf_op jit(solution)/shard_map/factor/pallas_call | solution.py:178
  85.7 1.6 collective-permute-start.28
  88.2 3.1 %collective-permute-done.26.refs_16_.refs_2_ = bf16[256,512]{1,0:T(8,128)(2,1)S(1)} collective-permute-done((bf16[256,512]{1,0:T(8,128)(2,1)S(1)}, bf16[256,512]{1,0:T(8,128)(2,1)S(1)}, u32[]{:S(2)}, u32[]{:S(2)}) %collective-permute-start.26) | collective-permute-done | bytes 262176 | tf_op jit(solution)/shard_map/ppermute | solution.py:556
  91.4 0.9 collective-permute-start.30
  92.3 1.5 collective-permute-start.31
  93.8 4.0 %own_panels.1 = (bf16[512,1024]{1,0:T(8,128)(2,1)S(1)}, bf16[4,528,256]{2,1,0:T(8,128)(2,1)}) custom-call(s32[32,4]{1,0:T(8,128)S(1)} %copy.54.mask, s32[4]{0:T(128)S(1)} %bitcast.8, s32[1]{0:T(128)} %bitcast.1.me, bf16[8192,1024]{1,0:T(8,128)(2,1)} %bitcast.17, bf16[256,512]{1,0:T(8,128)(2,1)} %copy-done.7, bf16[256,512]{1,0:T(8,128)(2,1)} %copy-done.22, ...), custom_call_target="tpu_custom_call" | custom-call | flops 268435456 | bytes 2621440 | tf_op jit(solution)/shard_map/own_panels/pallas_call | solution.py:238
  97.9 0.9 select_select_fusion.2
  98.8 1.6 collective-permute-start.34
  103.3 1.7 %collective-permute-start.32 = (bf16[256,512]{1,0:T(8,128)(2,1)}, bf16[256,512]{1,0:T(8,128)(2,1)S(1)}, u32[]{:S(2)}, u32[]{:S(2)}) collective-permute-start(bf16[256,512]{1,0:T(8,128)(2,1)} %get-tuple-element.257), channel_id=1, source_target_pairs={{0,2},{1,3},{2,4},{3,5},{4,6},{5,7},{6,0},{7,1},{8,10},{9,11},{10,... | collective-permute-start | bytes 786440 | tf_op jit(solution)/shard_map/ppermute | solution.py:556
  105.0 1.5 collective-permute-start.33
  106.5 3.5 %all-to-all-start = ((bf16[4,528,256]{2,1,0:T(8,128)(2,1)}), bf16[4,528,256]{2,1,0:T(8,128)(2,1)S(1)}, u32[]{:S(2)}, u32[]{:S(2)}) async-start(bf16[4,528,256]{2,1,0:T(8,128)(2,1)} %get-tuple-element.254), calls=%async_computation | async-start | bytes 2162688 | tf_op jit(solution)/shard_map/all_to_all | solution.py:527
  110.1 1.1 select_select_fusion
  111.1 1.6 collective-permute-start.38
  114.1 1.5 collective-permute-start.37
  115.6 4.4 %update.4.refs_16_ = bf16[8192,1024]{1,0:T(8,128)(2,1)} custom-call(s32[8,44]{1,0:T(8,128)S(1)} %copy-done.8, s32[32,4]{1,0:T(8,128)S(1)} %copy.54.mask, s32[1]{0:T(128)} %bitcast.1.me, bf16[512,1024]{1,0:T(8,128)(2,1)S(1)} %get-tuple-element.251.own, bf16[8192,1024]{1,0:T(8,128)(2,1)} %bitcast.18, bf16[256,512]{1,0:T(8,128)(2,1)} %copy-done.10, ...), custom_call_target="tpu_custom_call" | custom-call | flops 2147483648 | bytes 8388608 | tf_op jit(solution)/shard_map/update/pallas_call | solution.py:403
  120.0 2.1 %collective-permute-done.38.refs_12_ = bf16[256,512]{1,0:T(8,128)(2,1)S(1)} collective-permute-done((bf16[256,512]{1,0:T(8,128)(2,1)S(1)}, bf16[256,512]{1,0:T(8,128)(2,1)S(1)}, u32[]{:S(2)}, u32[]{:S(2)}) %collective-permute-start.38) | collective-permute-done | bytes 262176 | tf_op jit(solution)/shard_map/ppermute | solution.py:556
  122.2 1.0 collective-permute-start.40
  123.3 4.4 %collective-permute-done.36.refs_14_ = bf16[256,512]{1,0:T(8,128)(2,1)S(1)} collective-permute-done((bf16[256,512]{1,0:T(8,128)(2,1)S(1)}, bf16[256,512]{1,0:T(8,128)(2,1)S(1)}, u32[]{:S(2)}, u32[]{:S(2)}) %collective-permute-start.36) | collective-permute-done | bytes 262176 | tf_op jit(solution)/shard_map/ppermute | solution.py:556
  128.5 4.4 %collective-permute-done.40.refs_0_ = bf16[256,512]{1,0:T(8,128)(2,1)S(1)} collective-permute-done((bf16[256,512]{1,0:T(8,128)(2,1)S(1)}, bf16[256,512]{1,0:T(8,128)(2,1)S(1)}, u32[]{:S(2)}, u32[]{:S(2)}) %collective-permute-start.40) | collective-permute-done | bytes 262176 | tf_op jit(solution)/shard_map/ppermute | solution.py:556
  133.1 1.7 %relay.1 = bf16[8,272,256]{2,1,0:T(8,128)(2,1)} custom-call(s32[4,2]{1,0:T(4,128)S(1)} %copy.51.labels, bf16[4,528,256]{2,1,0:T(8,128)(2,1)S(1)} %all-to-all-done.arrived), custom_call_target="tpu_custom_call" | custom-call | bytes 2097152 | tf_op jit(solution)/shard_map/relay/pallas_call | solution.py:278
  134.9 3.6 %all-to-all-start.1 = ((bf16[8,272,256]{2,1,0:T(8,128)(2,1)}), bf16[8,272,256]{2,1,0:T(8,128)(2,1)S(1)}, u32[]{:S(2)}, u32[]{:S(2)}) async-start(bf16[8,272,256]{2,1,0:T(8,128)(2,1)} %relay.1), calls=%async_computation.1 | async-start | bytes 2228224 | tf_op jit(solution)/shard_map/all_to_all | solution.py:527
  138.5 1.9 %collective-permute-start.42 = (bf16[256,512]{1,0:T(8,128)(2,1)}, bf16[256,512]{1,0:T(8,128)(2,1)S(1)}, u32[]{:S(2)}, u32[]{:S(2)}) collective-permute-start(bf16[256,512]{1,0:T(8,128)(2,1)} %broadcast_select_fusion), channel_id=1, source_target_pairs={{0,1},{1,0},{2,3},{3,2},{4,5},{5,4},{6,7},{7,6},{8,9},{9,8},{10,11... | collective-permute-start | bytes 786440 | tf_op jit(solution)/shard_map/ppermute | solution.py:556
  140.4 9.4 %update.5.refs_16_ = bf16[8192,1024]{1,0:T(8,128)(2,1)} custom-call(s32[8,44]{1,0:T(8,128)S(1)} %copy-done.8, s32[32,4]{1,0:T(8,128)S(1)} %copy.54.mask, s32[1]{0:T(128)} %bitcast.1.me, bf16[512,1024]{1,0:T(8,128)(2,1)S(1)} %get-tuple-element.251.own, bf16[8192,1024]{1,0:T(8,128)(2,1)} %bitcast.19, ...), custom_call_target="tpu_custom_call", output_to_operand_aliasing={{}: (21, {})} | custom-call | flops 4294967296 | bytes 16777216 | tf_op jit(solution)/shard_map/update/pallas_call | solution.py:403
  149.8 9.4 %update.6.refs_3_ = bf16[8192,1024]{1,0:T(8,128)(2,1)} custom-call(s32[8,44]{1,0:T(8,128)S(1)} %copy-done.8, s32[32,4]{1,0:T(8,128)S(1)} %copy.54.mask, s32[1]{0:T(128)} %bitcast.1.me, bf16[512,1024]{1,0:T(8,128)(2,1)S(1)} %get-tuple-element.251.own, bf16[8192,1024]{1,0:T(8,128)(2,1)} %bitcast.20, ...), custom_call_target="tpu_custom_call", output_to_operand_aliasing={{}: (21, {})} | custom-call | flops 4294967296 | bytes 16777216 | tf_op jit(solution)/shard_map/update/pallas_call | solution.py:403
  159.9 3.7 %update.7 = bf16[8192,1024]{1,0:T(8,128)(2,1)} custom-call(s32[8,44]{1,0:T(8,128)S(1)} %copy-done.8, s32[32,4]{1,0:T(8,128)S(1)} %copy.54.mask, s32[1]{0:T(128)} %bitcast.1.me, bf16[512,1024]{1,0:T(8,128)(2,1)S(1)} %get-tuple-element.251.own, bf16[8192,1024]{1,0:T(8,128)(2,1)} %bitcast.21, ...), custom_call_target="tpu_custom_call", output_to_operand_aliasing={{}: (8, {})} | custom-call | flops 1073741824 | bytes 4194304 | tf_op jit(solution)/shard_map/update/pallas_call | solution.py:403
  163.6 2.2 %all-to-all-done.1.arrived = bf16[8,272,256]{2,1,0:T(8,128)(2,1)S(1)} async-done(((bf16[8,272,256]{2,1,0:T(8,128)(2,1)}), bf16[8,272,256]{2,1,0:T(8,128)(2,1)S(1)}, u32[]{:S(2)}, u32[]{:S(2)}) %all-to-all-start.1) | async-done | bytes 1114144 | tf_op jit(solution)/shard_map/all_to_all | solution.py:527
  166.0 1.7 %sum_parents.1 = f32[4,256,256]{2,1,0:T(8,128)} custom-call(s32[8]{0:T(128)S(1)} %convert_reduce_fusion.labels, bf16[8,272,256]{2,1,0:T(8,128)(2,1)S(1)} %all-to-all-done.1.arrived), custom_call_target="tpu_custom_call" | custom-call | bytes 2097152 | tf_op jit(solution)/shard_map/sum_parents/pallas_call | solution.py:301
  (169 shorter events, 13.6 us)
Async XLA Ops:
  5.2 9.7 %copy-start.6 = (bf16[256,512]{1,0:T(8,128)(2,1)}, bf16[256,512]{1,0:T(8,128)(2,1)S(1)}, u32[]{:S(2)}) copy-start(bf16[256,512]{1,0:T(8,128)(2,1)S(1)} %get-tuple-element.146.refs_18_) | copy-start | bytes 786436
  5.2 12.2 %collective-permute-start = (bf16[256,512]{1,0:T(8,128)(2,1)S(1)}, bf16[256,512]{1,0:T(8,128)(2,1)S(1)}, u32[]{:S(2)}, u32[]{:S(2)}) collective-permute-start(bf16[256,512]{1,0:T(8,128)(2,1)S(1)} %get-tuple-element.146.refs_18_), channel_id=1, source_target_pairs={{0,2},{1,3},{2,4},{3,5},{4,6},{5,7},{6,0},{7,1},{8,10},{9,11},{10,... | collective-permute-start | bytes 786440 | tf_op jit(solution)/shard_map/ppermute | solution.py:556
  8.3 9.2 %collective-permute-start.1 = (bf16[256,512]{1,0:T(8,128)(2,1)S(1)}, bf16[256,512]{1,0:T(8,128)(2,1)S(1)}, u32[]{:S(2)}, u32[]{:S(2)}) collective-permute-start(bf16[256,512]{1,0:T(8,128)(2,1)S(1)} %get-tuple-element.147), channel_id=1, source_target_pairs={{0,1},{1,0},{2,3},{3,2},{4,5},{5,4},{6,7},{7,6},{8,9},{9,8},{10,11... | collective-permute-start | bytes 786440 | tf_op jit(solution)/shard_map/ppermute | solution.py:556
  9.8 13.3 %collective-permute-start.4 = (bf16[256,512]{1,0:T(8,128)(2,1)S(1)}, bf16[256,512]{1,0:T(8,128)(2,1)S(1)}, u32[]{:S(2)}, u32[]{:S(2)}) collective-permute-start(bf16[256,512]{1,0:T(8,128)(2,1)S(1)} %get-tuple-element.148), channel_id=1, source_target_pairs={{0,2},{1,3},{2,4},{3,5},{4,6},{5,7},{6,0},{7,1},{8,10},{9,11},{10,... | collective-permute-start | bytes 786440 | tf_op jit(solution)/shard_map/ppermute | solution.py:556
  11.4 11.8 %collective-permute-start.5 = (bf16[256,512]{1,0:T(8,128)(2,1)S(1)}, bf16[256,512]{1,0:T(8,128)(2,1)S(1)}, u32[]{:S(2)}, u32[]{:S(2)}) collective-permute-start(bf16[256,512]{1,0:T(8,128)(2,1)S(1)} %get-tuple-element.149), channel_id=1, source_target_pairs={{0,1},{1,0},{2,3},{3,2},{4,5},{5,4},{6,7},{7,6},{8,9},{9,8},{10,11... | collective-permute-start | bytes 786440 | tf_op jit(solution)/shard_map/ppermute | solution.py:556
  17.6 11.8 %collective-permute-start.2 = (bf16[256,512]{1,0:T(8,128)(2,1)S(1)}, bf16[256,512]{1,0:T(8,128)(2,1)S(1)}, u32[]{:S(2)}, u32[]{:S(2)}) collective-permute-start(bf16[256,512]{1,0:T(8,128)(2,1)S(1)} %get-tuple-element.156), channel_id=1, source_target_pairs={{0,2},{1,3},{2,4},{3,5},{4,6},{5,7},{6,0},{7,1},{8,10},{9,11},{10,... | collective-permute-start | bytes 786440 | tf_op jit(solution)/shard_map/ppermute | solution.py:556
  19.2 10.2 %collective-permute-start.3 = (bf16[256,512]{1,0:T(8,128)(2,1)S(1)}, bf16[256,512]{1,0:T(8,128)(2,1)S(1)}, u32[]{:S(2)}, u32[]{:S(2)}) collective-permute-start(bf16[256,512]{1,0:T(8,128)(2,1)S(1)} %get-tuple-element.157), channel_id=1, source_target_pairs={{0,1},{1,0},{2,3},{3,2},{4,5},{5,4},{6,7},{7,6},{8,9},{9,8},{10,11... | collective-permute-start | bytes 786440 | tf_op jit(solution)/shard_map/ppermute | solution.py:556
  23.0 6.3 %copy-start.30 = (bf16[256,512]{1,0:T(8,128)(2,1)}, bf16[256,512]{1,0:T(8,128)(2,1)S(1)}, u32[]{:S(2)}) copy-start(bf16[256,512]{1,0:T(8,128)(2,1)S(1)} %collective-permute-done.4.refs_2_) | copy-start | bytes 786436
  23.1 6.2 %copy-start.31 = (bf16[256,512]{1,0:T(8,128)(2,1)}, bf16[256,512]{1,0:T(8,128)(2,1)S(1)}, u32[]{:S(2)}) copy-start(bf16[256,512]{1,0:T(8,128)(2,1)S(1)} %collective-permute-done.5.refs_3_) | copy-start | bytes 786436
  23.2 11.1 %collective-permute-start.8 = (bf16[256,512]{1,0:T(8,128)(2,1)S(1)}, bf16[256,512]{1,0:T(8,128)(2,1)S(1)}, u32[]{:S(2)}, u32[]{:S(2)}) collective-permute-start(bf16[256,512]{1,0:T(8,128)(2,1)S(1)} %get-tuple-element.165), channel_id=1, source_target_pairs={{0,2},{1,3},{2,4},{3,5},{4,6},{5,7},{6,0},{7,1},{8,10},{9,11},{10,... | collective-permute-start | bytes 786440 | tf_op jit(solution)/shard_map/ppermute | solution.py:556
  24.8 9.5 %collective-permute-start.9 = (bf16[256,512]{1,0:T(8,128)(2,1)S(1)}, bf16[256,512]{1,0:T(8,128)(2,1)S(1)}, u32[]{:S(2)}, u32[]{:S(2)}) collective-permute-start(bf16[256,512]{1,0:T(8,128)(2,1)S(1)} %get-tuple-element.166), channel_id=1, source_target_pairs={{0,1},{1,0},{2,3},{3,2},{4,5},{5,4},{6,7},{7,6},{8,9},{9,8},{10,11... | collective-permute-start | bytes 786440 | tf_op jit(solution)/shard_map/ppermute | solution.py:556
  29.5 11.1 %collective-permute-start.6 = (bf16[256,512]{1,0:T(8,128)(2,1)S(1)}, bf16[256,512]{1,0:T(8,128)(2,1)S(1)}, u32[]{:S(2)}, u32[]{:S(2)}) collective-permute-start(bf16[256,512]{1,0:T(8,128)(2,1)S(1)} %get-tuple-element.170), channel_id=1, source_target_pairs={{0,2},{1,3},{2,4},{3,5},{4,6},{5,7},{6,0},{7,1},{8,10},{9,11},{10,... | collective-permute-start | bytes 786440 | tf_op jit(solution)/shard_map/ppermute | solution.py:556
  31.1 9.5 %collective-permute-start.7 = (bf16[256,512]{1,0:T(8,128)(2,1)S(1)}, bf16[256,512]{1,0:T(8,128)(2,1)S(1)}, u32[]{:S(2)}, u32[]{:S(2)}) collective-permute-start(bf16[256,512]{1,0:T(8,128)(2,1)S(1)} %get-tuple-element.171), channel_id=1, source_target_pairs={{0,1},{1,0},{2,3},{3,2},{4,5},{5,4},{6,7},{7,6},{8,9},{9,8},{10,11... | collective-permute-start | bytes 786440 | tf_op jit(solution)/shard_map/ppermute | solution.py:556
  34.4 6.2 %copy-start.35 = (bf16[256,512]{1,0:T(8,128)(2,1)}, bf16[256,512]{1,0:T(8,128)(2,1)S(1)}, u32[]{:S(2)}) copy-start(bf16[256,512]{1,0:T(8,128)(2,1)S(1)} %collective-permute-done.9.refs_7_) | copy-start | bytes 786436
  35.0 11.0 %collective-permute-start.12 = (bf16[256,512]{1,0:T(8,128)(2,1)S(1)}, bf16[256,512]{1,0:T(8,128)(2,1)S(1)}, u32[]{:S(2)}, u32[]{:S(2)}) collective-permute-start(bf16[256,512]{1,0:T(8,128)(2,1)S(1)} %get-tuple-element.179), channel_id=1, source_target_pairs={{0,2},{1,3},{2,4},{3,5},{4,6},{5,7},{6,0},{7,1},{8,10},{9,11},{10,... | collective-permute-start | bytes 786440 | tf_op jit(solution)/shard_map/ppermute | solution.py:556
  36.1 10.0 %collective-permute-start.13 = (bf16[256,512]{1,0:T(8,128)(2,1)S(1)}, bf16[256,512]{1,0:T(8,128)(2,1)S(1)}, u32[]{:S(2)}, u32[]{:S(2)}) collective-permute-start(bf16[256,512]{1,0:T(8,128)(2,1)S(1)} %get-tuple-element.180), channel_id=1, source_target_pairs={{0,1},{1,0},{2,3},{3,2},{4,5},{5,4},{6,7},{7,6},{8,9},{9,8},{10,11... | collective-permute-start | bytes 786440 | tf_op jit(solution)/shard_map/ppermute | solution.py:556
  40.7 11.1 %collective-permute-start.10 = (bf16[256,512]{1,0:T(8,128)(2,1)S(1)}, bf16[256,512]{1,0:T(8,128)(2,1)S(1)}, u32[]{:S(2)}, u32[]{:S(2)}) collective-permute-start(bf16[256,512]{1,0:T(8,128)(2,1)S(1)} %get-tuple-element.184), channel_id=1, source_target_pairs={{0,2},{1,3},{2,4},{3,5},{4,6},{5,7},{6,0},{7,1},{8,10},{9,11},{10,... | collective-permute-start | bytes 786440 | tf_op jit(solution)/shard_map/ppermute | solution.py:556
  42.3 9.5 %collective-permute-start.11 = (bf16[256,512]{1,0:T(8,128)(2,1)S(1)}, bf16[256,512]{1,0:T(8,128)(2,1)S(1)}, u32[]{:S(2)}, u32[]{:S(2)}) collective-permute-start(bf16[256,512]{1,0:T(8,128)(2,1)S(1)} %get-tuple-element.185), channel_id=1, source_target_pairs={{0,1},{1,0},{2,3},{3,2},{4,5},{5,4},{6,7},{7,6},{8,9},{9,8},{10,11... | collective-permute-start | bytes 786440 | tf_op jit(solution)/shard_map/ppermute | solution.py:556
  46.0 5.8 %copy-start.32 = (bf16[256,512]{1,0:T(8,128)(2,1)}, bf16[256,512]{1,0:T(8,128)(2,1)S(1)}, u32[]{:S(2)}) copy-start(bf16[256,512]{1,0:T(8,128)(2,1)S(1)} %collective-permute-done.12.refs_2_) | copy-start | bytes 786436
  46.0 5.8 %copy-start.33 = (bf16[256,512]{1,0:T(8,128)(2,1)}, bf16[256,512]{1,0:T(8,128)(2,1)S(1)}, u32[]{:S(2)}) copy-start(bf16[256,512]{1,0:T(8,128)(2,1)S(1)} %collective-permute-done.13.refs_3_) | copy-start | bytes 786436
  46.1 11.3 %collective-permute-start.16 = (bf16[256,512]{1,0:T(8,128)(2,1)S(1)}, bf16[256,512]{1,0:T(8,128)(2,1)S(1)}, u32[]{:S(2)}, u32[]{:S(2)}) collective-permute-start(bf16[256,512]{1,0:T(8,128)(2,1)S(1)} %get-tuple-element.193), channel_id=1, source_target_pairs={{0,2},{1,3},{2,4},{3,5},{4,6},{5,7},{6,0},{7,1},{8,10},{9,11},{10,... | collective-permute-start | bytes 786440 | tf_op jit(solution)/shard_map/ppermute | solution.py:556
  47.3 10.1 %collective-permute-start.17 = (bf16[256,512]{1,0:T(8,128)(2,1)S(1)}, bf16[256,512]{1,0:T(8,128)(2,1)S(1)}, u32[]{:S(2)}, u32[]{:S(2)}) collective-permute-start(bf16[256,512]{1,0:T(8,128)(2,1)S(1)} %get-tuple-element.194), channel_id=1, source_target_pairs={{0,1},{1,0},{2,3},{3,2},{4,5},{5,4},{6,7},{7,6},{8,9},{9,8},{10,11... | collective-permute-start | bytes 786440 | tf_op jit(solution)/shard_map/ppermute | solution.py:556
  51.9 11.1 %collective-permute-start.14 = (bf16[256,512]{1,0:T(8,128)(2,1)S(1)}, bf16[256,512]{1,0:T(8,128)(2,1)S(1)}, u32[]{:S(2)}, u32[]{:S(2)}) collective-permute-start(bf16[256,512]{1,0:T(8,128)(2,1)S(1)} %get-tuple-element.198), channel_id=1, source_target_pairs={{0,2},{1,3},{2,4},{3,5},{4,6},{5,7},{6,0},{7,1},{8,10},{9,11},{10,... | collective-permute-start | bytes 786440 | tf_op jit(solution)/shard_map/ppermute | solution.py:556
  53.6 9.5 %collective-permute-start.15 = (bf16[256,512]{1,0:T(8,128)(2,1)S(1)}, bf16[256,512]{1,0:T(8,128)(2,1)S(1)}, u32[]{:S(2)}, u32[]{:S(2)}) collective-permute-start(bf16[256,512]{1,0:T(8,128)(2,1)S(1)} %get-tuple-element.199), channel_id=1, source_target_pairs={{0,1},{1,0},{2,3},{3,2},{4,5},{5,4},{6,7},{7,6},{8,9},{9,8},{10,11... | collective-permute-start | bytes 786440 | tf_op jit(solution)/shard_map/ppermute | solution.py:556
  57.5 11.1 %collective-permute-start.20 = (bf16[256,512]{1,0:T(8,128)(2,1)S(1)}, bf16[256,512]{1,0:T(8,128)(2,1)S(1)}, u32[]{:S(2)}, u32[]{:S(2)}) collective-permute-start(bf16[256,512]{1,0:T(8,128)(2,1)S(1)} %get-tuple-element.207), channel_id=1, source_target_pairs={{0,2},{1,3},{2,4},{3,5},{4,6},{5,7},{6,0},{7,1},{8,10},{9,11},{10,... | collective-permute-start | bytes 786440 | tf_op jit(solution)/shard_map/ppermute | solution.py:556
  58.5 10.1 %collective-permute-start.21 = (bf16[256,512]{1,0:T(8,128)(2,1)S(1)}, bf16[256,512]{1,0:T(8,128)(2,1)S(1)}, u32[]{:S(2)}, u32[]{:S(2)}) collective-permute-start(bf16[256,512]{1,0:T(8,128)(2,1)S(1)} %get-tuple-element.208), channel_id=1, source_target_pairs={{0,1},{1,0},{2,3},{3,2},{4,5},{5,4},{6,7},{7,6},{8,9},{9,8},{10,11... | collective-permute-start | bytes 786440 | tf_op jit(solution)/shard_map/ppermute | solution.py:556
  63.2 11.3 %collective-permute-start.18 = (bf16[256,512]{1,0:T(8,128)(2,1)S(1)}, bf16[256,512]{1,0:T(8,128)(2,1)S(1)}, u32[]{:S(2)}, u32[]{:S(2)}) collective-permute-start(bf16[256,512]{1,0:T(8,128)(2,1)S(1)} %get-tuple-element.212), channel_id=1, source_target_pairs={{0,2},{1,3},{2,4},{3,5},{4,6},{5,7},{6,0},{7,1},{8,10},{9,11},{10,... | collective-permute-start | bytes 786440 | tf_op jit(solution)/shard_map/ppermute | solution.py:556
  64.8 9.7 %collective-permute-start.19 = (bf16[256,512]{1,0:T(8,128)(2,1)S(1)}, bf16[256,512]{1,0:T(8,128)(2,1)S(1)}, u32[]{:S(2)}, u32[]{:S(2)}) collective-permute-start(bf16[256,512]{1,0:T(8,128)(2,1)S(1)} %get-tuple-element.213), channel_id=1, source_target_pairs={{0,1},{1,0},{2,3},{3,2},{4,5},{5,4},{6,7},{7,6},{8,9},{9,8},{10,11... | collective-permute-start | bytes 786440 | tf_op jit(solution)/shard_map/ppermute | solution.py:556
  68.6 5.8 %copy-start.20 = (bf16[256,512]{1,0:T(8,128)(2,1)}, bf16[256,512]{1,0:T(8,128)(2,1)S(1)}, u32[]{:S(2)}) copy-start(bf16[256,512]{1,0:T(8,128)(2,1)S(1)} %collective-permute-done.20.refs_8_.refs_10_) | copy-start | bytes 786436
  68.7 5.8 %copy-start.37 = (bf16[256,512]{1,0:T(8,128)(2,1)}, bf16[256,512]{1,0:T(8,128)(2,1)S(1)}, u32[]{:S(2)}) copy-start(bf16[256,512]{1,0:T(8,128)(2,1)S(1)} %collective-permute-done.21.refs_11_) | copy-start | bytes 786436
  68.7 11.3 %collective-permute-start.22 = (bf16[256,512]{1,0:T(8,128)(2,1)S(1)}, bf16[256,512]{1,0:T(8,128)(2,1)S(1)}, u32[]{:S(2)}, u32[]{:S(2)}) collective-permute-start(bf16[256,512]{1,0:T(8,128)(2,1)S(1)} %get-tuple-element.221), channel_id=1, source_target_pairs={{0,2},{1,3},{2,4},{3,5},{4,6},{5,7},{6,0},{7,1},{8,10},{9,11},{10,... | collective-permute-start | bytes 786440 | tf_op jit(solution)/shard_map/ppermute | solution.py:556
  70.0 10.1 %collective-permute-start.23 = (bf16[256,512]{1,0:T(8,128)(2,1)S(1)}, bf16[256,512]{1,0:T(8,128)(2,1)S(1)}, u32[]{:S(2)}, u32[]{:S(2)}) collective-permute-start(bf16[256,512]{1,0:T(8,128)(2,1)S(1)} %get-tuple-element.222), channel_id=1, source_target_pairs={{0,1},{1,0},{2,3},{3,2},{4,5},{5,4},{6,7},{7,6},{8,9},{9,8},{10,11... | collective-permute-start | bytes 786440 | tf_op jit(solution)/shard_map/ppermute | solution.py:556
  74.6 11.0 %collective-permute-start.24 = (bf16[256,512]{1,0:T(8,128)(2,1)S(1)}, bf16[256,512]{1,0:T(8,128)(2,1)S(1)}, u32[]{:S(2)}, u32[]{:S(2)}) collective-permute-start(bf16[256,512]{1,0:T(8,128)(2,1)S(1)} %get-tuple-element.226), channel_id=1, source_target_pairs={{0,2},{1,3},{2,4},{3,5},{4,6},{5,7},{6,0},{7,1},{8,10},{9,11},{10,... | collective-permute-start | bytes 786440 | tf_op jit(solution)/shard_map/ppermute | solution.py:556
  76.2 9.4 %collective-permute-start.25 = (bf16[256,512]{1,0:T(8,128)(2,1)S(1)}, bf16[256,512]{1,0:T(8,128)(2,1)S(1)}, u32[]{:S(2)}, u32[]{:S(2)}) collective-permute-start(bf16[256,512]{1,0:T(8,128)(2,1)S(1)} %get-tuple-element.227), channel_id=1, source_target_pairs={{0,1},{1,0},{2,3},{3,2},{4,5},{5,4},{6,7},{7,6},{8,9},{9,8},{10,11... | collective-permute-start | bytes 786440 | tf_op jit(solution)/shard_map/ppermute | solution.py:556
  80.1 11.1 %collective-permute-start.26 = (bf16[256,512]{1,0:T(8,128)(2,1)S(1)}, bf16[256,512]{1,0:T(8,128)(2,1)S(1)}, u32[]{:S(2)}, u32[]{:S(2)}) collective-permute-start(bf16[256,512]{1,0:T(8,128)(2,1)S(1)} %get-tuple-element.237), channel_id=1, source_target_pairs={{0,2},{1,3},{2,4},{3,5},{4,6},{5,7},{6,0},{7,1},{8,10},{9,11},{10,... | collective-permute-start | bytes 786440 | tf_op jit(solution)/shard_map/ppermute | solution.py:556
  81.0 10.2 %collective-permute-start.27 = (bf16[256,512]{1,0:T(8,128)(2,1)S(1)}, bf16[256,512]{1,0:T(8,128)(2,1)S(1)}, u32[]{:S(2)}, u32[]{:S(2)}) collective-permute-start(bf16[256,512]{1,0:T(8,128)(2,1)S(1)} %get-tuple-element.238), channel_id=1, source_target_pairs={{0,1},{1,0},{2,3},{3,2},{4,5},{5,4},{6,7},{7,6},{8,9},{9,8},{10,11... | collective-permute-start | bytes 786440 | tf_op jit(solution)/shard_map/ppermute | solution.py:556
  85.5 5.8 %copy-start = (bf16[256,512]{1,0:T(8,128)(2,1)}, bf16[256,512]{1,0:T(8,128)(2,1)S(1)}, u32[]{:S(2)}) copy-start(bf16[256,512]{1,0:T(8,128)(2,1)S(1)} %get-tuple-element.234.refs_11_) | copy-start | bytes 786436
  85.6 5.8 %copy-start.2 = (bf16[256,512]{1,0:T(8,128)(2,1)}, bf16[256,512]{1,0:T(8,128)(2,1)S(1)}, u32[]{:S(2)}) copy-start(bf16[256,512]{1,0:T(8,128)(2,1)S(1)} %get-tuple-element.241.refs_14_) | copy-start | bytes 786436
  85.6 5.8 %copy-start.4 = (bf16[256,512]{1,0:T(8,128)(2,1)}, bf16[256,512]{1,0:T(8,128)(2,1)S(1)}, u32[]{:S(2)}) copy-start(bf16[256,512]{1,0:T(8,128)(2,1)S(1)} %get-tuple-element.231.refs_5_) | copy-start | bytes 786436
  85.6 5.8 %copy-start.7 = (bf16[256,512]{1,0:T(8,128)(2,1)}, bf16[256,512]{1,0:T(8,128)(2,1)S(1)}, u32[]{:S(2)}) copy-start(bf16[256,512]{1,0:T(8,128)(2,1)S(1)} %get-tuple-element.230.refs_0_) | copy-start | bytes 786436
  85.7 8.1 %copy-start.9 = (s32[1,1,4]{2,1,0:T(1,128)S(1)}, s32[1,1,4]{2,1,0:T(1,128)}, u32[]{:S(2)}) copy-start(s32[1,1,4]{2,1,0:T(1,128)} %param.8) | copy-start | bytes 52
  85.7 12.1 %collective-permute-start.28 = (bf16[256,512]{1,0:T(8,128)(2,1)S(1)}, bf16[256,512]{1,0:T(8,128)(2,1)S(1)}, u32[]{:S(2)}, u32[]{:S(2)}) collective-permute-start(bf16[256,512]{1,0:T(8,128)(2,1)S(1)} %get-tuple-element.242), channel_id=1, source_target_pairs={{0,2},{1,3},{2,4},{3,5},{4,6},{5,7},{6,0},{7,1},{8,10},{9,11},{10,... | collective-permute-start | bytes 786440 | tf_op jit(solution)/shard_map/ppermute | solution.py:556
  87.4 10.5 %collective-permute-start.29 = (bf16[256,512]{1,0:T(8,128)(2,1)S(1)}, bf16[256,512]{1,0:T(8,128)(2,1)S(1)}, u32[]{:S(2)}, u32[]{:S(2)}) collective-permute-start(bf16[256,512]{1,0:T(8,128)(2,1)S(1)} %get-tuple-element.243), channel_id=1, source_target_pairs={{0,1},{1,0},{2,3},{3,2},{4,5},{5,4},{6,7},{7,6},{8,9},{9,8},{10,11... | collective-permute-start | bytes 786440 | tf_op jit(solution)/shard_map/ppermute | solution.py:556
  91.4 10.3 %collective-permute-start.30 = (bf16[256,512]{1,0:T(8,128)(2,1)S(1)}, bf16[256,512]{1,0:T(8,128)(2,1)S(1)}, u32[]{:S(2)}, u32[]{:S(2)}) collective-permute-start(bf16[256,512]{1,0:T(8,128)(2,1)S(1)} %get-tuple-element.247), channel_id=1, source_target_pairs={{0,2},{1,3},{2,4},{3,5},{4,6},{5,7},{6,0},{7,1},{8,10},{9,11},{10,... | collective-permute-start | bytes 786440 | tf_op jit(solution)/shard_map/ppermute | solution.py:556
  92.3 9.4 %collective-permute-start.31 = (bf16[256,512]{1,0:T(8,128)(2,1)S(1)}, bf16[256,512]{1,0:T(8,128)(2,1)S(1)}, u32[]{:S(2)}, u32[]{:S(2)}) collective-permute-start(bf16[256,512]{1,0:T(8,128)(2,1)S(1)} %get-tuple-element.248), channel_id=1, source_target_pairs={{0,1},{1,0},{2,3},{3,2},{4,5},{5,4},{6,7},{7,6},{8,9},{9,8},{10,11... | collective-permute-start | bytes 786440 | tf_op jit(solution)/shard_map/ppermute | solution.py:556
  98.8 11.3 %collective-permute-start.34 = (bf16[256,512]{1,0:T(8,128)(2,1)}, bf16[256,512]{1,0:T(8,128)(2,1)}, u32[]{:S(2)}, u32[]{:S(2)}) collective-permute-start(bf16[256,512]{1,0:T(8,128)(2,1)} %get-tuple-element.252), channel_id=1, source_target_pairs={{0,2},{1,3},{2,4},{3,5},{4,6},{5,7},{6,0},{7,1},{8,10},{9,11},{10,... | collective-permute-start | bytes 786440 | tf_op jit(solution)/shard_map/ppermute | solution.py:556
  100.3 9.7 %collective-permute-start.35 = (bf16[256,512]{1,0:T(8,128)(2,1)}, bf16[256,512]{1,0:T(8,128)(2,1)}, u32[]{:S(2)}, u32[]{:S(2)}) collective-permute-start(bf16[256,512]{1,0:T(8,128)(2,1)} %get-tuple-element.253), channel_id=1, source_target_pairs={{0,1},{1,0},{2,3},{3,2},{4,5},{5,4},{6,7},{7,6},{8,9},{9,8},{10,11... | collective-permute-start | bytes 786440 | tf_op jit(solution)/shard_map/ppermute | solution.py:556
  103.3 6.8 %copy-start.3 = (bf16[256,512]{1,0:T(8,128)(2,1)S(1)}, bf16[256,512]{1,0:T(8,128)(2,1)}, u32[]{:S(2)}) copy-start(bf16[256,512]{1,0:T(8,128)(2,1)} %copy-done.2) | copy-start | bytes 786436
  103.3 10.0 %collective-permute-start.32 = (bf16[256,512]{1,0:T(8,128)(2,1)}, bf16[256,512]{1,0:T(8,128)(2,1)S(1)}, u32[]{:S(2)}, u32[]{:S(2)}) collective-permute-start(bf16[256,512]{1,0:T(8,128)(2,1)} %get-tuple-element.257), channel_id=1, source_target_pairs={{0,2},{1,3},{2,4},{3,5},{4,6},{5,7},{6,0},{7,1},{8,10},{9,11},{10,... | collective-permute-start | bytes 786440 | tf_op jit(solution)/shard_map/ppermute | solution.py:556
  105.0 8.3 %collective-permute-start.33 = (bf16[256,512]{1,0:T(8,128)(2,1)}, bf16[256,512]{1,0:T(8,128)(2,1)S(1)}, u32[]{:S(2)}, u32[]{:S(2)}) collective-permute-start(bf16[256,512]{1,0:T(8,128)(2,1)} %get-tuple-element.258), channel_id=1, source_target_pairs={{0,1},{1,0},{2,3},{3,2},{4,5},{5,4},{6,7},{7,6},{8,9},{9,8},{10,11... | collective-permute-start | bytes 786440 | tf_op jit(solution)/shard_map/ppermute | solution.py:556
  106.5 26.4 %all-to-all-start = ((bf16[4,528,256]{2,1,0:T(8,128)(2,1)}), bf16[4,528,256]{2,1,0:T(8,128)(2,1)S(1)}, u32[]{:S(2)}, u32[]{:S(2)}) async-start(bf16[4,528,256]{2,1,0:T(8,128)(2,1)} %get-tuple-element.254), calls=%async_computation | async-start | bytes 2162688 | tf_op jit(solution)/shard_map/all_to_all | solution.py:527
  111.1 11.0 %collective-permute-start.38 = (bf16[256,512]{1,0:T(8,128)(2,1)S(1)}, bf16[256,512]{1,0:T(8,128)(2,1)S(1)}, u32[]{:S(2)}, u32[]{:S(2)}) collective-permute-start(bf16[256,512]{1,0:T(8,128)(2,1)S(1)} %get-tuple-element.261), channel_id=1, source_target_pairs={{0,2},{1,3},{2,4},{3,5},{4,6},{5,7},{6,0},{7,1},{8,10},{9,11},{10,... | collective-permute-start | bytes 786440 | tf_op jit(solution)/shard_map/ppermute | solution.py:556
  112.8 9.3 %collective-permute-start.39 = (bf16[256,512]{1,0:T(8,128)(2,1)S(1)}, bf16[256,512]{1,0:T(8,128)(2,1)S(1)}, u32[]{:S(2)}, u32[]{:S(2)}) collective-permute-start(bf16[256,512]{1,0:T(8,128)(2,1)S(1)} %get-tuple-element.262), channel_id=1, source_target_pairs={{0,1},{1,0},{2,3},{3,2},{4,5},{5,4},{6,7},{7,6},{8,9},{9,8},{10,11... | collective-permute-start | bytes 786440 | tf_op jit(solution)/shard_map/ppermute | solution.py:556
  113.3 6.7 %copy-start.40 = (bf16[256,512]{1,0:T(8,128)(2,1)}, bf16[256,512]{1,0:T(8,128)(2,1)S(1)}, u32[]{:S(2)}) copy-start(bf16[256,512]{1,0:T(8,128)(2,1)S(1)} %collective-permute-done.32.refs_10_) | copy-start | bytes 786436
  113.3 6.7 %copy-start.41 = (bf16[256,512]{1,0:T(8,128)(2,1)}, bf16[256,512]{1,0:T(8,128)(2,1)S(1)}, u32[]{:S(2)}) copy-start(bf16[256,512]{1,0:T(8,128)(2,1)S(1)} %collective-permute-done.33.refs_11_) | copy-start | bytes 786436
  113.4 14.4 %collective-permute-start.36 = (bf16[256,512]{1,0:T(8,128)(2,1)S(1)}, bf16[256,512]{1,0:T(8,128)(2,1)S(1)}, u32[]{:S(2)}, u32[]{:S(2)}) collective-permute-start(bf16[256,512]{1,0:T(8,128)(2,1)S(1)} %get-tuple-element.265), channel_id=1, source_target_pairs={{0,2},{1,3},{2,4},{3,5},{4,6},{5,7},{6,0},{7,1},{8,10},{9,11},{10,... | collective-permute-start | bytes 786440 | tf_op jit(solution)/shard_map/ppermute | solution.py:556
  114.1 13.6 %collective-permute-start.37 = (bf16[256,512]{1,0:T(8,128)(2,1)S(1)}, bf16[256,512]{1,0:T(8,128)(2,1)S(1)}, u32[]{:S(2)}, u32[]{:S(2)}) collective-permute-start(bf16[256,512]{1,0:T(8,128)(2,1)S(1)} %get-tuple-element.266), channel_id=1, source_target_pairs={{0,1},{1,0},{2,3},{3,2},{4,5},{5,4},{6,7},{7,6},{8,9},{9,8},{10,11... | collective-permute-start | bytes 786440 | tf_op jit(solution)/shard_map/ppermute | solution.py:556
  122.1 12.8 %copy-start.42 = (bf16[256,512]{1,0:T(8,128)(2,1)}, bf16[256,512]{1,0:T(8,128)(2,1)S(1)}, u32[]{:S(2)}) copy-start(bf16[256,512]{1,0:T(8,128)(2,1)S(1)} %collective-permute-done.38.refs_12_) | copy-start | bytes 786436
  122.1 12.8 %copy-start.43 = (bf16[256,512]{1,0:T(8,128)(2,1)}, bf16[256,512]{1,0:T(8,128)(2,1)S(1)}, u32[]{:S(2)}) copy-start(bf16[256,512]{1,0:T(8,128)(2,1)S(1)} %collective-permute-done.39.refs_13_) | copy-start | bytes 786436
  122.2 10.7 %collective-permute-start.40 = (bf16[256,512]{1,0:T(8,128)(2,1)S(1)}, bf16[256,512]{1,0:T(8,128)(2,1)S(1)}, u32[]{:S(2)}, u32[]{:S(2)}) collective-permute-start(bf16[256,512]{1,0:T(8,128)(2,1)S(1)} %get-tuple-element.270), channel_id=1, source_target_pairs={{0,2},{1,3},{2,4},{3,5},{4,6},{5,7},{6,0},{7,1},{8,10},{9,11},{10,... | collective-permute-start | bytes 786440 | tf_op jit(solution)/shard_map/ppermute | solution.py:556
  123.1 9.8 %collective-permute-start.41 = (bf16[256,512]{1,0:T(8,128)(2,1)S(1)}, bf16[256,512]{1,0:T(8,128)(2,1)S(1)}, u32[]{:S(2)}, u32[]{:S(2)}) collective-permute-start(bf16[256,512]{1,0:T(8,128)(2,1)S(1)} %get-tuple-element.271), channel_id=1, source_target_pairs={{0,1},{1,0},{2,3},{3,2},{4,5},{5,4},{6,7},{7,6},{8,9},{9,8},{10,11... | collective-permute-start | bytes 786440 | tf_op jit(solution)/shard_map/ppermute | solution.py:556
  127.7 7.2 %copy-start.46 = (bf16[256,512]{1,0:T(8,128)(2,1)}, bf16[256,512]{1,0:T(8,128)(2,1)S(1)}, u32[]{:S(2)}) copy-start(bf16[256,512]{1,0:T(8,128)(2,1)S(1)} %collective-permute-done.36.refs_14_) | copy-start | bytes 786436
  134.9 30.9 %all-to-all-start.1 = ((bf16[8,272,256]{2,1,0:T(8,128)(2,1)}), bf16[8,272,256]{2,1,0:T(8,128)(2,1)S(1)}, u32[]{:S(2)}, u32[]{:S(2)}) async-start(bf16[8,272,256]{2,1,0:T(8,128)(2,1)} %relay.1), calls=%async_computation.1 | async-start | bytes 2228224 | tf_op jit(solution)/shard_map/all_to_all | solution.py:527
  138.5 20.7 %collective-permute-start.42 = (bf16[256,512]{1,0:T(8,128)(2,1)}, bf16[256,512]{1,0:T(8,128)(2,1)S(1)}, u32[]{:S(2)}, u32[]{:S(2)}) collective-permute-start(bf16[256,512]{1,0:T(8,128)(2,1)} %broadcast_select_fusion), channel_id=1, source_target_pairs={{0,1},{1,0},{2,3},{3,2},{4,5},{5,4},{6,7},{7,6},{8,9},{9,8},{10,11... | collective-permute-start | bytes 786440 | tf_op jit(solution)/shard_map/ppermute | solution.py:556
  (32 other events, 146.3 us)
